TPU v7x, 32 devices: a whole 2x2x4 slice. The times are simulated.
32 devices in a mesh: gx: 4 (over x, core), bulk: 8 (over z, y).
Axes of the slice: x: 2, y: 2, z: 4, core: 2. Of those that a mesh axis runs over, the one named last changes fastest.
Arguments:
- basis: bfloat16 [8, 64, 131072], P(None, None, ('gx', 'bulk')), may hold values from -6 to 6
- near_blocks: bfloat16 [512, 8, 256, 256], P(('gx', 'bulk')), may hold values from -0.125 to 0.125
- near_src: int32 [512, 8], P(('gx', 'bulk')), may hold values from 0 to 47
- near_count: int32 [512], P(('gx', 'bulk')), may hold values from 1 to 8
- p2m: bfloat16 [512, 256, 128], P(('gx', 'bulk')), may hold values from -0.375 to 0.375
- m2l: bfloat16 [16, 128, 128], replicated, may hold values from -0.25 to 0.25
- send_list: int32 [32, 32, 4], P(('gx', 'bulk')), may hold values from 0 to 15
- send_count: int32 [32, 32], P(('gx', 'bulk')), may hold values from 0 to 4
- far_src: int32 [512, 32], P(('gx', 'bulk')), may hold values from 0 to 127
- far_class: int32 [512, 32], P(('gx', 'bulk')), may hold values from 0 to 15
Outputs:
- next_block: bfloat16 [64, 131072], P(None, ('gx', 'bulk'))
- projections: float32 [8, 64, 64], replicated
- factor: float32 [64, 64], replicated
All inputs are finite; a program needn't handle non-finite values.
Results may differ from a plain program's by a relative error of at most 0.012.
Values may be sent and summed in bfloat16 or wider, within the bound.
No kernel may reach another device: no remote copies, remote signals or barrier semaphores. Data moves between devices by JAX's collectives and lax.ppermute only.
A program may use at most 128 MiB of HBM per device.

v0:
```python
import jax
import jax.numpy as jnp
from jax import lax
from jax.sharding import PartitionSpec as P


def extended(array, sides, width):
    for axis, dim in sides:
        devices, length = (lax.axis_size(axis), array.shape[dim])
        up = [(i, (i + 1) % devices) for i in range(devices - 1)]
        down = [(j, i) for i, j in up]
        last = lax.slice_in_dim(array, length - width, length, axis=dim)
        first = lax.slice_in_dim(array, 0, width, axis=dim)
        before = lax.ppermute(last, axis, up)
        after = lax.ppermute(first, axis, down)
        array = jnp.concatenate([before, array, after], axis=dim)
    return array


def split_parts(values):
    upper = values.astype(jnp.bfloat16)
    lower = (values - upper.astype(jnp.float32)).astype(jnp.bfloat16)
    return (upper, lower)


def basis_times(basis, image):
    upper, lower = split_parts(image)
    first = jnp.einsum("krn,sn->krs", basis, upper, preferred_element_type=jnp.float32)
    second = jnp.einsum("krn,sn->krs", basis, lower, preferred_element_type=jnp.float32)
    return first + second


def combine_basis(projections, basis):
    upper, lower = split_parts(projections)
    first = jnp.einsum("krs,krn->sn", upper, basis, preferred_element_type=jnp.float32)
    second = jnp.einsum("krs,krn->sn", lower, basis, preferred_element_type=jnp.float32)
    return first + second


def shards(
    basis, near_blocks, near_src, near_count, p2m, m2l, send_list, send_count, far_src, far_class
):
    blocks, rhs_count, columns = basis.shape
    leaves, slots_near = near_src.shape
    panels = near_blocks.shape[2]
    terms = p2m.shape[2]
    classes = m2l.shape[0]
    col_groups = lax.axis_size("gx")
    segments = lax.axis_size("bulk")
    peers = col_groups * segments
    slot_count = send_list.shape[2]
    total_rows = columns * peers
    source = basis[blocks - 1].reshape(rhs_count, leaves, panels)
    padded = extended(source, (("gx", 1),), leaves)
    picked = jnp.take(padded, near_src.reshape(-1), axis=1).reshape(
        rhs_count, leaves, slots_near, panels
    )
    live = (lax.broadcasted_iota(jnp.int32, (leaves, slots_near), 1) < near_count[:, None]).astype(
        jnp.bfloat16
    )
    picked = picked * live[None, :, :, None]
    near = jnp.einsum("rlkq,lkpq->rlp", picked, near_blocks, preferred_element_type=jnp.float32)
    mult = jnp.einsum("rlp,lpq->lrq", source, p2m, preferred_element_type=jnp.float32).astype(
        jnp.bfloat16
    )
    outgoing = jnp.take(mult, send_list[0].reshape(-1), axis=0).reshape(
        peers, slot_count, rhs_count, terms
    )
    filled = (
        lax.broadcasted_iota(jnp.int32, (peers, slot_count), 1) < send_count[0][:, None]
    ).astype(jnp.bfloat16)
    outgoing = outgoing * filled[:, :, None, None]
    received = lax.all_to_all(outgoing, ("gx", "bulk"), split_axis=0, concat_axis=0, tiled=True)
    flat = received.reshape(peers * slot_count, rhs_count, terms)
    sources = jnp.take(flat, far_src.reshape(-1), axis=0).reshape(leaves, -1, rhs_count, terms)
    onehot = (far_class[:, :, None] == lax.broadcasted_iota(jnp.int32, (1, 1, classes), 2)).astype(
        jnp.bfloat16
    )
    gathered = jnp.einsum(
        "lec,lerq->clrq", onehot, sources, preferred_element_type=jnp.float32
    ).astype(jnp.bfloat16)
    local = jnp.einsum("clrq,cqs->lrs", gathered, m2l, preferred_element_type=jnp.float32).astype(
        jnp.bfloat16
    )
    far = jnp.einsum("lrq,lpq->rlp", local, p2m, preferred_element_type=jnp.float32)
    image = (source.astype(jnp.float32) + near + far).reshape(rhs_count, columns)
    highest = lax.Precision.HIGHEST
    inner_vw = basis_times(basis, image)
    inner_ww = jnp.dot(image, image.T, precision=highest)
    inner_vv = jnp.einsum("jrn,ksn->jkrs", basis, basis, preferred_element_type=jnp.float32)
    sum_vw, sum_ww, sum_vv = lax.psum((inner_vw, inner_ww, inner_vv), ("gx", "bulk"))
    projections = sum_vw / total_rows
    basis_gram = sum_vv / total_rows
    resid = image - combine_basis(projections, basis)
    twice = jnp.einsum("krs,krt->st", projections, projections, precision=highest)
    mixed = jnp.einsum("jrs,jkrt,ktu->su", projections, basis_gram, projections, precision=highest)
    gram = sum_ww / total_rows - 2.0 * twice + mixed
    factor = jnp.linalg.cholesky(gram)
    next_block = lax.linalg.triangular_solve(factor, resid, left_side=True, lower=True).astype(
        jnp.bfloat16
    )
    return (next_block, projections, factor)


def solution(mesh):
    return jax.shard_map(
        shards,
        mesh=mesh,
        in_specs=(
            P(None, None, ("gx", "bulk")),
            P(("gx", "bulk"), None, None, None),
            P(("gx", "bulk"), None),
            P(("gx", "bulk")),
            P(("gx", "bulk"), None, None),
            P(),
            P(("gx", "bulk"), None, None),
            P(("gx", "bulk"), None),
            P(("gx", "bulk"), None),
            P(("gx", "bulk"), None),
        ),
        out_specs=(P(None, ("gx", "bulk")), P(), P()),
        check_vma=False,
    )
```

profile of v0, /device:TPU:0, one launch (start us, length us, event | category | flops | bytes accessed | tf_op | source)
XLA Modules:
  0.0 282.3 jit_solution(3606217046359961500)
XLA Ops:
  12.2 1.7 select_multiply_fusion
  13.9 7.3 %all-to-all-start = ((bf16[32,4,64,128]{3,2,1,0:T(8,128)(2,1)}), bf16[32,4,64,128]{3,2,1,0:T(8,128)(2,1)S(1)}, u32[]{:S(2)}, u32[]{:S(2)}) async-start(bf16[32,4,64,128]{3,2,1,0:T(8,128)(2,1)} %select_multiply_fusion), calls=%async_computation | async-start | bytes 4194304 | tf_op jit(solution)/shard_map/all_to_all | solution.py:73
  21.3 2.0 copy.59
  23.3 1.3 collective-permute-start.1
  24.6 3.8 %collective-permute-start = (bf16[64,16,256]{2,0,1:T(8,128)(2,1)}, bf16[64,16,256]{2,0,1:T(8,128)(2,1)}, u32[]{:S(2)}, u32[]{:S(2)}) collective-permute-start(bf16[64,16,256]{2,0,1:T(8,128)(2,1)} %copy.59), channel_id=1, source_target_pairs={{0,8},{8,16},{16,24},{1,9},{9,17},{17,25},{2,10},{10,18},{18,26},{... | collective-permute-start | bytes 1572872 | tf_op jit(solution)/shard_map/ppermute | solution.py:14
  28.8 9.1 %fusion.19 = f32[8,8,64,64]{2,3,0,1:T(8,128)} fusion(bf16[8,64,4096]{2,1,0:T(8,128)(2,1)} %param.10), kind=kOutput, calls=%fused_computation.26 | convolution fusion | flops 2147483648 | bytes 5242880 | tf_op jit(solution)/shard_map/jrn,ksn->jkrs/dot_general | solution.py:90
  38.0 2.7 pad_maximum_fusion
  40.7 4.2 %gather_fusion = bf16[128,64,256]{2,1,0:T(8,128)(2,1)} fusion(bf16[64,48,256]{2,0,1:T(8,128)(2,1)} %pad_maximum_fusion, s32[1024]{0:T(1024)S(1)} %pad_clamp_fusion.2), kind=kCustom, calls=%fused_computation | custom fusion | bytes 8389120 | tf_op jit(solution)/shard_map/jit(_take)/gather | solution.py:55
  44.9 26.4 %all-to-all-done = bf16[32,4,64,128]{3,2,1,0:T(8,128)(2,1)S(1)} async-done(((bf16[32,4,64,128]{3,2,1,0:T(8,128)(2,1)}), bf16[32,4,64,128]{3,2,1,0:T(8,128)(2,1)S(1)}, u32[]{:S(2)}, u32[]{:S(2)}) %all-to-all-start) | async-done | bytes 2097184 | tf_op jit(solution)/shard_map/all_to_all | solution.py:73
  71.3 13.5 %gather_fusion.2 = bf16[512,64,128]{2,1,0:T(8,128)(2,1)} fusion(bf16[128,64,128]{2,1,0:T(8,128)(2,1)S(1)} %bitcast.116, s32[1024]{0:T(1024)S(1)} %pad_clamp_fusion), kind=kCustom, calls=%fused_computation.2 | custom fusion | bytes 16779264 | tf_op jit(solution)/shard_map/jit(_take)/gather | solution.py:75
  84.8 4.7 %broadcast_select_fusion = bf16[16,32,64,128]{3,2,1,0:T(8,128)(2,1)S(1)} fusion(bf16[16,32,64,128]{3,2,1,0:T(8,128)(2,1)} %bitcast.117, pred[16,32]{1,0:T(8,128)(4,1)S(1)} %compare_and_fusion), kind=kLoop, calls=%fused_computation.5 | loop fusion | flops 4194304 | bytes 16777728 | tf_op jit(solution)/shard_map/jit(_take)/select_n | solution.py:75
  89.5 7.1 %convert_bitcast_fusion = bf16[16,16,64,128]{3,0,2,1:T(8,128)(2,1)} fusion(bf16[16,32,64,128]{3,2,1,0:T(8,128)(2,1)S(1)} %broadcast_select_fusion, s32[16,32]{1,0:T(8,128)S(1)} %copy-done.10), kind=kOutput, calls=%fused_computation.16 | convolution fusion | flops 136323072 | bytes 12584960 | tf_op jit(solution)/shard_map/lec,lerq->clrq/dot_general | solution.py:79
  96.6 5.3 %convolution_bitcast_fusion.2 = f32[64,16,256]{2,0,1:T(8,128)} fusion(bf16[16,256,128]{2,1,0:T(8,128)(2,1)S(1)} %copy-done, bf16[16,16,64,128]{3,0,2,1:T(8,128)(2,1)} %convert_bitcast_fusion, bf16[16,128,128]{2,1,0:T(8,128)(2,1)} %param.15), kind=kOutput, calls=%fused_computation.29 | convolution fusion | flops 604110848 | bytes 6815744 | tf_op jit(solution)/shard_map/lrq,lpq->rlp/dot_general | solution.py:85
  101.9 10.6 %fusion.33 = f32[64,16,256]{2,0,1:T(8,128)S(1)} fusion(f32[64,16,256]{2,0,1:T(8,128)} %convolution_bitcast_fusion.2, bf16[16,8,256,256]{3,2,1,0:T(8,128)(2,1)} %param.11, bf16[64,16,8,256]{3,0,2,1:T(8,128)(2,1)} %bitcast.126, pred[16,8]{1,0:T(8,128)(4,1)S(1)} %copy.60, bf16[16,8]{1,0:T(8,128)(2,1)S(1)} %fusion.66, bf16[64,16,256]{2,1,0:T(8,128)(2,1)S(1)} %bitcast.125), kind=kOutput, calls=%fused_computation.32 | convolution fusion | flops 1078722560 | bytes 23593344 | tf_op jit(solution)/shard_map/rlkq,lkpq->rlp/dot_general | solution.py:62
  112.6 2.1 fusion.51
  114.8 2.8 fusion.44
  118.6 37.6 %psum.21 = f32[64,64]{0,1:T(8,128)S(1)} all-reduce(f32[64,64]{0,1:T(8,128)S(1)} %convolution_bitcast_fusion.3), channel_id=1, replica_groups=mesh['gx'=4,'bulk'=8] {'gx','bulk'}, use_global_device_ids=true, to_apply=%region_0.1 | all-reduce | flops 4096 | bytes 32768 | tf_op jit(solution)/shard_map/psum | solution.py:91
  156.2 94.9 %all-reduce.3.cloned.1.call-done = (f32[8,64,64]{1,2,0:T(8,128)}, f32[8,8,64,64]{2,3,0,1:T(8,128)}) async-done(((f32[8,64,64]{1,2,0:T(8,128)}, f32[8,8,64,64]{2,3,0,1:T(8,128)}), (f32[8,64,64]{1,2,0:T(8,128)}, f32[8,8,64,64]{2,3,0,1:T(8,128)})) %all-reduce.3.cloned.1.call-update) | async-done | bytes 1179664 | tf_op jit(solution)/shard_map/psum | solution.py:91
  251.0 3.3 %convolution_bitcast_fusion = f32[64,4096]{1,0:T(8,128)S(1)} fusion(bf16[8,64,4096]{2,1,0:T(8,128)(2,1)} %param.10, f32[8,64,64]{1,2,0:T(8,128)} %get-tuple-element.15), kind=kOutput, calls=%fused_computation.6 | convolution fusion | flops 268599296 | bytes 5373952 | tf_op jit(solution)/shard_map/krs,krn->sn/dot_general | solution.py:36
  256.0 3.2 %fusion.41 = f32[8,64,64]{1,2,0:T(8,128)S(1)} fusion(f32[8,8,64,64]{2,3,0,1:T(8,128)S(1)} %copy-done.6, f32[8,64,64]{1,2,0:T(8,128)S(1)} %copy-done.3), kind=kOutput, calls=%fused_computation.35 | convolution fusion | flops 201621504 | bytes 1310720 | tf_op jit(solution)/shard_map/jrs,jkrt,ktu->su/dot_general | solution.py:96
  260.1 5.8 %cholesky.16 = f32[64,64]{1,0:T(8,128)S(1)} custom-call(f32[64,64]{1,0:T(8,128)S(1)} %fusion.64), custom_call_target="Cholesky" | custom-call | tf_op jit(solution)/shard_map/jit(cholesky)/cholesky | solution.py:98
  266.6 1.3 select_bitcast_fusion
  267.9 4.9 %custom-call.6 = f32[1,64,64]{1,2,0:T(8,128)S(1)} custom-call(f32[1,64,64]{2,1,0:T(8,128)S(1)} %get-tuple-element.17), custom_call_target="InvertDiagBlocksLowerTriangular" | custom-call | tf_op jit(solution)/shard_map/triangular_solve | solution.py:99
  273.6 1.8 convolution_convert_fusion
  (59 shorter events, 10.6 us)
Async XLA Ops:
  7.2 3.7 %copy-start = (bf16[16,256,128]{2,1,0:T(8,128)(2,1)S(1)}, bf16[16,256,128]{2,1,0:T(8,128)(2,1)}, u32[]{:S(2)}) copy-start(bf16[16,256,128]{2,1,0:T(8,128)(2,1)} %param.14) | copy-start | bytes 3145732
  9.9 1.0 copy-start.4
  12.2 16.2 %copy-start.7 = (s32[16,32]{1,0:T(8,128)S(1)}, s32[16,32]{1,0:T(8,128)}, u32[]{:S(2)}) copy-start(s32[16,32]{1,0:T(8,128)} %param.18) | copy-start | bytes 6148
  12.2 16.3 %copy-start.8 = (s32[16,8]{0,1:T(8,128)S(1)}, s32[16,8]{0,1:T(8,128)}, u32[]{:S(2)}) copy-start(s32[16,8]{0,1:T(8,128)} %param.12) | copy-start | bytes 1540
  13.9 57.4 %all-to-all-start = ((bf16[32,4,64,128]{3,2,1,0:T(8,128)(2,1)}), bf16[32,4,64,128]{3,2,1,0:T(8,128)(2,1)S(1)}, u32[]{:S(2)}, u32[]{:S(2)}) async-start(bf16[32,4,64,128]{3,2,1,0:T(8,128)(2,1)} %select_multiply_fusion), calls=%async_computation | async-start | bytes 4194304 | tf_op jit(solution)/shard_map/all_to_all | solution.py:73
  21.2 229.8 %all-reduce.3.cloned.1.call-start = ((), (), s32[]{:S(2)}) async-start(), calls=%async_computation.1 | async-start | bytes 4718592 | tf_op jit(solution)/shard_map/psum | solution.py:91
  23.3 14.7 %collective-permute-start.1 = (bf16[64,16,256]{2,0,1:T(8,128)(2,1)}, bf16[64,16,256]{2,0,1:T(8,128)(2,1)}, u32[]{:S(2)}, u32[]{:S(2)}) collective-permute-start(bf16[64,16,256]{2,0,1:T(8,128)(2,1)} %copy.59), channel_id=1, source_target_pairs={{8,0},{16,8},{24,16},{9,1},{17,9},{25,17},{10,2},{18,10},{26,18},{... | collective-permute-start | bytes 1572872 | tf_op jit(solution)/shard_map/ppermute | solution.py:15
  24.6 13.5 %collective-permute-start = (bf16[64,16,256]{2,0,1:T(8,128)(2,1)}, bf16[64,16,256]{2,0,1:T(8,128)(2,1)}, u32[]{:S(2)}, u32[]{:S(2)}) collective-permute-start(bf16[64,16,256]{2,0,1:T(8,128)(2,1)} %copy.59), channel_id=1, source_target_pairs={{0,8},{8,16},{16,24},{1,9},{9,17},{17,25},{2,10},{10,18},{18,26},{... | collective-permute-start | bytes 1572872 | tf_op jit(solution)/shard_map/ppermute | solution.py:14
  28.8 9.1 %copy-start.9 = (s32[16]{0:T(128)S(1)}, s32[16]{0:T(128)}, u32[]{:S(2)}) copy-start(s32[16]{0:T(128)} %param.13) | copy-start | bytes 196
  84.8 4.7 %copy-start.10 = (s32[16,32]{1,0:T(8,128)S(1)}, s32[16,32]{1,0:T(8,128)}, u32[]{:S(2)}) copy-start(s32[16,32]{1,0:T(8,128)} %param.19) | copy-start | bytes 6148
  96.6 5.3 %copy-start.5 = (bf16[8,8,16,256]{3,2,1,0:T(8,128)(2,1)S(1)}, bf16[8,8,16,256]{3,2,1,0:T(8,128)(2,1)}, u32[]{:S(2)}) copy-start(bf16[8,8,16,256]{3,2,1,0:T(8,128)(2,1)} %copy-done.4) | copy-start | bytes 1572868
  101.9 10.7 %copy-start.1 = (bf16[8,64,4096]{2,1,0:T(8,128)(2,1)S(1)}, bf16[8,64,4096]{2,1,0:T(8,128)(2,1)}, u32[]{:S(2)}) copy-start(bf16[8,64,4096]{2,1,0:T(8,128)(2,1)} %param.10) | copy-start | bytes 12582916
  251.0 3.3 %copy-start.3 = (f32[8,64,64]{1,2,0:T(8,128)S(1)}, f32[8,64,64]{1,2,0:T(8,128)}, u32[]{:S(2)}) copy-start(f32[8,64,64]{1,2,0:T(8,128)} %get-tuple-element.15) | copy-start | bytes 393220
  251.0 3.6 %copy-start.2 = (bf16[8,64,4096]{2,1,0:T(8,128)(2,1)S(1)}, bf16[8,64,4096]{2,1,0:T(8,128)(2,1)}, u32[]{:S(2)}) copy-start(bf16[8,64,4096]{2,1,0:T(8,128)(2,1)} %param.10) | copy-start | bytes 12582916
  254.4 1.7 copy-start.6
Sparse Core Ops, SparseCore 0:
  117.7 133.2 all-reduce.2
where the time goes:
time: 283 us; the launch traced here: 282 us
  waiting for transfers between devices  121 us (43%)
  matrix products  48.4 us (17%)
  blocking collectives  37.6 us (13%)
  local copies, waits for them, and re-layouts  24.9 us (9%)
  other arithmetic  23.3 us (8%)
  between operations  14.3 us (5%)
  starting transfers between devices  12.5 us (4%)
    psum x1, waiting for transfers between devices, shards(): lax.psum((inner_vw, inner_ww, inner_vv), ('gx', 'bulk'))  94.9 us
    psum x1, blocking collectives, shards(): lax.psum((inner_vw, inner_ww, inner_vv), ('gx', 'bulk'))  37.6 us
    all_to_all x1, waiting for transfers between devices, shards(): lax.all_to_all(outgoing, ('gx', 'bulk'), split_axis=0, concat_axis=0, til...  26.4 us
    gather x1, local copies, waits for them, and re-layouts, shards(): jnp.take(flat, far_src.reshape(-1), axis=0)  13.5 us
    dot_general x1, matrix products, shards(): jnp.einsum('rlkq,lkpq->rlp', picked, near_blocks, preferred_element_type=...  10.6 us
    dot_general x1, matrix products, shards(): jnp.einsum('jrn,ksn->jkrs', basis, basis, preferred_element_type=jnp.floa...  9.12 us
    all_to_all x1, starting transfers between devices, shards(): lax.all_to_all(outgoing, ('gx', 'bulk'), split_axis=0, concat_axis=0, til...  7.3 us
    dot_general x1, matrix products, shards(): jnp.einsum('lec,lerq->clrq', onehot, sources, preferred_element_type=jnp....  7.1 us
  transfers between devices with their start and end apart: 4, of which 2 were waited for; matrix products, arithmetic and copies ran while one was open for 7% of the time, Pallas kernels for 0%

commit v1 on v0

v1 whole, which is shorter than its diff:
```python
import functools

import jax
import jax.numpy as jnp
from jax import lax
from jax.experimental import pallas as pl
from jax.experimental.pallas import tpu as pltpu
from jax.sharding import PartitionSpec as P

F32 = jnp.float32
BF16 = jnp.bfloat16
AXES = ("gx", "bulk")
HIGHEST = lax.Precision.HIGHEST
VMEM_LIMIT = 48 * 1024 * 1024


def dot(a, b, dims=((1,), (0,)), precision=None):
    return lax.dot_general(a, b, (dims, ((), ())), precision=precision, preferred_element_type=F32)


def dot_nt(a, b, precision=None):
    return dot(a, b, ((1,), (1,)), precision)


def split_parts(values):
    upper = values.astype(BF16)
    lower = (values - upper.astype(F32)).astype(BF16)
    return (upper, lower)


def params(**kwargs):
    return pltpu.CompilerParams(vmem_limit_bytes=VMEM_LIMIT, **kwargs)


def whole(shape):
    return pl.BlockSpec(shape, lambda *_: (0,) * len(shape))


def send_kernel(halves, x_ref, p2m_ref, list_ref, count_ref, out_ref, copy_ref, scratch):
    leaves, panels, terms = p2m_ref.shape
    rhs = x_ref.shape[1]
    peers, slots = list_ref.shape
    part = rhs // halves
    rows = peers * slots * halves
    copy_ref[...] = x_ref[0]
    for g in range(leaves):
        mult = dot(x_ref[0, :, g * panels : (g + 1) * panels], p2m_ref[g])
        for h in range(halves):
            scratch[:, g * halves + h, :] = mult[h * part : (h + 1) * part]
    row = lax.broadcasted_iota(jnp.int32, (rows, peers), 0) // (slots * halves)
    peer_hot = row == lax.broadcasted_iota(jnp.int32, (rows, peers), 1)
    listed = dot(peer_hot.astype(BF16), list_ref[...].astype(F32).astype(BF16))
    row_s = lax.broadcasted_iota(jnp.int32, (rows, slots), 0) // halves % slots
    lane_s = lax.broadcasted_iota(jnp.int32, (rows, slots), 1)
    leaf = jnp.sum(jnp.where(row_s == lane_s, listed, 0.0), axis=1, keepdims=True)
    counts = jnp.broadcast_to(count_ref[...].astype(F32), (rows, peers))
    live = jnp.sum(jnp.where(peer_hot, counts, 0.0), axis=1, keepdims=True)
    row_k = lax.broadcasted_iota(jnp.int32, (rows, leaves * halves), 0)
    lane_k = lax.broadcasted_iota(jnp.int32, (rows, leaves * halves), 1)
    half = row_k % halves
    slot = (row_k // halves % slots).astype(F32)
    wanted = leaf * halves + half.astype(F32)
    chosen = ((lane_k.astype(F32) == wanted) & (slot < live)).astype(F32).astype(BF16)
    for j in range(part // 2):
        pair = jnp.concatenate([scratch[2 * j], scratch[2 * j + 1]], axis=1).astype(BF16)
        out_ref[:, j * 2 * terms : (j + 1) * 2 * terms] = dot(chosen, pair).astype(BF16)


def sent_multipoles(basis, p2m, send_list, send_count, halves):
    blocks, rhs, columns = basis.shape
    leaves, panels, terms = p2m.shape
    peers, slots = send_list.shape
    rows, width = peers * slots * halves, rhs // halves * terms
    return pl.pallas_call(
        functools.partial(send_kernel, halves),
        grid=(1,),
        out_shape=(
            jax.ShapeDtypeStruct((rows, width), BF16),
            jax.ShapeDtypeStruct((rhs, columns), BF16),
        ),
        in_specs=[
            pl.BlockSpec((1, rhs, columns), lambda i: (blocks - 1, 0, 0)),
            whole(p2m.shape),
            whole(send_list.shape),
            whole(send_count.shape),
        ],
        out_specs=(whole((rows, width)), whole((rhs, columns))),
        scratch_shapes=[pltpu.VMEM((rhs // halves, leaves * halves, terms), F32)],
        compiler_params=params(),
        name="send",
    )(basis, p2m, send_list, send_count)


def basis_gram_kernel(v_ref, out_ref):
    blocks, rhs, width = v_ref.shape
    half = blocks * rhs // 2
    v = v_ref[...].reshape(2 * half, width)
    top, bottom = v[:half], v[half:]

    @pl.when(pl.program_id(0) == 0)
    def _():
        out_ref[...] = jnp.zeros_like(out_ref)

    out_ref[0] += dot_nt(top, top)
    out_ref[1] += dot_nt(top, bottom)
    out_ref[2] += dot_nt(bottom, bottom)


def basis_grams(basis, steps):
    blocks, rhs, columns = basis.shape
    half = blocks * rhs // 2
    return pl.pallas_call(
        basis_gram_kernel,
        grid=(steps,),
        out_shape=jax.ShapeDtypeStruct((3, half, half), F32),
        in_specs=[pl.BlockSpec((blocks, rhs, columns // steps), lambda i: (0, 0, i))],
        out_specs=whole((3, half, half)),
        compiler_params=params(),
        cost_estimate=pl.CostEstimate(
            flops=6 * half * half * columns,
            bytes_accessed=basis.size * 2 + 12 * half * half,
            transcendentals=0,
        ),
        name="basis_gram",
    )(basis)


def near_kernel(src_ref, count_ref, before, own, after, blocks_ref, out_ref, wide):
    columns = own.shape[1]
    slots, panels = blocks_ref.shape[1], blocks_ref.shape[2]
    g = pl.program_id(0)

    @pl.when(g == 0)
    def _():
        wide[:, :columns] = before[...]
        wide[:, columns : 2 * columns] = own[...]
        wide[:, 2 * columns :] = after[...]

    here = pl.ds(pl.multiple_of(columns + g * panels, panels), panels)
    total = wide[:, here].astype(F32)
    for k in range(slots):
        place = pl.multiple_of(src_ref[g, k] * panels, panels)
        source = wide[:, pl.ds(place, panels)]
        source = jnp.where(k < count_ref[g], source, jnp.zeros_like(source))
        total += dot_nt(source, blocks_ref[0, k])
    out_ref[...] = total


def near_field(near_src, near_count, before, own, after, near_blocks):
    leaves, slots, panels, _ = near_blocks.shape
    rhs, columns = own.shape
    grid_spec = pltpu.PrefetchScalarGridSpec(
        num_scalar_prefetch=2,
        grid=(leaves,),
        in_specs=[
            whole((rhs, columns)),
            whole((rhs, columns)),
            whole((rhs, columns)),
            pl.BlockSpec((1, slots, panels, panels), lambda g, *_: (g, 0, 0, 0)),
        ],
        out_specs=pl.BlockSpec((rhs, panels), lambda g, *_: (0, g)),
        scratch_shapes=[pltpu.VMEM((rhs, 3 * columns), BF16)],
    )
    return pl.pallas_call(
        near_kernel,
        grid_spec=grid_spec,
        out_shape=jax.ShapeDtypeStruct((rhs, columns), F32),
        compiler_params=params(),
        cost_estimate=pl.CostEstimate(
            flops=2 * rhs * near_blocks.size,
            bytes_accessed=near_blocks.size * 2 + 7 * rhs * columns * 2,
            transcendentals=0,
        ),
        name="near",
    )(near_src, near_count, before, own, after, near_blocks)


def far_kernel(halves, peers, recv, pick, m2l, p2m, near, basis, image_ref, sums_ref, lhs, loc):
    leaves, panels, terms = p2m.shape
    classes = m2l.shape[0]
    blocks, rhs, columns = basis.shape
    part = rhs // halves
    for h in range(halves):

        def step(j, carry, h=h):
            lanes = pl.ds(pl.multiple_of(j * 2 * terms, 2 * terms), 2 * terms)
            got = dot(pick[h], recv[:, lanes]).astype(BF16)
            base = pl.multiple_of((h * part + 2 * j) * leaves, 2 * leaves)
            for t in range(2):
                for c in range(classes):
                    lhs[pl.ds(base + t * leaves, leaves), c * terms : (c + 1) * terms] = got[
                        c * leaves : (c + 1) * leaves, t * terms : (t + 1) * terms
                    ]
            return carry

        lax.fori_loop(0, part // 2, step, 0)
    weights = m2l[...].reshape(classes * terms, terms)
    tall = 256
    for i in range(rhs * leaves // tall):
        got = dot(lhs[i * tall : (i + 1) * tall, :], weights)
        loc[i * tall // leaves : (i + 1) * tall // leaves] = got.reshape(
            tall // leaves, leaves, terms
        )
    inner = jnp.zeros((2 * rhs, blocks * rhs), F32)
    square = jnp.zeros((2 * rhs, 2 * rhs), F32)
    for g in range(leaves):
        cols = slice(g * panels, (g + 1) * panels)
        far = dot_nt(loc[:, g, :].astype(BF16), p2m[g])
        image = near[:, cols] + far
        image_ref[:, cols] = image
        both = jnp.concatenate(split_parts(image), axis=0)
        inner += dot_nt(both, basis[:, :, cols].reshape(blocks * rhs, panels))
        square += dot_nt(both, both)
    products = inner[:rhs] + inner[rhs:]
    ww = square[:rhs, :rhs] + square[:rhs, rhs:] + square[rhs:, :rhs] + square[rhs:, rhs:]
    pack(products, ww, sums_ref)


def pack_sizes(rhs, wide, peers):
    rows = rhs * wide // 128 // peers
    return rows, -(-(rows + 1) // 8) * 8


def pack(products, ww, out_ref):
    peers, _, lanes = out_ref.shape
    rhs, wide = products.shape
    rows, _ = pack_sizes(rhs, wide, peers)
    out_ref[...] = jnp.zeros_like(out_ref)
    tall = jnp.concatenate(
        [products[:, i * lanes : (i + 1) * lanes] for i in range(wide // lanes)], axis=0
    )
    for p in range(peers):
        out_ref[p, :rows, :] = tall[p * rows : (p + 1) * rows]
    half = rhs // 2
    folded = jnp.concatenate([ww[:half], ww[half:]], axis=1)
    for i in range(half):
        out_ref[i, rows : rows + 1, :] = folded[i : i + 1]


def unpack(in_ref, rhs, wide):
    peers, _, lanes = in_ref.shape
    rows, _ = pack_sizes(rhs, wide, peers)
    tall = jnp.concatenate([in_ref[p, :rows, :] for p in range(peers)], axis=0)
    products = jnp.concatenate(
        [tall[i * rhs : (i + 1) * rhs] for i in range(wide // lanes)], axis=1
    )
    half = rhs // 2
    folded = jnp.concatenate([in_ref[i, rows : rows + 1, :] for i in range(half)], axis=0)
    ww = jnp.concatenate([folded[:, :rhs], folded[:, rhs:]], axis=0)
    return products, ww


def far_field(recv, pick, m2l, p2m, near, basis, halves, peers):
    leaves, panels, terms = p2m.shape
    classes = m2l.shape[0]
    blocks, rhs, columns = basis.shape
    _, piece = pack_sizes(rhs, blocks * rhs, peers)
    args = (recv, pick, m2l, p2m, near, basis)
    return pl.pallas_call(
        functools.partial(far_kernel, halves, peers),
        grid=(1,),
        out_shape=(
            jax.ShapeDtypeStruct((rhs, columns), F32),
            jax.ShapeDtypeStruct((peers, piece, 128), F32),
        ),
        in_specs=[whole(a.shape) for a in args],
        out_specs=(whole((rhs, columns)), whole((peers, piece, 128))),
        scratch_shapes=[
            pltpu.VMEM((rhs * leaves, classes * terms), BF16),
            pltpu.VMEM((rhs, leaves, terms), F32),
        ],
        compiler_params=params(),
        name="far",
    )(*args)


def add_kernel(in_ref, out_ref):
    total = jnp.sum(in_ref[...], axis=0)
    out_ref[...] = jnp.broadcast_to(total[None], out_ref.shape)


def all_sum(pieces):
    got = lax.all_to_all(pieces, AXES, split_axis=0, concat_axis=0, tiled=True)
    added = pl.pallas_call(
        add_kernel,
        grid=(1,),
        out_shape=jax.ShapeDtypeStruct(pieces.shape, F32),
        in_specs=[whole(pieces.shape)],
        out_specs=whole(pieces.shape),
        compiler_params=params(),
        name="add",
    )(got)
    return lax.all_to_all(added, AXES, split_axis=0, concat_axis=0, tiled=True)


def factored(gram):
    size = gram.shape[0]
    rows = lax.broadcasted_iota(jnp.int32, (size, size), 0)
    cols = lax.broadcasted_iota(jnp.int32, (size, size), 1)
    eye = (rows == cols).astype(F32)
    both = jnp.concatenate([gram, eye], axis=1)
    tiles = [both[8 * i : 8 * i + 8] for i in range(size // 8)]
    sub = lax.broadcasted_iota(jnp.int32, (8, 2 * size), 0)
    for j in range(size):
        t, o = divmod(j, 8)
        row = tiles[t][o : o + 1]
        pivot = 1.0 / row[:, j : j + 1]
        scaled = row * pivot
        for i in range(t, size // 8):
            column = tiles[i][:, j : j + 1]
            change = column * scaled
            if i == t:
                change = jnp.where(sub > o, change, 0.0)
            tiles[i] = tiles[i] - change
    both = jnp.concatenate(tiles, axis=0)
    pivots = jnp.sum(both[:, :size] * eye, axis=1, keepdims=True)
    both = both * (1.0 / jnp.sqrt(pivots))
    upper = jnp.where(cols >= rows, both[:, :size], 0.0)
    return upper.T, both[:, size:]


def tail_kernel(total_rows, sums, grams, basis, image, next_ref, proj_ref, factor_ref, coef):
    blocks, rhs, width = basis.shape
    wide = blocks * rhs

    @pl.when(pl.program_id(0) == 0)
    def _():
        products, ww = unpack(sums, rhs, wide)
        proj = products * (1.0 / total_rows)
        half = wide // 2
        left, right = proj[:, :half], proj[:, half:]
        scale = 1.0 / total_rows
        g00, g01, g11 = grams[0] * scale, grams[1] * scale, grams[2] * scale
        first = dot(left, g00, precision=HIGHEST) + dot_nt(right, g01, HIGHEST) - 2.0 * left
        second = dot(left, g01, precision=HIGHEST) + dot(right, g11, precision=HIGHEST)
        second = second - 2.0 * right
        gram = ww * scale + dot_nt(first, left, HIGHEST) + dot_nt(second, right, HIGHEST)
        lower, inverse = factored(gram)
        factor_ref[...] = lower
        proj_ref[...] = proj.T
        mixed = dot(inverse, proj, precision=HIGHEST)
        coef[:rhs, :wide], coef[rhs:, :wide] = split_parts(-mixed)
        coef[:rhs, wide : wide + rhs], coef[rhs:, wide : wide + rhs] = split_parts(inverse)

    upper, lower = split_parts(image[...])
    by_basis = dot(coef[:, :wide], basis[...].reshape(wide, width))
    by_image = dot(coef[:, wide : wide + rhs], upper)
    rest = dot(coef[:rhs, wide : wide + rhs], lower)
    total = by_basis + by_image
    next_ref[...] = (total[:rhs] + total[rhs:] + rest).astype(BF16)


def tail(sums, grams, basis, image, total_rows, steps):
    blocks, rhs, columns = basis.shape
    width = columns // steps
    return pl.pallas_call(
        functools.partial(tail_kernel, total_rows),
        grid=(steps,),
        out_shape=(
            jax.ShapeDtypeStruct((rhs, columns), BF16),
            jax.ShapeDtypeStruct((blocks * rhs, rhs), F32),
            jax.ShapeDtypeStruct((rhs, rhs), F32),
        ),
        in_specs=[
            whole(sums.shape),
            whole(grams.shape),
            pl.BlockSpec((blocks, rhs, width), lambda i: (0, 0, i)),
            pl.BlockSpec((rhs, width), lambda i: (0, i)),
        ],
        out_specs=(
            pl.BlockSpec((rhs, width), lambda i: (0, i)),
            whole((blocks * rhs, rhs)),
            whole((rhs, rhs)),
        ),
        scratch_shapes=[pltpu.VMEM((2 * rhs, blocks * rhs + 128), BF16)],
        compiler_params=params(),
        name="tail",
    )(sums, grams, basis, image)


def shards(
    basis, near_blocks, near_src, near_count, p2m, m2l, send_list, send_count, far_src, far_class
):
    blocks, rhs, columns = basis.shape
    leaves = near_src.shape[0]
    classes, terms, _ = m2l.shape
    devices = lax.axis_size("gx")
    peers = devices * lax.axis_size("bulk")
    slots = send_list.shape[2]
    total_rows = columns * peers
    halves = 2

    sent, own = sent_multipoles(basis, p2m, send_list[0], send_count, halves)
    sent = sent.reshape(peers, slots * halves, sent.shape[1])
    received = lax.all_to_all(sent, AXES, split_axis=0, concat_axis=0, tiled=True)
    received = received.reshape(peers * slots * halves, received.shape[2])

    up = [(i, i + 1) for i in range(devices - 1)]
    down = [(j, i) for i, j in up]
    before = lax.ppermute(own, "gx", up)
    after = lax.ppermute(own, "gx", down)

    grams = lax.psum(basis_grams(basis, 4), AXES)
    near = near_field(near_src, near_count, before, own, after, near_blocks)

    class_hot = (far_class[:, None, :] == jnp.arange(classes)[None, :, None]).astype(BF16)
    rows = jnp.arange(peers * slots * halves)[None, None, None, :]
    wanted = far_src[None, :, :, None] * halves + jnp.arange(halves)[:, None, None, None]
    source_hot = (wanted == rows).astype(BF16)
    pick = jnp.einsum("gce,hgef->hcgf", class_hot, source_hot, preferred_element_type=F32)
    pick = pick.astype(BF16).reshape(halves, classes * leaves, -1)

    image, sums = far_field(received, pick, m2l, p2m, near, basis, halves, peers)
    sums = all_sum(sums)
    next_block, projections, factor = tail(sums, grams, basis, image, total_rows, 4)
    return (next_block, projections.reshape(blocks, rhs, rhs), factor)


def solution(mesh):
    return jax.shard_map(
        shards,
        mesh=mesh,
        in_specs=(
            P(None, None, AXES),
            P(AXES, None, None, None),
            P(AXES, None),
            P(AXES),
            P(AXES, None, None),
            P(),
            P(AXES, None, None),
            P(AXES, None),
            P(AXES, None),
            P(AXES, None),
        ),
        out_specs=(P(None, AXES), P(), P()),
        check_vma=False,
    )
```

time: 283 us -> 259 us (0.915)
  Pallas kernels: 0 us -> 48.5 us
  matrix products: 48.4 us -> 0.36 us
  waiting for transfers between devices: 121 us -> 159 us
  blocking collectives: 37.6 us -> 12.9 us
  other arithmetic: 23.3 us -> 0.01 us
  local copies, waits for them, and re-layouts: 24.9 us -> 9.08 us
    pallas_call x0 -> x6, Pallas kernels: none -> 48.5 us  [the longest x1 15.2 us: near_field(): pl.pallas_call(near_kernel, grid_spec=grid_spec, out_shape=jax.ShapeDtype...]
    dot_general x13 -> x1, matrix products: 46.6 us -> 0.36 us  [shards(): jnp.einsum('gce,hgef->hcgf', class_hot, source_hot, preferred_element_typ...]
    psum x1 -> x0, blocking collectives: 37.6 us -> none  [shards(): lax.psum((inner_vw, inner_ww, inner_vv), ('gx', 'bulk'))]
    psum x1, waiting for transfers between devices: 94.9 us -> 130 us  [shards(): grams = lax.psum(basis_grams(basis, 4), AXES)]
    gather x3 -> x0, local copies, waits for them, and re-layouts: 18.6 us -> none  [the longest x1 13.5 us: shards(): jnp.take(flat, far_src.reshape(-1), axis=0)]
    all_to_all x0 -> x1, blocking collectives: none -> 12.9 us  [all_sum(): got = lax.all_to_all(pieces, AXES, split_axis=0, concat_axis=0, tiled=True)]
    another operation x5 -> x0, other arithmetic: 12.7 us -> none  [the longest x3 6.52 us: shards(): factor = jnp.linalg.cholesky(gram)]
    unnamed x26 -> x25, local copies, waits for them, and re-layouts: 2.62 us -> 8.16 us
  transfers between devices with their start and end apart: 4 -> 5, of which waited for: 2 -> 3; matrix products, arithmetic and copies ran while one was open for 7% -> 0% of each run, Pallas kernels for 0% -> 7%
where the time goes in v1:
time: 259 us; the launch traced here: 258 us
  waiting for transfers between devices  159 us (61%)
  Pallas kernels  48.5 us (19%)
  between operations  14.1 us (5%)
  starting transfers between devices  13.5 us (5%)
  blocking collectives  12.9 us (5%)
  local copies, waits for them, and re-layouts  9.08 us (4%)
    psum x1, waiting for transfers between devices, shards(): grams = lax.psum(basis_grams(basis, 4), AXES)  130 us
    all_to_all x1, waiting for transfers between devices, shards(): lax.all_to_all(sent, AXES, split_axis=0, concat_axis=0, tiled=True)  26 us
    pallas_call x1, Pallas kernels, near_field(): pl.pallas_call(near_kernel, grid_spec=grid_spec, out_shape=jax.ShapeDtype...  15.2 us
    pallas_call x1, Pallas kernels, far_field(): pl.pallas_call(functools.partial(far_kernel, halves, peers), grid=(1,), o...  13.3 us
    all_to_all x1, blocking collectives, all_sum(): got = lax.all_to_all(pieces, AXES, split_axis=0, concat_axis=0, tiled=True)  12.9 us
    pallas_call x1, Pallas kernels, tail(): pl.pallas_call(functools.partial(tail_kernel, total_rows), grid=(steps,),...  11.6 us
    unnamed x25, local copies, waits for them, and re-layouts  8.16 us
    all_to_all x1, starting transfers between devices, shards(): lax.all_to_all(sent, AXES, split_axis=0, concat_axis=0, tiled=True)  7.42 us
  transfers between devices with their start and end apart: 5, of which 3 were waited for; matrix products, arithmetic and copies ran while one was open for 0% of the time, Pallas kernels for 7%

profile of v1, /device:TPU:0, one launch (start us, length us, event | category | flops | bytes accessed | tf_op | source)
XLA Modules:
  0.0 257.8 jit_solution(3943429257612657603)
XLA Ops:
  7.2 0.8 copy.13.list_ref
  7.9 1.2 copy-done.1
  9.2 0.7 copy-done.8
  9.8 3.7 %send.1 = (bf16[256,4096]{1,0:T(8,128)(2,1)}, bf16[64,4096]{1,0:T(8,128)(2,1)S(1)}) custom-call(bf16[8,64,4096]{2,1,0:T(8,128)(2,1)} %basis.3, bf16[16,256,128]{2,1,0:T(8,128)(2,1)S(1)} %copy-done.1, s32[32,4]{1,0:T(8,128)S(1)} %copy.13.list_ref, s32[1,32]{1,0:T(1,128)S(1)} %copy-done.8), custom_call_target="tpu_custom_call" | custom-call | tf_op jit(solution)/shard_map/send/pallas_call | solution.py:74
  13.6 7.4 %all-to-all-start = ((bf16[32,8,4096]{2,1,0:T(8,128)(2,1)}), bf16[32,8,4096]{2,1,0:T(8,128)(2,1)}, u32[]{:S(2)}, u32[]{:S(2)}) async-start(bf16[32,8,4096]{2,1,0:T(8,128)(2,1)} %bitcast.1), calls=%async_computation | async-start | bytes 4194304 | tf_op jit(solution)/shard_map/all_to_all | solution.py:395
  21.0 2.1 collective-permute-start
  23.1 1.3 collective-permute-start.1
  24.5 0.4 fusion
  24.8 0.2 copy.14
  25.1 3.0 %collective-permute-done.1.after = bf16[64,4096]{1,0:T(8,128)(2,1)S(1)} collective-permute-done((bf16[64,4096]{1,0:T(8,128)(2,1)S(1)}, bf16[64,4096]{1,0:T(8,128)(2,1)S(1)}, u32[]{:S(2)}, u32[]{:S(2)}) %collective-permute-start.1) | collective-permute-done | bytes 524320 | tf_op jit(solution)/shard_map/ppermute | solution.py:401
  28.0 0.8 copy-done.5
  28.8 1.0 copy-done.6
  29.9 15.2 %near.1 = f32[64,4096]{1,0:T(8,128)S(1)} custom-call(s32[16,8]{1,0:T(8,128)S(1)} %copy.15.src_ref, s32[16]{0:T(128)S(1)} %copy-done.7, bf16[64,4096]{1,0:T(8,128)(2,1)S(1)} %collective-permute-done.before, bf16[64,4096]{1,0:T(8,128)(2,1)S(1)} %get-tuple-element.11.own, bf16[64,4096]{1,0:T(8,128)(2,1)S(1)} %copy-done.6, bf16[16,8,256,256]{3,2,1,0:T(8,128)(2,1)} %blocks_ref.1), custom_call_target="tpu_custom_call" | custom-call | flops 1073741824 | bytes 20447232 | tf_op jit(solution)/shard_map/near/pallas_call | solution.py:164
  45.0 26.0 %all-to-all-done = bf16[32,8,4096]{2,1,0:T(8,128)(2,1)} async-done(((bf16[32,8,4096]{2,1,0:T(8,128)(2,1)}), bf16[32,8,4096]{2,1,0:T(8,128)(2,1)}, u32[]{:S(2)}, u32[]{:S(2)}) %all-to-all-start) | async-done | bytes 2097184 | tf_op jit(solution)/shard_map/all_to_all | solution.py:395
  71.1 1.0 copy-done.4
  72.1 13.3 %far.1 = (f32[64,4096]{1,0:T(8,128)S(1)}, f32[32,16,128]{2,1,0:T(8,128)S(1)}) custom-call(bf16[256,4096]{1,0:T(8,128)(2,1)} %bitcast.2.recv, bf16[2,256,256]{2,1,0:T(8,128)(2,1)S(1)} %bitcast.12, bf16[16,128,128]{2,1,0:T(8,128)(2,1)S(1)} %copy-done.4, bf16[16,256,128]{2,1,0:T(8,128)(2,1)S(1)} %copy-done.2, f32[64,4096]{1,0:T(8,128)S(1)} %near.1, ...), custom_call_target="tpu_custom_call" | custom-call | tf_op jit(solution)/shard_map/far/pallas_call | solution.py:259
  85.4 12.9 %all_to_all.15.in_ref = f32[32,16,128]{2,1,0:T(8,128)S(1)} all-to-all(f32[32,16,128]{2,1,0:T(8,128)S(1)} %get-tuple-element.12), channel_id=1, replica_groups=mesh['gx'=4,'bulk'=8] {'gx','bulk'}, dimensions={0} | all-to-all | bytes 524288 | tf_op jit(solution)/shard_map/all_to_all | solution.py:283
  98.3 0.8 add.28
  99.0 2.6 %all-to-all-start.2 = ((f32[32,16,128]{2,1,0:T(8,128)}), f32[32,16,128]{2,1,0:T(8,128)S(1)}, u32[]{:S(2)}, u32[]{:S(2)}) async-start(f32[32,16,128]{2,1,0:T(8,128)} %add.28), calls=%async_computation.2 | async-start | bytes 524288 | tf_op jit(solution)/shard_map/all_to_all | solution.py:293
  101.7 2.2 copy-done
  103.9 4.0 %basis_gram.1 = f32[3,256,256]{2,1,0:T(8,128)} custom-call(bf16[8,64,4096]{2,1,0:T(8,128)(2,1)S(1)} %copy-done), custom_call_target="tpu_custom_call" | custom-call | flops 1610612736 | bytes 4980736 | tf_op jit(solution)/shard_map/basis_gram/pallas_call | solution.py:112
  107.9 130.4 %all-reduce.2.cloned.1.call-done.grams = f32[3,256,256]{2,1,0:T(8,128)} async-done(((f32[3,256,256]{2,1,0:T(8,128)}), f32[3,256,256]{2,1,0:T(8,128)}) %all-reduce.2.cloned.1.call-update) | async-done | bytes 786448 | tf_op jit(solution)/shard_map/psum | solution.py:403
  238.3 1.1 copy-done.3
  239.4 11.6 %tail.1 = (bf16[64,4096]{1,0:T(8,128)(2,1)}, f32[512,64]{1,0:T(8,128)}, f32[64,64]{1,0:T(8,128)}) custom-call(f32[32,16,128]{2,1,0:T(8,128)S(1)} %all-to-all-done.2.sums, f32[3,256,256]{2,1,0:T(8,128)S(1)} %copy-done.3, bf16[8,64,4096]{2,1,0:T(8,128)(2,1)} %basis.3, f32[64,4096]{1,0:T(8,128)S(1)} %get-tuple-element.13.image), custom_call_target="tpu_custom_call" | custom-call | tf_op jit(solution)/shard_map/tail/pallas_call | solution.py:356
  (24 shorter events, 0.2 us)
Async XLA Ops:
  7.9 1.2 copy-start.1
  9.2 0.7 copy-start.8
  9.8 14.6 %copy-start.9 = (s32[16,32]{1,0:T(8,128)S(1)}, s32[16,32]{1,0:T(8,128)}, u32[]{:S(2)}) copy-start(s32[16,32]{1,0:T(8,128)} %param.18) | copy-start | bytes 6148
  9.8 14.6 %copy-start.11 = (s32[16,32]{1,0:T(8,128)S(1)}, s32[16,32]{1,0:T(8,128)}, u32[]{:S(2)}) copy-start(s32[16,32]{1,0:T(8,128)} %param.19) | copy-start | bytes 6148
  9.8 15.2 %copy-start.10 = (s32[16,8]{0,1:T(8,128)S(1)}, s32[16,8]{0,1:T(8,128)}, u32[]{:S(2)}) copy-start(s32[16,8]{0,1:T(8,128)} %param.12) | copy-start | bytes 1540
  13.6 15.3 %copy-start.7 = (s32[16]{0:T(128)S(1)}, s32[16]{0:T(128)}, u32[]{:S(2)}) copy-start(s32[16]{0:T(128)} %count_ref.3) | copy-start | bytes 196
  13.6 57.5 %all-to-all-start = ((bf16[32,8,4096]{2,1,0:T(8,128)(2,1)}), bf16[32,8,4096]{2,1,0:T(8,128)(2,1)}, u32[]{:S(2)}, u32[]{:S(2)}) async-start(bf16[32,8,4096]{2,1,0:T(8,128)(2,1)} %bitcast.1), calls=%async_computation | async-start | bytes 4194304 | tf_op jit(solution)/shard_map/all_to_all | solution.py:395
  21.0 4.1 %collective-permute-start = (bf16[64,4096]{1,0:T(8,128)(2,1)S(1)}, bf16[64,4096]{1,0:T(8,128)(2,1)S(1)}, u32[]{:S(2)}, u32[]{:S(2)}) collective-permute-start(bf16[64,4096]{1,0:T(8,128)(2,1)S(1)} %get-tuple-element.11.own), channel_id=1, source_target_pairs={{0,8},{8,16},{16,24},{1,9},{9,17},{17,25},{2,10},{10,18},{18,26},{... | collective-permute-start | bytes 1572872 | tf_op jit(solution)/shard_map/ppermute | solution.py:400
  23.1 4.9 %collective-permute-start.1 = (bf16[64,4096]{1,0:T(8,128)(2,1)S(1)}, bf16[64,4096]{1,0:T(8,128)(2,1)S(1)}, u32[]{:S(2)}, u32[]{:S(2)}) collective-permute-start(bf16[64,4096]{1,0:T(8,128)(2,1)S(1)} %get-tuple-element.11.own), channel_id=1, source_target_pairs={{8,0},{16,8},{24,16},{9,1},{17,9},{25,17},{10,2},{18,10},{26,18},{... | collective-permute-start | bytes 1572872 | tf_op jit(solution)/shard_map/ppermute | solution.py:401
  25.1 46.0 %copy-start.2 = (bf16[16,256,128]{2,1,0:T(8,128)(2,1)S(1)}, bf16[16,256,128]{2,1,0:T(8,128)(2,1)}, u32[]{:S(2)}) copy-start(bf16[16,256,128]{2,1,0:T(8,128)(2,1)} %p2m.1) | copy-start | bytes 3145732
  28.0 0.8 copy-start.5
  28.8 1.0 copy-start.6
  71.1 1.0 copy-start.4
  99.0 139.2 %all-to-all-start.2 = ((f32[32,16,128]{2,1,0:T(8,128)}), f32[32,16,128]{2,1,0:T(8,128)S(1)}, u32[]{:S(2)}, u32[]{:S(2)}) async-start(f32[32,16,128]{2,1,0:T(8,128)} %add.28), calls=%async_computation.2 | async-start | bytes 524288 | tf_op jit(solution)/shard_map/all_to_all | solution.py:293
  101.6 136.6 %all-reduce.2.cloned.1.call-start = ((), (), s32[]{:S(2)}) async-start(), calls=%async_computation.3 | async-start | bytes 1572864 | tf_op jit(solution)/shard_map/psum | solution.py:403
  101.7 2.2 copy-start
  238.3 1.1 copy-start.3
Sparse Core Ops, SparseCore 0:
  108.0 130.2 all-reduce.1

commit v2 on v1

--- a/solution.py
+++ b/solution.py
@@ -11,7 +11,7 @@
 BF16 = jnp.bfloat16
 AXES = ("gx", "bulk")
 HIGHEST = lax.Precision.HIGHEST
-VMEM_LIMIT = 48 * 1024 * 1024
+VMEM_LIMIT = 36 * 1024 * 1024
 
 
 def dot(a, b, dims=((1,), (0,)), precision=None):
@@ -91,40 +91,6 @@
     )(basis, p2m, send_list, send_count)
 
 
-def basis_gram_kernel(v_ref, out_ref):
-    blocks, rhs, width = v_ref.shape
-    half = blocks * rhs // 2
-    v = v_ref[...].reshape(2 * half, width)
-    top, bottom = v[:half], v[half:]
-
-    @pl.when(pl.program_id(0) == 0)
-    def _():
-        out_ref[...] = jnp.zeros_like(out_ref)
-
-    out_ref[0] += dot_nt(top, top)
-    out_ref[1] += dot_nt(top, bottom)
-    out_ref[2] += dot_nt(bottom, bottom)
-
-
-def basis_grams(basis, steps):
-    blocks, rhs, columns = basis.shape
-    half = blocks * rhs // 2
-    return pl.pallas_call(
-        basis_gram_kernel,
-        grid=(steps,),
-        out_shape=jax.ShapeDtypeStruct((3, half, half), F32),
-        in_specs=[pl.BlockSpec((blocks, rhs, columns // steps), lambda i: (0, 0, i))],
-        out_specs=whole((3, half, half)),
-        compiler_params=params(),
-        cost_estimate=pl.CostEstimate(
-            flops=6 * half * half * columns,
-            bytes_accessed=basis.size * 2 + 12 * half * half,
-            transcendentals=0,
-        ),
-        name="basis_gram",
-    )(basis)
-
-
 def near_kernel(src_ref, count_ref, before, own, after, blocks_ref, out_ref, wide):
     columns = own.shape[1]
     slots, panels = blocks_ref.shape[1], blocks_ref.shape[2]
@@ -175,25 +141,21 @@
     )(near_src, near_count, before, own, after, near_blocks)
 
 
-def far_kernel(halves, peers, recv, pick, m2l, p2m, near, basis, image_ref, sums_ref, lhs, loc):
+def far_kernel(halves, recv, pick, m2l, p2m, near, basis, image_ref, sums_ref, lhs, loc, both):
     leaves, panels, terms = p2m.shape
     classes = m2l.shape[0]
     blocks, rhs, columns = basis.shape
     part = rhs // halves
+    group = 8
     for h in range(halves):
-
-        def step(j, carry, h=h):
-            lanes = pl.ds(pl.multiple_of(j * 2 * terms, 2 * terms), 2 * terms)
-            got = dot(pick[h], recv[:, lanes]).astype(BF16)
-            base = pl.multiple_of((h * part + 2 * j) * leaves, 2 * leaves)
-            for t in range(2):
+        for j in range(0, part, group):
+            got = dot(pick[h], recv[:, j * terms : (j + group) * terms]).astype(BF16)
+            for t in range(group):
+                base = (h * part + j + t) * leaves
                 for c in range(classes):
-                    lhs[pl.ds(base + t * leaves, leaves), c * terms : (c + 1) * terms] = got[
+                    lhs[base : base + leaves, c * terms : (c + 1) * terms] = got[
                         c * leaves : (c + 1) * leaves, t * terms : (t + 1) * terms
                     ]
-            return carry
-
-        lax.fori_loop(0, part // 2, step, 0)
     weights = m2l[...].reshape(classes * terms, terms)
     tall = 256
     for i in range(rhs * leaves // tall):
@@ -201,53 +163,40 @@
         loc[i * tall // leaves : (i + 1) * tall // leaves] = got.reshape(
             tall // leaves, leaves, terms
         )
-    inner = jnp.zeros((2 * rhs, blocks * rhs), F32)
-    square = jnp.zeros((2 * rhs, 2 * rhs), F32)
     for g in range(leaves):
         cols = slice(g * panels, (g + 1) * panels)
-        far = dot_nt(loc[:, g, :].astype(BF16), p2m[g])
-        image = near[:, cols] + far
+        image = near[:, cols] + dot_nt(loc[:, g, :].astype(BF16), p2m[g])
         image_ref[:, cols] = image
-        both = jnp.concatenate(split_parts(image), axis=0)
-        inner += dot_nt(both, basis[:, :, cols].reshape(blocks * rhs, panels))
-        square += dot_nt(both, both)
-    products = inner[:rhs] + inner[rhs:]
-    ww = square[:rhs, :rhs] + square[:rhs, rhs:] + square[rhs:, :rhs] + square[rhs:, rhs:]
-    pack(products, ww, sums_ref)
+        both[:rhs, cols], both[rhs:, cols] = split_parts(image)
+    inner = dot_nt(both[...], basis[...].reshape(blocks * rhs, columns))
+    pack(inner[:rhs] + inner[rhs:], sums_ref)
 
 
 def pack_sizes(rhs, wide, peers):
     rows = rhs * wide // 128 // peers
-    return rows, -(-(rows + 1) // 8) * 8
-
-
-def pack(products, ww, out_ref):
-    peers, _, lanes = out_ref.shape
+    return rows, -(-rows // 8) * 8
+
+
+def pack(products, out_ref):
+    peers, piece, lanes = out_ref.shape
     rhs, wide = products.shape
     rows, _ = pack_sizes(rhs, wide, peers)
-    out_ref[...] = jnp.zeros_like(out_ref)
+    if rows < piece:
+        out_ref[...] = jnp.zeros_like(out_ref)
     tall = jnp.concatenate(
         [products[:, i * lanes : (i + 1) * lanes] for i in range(wide // lanes)], axis=0
     )
     for p in range(peers):
         out_ref[p, :rows, :] = tall[p * rows : (p + 1) * rows]
-    half = rhs // 2
-    folded = jnp.concatenate([ww[:half], ww[half:]], axis=1)
-    for i in range(half):
-        out_ref[i, rows : rows + 1, :] = folded[i : i + 1]
 
 
 def unpack(in_ref, rhs, wide):
     peers, _, lanes = in_ref.shape
     rows, _ = pack_sizes(rhs, wide, peers)
     tall = jnp.concatenate([in_ref[p, :rows, :] for p in range(peers)], axis=0)
-    products = jnp.concatenate(
+    return jnp.concatenate(
         [tall[i * rhs : (i + 1) * rhs] for i in range(wide // lanes)], axis=1
     )
-    half = rhs // 2
-    folded = jnp.concatenate([in_ref[i, rows : rows + 1, :] for i in range(half)], axis=0)
-    ww = jnp.concatenate([folded[:, :rhs], folded[:, rhs:]], axis=0)
-    return products, ww
 
 
 def far_field(recv, pick, m2l, p2m, near, basis, halves, peers):
@@ -257,7 +206,7 @@
     _, piece = pack_sizes(rhs, blocks * rhs, peers)
     args = (recv, pick, m2l, p2m, near, basis)
     return pl.pallas_call(
-        functools.partial(far_kernel, halves, peers),
+        functools.partial(far_kernel, halves),
         grid=(1,),
         out_shape=(
             jax.ShapeDtypeStruct((rhs, columns), F32),
@@ -268,10 +217,15 @@
         scratch_shapes=[
             pltpu.VMEM((rhs * leaves, classes * terms), BF16),
             pltpu.VMEM((rhs, leaves, terms), F32),
+            pltpu.VMEM((2 * rhs, columns), BF16),
         ],
         compiler_params=params(),
         name="far",
     )(*args)
+
+
+def exchange(pieces):
+    return lax.all_to_all(pieces, AXES, split_axis=0, concat_axis=0, tiled=True)
 
 
 def add_kernel(in_ref, out_ref):
@@ -280,7 +234,7 @@
 
 
 def all_sum(pieces):
-    got = lax.all_to_all(pieces, AXES, split_axis=0, concat_axis=0, tiled=True)
+    got = exchange(pieces)
     added = pl.pallas_call(
         add_kernel,
         grid=(1,),
@@ -290,7 +244,47 @@
         compiler_params=params(),
         name="add",
     )(got)
-    return lax.all_to_all(added, AXES, split_axis=0, concat_axis=0, tiled=True)
+    return exchange(added)
+
+
+def resid_kernel(total_rows, sums, basis, image, resid_ref, gram_ref, proj_ref):
+    blocks, rhs, columns = basis.shape
+    wide = blocks * rhs
+    proj = unpack(sums, rhs, wide) * (1.0 / total_rows)
+    proj_ref[...] = proj.T
+    coef = jnp.concatenate(split_parts(proj), axis=0)
+    step = 1024
+    for i in range(columns // step):
+        cols = slice(i * step, (i + 1) * step)
+        by_basis = dot(coef, basis[:, :, cols].reshape(wide, step))
+        resid = image[:, cols] - (by_basis[:rhs] + by_basis[rhs:])
+        resid_ref[:rhs, cols], resid_ref[rhs:, cols] = split_parts(resid)
+    both = resid_ref[...]
+    square = dot_nt(both, both)
+    gram = square[:rhs, :rhs] + square[:rhs, rhs:] + square[rhs:, :rhs] + square[rhs:, rhs:]
+    half = rhs // 2
+    folded = jnp.concatenate([gram[:half], gram[half:]], axis=1) * (1.0 / total_rows)
+    gram_ref[...] = jnp.broadcast_to(folded[None], gram_ref.shape)
+
+
+def residual(sums, basis, image, total_rows):
+    blocks, rhs, columns = basis.shape
+    peers = sums.shape[0]
+    args = (sums, basis, image)
+    shapes = (
+        jax.ShapeDtypeStruct((2 * rhs, columns), BF16),
+        jax.ShapeDtypeStruct((peers, rhs // 2, 2 * rhs), F32),
+        jax.ShapeDtypeStruct((blocks * rhs, rhs), F32),
+    )
+    return pl.pallas_call(
+        functools.partial(resid_kernel, total_rows),
+        grid=(1,),
+        out_shape=shapes,
+        in_specs=[whole(a.shape) for a in args],
+        out_specs=tuple(whole(s.shape) for s in shapes),
+        compiler_params=params(),
+        name="residual",
+    )(*args)
 
 
 def factored(gram):
@@ -319,63 +313,38 @@
     return upper.T, both[:, size:]
 
 
-def tail_kernel(total_rows, sums, grams, basis, image, next_ref, proj_ref, factor_ref, coef):
-    blocks, rhs, width = basis.shape
-    wide = blocks * rhs
-
-    @pl.when(pl.program_id(0) == 0)
-    def _():
-        products, ww = unpack(sums, rhs, wide)
-        proj = products * (1.0 / total_rows)
-        half = wide // 2
-        left, right = proj[:, :half], proj[:, half:]
-        scale = 1.0 / total_rows
-        g00, g01, g11 = grams[0] * scale, grams[1] * scale, grams[2] * scale
-        first = dot(left, g00, precision=HIGHEST) + dot_nt(right, g01, HIGHEST) - 2.0 * left
-        second = dot(left, g01, precision=HIGHEST) + dot(right, g11, precision=HIGHEST)
-        second = second - 2.0 * right
-        gram = ww * scale + dot_nt(first, left, HIGHEST) + dot_nt(second, right, HIGHEST)
-        lower, inverse = factored(gram)
-        factor_ref[...] = lower
-        proj_ref[...] = proj.T
-        mixed = dot(inverse, proj, precision=HIGHEST)
-        coef[:rhs, :wide], coef[rhs:, :wide] = split_parts(-mixed)
-        coef[:rhs, wide : wide + rhs], coef[rhs:, wide : wide + rhs] = split_parts(inverse)
-
-    upper, lower = split_parts(image[...])
-    by_basis = dot(coef[:, :wide], basis[...].reshape(wide, width))
-    by_image = dot(coef[:, wide : wide + rhs], upper)
-    rest = dot(coef[:rhs, wide : wide + rhs], lower)
-    total = by_basis + by_image
-    next_ref[...] = (total[:rhs] + total[rhs:] + rest).astype(BF16)
-
-
-def tail(sums, grams, basis, image, total_rows, steps):
-    blocks, rhs, columns = basis.shape
-    width = columns // steps
+def tail_kernel(grams, resid, next_ref, factor_ref):
+    rhs = factor_ref.shape[0]
+    columns = resid.shape[1]
+    folded = jnp.sum(grams[...], axis=0)
+    gram = jnp.concatenate([folded[:, :rhs], folded[:, rhs:]], axis=0)
+    lower, inverse = factored(gram)
+    factor_ref[...] = lower
+    coef = jnp.concatenate(split_parts(inverse), axis=0)
+    step = 1024
+    for i in range(columns // step):
+        cols = slice(i * step, (i + 1) * step)
+        first = dot(coef, resid[:rhs, cols])
+        second = dot(coef[:rhs], resid[rhs:, cols])
+        next_ref[:, cols] = (first[:rhs] + first[rhs:] + second).astype(BF16)
+
+
+def tail(grams, resid):
+    rhs, columns = resid.shape[0] // 2, resid.shape[1]
+    args = (grams, resid)
+    shapes = (
+        jax.ShapeDtypeStruct((rhs, columns), BF16),
+        jax.ShapeDtypeStruct((rhs, rhs), F32),
+    )
     return pl.pallas_call(
-        functools.partial(tail_kernel, total_rows),
-        grid=(steps,),
-        out_shape=(
-            jax.ShapeDtypeStruct((rhs, columns), BF16),
-            jax.ShapeDtypeStruct((blocks * rhs, rhs), F32),
-            jax.ShapeDtypeStruct((rhs, rhs), F32),
-        ),
-        in_specs=[
-            whole(sums.shape),
-            whole(grams.shape),
-            pl.BlockSpec((blocks, rhs, width), lambda i: (0, 0, i)),
-            pl.BlockSpec((rhs, width), lambda i: (0, i)),
-        ],
-        out_specs=(
-            pl.BlockSpec((rhs, width), lambda i: (0, i)),
-            whole((blocks * rhs, rhs)),
-            whole((rhs, rhs)),
-        ),
-        scratch_shapes=[pltpu.VMEM((2 * rhs, blocks * rhs + 128), BF16)],
+        tail_kernel,
+        grid=(1,),
+        out_shape=shapes,
+        in_specs=[whole(a.shape) for a in args],
+        out_specs=tuple(whole(s.shape) for s in shapes),
         compiler_params=params(),
         name="tail",
-    )(sums, grams, basis, image)
+    )(*args)
 
 
 def shards(
@@ -392,15 +361,13 @@
 
     sent, own = sent_multipoles(basis, p2m, send_list[0], send_count, halves)
     sent = sent.reshape(peers, slots * halves, sent.shape[1])
-    received = lax.all_to_all(sent, AXES, split_axis=0, concat_axis=0, tiled=True)
-    received = received.reshape(peers * slots * halves, received.shape[2])
+    received = exchange(sent).reshape(peers * slots * halves, sent.shape[2])
 
     up = [(i, i + 1) for i in range(devices - 1)]
     down = [(j, i) for i, j in up]
     before = lax.ppermute(own, "gx", up)
     after = lax.ppermute(own, "gx", down)
 
-    grams = lax.psum(basis_grams(basis, 4), AXES)
     near = near_field(near_src, near_count, before, own, after, near_blocks)
 
     class_hot = (far_class[:, None, :] == jnp.arange(classes)[None, :, None]).astype(BF16)
@@ -412,7 +379,8 @@
 
     image, sums = far_field(received, pick, m2l, p2m, near, basis, halves, peers)
     sums = all_sum(sums)
-    next_block, projections, factor = tail(sums, grams, basis, image, total_rows, 4)
+    resid, grams, projections = residual(sums, basis, image, total_rows)
+    next_block, factor = tail(exchange(grams), resid)
     return (next_block, projections.reshape(blocks, rhs, rhs), factor)
 
 

time: 259 us -> 123 us (0.47)
  waiting for transfers between devices: 159 us -> 28.5 us
  blocking collectives: 12.9 us -> 38.6 us
  Pallas kernels: 48.5 us -> 30.9 us
  between operations: 14.1 us -> 0.74 us
  local copies, waits for them, and re-layouts: 9.08 us -> 11.8 us
    psum x1 -> x0, waiting for transfers between devices: 130 us -> none  [shards(): grams = lax.psum(basis_grams(basis, 4), AXES)]
    all_to_all x1 -> x3, blocking collectives: 12.9 us -> 38.6 us  [exchange(): return lax.all_to_all(pieces, AXES, split_axis=0, concat_axis=0, tiled=True)]
    pallas_call x3, Pallas kernels: 28.8 us -> 13.2 us  [the longest x1 6.84 us: tail(): pl.pallas_call(tail_kernel, grid=(1,), out_shape=shapes, in_specs=[whole(...]
    unnamed x25 -> x29, local copies, waits for them, and re-layouts: 8.16 us -> 10.9 us
    all_to_all x2 -> x1, starting transfers between devices: 10 us -> 7.3 us  [exchange(): return lax.all_to_all(pieces, AXES, split_axis=0, concat_axis=0, tiled=True)]
    all_to_all x2 -> x1, waiting for transfers between devices: 26 us -> 26 us  [exchange(): return lax.all_to_all(pieces, AXES, split_axis=0, concat_axis=0, tiled=True)]
  transfers between devices with their start and end apart: 5 -> 3, of which waited for: 3 -> 2; matrix products, arithmetic and copies ran while one was open for 0% -> 0% of each run, Pallas kernels for 7% -> 13%
where the time goes in v2:
time: 123 us
  blocking collectives  38.6 us (31%)
  Pallas kernels  30.9 us (25%)
  waiting for transfers between devices  28.5 us (23%)
  local copies, waits for them, and re-layouts  11.8 us (10%)
  starting transfers between devices  11.5 us (9%)
    all_to_all x3, blocking collectives, exchange(): return lax.all_to_all(pieces, AXES, split_axis=0, concat_axis=0, tiled=True)  38.6 us
    all_to_all x1, waiting for transfers between devices, exchange(): return lax.all_to_all(pieces, AXES, split_axis=0, concat_axis=0, tiled=True)  26 us
    pallas_call x1, Pallas kernels, near_field(): pl.pallas_call(near_kernel, grid_spec=grid_spec, out_shape=jax.ShapeDtype...  15.7 us
    unnamed x29, local copies, waits for them, and re-layouts  10.9 us
    all_to_all x1, starting transfers between devices, exchange(): return lax.all_to_all(pieces, AXES, split_axis=0, concat_axis=0, tiled=True)  7.3 us
    pallas_call x1, Pallas kernels, tail(): pl.pallas_call(tail_kernel, grid=(1,), out_shape=shapes, in_specs=[whole(...  6.84 us
    pallas_call x1, Pallas kernels, far_field(): pl.pallas_call(functools.partial(far_kernel, halves), grid=(1,), out_shap...  4.2 us
    ppermute x1, starting transfers between devices, shards(): before = lax.ppermute(own, 'gx', up)  2.95 us
  transfers between devices with their start and end apart: 3, of which 2 were waited for; matrix products, arithmetic and copies ran while one was open for 0% of the time, Pallas kernels for 13%

profile of v2, /device:TPU:0, one launch (start us, length us, event | category | flops | bytes accessed | tf_op | source)
XLA Modules:
  0.0 122.5 jit_solution(5995036328437368681)
XLA Ops:
  0.6 0.8 copy.13.list_ref
  1.4 2.2 %copy-done = bf16[8,64,4096]{2,1,0:T(8,128)(2,1)S(1)} copy-done((bf16[8,64,4096]{2,1,0:T(8,128)(2,1)S(1)}, bf16[8,64,4096]{2,1,0:T(8,128)(2,1)}, u32[]{:S(2)}) %copy-start) | copy-done | bytes 4194328
  3.6 1.2 copy-done.3
  4.8 0.7 copy-done.10
  5.5 2.1 %send.1 = (bf16[256,4096]{1,0:T(8,128)(2,1)S(1)}, bf16[64,4096]{1,0:T(8,128)(2,1)}) custom-call(bf16[8,64,4096]{2,1,0:T(8,128)(2,1)S(1)} %copy-done, bf16[16,256,128]{2,1,0:T(8,128)(2,1)S(1)} %copy-done.3, s32[32,4]{1,0:T(8,128)S(1)} %copy.13.list_ref, s32[1,32]{1,0:T(1,128)S(1)} %copy-done.10), custom_call_target="tpu_custom_call" | custom-call | tf_op jit(solution)/shard_map/send/pallas_call | solution.py:74
  7.5 1.3 %copy-done.7 = bf16[256,4096]{1,0:T(8,128)(2,1)} copy-done((bf16[256,4096]{1,0:T(8,128)(2,1)}, bf16[256,4096]{1,0:T(8,128)(2,1)S(1)}, u32[]{:S(2)}) %copy-start.7) | copy-done | bytes 2097176
  8.9 7.3 %all-to-all-start = ((bf16[32,8,4096]{2,1,0:T(8,128)(2,1)}), bf16[32,8,4096]{2,1,0:T(8,128)(2,1)S(1)}, u32[]{:S(2)}, u32[]{:S(2)}) async-start(bf16[32,8,4096]{2,1,0:T(8,128)(2,1)} %bitcast.13), calls=%async_computation | async-start | bytes 4194304 | tf_op jit(solution)/shard_map/all_to_all | solution.py:228
  16.2 3.0 %collective-permute-start = (bf16[64,4096]{1,0:T(8,128)(2,1)}, bf16[64,4096]{1,0:T(8,128)(2,1)}, u32[]{:S(2)}, u32[]{:S(2)}) collective-permute-start(bf16[64,4096]{1,0:T(8,128)(2,1)} %get-tuple-element.13.own), channel_id=1, source_target_pairs={{0,8},{8,16},{16,24},{1,9},{9,17},{17,25},{2,10},{10,18},{18,26},{... | collective-permute-start | bytes 1572872 | tf_op jit(solution)/shard_map/ppermute | solution.py:368
  19.1 1.3 %collective-permute-start.1 = (bf16[64,4096]{1,0:T(8,128)(2,1)}, bf16[64,4096]{1,0:T(8,128)(2,1)}, u32[]{:S(2)}, u32[]{:S(2)}) collective-permute-start(bf16[64,4096]{1,0:T(8,128)(2,1)} %get-tuple-element.13.own), channel_id=1, source_target_pairs={{8,0},{16,8},{24,16},{9,1},{17,9},{25,17},{10,2},{18,10},{26,18},{... | collective-permute-start | bytes 1572872 | tf_op jit(solution)/shard_map/ppermute | solution.py:369
  20.5 0.4 fusion
  20.8 0.2 copy.14
  21.1 2.6 %collective-permute-done.1.after = bf16[64,4096]{1,0:T(8,128)(2,1)} collective-permute-done((bf16[64,4096]{1,0:T(8,128)(2,1)}, bf16[64,4096]{1,0:T(8,128)(2,1)}, u32[]{:S(2)}, u32[]{:S(2)}) %collective-permute-start.1) | collective-permute-done | bytes 524320 | tf_op jit(solution)/shard_map/ppermute | solution.py:369
  23.6 15.7 %near.1 = f32[64,4096]{1,0:T(8,128)S(1)} custom-call(s32[16,8]{1,0:T(8,128)S(1)} %copy.15.src_ref, s32[16]{0:T(128)S(1)} %copy-done.9, bf16[64,4096]{1,0:T(8,128)(2,1)} %collective-permute-done.before, bf16[64,4096]{1,0:T(8,128)(2,1)} %get-tuple-element.13.own, bf16[64,4096]{1,0:T(8,128)(2,1)} %collective-permute-done.1.after, ...), custom_call_target="tpu_custom_call" | custom-call | flops 1073741824 | bytes 20447232 | tf_op jit(solution)/shard_map/near/pallas_call | solution.py:130
  39.3 1.0 copy-done.5
  40.3 26.0 %all-to-all-done = bf16[32,8,4096]{2,1,0:T(8,128)(2,1)S(1)} async-done(((bf16[32,8,4096]{2,1,0:T(8,128)(2,1)}), bf16[32,8,4096]{2,1,0:T(8,128)(2,1)S(1)}, u32[]{:S(2)}, u32[]{:S(2)}) %all-to-all-start) | async-done | bytes 2097184 | tf_op jit(solution)/shard_map/all_to_all | solution.py:228
  66.3 2.2 %copy-done.1 = bf16[8,64,4096]{2,1,0:T(8,128)(2,1)S(1)} copy-done((bf16[8,64,4096]{2,1,0:T(8,128)(2,1)S(1)}, bf16[8,64,4096]{2,1,0:T(8,128)(2,1)}, u32[]{:S(2)}) %copy-start.1) | copy-done | bytes 4194328
  68.5 1.2 copy-done.6
  69.7 1.0 copy-done.8
  70.7 4.2 %far.1 = (f32[64,4096]{1,0:T(8,128)S(1)}, f32[32,8,128]{2,1,0:T(8,128)S(1)}) custom-call(bf16[256,4096]{1,0:T(8,128)(2,1)S(1)} %bitcast.12, bf16[2,256,256]{2,1,0:T(8,128)(2,1)S(1)} %bitcast.14, bf16[16,128,128]{2,1,0:T(8,128)(2,1)S(1)} %copy-done.8, bf16[16,256,128]{2,1,0:T(8,128)(2,1)S(1)} %copy-done.4, f32[64,4096]{1,0:T(8,128)S(1)} %copy-done.6, ...), custom_call_target="tpu_custom_call" | custom-call | tf_op jit(solution)/shard_map/far/pallas_call | solution.py:208
  74.9 10.0 %all_to_all.20.in_ref = f32[32,8,128]{2,1,0:T(8,128)S(1)} all-to-all(f32[32,8,128]{2,1,0:T(8,128)S(1)} %get-tuple-element.14), channel_id=1, replica_groups=mesh['gx'=4,'bulk'=8] {'gx','bulk'}, dimensions={0} | all-to-all | bytes 262144 | tf_op jit(solution)/shard_map/all_to_all | solution.py:228
  85.0 10.0 %all_to_all.21.sums = f32[32,8,128]{2,1,0:T(8,128)S(1)} all-to-all(f32[32,8,128]{2,1,0:T(8,128)S(1)} %add.25), channel_id=1, replica_groups=mesh['gx'=4,'bulk'=8] {'gx','bulk'}, dimensions={0} | all-to-all | bytes 262144 | tf_op jit(solution)/shard_map/all_to_all | solution.py:228
  95.0 2.1 %residual.1 = (bf16[128,4096]{1,0:T(8,128)(2,1)S(1)}, f32[32,32,128]{2,1,0:T(8,128)S(1)}, f32[512,64]{1,0:T(8,128)}) custom-call(f32[32,8,128]{2,1,0:T(8,128)S(1)} %all_to_all.21.sums, bf16[8,64,4096]{2,1,0:T(8,128)(2,1)S(1)} %copy-done.2, f32[64,4096]{1,0:T(8,128)S(1)} %get-tuple-element.15.image), custom_call_target="tpu_custom_call" | custom-call | tf_op jit(solution)/shard_map/residual/pallas_call | solution.py:279
  97.1 18.6 %all_to_all.22.grams = f32[32,32,128]{2,1,0:T(8,128)S(1)} all-to-all(f32[32,32,128]{2,1,0:T(8,128)S(1)} %get-tuple-element.16), channel_id=1, replica_groups=mesh['gx'=4,'bulk'=8] {'gx','bulk'}, dimensions={0} | all-to-all | bytes 1048576 | tf_op jit(solution)/shard_map/all_to_all | solution.py:228
  115.7 6.8 %tail.1 = (bf16[64,4096]{1,0:T(8,128)(2,1)}, f32[64,64]{1,0:T(8,128)}) custom-call(f32[32,32,128]{2,1,0:T(8,128)S(1)} %all_to_all.22.grams, bf16[128,4096]{1,0:T(8,128)(2,1)S(1)} %get-tuple-element.17.resid), custom_call_target="tpu_custom_call" | custom-call | tf_op jit(solution)/shard_map/tail/pallas_call | solution.py:339
  (25 shorter events, 0.2 us)
Async XLA Ops:
  1.4 2.2 %copy-start = (bf16[8,64,4096]{2,1,0:T(8,128)(2,1)S(1)}, bf16[8,64,4096]{2,1,0:T(8,128)(2,1)}, u32[]{:S(2)}) copy-start(bf16[8,64,4096]{2,1,0:T(8,128)(2,1)} %basis.3) | copy-start | bytes 12582916
  3.6 1.2 copy-start.3
  4.8 0.7 copy-start.10
  5.5 15.0 %copy-start.11 = (s32[16,32]{1,0:T(8,128)S(1)}, s32[16,32]{1,0:T(8,128)}, u32[]{:S(2)}) copy-start(s32[16,32]{1,0:T(8,128)} %param.18) | copy-start | bytes 6148
  5.5 15.0 %copy-start.13 = (s32[16,32]{1,0:T(8,128)S(1)}, s32[16,32]{1,0:T(8,128)}, u32[]{:S(2)}) copy-start(s32[16,32]{1,0:T(8,128)} %param.19) | copy-start | bytes 6148
  5.5 15.5 %copy-start.12 = (s32[16,8]{0,1:T(8,128)S(1)}, s32[16,8]{0,1:T(8,128)}, u32[]{:S(2)}) copy-start(s32[16,8]{0,1:T(8,128)} %param.12) | copy-start | bytes 1540
  7.5 1.3 %copy-start.7 = (bf16[256,4096]{1,0:T(8,128)(2,1)}, bf16[256,4096]{1,0:T(8,128)(2,1)S(1)}, u32[]{:S(2)}) copy-start(bf16[256,4096]{1,0:T(8,128)(2,1)S(1)} %get-tuple-element.12) | copy-start | bytes 6291460
  8.9 14.8 %copy-start.9 = (s32[16]{0:T(128)S(1)}, s32[16]{0:T(128)}, u32[]{:S(2)}) copy-start(s32[16]{0:T(128)} %count_ref.3) | copy-start | bytes 196
  8.9 57.4 %all-to-all-start = ((bf16[32,8,4096]{2,1,0:T(8,128)(2,1)}), bf16[32,8,4096]{2,1,0:T(8,128)(2,1)S(1)}, u32[]{:S(2)}, u32[]{:S(2)}) async-start(bf16[32,8,4096]{2,1,0:T(8,128)(2,1)} %bitcast.13), calls=%async_computation | async-start | bytes 4194304 | tf_op jit(solution)/shard_map/all_to_all | solution.py:228
  16.2 4.9 %collective-permute-start = (bf16[64,4096]{1,0:T(8,128)(2,1)}, bf16[64,4096]{1,0:T(8,128)(2,1)}, u32[]{:S(2)}, u32[]{:S(2)}) collective-permute-start(bf16[64,4096]{1,0:T(8,128)(2,1)} %get-tuple-element.13.own), channel_id=1, source_target_pairs={{0,8},{8,16},{16,24},{1,9},{9,17},{17,25},{2,10},{10,18},{18,26},{... | collective-permute-start | bytes 1572872 | tf_op jit(solution)/shard_map/ppermute | solution.py:368
  19.1 4.5 %collective-permute-start.1 = (bf16[64,4096]{1,0:T(8,128)(2,1)}, bf16[64,4096]{1,0:T(8,128)(2,1)}, u32[]{:S(2)}, u32[]{:S(2)}) collective-permute-start(bf16[64,4096]{1,0:T(8,128)(2,1)} %get-tuple-element.13.own), channel_id=1, source_target_pairs={{8,0},{16,8},{24,16},{9,1},{17,9},{25,17},{10,2},{18,10},{26,18},{... | collective-permute-start | bytes 1572872 | tf_op jit(solution)/shard_map/ppermute | solution.py:369
  21.1 45.2 %copy-start.4 = (bf16[16,256,128]{2,1,0:T(8,128)(2,1)S(1)}, bf16[16,256,128]{2,1,0:T(8,128)(2,1)}, u32[]{:S(2)}) copy-start(bf16[16,256,128]{2,1,0:T(8,128)(2,1)} %p2m.1) | copy-start | bytes 3145732
  39.3 1.0 copy-start.5
  66.3 2.2 %copy-start.1 = (bf16[8,64,4096]{2,1,0:T(8,128)(2,1)S(1)}, bf16[8,64,4096]{2,1,0:T(8,128)(2,1)}, u32[]{:S(2)}) copy-start(bf16[8,64,4096]{2,1,0:T(8,128)(2,1)} %basis.3) | copy-start | bytes 12582916
  68.5 1.2 copy-start.6
  69.7 1.0 copy-start.8
  70.7 24.2 %copy-start.2 = (bf16[8,64,4096]{2,1,0:T(8,128)(2,1)S(1)}, bf16[8,64,4096]{2,1,0:T(8,128)(2,1)}, u32[]{:S(2)}) copy-start(bf16[8,64,4096]{2,1,0:T(8,128)(2,1)} %basis.3) | copy-start | bytes 12582916

commit v3 on v2

--- a/solution.py
+++ b/solution.py
@@ -9,9 +9,8 @@
 
 F32 = jnp.float32
 BF16 = jnp.bfloat16
-AXES = ("gx", "bulk")
-HIGHEST = lax.Precision.HIGHEST
-VMEM_LIMIT = 36 * 1024 * 1024
+AXES = ("gx", "hi", "lo")
+MIB = 1024 * 1024
 
 
 def dot(a, b, dims=((1,), (0,)), precision=None):
@@ -28,67 +27,115 @@
     return (upper, lower)
 
 
-def params(**kwargs):
-    return pltpu.CompilerParams(vmem_limit_bytes=VMEM_LIMIT, **kwargs)
+def params(mib):
+    return pltpu.CompilerParams(vmem_limit_bytes=mib * MIB)
+
+
+def in_hbm(array):
+    return pltpu.with_memory_space_constraint(array, pltpu.HBM)
 
 
 def whole(shape):
     return pl.BlockSpec(shape, lambda *_: (0,) * len(shape))
 
 
-def send_kernel(halves, x_ref, p2m_ref, list_ref, count_ref, out_ref, copy_ref, scratch):
-    leaves, panels, terms = p2m_ref.shape
-    rhs = x_ref.shape[1]
-    peers, slots = list_ref.shape
+def chosen_rows(listing, leaves, slots, halves):
+    receivers = listing.shape[0]
+    rows = receivers * slots * halves
+    row = lax.broadcasted_iota(jnp.int32, (rows, receivers), 0) // (slots * halves)
+    hot = row == lax.broadcasted_iota(jnp.int32, (rows, receivers), 1)
+    spread = dot(hot.astype(F32).astype(BF16), listing)
+    row = lax.broadcasted_iota(jnp.int32, spread.shape, 0)
+    lane = lax.broadcasted_iota(jnp.int32, spread.shape, 1)
+    slot = row // halves % slots
+    leaf = jnp.sum(jnp.where(lane == slot, spread, 0.0), axis=1, keepdims=True)
+    live = jnp.sum(jnp.where(lane == slots, spread, 0.0), axis=1, keepdims=True)
+    row = lax.broadcasted_iota(jnp.int32, (rows, leaves * halves), 0)
+    lane = lax.broadcasted_iota(jnp.int32, (rows, leaves * halves), 1)
+    wanted = leaf * halves + (row % halves).astype(F32)
+    held = (row // halves % slots).astype(F32) < live
+    return ((lane.astype(F32) == wanted) & held).astype(F32).astype(BF16)
+
+
+def one_side(listing, side, near_devices):
+    peers = listing.shape[0]
+    rows = lax.broadcasted_iota(jnp.int32, (peers // 2, peers), 0)
+    wanted = rows // near_devices * (2 * near_devices) + side * near_devices + rows % near_devices
+    hot = wanted == lax.broadcasted_iota(jnp.int32, (peers // 2, peers), 1)
+    return dot(hot.astype(F32).astype(BF16), listing).astype(BF16)
+
+
+def send_kernel(halves, slots, near_devices, side, x, p2m, listing, out, whole_out, own, scratch):
+    leaves, panels, terms = p2m.shape
+    rhs = x.shape[1]
     part = rhs // halves
-    rows = peers * slots * halves
-    copy_ref[...] = x_ref[0]
+    own[...] = x[0]
     for g in range(leaves):
-        mult = dot(x_ref[0, :, g * panels : (g + 1) * panels], p2m_ref[g])
+        mult = dot(x[0, :, g * panels : (g + 1) * panels], p2m[g])
         for h in range(halves):
             scratch[:, g * halves + h, :] = mult[h * part : (h + 1) * part]
-    row = lax.broadcasted_iota(jnp.int32, (rows, peers), 0) // (slots * halves)
-    peer_hot = row == lax.broadcasted_iota(jnp.int32, (rows, peers), 1)
-    listed = dot(peer_hot.astype(BF16), list_ref[...].astype(F32).astype(BF16))
-    row_s = lax.broadcasted_iota(jnp.int32, (rows, slots), 0) // halves % slots
-    lane_s = lax.broadcasted_iota(jnp.int32, (rows, slots), 1)
-    leaf = jnp.sum(jnp.where(row_s == lane_s, listed, 0.0), axis=1, keepdims=True)
-    counts = jnp.broadcast_to(count_ref[...].astype(F32), (rows, peers))
-    live = jnp.sum(jnp.where(peer_hot, counts, 0.0), axis=1, keepdims=True)
-    row_k = lax.broadcasted_iota(jnp.int32, (rows, leaves * halves), 0)
-    lane_k = lax.broadcasted_iota(jnp.int32, (rows, leaves * halves), 1)
-    half = row_k % halves
-    slot = (row_k // halves % slots).astype(F32)
-    wanted = leaf * halves + half.astype(F32)
-    chosen = ((lane_k.astype(F32) == wanted) & (slot < live)).astype(F32).astype(BF16)
+    lists = listing[...]
+    chosen = chosen_rows(one_side(lists, side[0], near_devices), leaves, slots, halves)
+    tall = leaves * halves
     for j in range(part // 2):
-        pair = jnp.concatenate([scratch[2 * j], scratch[2 * j + 1]], axis=1).astype(BF16)
-        out_ref[:, j * 2 * terms : (j + 1) * 2 * terms] = dot(chosen, pair).astype(BF16)
-
-
-def sent_multipoles(basis, p2m, send_list, send_count, halves):
+        first, second = scratch[2 * j].astype(BF16), scratch[2 * j + 1].astype(BF16)
+        whole_out[2 * j * tall : (2 * j + 1) * tall, :] = first
+        whole_out[(2 * j + 1) * tall : (2 * j + 2) * tall, :] = second
+        pair = jnp.concatenate([first, second], axis=1)
+        out[:, j * 2 * terms : (j + 1) * 2 * terms] = dot(chosen, pair).astype(BF16)
+    whole_out[part * tall :, :] = one_side(lists, 1 - side[0], near_devices)
+
+
+def relay_kernel(halves, slots, leaves, given, out):
+    tall, terms = leaves * halves, given.shape[1]
+    part = out.shape[1] // terms
+    chosen = chosen_rows(given[part * tall :, :], leaves, slots, halves)
+    for j in range(part // 2):
+        rows = [given[i * tall : (i + 1) * tall, :] for i in (2 * j, 2 * j + 1)]
+        pair = jnp.concatenate(rows, axis=1)
+        out[:, j * 2 * terms : (j + 1) * 2 * terms] = dot(chosen, pair).astype(BF16)
+
+
+def sent_multipoles(side, basis, p2m, listing, slots, halves):
     blocks, rhs, columns = basis.shape
     leaves, panels, terms = p2m.shape
-    peers, slots = send_list.shape
-    rows, width = peers * slots * halves, rhs // halves * terms
-    return pl.pallas_call(
-        functools.partial(send_kernel, halves),
-        grid=(1,),
-        out_shape=(
-            jax.ShapeDtypeStruct((rows, width), BF16),
-            jax.ShapeDtypeStruct((rhs, columns), BF16),
-        ),
+    peers = listing.shape[0]
+    rows, width = peers // 2 * slots * halves, rhs // halves * terms
+    shapes = (
+        jax.ShapeDtypeStruct((rows, width), BF16),
+        jax.ShapeDtypeStruct((rhs * leaves + peers // 2, terms), BF16),
+        jax.ShapeDtypeStruct((rhs, columns), BF16),
+    )
+    return pl.pallas_call(
+        functools.partial(send_kernel, halves, slots, lax.axis_size("lo")),
+        grid=(1,),
+        out_shape=shapes,
         in_specs=[
+            pl.BlockSpec(memory_space=pltpu.SMEM),
             pl.BlockSpec((1, rhs, columns), lambda i: (blocks - 1, 0, 0)),
             whole(p2m.shape),
-            whole(send_list.shape),
-            whole(send_count.shape),
+            whole(listing.shape),
         ],
-        out_specs=(whole((rows, width)), whole((rhs, columns))),
+        out_specs=tuple(whole(s.shape) for s in shapes),
         scratch_shapes=[pltpu.VMEM((rhs // halves, leaves * halves, terms), F32)],
-        compiler_params=params(),
+        compiler_params=params(20),
         name="send",
-    )(basis, p2m, send_list, send_count)
+    )(side, in_hbm(basis), in_hbm(p2m), listing)
+
+
+def relayed_multipoles(given, leaves, slots, halves, rhs):
+    receivers = given.shape[0] - rhs * leaves
+    shape = (receivers * slots * halves, rhs // halves * given.shape[1])
+    return pl.pallas_call(
+        functools.partial(relay_kernel, halves, slots, leaves),
+        grid=(1,),
+        out_shape=jax.ShapeDtypeStruct(shape, BF16),
+        in_specs=[whole(given.shape)],
+        out_specs=whole(shape),
+        compiler_params=params(16),
+        cost_estimate=pl.CostEstimate(flops=shape[0] * shape[1] * 64, bytes_accessed=2**21, transcendentals=0),
+        name="relay",
+    )(given)
 
 
 def near_kernel(src_ref, count_ref, before, own, after, blocks_ref, out_ref, wide):
@@ -102,14 +149,16 @@
         wide[:, columns : 2 * columns] = own[...]
         wide[:, 2 * columns :] = after[...]
 
-    here = pl.ds(pl.multiple_of(columns + g * panels, panels), panels)
-    total = wide[:, here].astype(F32)
-    for k in range(slots):
-        place = pl.multiple_of(src_ref[g, k] * panels, panels)
-        source = wide[:, pl.ds(place, panels)]
-        source = jnp.where(k < count_ref[g], source, jnp.zeros_like(source))
-        total += dot_nt(source, blocks_ref[0, k])
-    out_ref[...] = total
+    for i in range(blocks_ref.shape[0]):
+        leaf = g * blocks_ref.shape[0] + i
+        here = pl.ds(pl.multiple_of(columns + leaf * panels, panels), panels)
+        total = [wide[:, here].astype(F32), 0.0]
+        for k in range(slots):
+            place = pl.multiple_of(src_ref[leaf, k] * panels, panels)
+            source = wide[:, pl.ds(place, panels)]
+            source = jnp.where(k < count_ref[leaf], source, jnp.zeros_like(source))
+            total[k % 2] += dot_nt(source, blocks_ref[i, k])
+        out_ref[:, i * panels : (i + 1) * panels] = total[0] + total[1]
 
 
 def near_field(near_src, near_count, before, own, after, near_blocks):
@@ -117,21 +166,21 @@
     rhs, columns = own.shape
     grid_spec = pltpu.PrefetchScalarGridSpec(
         num_scalar_prefetch=2,
-        grid=(leaves,),
+        grid=(leaves // 2,),
         in_specs=[
             whole((rhs, columns)),
             whole((rhs, columns)),
             whole((rhs, columns)),
-            pl.BlockSpec((1, slots, panels, panels), lambda g, *_: (g, 0, 0, 0)),
+            pl.BlockSpec((2, slots, panels, panels), lambda g, *_: (g, 0, 0, 0)),
         ],
-        out_specs=pl.BlockSpec((rhs, panels), lambda g, *_: (0, g)),
+        out_specs=pl.BlockSpec((rhs, 2 * panels), lambda g, *_: (0, g)),
         scratch_shapes=[pltpu.VMEM((rhs, 3 * columns), BF16)],
     )
     return pl.pallas_call(
         near_kernel,
         grid_spec=grid_spec,
         out_shape=jax.ShapeDtypeStruct((rhs, columns), F32),
-        compiler_params=params(),
+        compiler_params=params(16),
         cost_estimate=pl.CostEstimate(
             flops=2 * rhs * near_blocks.size,
             bytes_accessed=near_blocks.size * 2 + 7 * rhs * columns * 2,
@@ -141,12 +190,25 @@
     )(near_src, near_count, before, own, after, near_blocks)
 
 
-def far_kernel(halves, recv, pick, m2l, p2m, near, basis, image_ref, sums_ref, lhs, loc, both):
+def far_kernel(
+    halves, ours, theirs, pick, near, m2l_hbm, p2m_hbm, basis_hbm, image_ref, sums_ref, *scratch
+):
+    recv, lhs, loc, both, m2l, p2m, basis, sems = scratch
+    moves = [
+        pltpu.make_async_copy(source, target, sems.at[i])
+        for i, (source, target) in enumerate(
+            ((m2l_hbm, m2l), (p2m_hbm, p2m), (basis_hbm, basis))
+        )
+    ]
+    for move in moves:
+        move.start()
     leaves, panels, terms = p2m.shape
     classes = m2l.shape[0]
     blocks, rhs, columns = basis.shape
     part = rhs // halves
     group = 8
+    rows = ours.shape[0]
+    recv[:rows], recv[rows:] = ours[...], theirs[...]
     for h in range(halves):
         for j in range(0, part, group):
             got = dot(pick[h], recv[:, j * terms : (j + group) * terms]).astype(BF16)
@@ -156,6 +218,7 @@
                     lhs[base : base + leaves, c * terms : (c + 1) * terms] = got[
                         c * leaves : (c + 1) * leaves, t * terms : (t + 1) * terms
                     ]
+    moves[0].wait()
     weights = m2l[...].reshape(classes * terms, terms)
     tall = 256
     for i in range(rhs * leaves // tall):
@@ -163,11 +226,13 @@
         loc[i * tall // leaves : (i + 1) * tall // leaves] = got.reshape(
             tall // leaves, leaves, terms
         )
+    moves[1].wait()
     for g in range(leaves):
         cols = slice(g * panels, (g + 1) * panels)
         image = near[:, cols] + dot_nt(loc[:, g, :].astype(BF16), p2m[g])
         image_ref[:, cols] = image
         both[:rhs, cols], both[rhs:, cols] = split_parts(image)
+    moves[2].wait()
     inner = dot_nt(both[...], basis[...].reshape(blocks * rhs, columns))
     pack(inner[:rhs] + inner[rhs:], sums_ref)
 
@@ -199,12 +264,13 @@
     )
 
 
-def far_field(recv, pick, m2l, p2m, near, basis, halves, peers):
+def far_field(ours, theirs, pick, m2l, p2m, near, basis, halves, peers):
     leaves, panels, terms = p2m.shape
     classes = m2l.shape[0]
     blocks, rhs, columns = basis.shape
     _, piece = pack_sizes(rhs, blocks * rhs, peers)
-    args = (recv, pick, m2l, p2m, near, basis)
+    args = (ours, theirs, pick, near)
+    anywhere = pl.BlockSpec(memory_space=pl.ANY)
     return pl.pallas_call(
         functools.partial(far_kernel, halves),
         grid=(1,),
@@ -212,20 +278,25 @@
             jax.ShapeDtypeStruct((rhs, columns), F32),
             jax.ShapeDtypeStruct((peers, piece, 128), F32),
         ),
-        in_specs=[whole(a.shape) for a in args],
+        in_specs=[whole(a.shape) for a in args] + [anywhere] * 3,
         out_specs=(whole((rhs, columns)), whole((peers, piece, 128))),
         scratch_shapes=[
+            pltpu.VMEM((2 * ours.shape[0], ours.shape[1]), BF16),
             pltpu.VMEM((rhs * leaves, classes * terms), BF16),
             pltpu.VMEM((rhs, leaves, terms), F32),
             pltpu.VMEM((2 * rhs, columns), BF16),
+            pltpu.VMEM(m2l.shape, BF16),
+            pltpu.VMEM(p2m.shape, BF16),
+            pltpu.VMEM(basis.shape, BF16),
+            pltpu.SemaphoreType.DMA((3,)),
         ],
-        compiler_params=params(),
+        compiler_params=params(32),
         name="far",
-    )(*args)
-
-
-def exchange(pieces):
-    return lax.all_to_all(pieces, AXES, split_axis=0, concat_axis=0, tiled=True)
+    )(*args, in_hbm(m2l), in_hbm(p2m), in_hbm(basis))
+
+
+def exchange(pieces, axes=AXES):
+    return lax.all_to_all(pieces, axes, split_axis=0, concat_axis=0, tiled=True)
 
 
 def add_kernel(in_ref, out_ref):
@@ -233,18 +304,17 @@
     out_ref[...] = jnp.broadcast_to(total[None], out_ref.shape)
 
 
-def all_sum(pieces):
-    got = exchange(pieces)
-    added = pl.pallas_call(
+def added(pieces, copies):
+    shape = (copies, *pieces.shape[1:])
+    return pl.pallas_call(
         add_kernel,
         grid=(1,),
-        out_shape=jax.ShapeDtypeStruct(pieces.shape, F32),
+        out_shape=jax.ShapeDtypeStruct(shape, F32),
         in_specs=[whole(pieces.shape)],
-        out_specs=whole(pieces.shape),
-        compiler_params=params(),
+        out_specs=whole(shape),
+        compiler_params=params(16),
         name="add",
-    )(got)
-    return exchange(added)
+    )(pieces)
 
 
 def resid_kernel(total_rows, sums, basis, image, resid_ref, gram_ref, proj_ref):
@@ -267,13 +337,12 @@
     gram_ref[...] = jnp.broadcast_to(folded[None], gram_ref.shape)
 
 
-def residual(sums, basis, image, total_rows):
-    blocks, rhs, columns = basis.shape
-    peers = sums.shape[0]
+def residual(sums, basis, image, total_rows, copies):
+    blocks, rhs, columns = basis.shape
     args = (sums, basis, image)
     shapes = (
         jax.ShapeDtypeStruct((2 * rhs, columns), BF16),
-        jax.ShapeDtypeStruct((peers, rhs // 2, 2 * rhs), F32),
+        jax.ShapeDtypeStruct((copies, rhs // 2, 2 * rhs), F32),
         jax.ShapeDtypeStruct((blocks * rhs, rhs), F32),
     )
     return pl.pallas_call(
@@ -282,7 +351,7 @@
         out_shape=shapes,
         in_specs=[whole(a.shape) for a in args],
         out_specs=tuple(whole(s.shape) for s in shapes),
-        compiler_params=params(),
+        compiler_params=params(24),
         name="residual",
     )(*args)
 
@@ -342,7 +411,7 @@
         out_shape=shapes,
         in_specs=[whole(a.shape) for a in args],
         out_specs=tuple(whole(s.shape) for s in shapes),
-        compiler_params=params(),
+        compiler_params=params(16),
         name="tail",
     )(*args)
 
@@ -353,38 +422,53 @@
     blocks, rhs, columns = basis.shape
     leaves = near_src.shape[0]
     classes, terms, _ = m2l.shape
-    devices = lax.axis_size("gx")
-    peers = devices * lax.axis_size("bulk")
+    devices, near_devices = lax.axis_size("gx"), lax.axis_size("lo")
+    peers = 2 * devices * near_devices
     slots = send_list.shape[2]
     total_rows = columns * peers
     halves = 2
-
-    sent, own = sent_multipoles(basis, p2m, send_list[0], send_count, halves)
-    sent = sent.reshape(peers, slots * halves, sent.shape[1])
-    received = exchange(sent).reshape(peers * slots * halves, sent.shape[2])
+    side = lax.axis_index("hi")
+    same_side = ("gx", "lo")
+
+    listing = jnp.concatenate([send_list[0], send_count[0][:, None]], axis=1)
+    listing = jnp.pad(listing, ((0, 0), (0, terms - slots - 1))).astype(BF16)
+    sent, given, own = sent_multipoles(side[None], basis, p2m, listing, slots, halves)
+    given = lax.ppermute(given, "hi", [(0, 1), (1, 0)])
+    ours = exchange(sent.reshape(peers // 2, slots * halves, -1), same_side).reshape(sent.shape)
 
     up = [(i, i + 1) for i in range(devices - 1)]
     down = [(j, i) for i, j in up]
     before = lax.ppermute(own, "gx", up)
     after = lax.ppermute(own, "gx", down)
 
+    relayed = relayed_multipoles(given, leaves, slots, halves, rhs)
+    theirs = exchange(relayed.reshape(peers // 2, slots * halves, -1), same_side)
+    theirs = theirs.reshape(sent.shape)
+
     near = near_field(near_src, near_count, before, own, after, near_blocks)
 
+    sender = far_src // slots
+    place = sender // (2 * near_devices) * near_devices + sender % near_devices
+    place = place + jnp.where(sender // near_devices % 2 == side, 0, peers // 2)
+    place = place * slots + far_src % slots
     class_hot = (far_class[:, None, :] == jnp.arange(classes)[None, :, None]).astype(BF16)
     rows = jnp.arange(peers * slots * halves)[None, None, None, :]
-    wanted = far_src[None, :, :, None] * halves + jnp.arange(halves)[:, None, None, None]
+    wanted = place[None, :, :, None] * halves + jnp.arange(halves)[:, None, None, None]
     source_hot = (wanted == rows).astype(BF16)
     pick = jnp.einsum("gce,hgef->hcgf", class_hot, source_hot, preferred_element_type=F32)
     pick = pick.astype(BF16).reshape(halves, classes * leaves, -1)
 
-    image, sums = far_field(received, pick, m2l, p2m, near, basis, halves, peers)
-    sums = all_sum(sums)
-    resid, grams, projections = residual(sums, basis, image, total_rows)
-    next_block, factor = tail(exchange(grams), resid)
+    image, sums = far_field(ours, theirs, pick, m2l, p2m, near, basis, halves, peers)
+    sums = exchange(added(exchange(sums), peers))
+    resid, grams, projections = residual(sums, basis, image, total_rows, 2 * near_devices)
+    grams = exchange(added(exchange(grams, ("hi", "lo")), devices), ("gx",))
+    next_block, factor = tail(grams, resid)
     return (next_block, projections.reshape(blocks, rhs, rhs), factor)
 
 
 def solution(mesh):
+    devices, segments = mesh.shape["gx"], mesh.shape["bulk"]
+    mesh = jax.sharding.Mesh(mesh.devices.reshape(devices, 2, segments // 2), AXES)
     return jax.shard_map(
         shards,
         mesh=mesh,

time: 123 us -> 133 us (1.081)
  waiting for transfers between devices: 28.5 us -> 16.3 us
  blocking collectives: 38.6 us -> 49.9 us
  starting transfers between devices: 11.5 us -> 21.3 us
  Pallas kernels: 30.9 us -> 27.8 us
  other arithmetic: 0.01 us -> 2.09 us
    all_to_all x1 -> x2, waiting for transfers between devices: 26 us -> 0.8 us  [exchange(): return lax.all_to_all(pieces, axes, split_axis=0, concat_axis=0, tiled=True)]
    ppermute x0 -> x1, waiting for transfers between devices: none -> 15.5 us  [shards(): given = lax.ppermute(given, 'hi', [(0, 1), (1, 0)])]
    all_to_all x3 -> x4, blocking collectives: 38.6 us -> 49.9 us  [exchange(): return lax.all_to_all(pieces, axes, split_axis=0, concat_axis=0, tiled=True)]
    pallas_call x1, Pallas kernels: 15.7 us -> 8 us  [near_field(): pl.pallas_call(near_kernel, grid_spec=grid_spec, out_shape=jax.ShapeDtype...]
    all_to_all x1 -> x2, starting transfers between devices: 7.3 us -> 13.5 us  [exchange(): return lax.all_to_all(pieces, axes, split_axis=0, concat_axis=0, tiled=True)]
    pallas_call x2 -> x4, Pallas kernels: 2.11 us -> 5.25 us  [the longest x1 3.6 us: sent_multipoles(): pl.pallas_call(functools.partial(send_kernel, halves, slots, lax.axis_siz...]
    ppermute x0 -> x1, starting transfers between devices: none -> 2.65 us  [shards(): given = lax.ppermute(given, 'hi', [(0, 1), (1, 0)])]
    ppermute x1, waiting for transfers between devices: 2.55 us -> 0.01 us  [shards(): after = lax.ppermute(own, 'gx', down)]
  transfers between devices with their start and end apart: 3 -> 5, of which waited for: 2 -> 2; matrix products, arithmetic and copies ran while one was open for 0% -> 2% of each run, Pallas kernels for 13% -> 7%
where the time goes in v3:
time: 133 us; the launch traced here: 132 us
  blocking collectives  49.9 us (38%)
  Pallas kernels  27.8 us (21%)
  starting transfers between devices  21.3 us (16%)
  waiting for transfers between devices  16.3 us (12%)
  local copies, waits for them, and re-layouts  12.5 us (9%)
  other arithmetic  2.09 us (2%)
    all_to_all x4, blocking collectives, exchange(): return lax.all_to_all(pieces, axes, split_axis=0, concat_axis=0, tiled=True)  49.9 us
    ppermute x1, waiting for transfers between devices, shards(): given = lax.ppermute(given, 'hi', [(0, 1), (1, 0)])  15.5 us
    all_to_all x2, starting transfers between devices, exchange(): return lax.all_to_all(pieces, axes, split_axis=0, concat_axis=0, tiled=True)  13.5 us
    unnamed x15, local copies, waits for them, and re-layouts  12.3 us
    pallas_call x1, Pallas kernels, near_field(): pl.pallas_call(near_kernel, grid_spec=grid_spec, out_shape=jax.ShapeDtype...  8 us
    pallas_call x1, Pallas kernels, tail(): pl.pallas_call(tail_kernel, grid=(1,), out_shape=shapes, in_specs=[whole(...  6.84 us
    pallas_call x1, Pallas kernels, far_field(): pl.pallas_call(functools.partial(far_kernel, halves), grid=(1,), out_shap...  5.62 us
    ppermute x1, starting transfers between devices, shards(): before = lax.ppermute(own, 'gx', up)  3.86 us
  transfers between devices with their start and end apart: 5, of which 2 were waited for; matrix products, arithmetic and copies ran while one was open for 2% of the time, Pallas kernels for 7%

profile of v3, /device:TPU:0, one launch (start us, length us, event | category | flops | bytes accessed | tf_op | source)
XLA Modules:
  0.0 131.7 jit_solution(6965974328093567211)
XLA Ops:
  2.1 3.6 %send.1 = (bf16[128,4096]{1,0:T(8,128)(2,1)}, bf16[1040,128]{1,0:T(8,128)(2,1)S(1)}, bf16[64,4096]{1,0:T(8,128)(2,1)S(1)}) custom-call(s32[1]{0:T(128)} %bitcast.side, bf16[8,64,4096]{2,1,0:T(8,128)(2,1)} %basis.1, bf16[16,256,128]{2,1,0:T(8,128)(2,1)} %p2m_hbm.1, bf16[32,128]{1,0:T(8,128)(2,1)S(1)} %pad.5.listing), custom_call_target="tpu_custom_call" | custom-call | tf_op jit(solution)/shard_map/send/pallas_call | solution.py:109
  5.7 6.3 %all-to-all-start = ((bf16[16,8,4096]{2,1,0:T(8,128)(2,1)}), bf16[16,8,4096]{2,1,0:T(8,128)(2,1)S(1)}, u32[]{:S(2)}, u32[]{:S(2)}) async-start(bf16[16,8,4096]{2,1,0:T(8,128)(2,1)} %bitcast.3), calls=%async_computation | async-start | bytes 2097152 | tf_op jit(solution)/shard_map/all_to_all | solution.py:299
  12.0 2.6 %collective-permute-start = (bf16[1040,128]{1,0:T(8,128)(2,1)S(1)}, bf16[1040,128]{1,0:T(8,128)(2,1)S(1)}, u32[]{:S(2)}, u32[]{:S(2)}) collective-permute-start(bf16[1040,128]{1,0:T(8,128)(2,1)S(1)} %get-tuple-element.14), channel_id=1, source_target_pairs={{0,4},{4,0},{1,5},{5,1},{2,6},{6,2},{3,7},{7,3},{8,12},{12,8},{9,1... | collective-permute-start | bytes 798728 | tf_op jit(solution)/shard_map/ppermute | solution.py:436
  14.7 15.5 %collective-permute-done.given = bf16[1040,128]{1,0:T(8,128)(2,1)S(1)} collective-permute-done((bf16[1040,128]{1,0:T(8,128)(2,1)S(1)}, bf16[1040,128]{1,0:T(8,128)(2,1)S(1)}, u32[]{:S(2)}, u32[]{:S(2)}) %collective-permute-start) | collective-permute-done | bytes 266272 | tf_op jit(solution)/shard_map/ppermute | solution.py:436
  30.1 1.6 %relay.1 = bf16[128,4096]{1,0:T(8,128)(2,1)} custom-call(bf16[1040,128]{1,0:T(8,128)(2,1)S(1)} %collective-permute-done.given), custom_call_target="tpu_custom_call" | custom-call | flops 33554432 | bytes 2097152 | tf_op jit(solution)/shard_map/relay/pallas_call | solution.py:129
  31.7 0.8 all-to-all-done
  32.5 7.2 %all-to-all-start.1 = ((bf16[16,8,4096]{2,1,0:T(8,128)(2,1)}), bf16[16,8,4096]{2,1,0:T(8,128)(2,1)S(1)}, u32[]{:S(2)}, u32[]{:S(2)}) async-start(bf16[16,8,4096]{2,1,0:T(8,128)(2,1)} %bitcast.5), calls=%async_computation.1 | async-start | bytes 2097152 | tf_op jit(solution)/shard_map/all_to_all | solution.py:299
  39.7 1.3 collective-permute-start.2
  41.0 3.9 %collective-permute-start.1 = (bf16[64,4096]{1,0:T(8,128)(2,1)S(1)}, bf16[64,4096]{1,0:T(8,128)(2,1)}, u32[]{:S(2)}, u32[]{:S(2)}) collective-permute-start(bf16[64,4096]{1,0:T(8,128)(2,1)S(1)} %get-tuple-element.15.own), channel_id=1, source_target_pairs={{0,8},{8,16},{16,24},{1,9},{9,17},{17,25},{2,10},{10,18},{18,26},{... | collective-permute-start | bytes 1572872 | tf_op jit(solution)/shard_map/ppermute | solution.py:441
  45.6 0.8 copy.19.src_ref
  46.4 1.1 fusion
  47.6 0.8 copy-done.4
  48.4 5.8 %copy-done.1 = bf16[16,8,256,256]{3,2,1,0:T(8,128)(2,1)S(1)} copy-done((bf16[16,8,256,256]{3,2,1,0:T(8,128)(2,1)S(1)}, bf16[16,8,256,256]{3,2,1,0:T(8,128)(2,1)}, u32[]{:S(2)}) %copy-start.1) | copy-done | bytes 16777240
  54.2 1.0 copy-done.3
  55.2 1.0 copy-done.5
  56.9 8.0 %near.1 = f32[64,4096]{1,0:T(8,128)S(1)} custom-call(s32[16,8]{1,0:T(8,128)S(1)} %copy.19.src_ref, s32[16]{0:T(128)S(1)} %copy-done.6, bf16[64,4096]{1,0:T(8,128)(2,1)} %collective-permute-done.1.before, bf16[64,4096]{1,0:T(8,128)(2,1)S(1)} %copy-done.3, bf16[64,4096]{1,0:T(8,128)(2,1)S(1)} %copy-done.5, bf16[16,8,256,256]{3,2,1,0:T(8,128)(2,1)S(1)} %copy-done.1), custom_call_target="tpu_custom_call" | custom-call | flops 1073741824 | bytes 20447232 | tf_op jit(solution)/shard_map/near/pallas_call | solution.py:179
  65.0 5.6 %far.1 = (f32[64,4096]{1,0:T(8,128)S(1)}, f32[32,8,128]{2,1,0:T(8,128)S(1)}) custom-call(bf16[128,4096]{1,0:T(8,128)(2,1)S(1)} %bitcast.18, bf16[128,4096]{1,0:T(8,128)(2,1)S(1)} %bitcast.19, bf16[2,256,256]{2,1,0:T(8,128)(2,1)S(1)} %bitcast.20, f32[64,4096]{1,0:T(8,128)S(1)} %near.1, bf16[16,128,128]{2,1,0:T(8,128)(2,1)} %m2l_hbm.1, ...), custom_call_target="tpu_custom_call" | custom-call | tf_op jit(solution)/shard_map/far/pallas_call | solution.py:274
  70.6 23.0 %all_to_all.30.in_ref = f32[32,8,128]{2,1,0:T(8,128)S(1)} all-to-all(f32[32,8,128]{2,1,0:T(8,128)S(1)} %get-tuple-element.16), channel_id=1, replica_groups=mesh['gx'=4,'hi'=2,'lo'=4] {'gx','hi','lo'}, dimensions={0} | all-to-all | bytes 262144 | tf_op jit(solution)/shard_map/all_to_all | solution.py:299
  93.6 10.0 %all_to_all.31.sums = f32[32,8,128]{2,1,0:T(8,128)S(1)} all-to-all(f32[32,8,128]{2,1,0:T(8,128)S(1)} %add.90), channel_id=1, replica_groups=mesh['gx'=4,'hi'=2,'lo'=4] {'gx','hi','lo'}, dimensions={0} | all-to-all | bytes 262144 | tf_op jit(solution)/shard_map/all_to_all | solution.py:299
  103.6 2.2 %copy-done = bf16[8,64,4096]{2,1,0:T(8,128)(2,1)S(1)} copy-done((bf16[8,64,4096]{2,1,0:T(8,128)(2,1)S(1)}, bf16[8,64,4096]{2,1,0:T(8,128)(2,1)}, u32[]{:S(2)}) %copy-start) | copy-done | bytes 4194328
  105.8 2.1 %residual.1 = (bf16[128,4096]{1,0:T(8,128)(2,1)S(1)}, f32[8,32,128]{2,1,0:T(8,128)S(1)}, f32[512,64]{1,0:T(8,128)}) custom-call(f32[32,8,128]{2,1,0:T(8,128)S(1)} %all_to_all.31.sums, bf16[8,64,4096]{2,1,0:T(8,128)(2,1)S(1)} %copy-done, f32[64,4096]{1,0:T(8,128)S(1)} %get-tuple-element.17.image), custom_call_target="tpu_custom_call" | custom-call | tf_op jit(solution)/shard_map/residual/pallas_call | solution.py:348
  107.9 10.4 %all_to_all.32.in_ref = f32[8,32,128]{2,1,0:T(8,128)S(1)} all-to-all(f32[8,32,128]{2,1,0:T(8,128)S(1)} %get-tuple-element.18), channel_id=1, replica_groups=mesh['gx'=4,'hi'=2,'lo'=4] {'hi','lo'}, dimensions={0} | all-to-all | bytes 262144 | tf_op jit(solution)/shard_map/all_to_all | solution.py:299
  118.4 6.5 %all_to_all.33.grams = f32[4,32,128]{2,1,0:T(8,128)S(1)} all-to-all(f32[4,32,128]{2,1,0:T(8,128)S(1)} %add.91), channel_id=1, replica_groups=mesh['gx'=4,'hi'=2,'lo'=4] {'gx'}, dimensions={0} | all-to-all | bytes 131072 | tf_op jit(solution)/shard_map/all_to_all | solution.py:299
  124.8 6.8 %tail.1 = (bf16[64,4096]{1,0:T(8,128)(2,1)}, f32[64,64]{1,0:T(8,128)}) custom-call(f32[4,32,128]{2,1,0:T(8,128)S(1)} %all_to_all.33.grams, bf16[128,4096]{1,0:T(8,128)(2,1)S(1)} %get-tuple-element.19.resid), custom_call_target="tpu_custom_call" | custom-call | tf_op jit(solution)/shard_map/tail/pallas_call | solution.py:408
  (22 shorter events, 3.1 us)
Async XLA Ops:
  5.7 41.9 %copy-start.2 = (bf16[64,4096]{1,0:T(8,128)(2,1)}, bf16[64,4096]{1,0:T(8,128)(2,1)S(1)}, u32[]{:S(2)}) copy-start(bf16[64,4096]{1,0:T(8,128)(2,1)S(1)} %get-tuple-element.15.own) | copy-start | bytes 1572868
  5.7 26.8 %all-to-all-start = ((bf16[16,8,4096]{2,1,0:T(8,128)(2,1)}), bf16[16,8,4096]{2,1,0:T(8,128)(2,1)S(1)}, u32[]{:S(2)}, u32[]{:S(2)}) async-start(bf16[16,8,4096]{2,1,0:T(8,128)(2,1)} %bitcast.3), calls=%async_computation | async-start | bytes 2097152 | tf_op jit(solution)/shard_map/all_to_all | solution.py:299
  12.0 18.1 %collective-permute-start = (bf16[1040,128]{1,0:T(8,128)(2,1)S(1)}, bf16[1040,128]{1,0:T(8,128)(2,1)S(1)}, u32[]{:S(2)}, u32[]{:S(2)}) collective-permute-start(bf16[1040,128]{1,0:T(8,128)(2,1)S(1)} %get-tuple-element.14), channel_id=1, source_target_pairs={{0,4},{4,0},{1,5},{5,1},{2,6},{6,2},{3,7},{7,3},{8,12},{12,8},{9,1... | collective-permute-start | bytes 798728 | tf_op jit(solution)/shard_map/ppermute | solution.py:436
  32.5 32.5 %all-to-all-start.1 = ((bf16[16,8,4096]{2,1,0:T(8,128)(2,1)}), bf16[16,8,4096]{2,1,0:T(8,128)(2,1)S(1)}, u32[]{:S(2)}, u32[]{:S(2)}) async-start(bf16[16,8,4096]{2,1,0:T(8,128)(2,1)} %bitcast.5), calls=%async_computation.1 | async-start | bytes 2097152 | tf_op jit(solution)/shard_map/all_to_all | solution.py:299
  39.7 7.9 %collective-permute-start.2 = (bf16[64,4096]{1,0:T(8,128)(2,1)S(1)}, bf16[64,4096]{1,0:T(8,128)(2,1)S(1)}, u32[]{:S(2)}, u32[]{:S(2)}) collective-permute-start(bf16[64,4096]{1,0:T(8,128)(2,1)S(1)} %get-tuple-element.15.own), channel_id=1, source_target_pairs={{8,0},{16,8},{24,16},{9,1},{17,9},{25,17},{10,2},{18,10},{26,18},{... | collective-permute-start | bytes 1572872 | tf_op jit(solution)/shard_map/ppermute | solution.py:442
  41.0 7.4 %collective-permute-start.1 = (bf16[64,4096]{1,0:T(8,128)(2,1)S(1)}, bf16[64,4096]{1,0:T(8,128)(2,1)}, u32[]{:S(2)}, u32[]{:S(2)}) collective-permute-start(bf16[64,4096]{1,0:T(8,128)(2,1)S(1)} %get-tuple-element.15.own), channel_id=1, source_target_pairs={{0,8},{8,16},{16,24},{1,9},{9,17},{17,25},{2,10},{10,18},{18,26},{... | collective-permute-start | bytes 1572872 | tf_op jit(solution)/shard_map/ppermute | solution.py:441
  47.6 0.8 copy-start.4
  48.4 5.8 %copy-start.1 = (bf16[16,8,256,256]{3,2,1,0:T(8,128)(2,1)S(1)}, bf16[16,8,256,256]{3,2,1,0:T(8,128)(2,1)}, u32[]{:S(2)}) copy-start(bf16[16,8,256,256]{3,2,1,0:T(8,128)(2,1)} %blocks_ref.1) | copy-start | bytes 50331652
  54.2 1.0 copy-start.3
  55.2 1.0 copy-start.5
  56.3 0.7 copy-start.6
  103.6 2.2 %copy-start = (bf16[8,64,4096]{2,1,0:T(8,128)(2,1)S(1)}, bf16[8,64,4096]{2,1,0:T(8,128)(2,1)}, u32[]{:S(2)}) copy-start(bf16[8,64,4096]{2,1,0:T(8,128)(2,1)} %basis.1) | copy-start | bytes 12582916

commit v4 on v3

--- a/solution.py
+++ b/solution.py
@@ -39,103 +39,100 @@
     return pl.BlockSpec(shape, lambda *_: (0,) * len(shape))
 
 
-def chosen_rows(listing, leaves, slots, halves):
-    receivers = listing.shape[0]
-    rows = receivers * slots * halves
-    row = lax.broadcasted_iota(jnp.int32, (rows, receivers), 0) // (slots * halves)
-    hot = row == lax.broadcasted_iota(jnp.int32, (rows, receivers), 1)
-    spread = dot(hot.astype(F32).astype(BF16), listing)
-    row = lax.broadcasted_iota(jnp.int32, spread.shape, 0)
-    lane = lax.broadcasted_iota(jnp.int32, spread.shape, 1)
-    slot = row // halves % slots
-    leaf = jnp.sum(jnp.where(lane == slot, spread, 0.0), axis=1, keepdims=True)
-    live = jnp.sum(jnp.where(lane == slots, spread, 0.0), axis=1, keepdims=True)
-    row = lax.broadcasted_iota(jnp.int32, (rows, leaves * halves), 0)
-    lane = lax.broadcasted_iota(jnp.int32, (rows, leaves * halves), 1)
-    wanted = leaf * halves + (row % halves).astype(F32)
-    held = (row // halves % slots).astype(F32) < live
-    return ((lane.astype(F32) == wanted) & held).astype(F32).astype(BF16)
-
-
-def one_side(listing, side, near_devices):
-    peers = listing.shape[0]
-    rows = lax.broadcasted_iota(jnp.int32, (peers // 2, peers), 0)
-    wanted = rows // near_devices * (2 * near_devices) + side * near_devices + rows % near_devices
-    hot = wanted == lax.broadcasted_iota(jnp.int32, (peers // 2, peers), 1)
-    return dot(hot.astype(F32).astype(BF16), listing).astype(BF16)
-
-
-def send_kernel(halves, slots, near_devices, side, x, p2m, listing, out, whole_out, own, scratch):
+def send_kernel(halves, x, p2m, listed, counts, out, own, scratch, lists):
     leaves, panels, terms = p2m.shape
     rhs = x.shape[1]
     part = rhs // halves
+    slots, peers = listed.shape
     own[...] = x[0]
     for g in range(leaves):
         mult = dot(x[0, :, g * panels : (g + 1) * panels], p2m[g])
         for h in range(halves):
             scratch[:, g * halves + h, :] = mult[h * part : (h + 1) * part]
-    lists = listing[...]
-    chosen = chosen_rows(one_side(lists, side[0], near_devices), leaves, slots, halves)
     tall = leaves * halves
+    for j in range(part):
+        out[j * tall : (j + 1) * tall, :] = scratch[j].astype(BF16)
+    lists[...] = jnp.zeros_like(lists)
+    lists[:slots, :peers] = listed[...].astype(F32)
+    lists[slots : slots + 1, :peers] = counts[...].astype(F32)
+    out[part * tall :, :] = lists[...].astype(BF16)
+
+
+def relay_kernel(halves, slots, leaves, near_devices, side, own, given, out):
+    tall, terms = leaves * halves, given.shape[1]
+    rows, part = out.shape[0], out.shape[1] // terms
+    each = 2 * slots * halves
+    peers = 2 * rows // each
+    receiver = lax.broadcasted_iota(jnp.int32, (rows, terms), 0) // each
+    far_part, near_part = receiver // near_devices, receiver % near_devices
+    device = far_part * (2 * near_devices) + side[0] * near_devices + near_part
+    hot = (device == lax.broadcasted_iota(jnp.int32, (rows, terms), 1)).astype(F32).astype(BF16)
+    spread = [dot_nt(hot, ref[part * tall :, :]) for ref in (own, given)]
+    row = lax.broadcasted_iota(jnp.int32, spread[0].shape, 0)
+    lane = lax.broadcasted_iota(jnp.int32, spread[0].shape, 1)
+    spread = jnp.where(row // (slots * halves) % 2 == 0, spread[0], spread[1])
+    slot = row // halves % slots
+    leaf = jnp.sum(jnp.where(lane == slot, spread, 0.0), axis=1, keepdims=True)
+    live = jnp.sum(jnp.where(lane == slots, spread, 0.0), axis=1, keepdims=True)
+    row = lax.broadcasted_iota(jnp.int32, (rows, 2 * tall), 0)
+    lane = lax.broadcasted_iota(jnp.int32, (rows, 2 * tall), 1).astype(F32)
+    offset = row // (slots * halves) % 2 * tall + row % halves
+    held = (row // halves % slots).astype(F32) < live
+    chosen = ((lane == leaf * halves + offset.astype(F32)) & held).astype(F32).astype(BF16)
     for j in range(part // 2):
-        first, second = scratch[2 * j].astype(BF16), scratch[2 * j + 1].astype(BF16)
-        whole_out[2 * j * tall : (2 * j + 1) * tall, :] = first
-        whole_out[(2 * j + 1) * tall : (2 * j + 2) * tall, :] = second
-        pair = jnp.concatenate([first, second], axis=1)
-        out[:, j * 2 * terms : (j + 1) * 2 * terms] = dot(chosen, pair).astype(BF16)
-    whole_out[part * tall :, :] = one_side(lists, 1 - side[0], near_devices)
-
-
-def relay_kernel(halves, slots, leaves, given, out):
-    tall, terms = leaves * halves, given.shape[1]
-    part = out.shape[1] // terms
-    chosen = chosen_rows(given[part * tall :, :], leaves, slots, halves)
-    for j in range(part // 2):
-        rows = [given[i * tall : (i + 1) * tall, :] for i in (2 * j, 2 * j + 1)]
-        pair = jnp.concatenate(rows, axis=1)
-        out[:, j * 2 * terms : (j + 1) * 2 * terms] = dot(chosen, pair).astype(BF16)
-
-
-def sent_multipoles(side, basis, p2m, listing, slots, halves):
+        pairs = [
+            jnp.concatenate(
+                [ref[i * tall : (i + 1) * tall, :] for i in (2 * j, 2 * j + 1)], axis=1
+            )
+            for ref in (own, given)
+        ]
+        got = dot(chosen, jnp.concatenate(pairs, axis=0))
+        out[:, j * 2 * terms : (j + 1) * 2 * terms] = got.astype(BF16)
+
+
+def all_multipoles(basis, p2m, listed, counts, halves):
     blocks, rhs, columns = basis.shape
     leaves, panels, terms = p2m.shape
-    peers = listing.shape[0]
-    rows, width = peers // 2 * slots * halves, rhs // halves * terms
     shapes = (
-        jax.ShapeDtypeStruct((rows, width), BF16),
-        jax.ShapeDtypeStruct((rhs * leaves + peers // 2, terms), BF16),
+        jax.ShapeDtypeStruct((rhs * leaves + 16, terms), BF16),
         jax.ShapeDtypeStruct((rhs, columns), BF16),
     )
     return pl.pallas_call(
-        functools.partial(send_kernel, halves, slots, lax.axis_size("lo")),
+        functools.partial(send_kernel, halves),
         grid=(1,),
         out_shape=shapes,
         in_specs=[
-            pl.BlockSpec(memory_space=pltpu.SMEM),
             pl.BlockSpec((1, rhs, columns), lambda i: (blocks - 1, 0, 0)),
             whole(p2m.shape),
-            whole(listing.shape),
+            whole(listed.shape),
+            whole(counts.shape),
         ],
         out_specs=tuple(whole(s.shape) for s in shapes),
-        scratch_shapes=[pltpu.VMEM((rhs // halves, leaves * halves, terms), F32)],
-        compiler_params=params(20),
+        scratch_shapes=[
+            pltpu.VMEM((rhs // halves, leaves * halves, terms), F32),
+            pltpu.VMEM((16, terms), F32),
+        ],
+        compiler_params=params(16),
         name="send",
-    )(side, in_hbm(basis), in_hbm(p2m), listing)
-
-
-def relayed_multipoles(given, leaves, slots, halves, rhs):
-    receivers = given.shape[0] - rhs * leaves
-    shape = (receivers * slots * halves, rhs // halves * given.shape[1])
-    return pl.pallas_call(
-        functools.partial(relay_kernel, halves, slots, leaves),
+    )(in_hbm(basis), in_hbm(p2m), listed, counts)
+
+
+def relayed_multipoles(side, own, given, leaves, slots, halves, rhs, receivers):
+    terms = own.shape[1]
+    shape = (receivers * 2 * slots * halves, rhs // halves * terms)
+    return pl.pallas_call(
+        functools.partial(relay_kernel, halves, slots, leaves, lax.axis_size("lo")),
         grid=(1,),
         out_shape=jax.ShapeDtypeStruct(shape, BF16),
-        in_specs=[whole(given.shape)],
+        in_specs=[
+            pl.BlockSpec(memory_space=pltpu.SMEM),
+            whole(own.shape),
+            whole(given.shape),
+        ],
         out_specs=whole(shape),
         compiler_params=params(16),
-        cost_estimate=pl.CostEstimate(flops=shape[0] * shape[1] * 64, bytes_accessed=2**21, transcendentals=0),
         name="relay",
-    )(given)
+    )(side, own, given)
 
 
 def near_kernel(src_ref, count_ref, before, own, after, blocks_ref, out_ref, wide):
@@ -187,13 +184,13 @@
             transcendentals=0,
         ),
         name="near",
-    )(near_src, near_count, before, own, after, near_blocks)
+    )(near_src, near_count, before, in_hbm(own), after, in_hbm(near_blocks))
 
 
 def far_kernel(
-    halves, ours, theirs, pick, near, m2l_hbm, p2m_hbm, basis_hbm, image_ref, sums_ref, *scratch
+    halves, recv, pick, near, m2l_hbm, p2m_hbm, basis_hbm, image_ref, sums_ref, *scratch
 ):
-    recv, lhs, loc, both, m2l, p2m, basis, sems = scratch
+    lhs, loc, both, m2l, p2m, basis, sems = scratch
     moves = [
         pltpu.make_async_copy(source, target, sems.at[i])
         for i, (source, target) in enumerate(
@@ -207,8 +204,6 @@
     blocks, rhs, columns = basis.shape
     part = rhs // halves
     group = 8
-    rows = ours.shape[0]
-    recv[:rows], recv[rows:] = ours[...], theirs[...]
     for h in range(halves):
         for j in range(0, part, group):
             got = dot(pick[h], recv[:, j * terms : (j + group) * terms]).astype(BF16)
@@ -264,12 +259,12 @@
     )
 
 
-def far_field(ours, theirs, pick, m2l, p2m, near, basis, halves, peers):
+def far_field(recv, pick, m2l, p2m, near, basis, halves, peers):
     leaves, panels, terms = p2m.shape
     classes = m2l.shape[0]
     blocks, rhs, columns = basis.shape
     _, piece = pack_sizes(rhs, blocks * rhs, peers)
-    args = (ours, theirs, pick, near)
+    args = (recv, pick, near)
     anywhere = pl.BlockSpec(memory_space=pl.ANY)
     return pl.pallas_call(
         functools.partial(far_kernel, halves),
@@ -281,7 +276,6 @@
         in_specs=[whole(a.shape) for a in args] + [anywhere] * 3,
         out_specs=(whole((rhs, columns)), whole((peers, piece, 128))),
         scratch_shapes=[
-            pltpu.VMEM((2 * ours.shape[0], ours.shape[1]), BF16),
             pltpu.VMEM((rhs * leaves, classes * terms), BF16),
             pltpu.VMEM((rhs, leaves, terms), F32),
             pltpu.VMEM((2 * rhs, columns), BF16),
@@ -317,15 +311,22 @@
     )(pieces)
 
 
-def resid_kernel(total_rows, sums, basis, image, resid_ref, gram_ref, proj_ref):
+def resid_kernel(total_rows, sums, image, basis_hbm, resid_ref, gram_ref, proj_ref, basis, sems):
     blocks, rhs, columns = basis.shape
     wide = blocks * rhs
+    steps = sems.shape[0]
+    step = columns // steps
+    moves = []
+    for i in range(steps):
+        part = (slice(None), slice(None), pl.ds(i * step, step))
+        moves.append(pltpu.make_async_copy(basis_hbm.at[part], basis.at[part], sems.at[i]))
+        moves[i].start()
     proj = unpack(sums, rhs, wide) * (1.0 / total_rows)
     proj_ref[...] = proj.T
     coef = jnp.concatenate(split_parts(proj), axis=0)
-    step = 1024
-    for i in range(columns // step):
+    for i in range(steps):
         cols = slice(i * step, (i + 1) * step)
+        moves[i].wait()
         by_basis = dot(coef, basis[:, :, cols].reshape(wide, step))
         resid = image[:, cols] - (by_basis[:rhs] + by_basis[rhs:])
         resid_ref[:rhs, cols], resid_ref[rhs:, cols] = split_parts(resid)
@@ -334,26 +335,27 @@
     gram = square[:rhs, :rhs] + square[:rhs, rhs:] + square[rhs:, :rhs] + square[rhs:, rhs:]
     half = rhs // 2
     folded = jnp.concatenate([gram[:half], gram[half:]], axis=1) * (1.0 / total_rows)
-    gram_ref[...] = jnp.broadcast_to(folded[None], gram_ref.shape)
-
-
-def residual(sums, basis, image, total_rows, copies):
-    blocks, rhs, columns = basis.shape
-    args = (sums, basis, image)
+    gram_ref[...] = folded
+
+
+def residual(sums, basis, image, total_rows):
+    blocks, rhs, columns = basis.shape
+    args = (sums, image)
     shapes = (
         jax.ShapeDtypeStruct((2 * rhs, columns), BF16),
-        jax.ShapeDtypeStruct((copies, rhs // 2, 2 * rhs), F32),
+        jax.ShapeDtypeStruct((rhs // 2, 2 * rhs), F32),
         jax.ShapeDtypeStruct((blocks * rhs, rhs), F32),
     )
     return pl.pallas_call(
         functools.partial(resid_kernel, total_rows),
         grid=(1,),
         out_shape=shapes,
-        in_specs=[whole(a.shape) for a in args],
+        in_specs=[whole(a.shape) for a in args] + [pl.BlockSpec(memory_space=pl.ANY)],
         out_specs=tuple(whole(s.shape) for s in shapes),
+        scratch_shapes=[pltpu.VMEM(basis.shape, BF16), pltpu.SemaphoreType.DMA((4,))],
         compiler_params=params(24),
         name="residual",
-    )(*args)
+    )(*args, in_hbm(basis))
 
 
 def factored(gram):
@@ -430,26 +432,25 @@
     side = lax.axis_index("hi")
     same_side = ("gx", "lo")
 
-    listing = jnp.concatenate([send_list[0], send_count[0][:, None]], axis=1)
-    listing = jnp.pad(listing, ((0, 0), (0, terms - slots - 1))).astype(BF16)
-    sent, given, own = sent_multipoles(side[None], basis, p2m, listing, slots, halves)
-    given = lax.ppermute(given, "hi", [(0, 1), (1, 0)])
-    ours = exchange(sent.reshape(peers // 2, slots * halves, -1), same_side).reshape(sent.shape)
-
+    payload, own = all_multipoles(basis, p2m, send_list[0].T, send_count, halves)
+    flip = [(0, 1), (1, 0)]
+    given = lax.ppermute(payload, "hi", flip)
     up = [(i, i + 1) for i in range(devices - 1)]
     down = [(j, i) for i, j in up]
     before = lax.ppermute(own, "gx", up)
     after = lax.ppermute(own, "gx", down)
-
-    relayed = relayed_multipoles(given, leaves, slots, halves, rhs)
-    theirs = exchange(relayed.reshape(peers // 2, slots * halves, -1), same_side)
-    theirs = theirs.reshape(sent.shape)
+    given, before, after = lax.optimization_barrier((given, before, after))
+    relayed = relayed_multipoles(
+        side[None], payload, given, leaves, slots, halves, rhs, peers // 2
+    )
+    received = exchange(relayed.reshape(peers // 2, 2 * slots * halves, -1), same_side)
+    received = received.reshape(relayed.shape)
 
     near = near_field(near_src, near_count, before, own, after, near_blocks)
 
     sender = far_src // slots
     place = sender // (2 * near_devices) * near_devices + sender % near_devices
-    place = place + jnp.where(sender // near_devices % 2 == side, 0, peers // 2)
+    place = place * 2 + (sender // near_devices % 2 != side).astype(jnp.int32)
     place = place * slots + far_src % slots
     class_hot = (far_class[:, None, :] == jnp.arange(classes)[None, :, None]).astype(BF16)
     rows = jnp.arange(peers * slots * halves)[None, None, None, :]
@@ -458,10 +459,11 @@
     pick = jnp.einsum("gce,hgef->hcgf", class_hot, source_hot, preferred_element_type=F32)
     pick = pick.astype(BF16).reshape(halves, classes * leaves, -1)
 
-    image, sums = far_field(ours, theirs, pick, m2l, p2m, near, basis, halves, peers)
+    image, sums = far_field(received, pick, m2l, p2m, near, basis, halves, peers)
     sums = exchange(added(exchange(sums), peers))
-    resid, grams, projections = residual(sums, basis, image, total_rows, 2 * near_devices)
-    grams = exchange(added(exchange(grams, ("hi", "lo")), devices), ("gx",))
+    resid, gram, projections = residual(sums, basis, image, total_rows)
+    pair = jnp.stack([gram, lax.ppermute(gram, "hi", flip)])
+    grams = exchange(added(pair, peers // 2), same_side)
     next_block, factor = tail(grams, resid)
     return (next_block, projections.reshape(blocks, rhs, rhs), factor)
 

time: 133 us -> 113 us (0.85)
  blocking collectives: 49.9 us -> 33 us
  waiting for transfers between devices: 16.3 us -> 28.4 us
  local copies, waits for them, and re-layouts: 12.5 us -> 3.67 us
  starting transfers between devices: 21.3 us -> 14.8 us
  Pallas kernels: 27.8 us -> 31.7 us
  other arithmetic: 2.09 us -> 0.05 us
    all_to_all x4 -> x3, blocking collectives: 49.9 us -> 33 us  [exchange(): return lax.all_to_all(pieces, axes, split_axis=0, concat_axis=0, tiled=True)]
    all_to_all x2 -> x1, waiting for transfers between devices: 0.8 us -> 13.7 us  [exchange(): return lax.all_to_all(pieces, axes, split_axis=0, concat_axis=0, tiled=True)]
    unnamed x15 -> x23, local copies, waits for them, and re-layouts: 12.3 us -> 3.52 us
    all_to_all x2 -> x1, starting transfers between devices: 13.5 us -> 6.1 us  [exchange(): return lax.all_to_all(pieces, axes, split_axis=0, concat_axis=0, tiled=True)]
    pallas_call x1, Pallas kernels: 8 us -> 11.5 us  [near_field(): pl.pallas_call(near_kernel, grid_spec=grid_spec, out_shape=jax.ShapeDtype...]
    ppermute x1 -> x2, starting transfers between devices: 2.65 us -> 4.91 us  [the longest x1 3.48 us: shards(): given = lax.ppermute(payload, 'hi', flip)]
    pallas_call x1, Pallas kernels: 2.09 us -> 3.42 us  [residual(): pl.pallas_call(functools.partial(resid_kernel, total_rows), grid=(1,), ou...]
    ppermute x1, starting transfers between devices: 3.86 us -> 2.52 us  [shards(): before = lax.ppermute(own, 'gx', up)]
  transfers between devices with their start and end apart: 5 -> 5, of which waited for: 2 -> 3; matrix products, arithmetic and copies ran while one was open for 2% -> 1% of each run, Pallas kernels for 7% -> 10%
where the time goes in v4:
time: 113 us
  blocking collectives  33 us (29%)
  Pallas kernels  31.7 us (28%)
  waiting for transfers between devices  28.4 us (25%)
  starting transfers between devices  14.8 us (13%)
  local copies, waits for them, and re-layouts  3.67 us (3%)
    all_to_all x3, blocking collectives, exchange(): return lax.all_to_all(pieces, axes, split_axis=0, concat_axis=0, tiled=True)  33 us
    all_to_all x1, waiting for transfers between devices, exchange(): return lax.all_to_all(pieces, axes, split_axis=0, concat_axis=0, tiled=True)  13.7 us
    pallas_call x1, Pallas kernels, near_field(): pl.pallas_call(near_kernel, grid_spec=grid_spec, out_shape=jax.ShapeDtype...  11.5 us
    ppermute x1, waiting for transfers between devices, shards(): given = lax.ppermute(payload, 'hi', flip)  11.4 us
    pallas_call x1, Pallas kernels, tail(): pl.pallas_call(tail_kernel, grid=(1,), out_shape=shapes, in_specs=[whole(...  6.84 us
    all_to_all x1, starting transfers between devices, exchange(): return lax.all_to_all(pieces, axes, split_axis=0, concat_axis=0, tiled=True)  6.1 us
    pallas_call x1, Pallas kernels, far_field(): pl.pallas_call(functools.partial(far_kernel, halves), grid=(1,), out_shap...  5.62 us
    unnamed x23, local copies, waits for them, and re-layouts  3.52 us
  transfers between devices with their start and end apart: 5, of which 3 were waited for; matrix products, arithmetic and copies ran while one was open for 1% of the time, Pallas kernels for 10%

profile of v4, /device:TPU:0, one launch (start us, length us, event | category | flops | bytes accessed | tf_op | source)
XLA Modules:
  0.0 112.8 jit_solution(174876986873778755)
XLA Ops:
  0.6 0.7 copy-done.5
  1.3 0.7 copy-done.6
  2.0 2.0 %send.1 = (bf16[1040,128]{1,0:T(8,128)(2,1)S(1)}, bf16[64,4096]{1,0:T(8,128)(2,1)S(1)}) custom-call(bf16[8,64,4096]{2,1,0:T(8,128)(2,1)} %basis_hbm.3, bf16[16,256,128]{2,1,0:T(8,128)(2,1)} %p2m_hbm.1, s32[4,32]{1,0:T(4,128)S(1)} %bitcast.20, s32[1,32]{1,0:T(1,128)S(1)} %copy-done.6), custom_call_target="tpu_custom_call" | custom-call | tf_op jit(solution)/shard_map/send/pallas_call | solution.py:100
  4.0 2.5 %collective-permute-start.1 = (bf16[64,4096]{1,0:T(8,128)(2,1)S(1)}, bf16[64,4096]{1,0:T(8,128)(2,1)S(1)}, u32[]{:S(2)}, u32[]{:S(2)}) collective-permute-start(bf16[64,4096]{1,0:T(8,128)(2,1)S(1)} %get-tuple-element.16.own), channel_id=1, source_target_pairs={{0,8},{8,16},{16,24},{1,9},{9,17},{17,25},{2,10},{10,18},{18,26},{... | collective-permute-start | bytes 1572872 | tf_op jit(solution)/shard_map/ppermute | solution.py:440
  6.5 1.3 %collective-permute-start.2 = (bf16[64,4096]{1,0:T(8,128)(2,1)S(1)}, bf16[64,4096]{1,0:T(8,128)(2,1)S(1)}, u32[]{:S(2)}, u32[]{:S(2)}) collective-permute-start(bf16[64,4096]{1,0:T(8,128)(2,1)S(1)} %get-tuple-element.16.own), channel_id=1, source_target_pairs={{8,0},{16,8},{24,16},{9,1},{17,9},{25,17},{10,2},{18,10},{26,18},{... | collective-permute-start | bytes 1572872 | tf_op jit(solution)/shard_map/ppermute | solution.py:441
  7.8 3.5 %collective-permute-start = (bf16[1040,128]{1,0:T(8,128)(2,1)S(1)}, bf16[1040,128]{1,0:T(8,128)(2,1)S(1)}, u32[]{:S(2)}, u32[]{:S(2)}) collective-permute-start(bf16[1040,128]{1,0:T(8,128)(2,1)S(1)} %get-tuple-element.15.own), channel_id=1, source_target_pairs={{0,4},{4,0},{1,5},{5,1},{2,6},{6,2},{3,7},{7,3},{8,12},{12,8},{9,1... | collective-permute-start | bytes 798728 | tf_op jit(solution)/shard_map/ppermute | solution.py:437
  11.3 11.4 %collective-permute-done.given = bf16[1040,128]{1,0:T(8,128)(2,1)S(1)} collective-permute-done((bf16[1040,128]{1,0:T(8,128)(2,1)S(1)}, bf16[1040,128]{1,0:T(8,128)(2,1)S(1)}, u32[]{:S(2)}, u32[]{:S(2)}) %collective-permute-start) | collective-permute-done | bytes 266272 | tf_op jit(solution)/shard_map/ppermute | solution.py:437
  22.8 2.2 %relay.1 = bf16[256,4096]{1,0:T(8,128)(2,1)} custom-call(s32[1]{0:T(128)} %bitcast.side, bf16[1040,128]{1,0:T(8,128)(2,1)S(1)} %get-tuple-element.15.own, bf16[1040,128]{1,0:T(8,128)(2,1)S(1)} %collective-permute-done.given), custom_call_target="tpu_custom_call" | custom-call | tf_op jit(solution)/shard_map/relay/pallas_call | solution.py:123
  25.0 6.1 %all-to-all-start = ((bf16[16,16,4096]{2,1,0:T(8,128)(2,1)}), bf16[16,16,4096]{2,1,0:T(8,128)(2,1)S(1)}, u32[]{:S(2)}, u32[]{:S(2)}) async-start(bf16[16,16,4096]{2,1,0:T(8,128)(2,1)} %bitcast.3), calls=%async_computation | async-start | bytes 4194304 | tf_op jit(solution)/shard_map/all_to_all | solution.py:293
  31.2 0.1 copy.14.src_ref
  31.3 0.4 fusion
  31.7 0.2 copy.13
  31.8 1.0 copy-done.2
  32.9 1.0 copy-done.4
  33.9 11.5 %near.1 = f32[64,4096]{1,0:T(8,128)S(1)} custom-call(s32[16,8]{1,0:T(8,128)S(1)} %copy.14.src_ref, s32[16]{0:T(128)S(1)} %copy-done.7, bf16[64,4096]{1,0:T(8,128)(2,1)S(1)} %copy-done.2, bf16[64,4096]{1,0:T(8,128)(2,1)} %copy-done, bf16[64,4096]{1,0:T(8,128)(2,1)S(1)} %copy-done.4, bf16[16,8,256,256]{3,2,1,0:T(8,128)(2,1)} %blocks_ref.1), custom_call_target="tpu_custom_call" | custom-call | flops 1073741824 | bytes 20447232 | tf_op jit(solution)/shard_map/near/pallas_call | solution.py:176
  45.5 13.7 %all-to-all-done = bf16[16,16,4096]{2,1,0:T(8,128)(2,1)S(1)} async-done(((bf16[16,16,4096]{2,1,0:T(8,128)(2,1)}), bf16[16,16,4096]{2,1,0:T(8,128)(2,1)S(1)}, u32[]{:S(2)}, u32[]{:S(2)}) %all-to-all-start) | async-done | bytes 2097184 | tf_op jit(solution)/shard_map/all_to_all | solution.py:293
  59.1 5.6 %far.1 = (f32[64,4096]{1,0:T(8,128)S(1)}, f32[32,8,128]{2,1,0:T(8,128)S(1)}) custom-call(bf16[256,4096]{1,0:T(8,128)(2,1)S(1)} %bitcast.17, bf16[2,256,256]{2,1,0:T(8,128)(2,1)S(1)} %bitcast.18, f32[64,4096]{1,0:T(8,128)S(1)} %near.1, bf16[16,128,128]{2,1,0:T(8,128)(2,1)} %m2l_hbm.1, bf16[16,256,128]{2,1,0:T(8,128)(2,1)} %p2m_hbm.1, ...), custom_call_target="tpu_custom_call" | custom-call | tf_op jit(solution)/shard_map/far/pallas_call | solution.py:269
  64.7 13.2 %all_to_all.20.in_ref = f32[32,8,128]{2,1,0:T(8,128)S(1)} all-to-all(f32[32,8,128]{2,1,0:T(8,128)S(1)} %get-tuple-element.20), channel_id=1, replica_groups=mesh['gx'=4,'hi'=2,'lo'=4] {'gx','hi','lo'}, dimensions={0} | all-to-all | bytes 262144 | tf_op jit(solution)/shard_map/all_to_all | solution.py:293
  78.0 10.0 %all_to_all.21.sums = f32[32,8,128]{2,1,0:T(8,128)S(1)} all-to-all(f32[32,8,128]{2,1,0:T(8,128)S(1)} %add.90), channel_id=1, replica_groups=mesh['gx'=4,'hi'=2,'lo'=4] {'gx','hi','lo'}, dimensions={0} | all-to-all | bytes 262144 | tf_op jit(solution)/shard_map/all_to_all | solution.py:293
  88.0 3.4 %residual.1 = (bf16[128,4096]{1,0:T(8,128)(2,1)S(1)}, f32[32,128]{1,0:T(8,128)S(1)}, f32[512,64]{1,0:T(8,128)}) custom-call(f32[32,8,128]{2,1,0:T(8,128)S(1)} %all_to_all.21.sums, f32[64,4096]{1,0:T(8,128)S(1)} %get-tuple-element.21.image, bf16[8,64,4096]{2,1,0:T(8,128)(2,1)} %basis_hbm.3), custom_call_target="tpu_custom_call" | custom-call | tf_op jit(solution)/shard_map/residual/pallas_call | solution.py:349
  91.4 1.4 %collective-permute-start.3 = (f32[32,128]{1,0:T(8,128)S(1)}, f32[32,128]{1,0:T(8,128)S(1)}, u32[]{:S(2)}, u32[]{:S(2)}) collective-permute-start(f32[32,128]{1,0:T(8,128)S(1)} %get-tuple-element.22), channel_id=1, source_target_pairs={{0,4},{4,0},{1,5},{5,1},{2,6},{6,2},{3,7},{7,3},{8,12},{12,8},{9,1... | collective-permute-start | bytes 49160 | tf_op jit(solution)/shard_map/ppermute | solution.py:465
  92.8 3.3 %collective-permute-done.3 = f32[32,128]{1,0:T(8,128)S(1)} collective-permute-done((f32[32,128]{1,0:T(8,128)S(1)}, f32[32,128]{1,0:T(8,128)S(1)}, u32[]{:S(2)}, u32[]{:S(2)}) %collective-permute-start.3) | collective-permute-done | bytes 16416 | tf_op jit(solution)/shard_map/ppermute | solution.py:465
  96.1 9.8 %all_to_all.22.grams = f32[16,32,128]{2,1,0:T(8,128)S(1)} all-to-all(f32[16,32,128]{2,1,0:T(8,128)S(1)} %add.91), channel_id=1, replica_groups=mesh['gx'=4,'hi'=2,'lo'=4] {'gx','lo'}, dimensions={0} | all-to-all | bytes 524288 | tf_op jit(solution)/shard_map/all_to_all | solution.py:293
  106.0 6.8 %tail.1 = (bf16[64,4096]{1,0:T(8,128)(2,1)}, f32[64,64]{1,0:T(8,128)}) custom-call(f32[16,32,128]{2,1,0:T(8,128)S(1)} %all_to_all.22.grams, bf16[128,4096]{1,0:T(8,128)(2,1)S(1)} %get-tuple-element.23.resid), custom_call_target="tpu_custom_call" | custom-call | tf_op jit(solution)/shard_map/tail/pallas_call | solution.py:410
  (25 shorter events, 0.2 us)
Async XLA Ops:
  0.6 0.7 copy-start.5
  1.3 0.7 copy-start.6
  3.9 21.1 %copy-start = (bf16[64,4096]{1,0:T(8,128)(2,1)}, bf16[64,4096]{1,0:T(8,128)(2,1)S(1)}, u32[]{:S(2)}) copy-start(bf16[64,4096]{1,0:T(8,128)(2,1)S(1)} %get-tuple-element.16.own) | copy-start | bytes 1572868
  3.9 27.2 %copy-start.9 = (s32[16,8]{0,1:T(8,128)S(1)}, s32[16,8]{0,1:T(8,128)}, u32[]{:S(2)}) copy-start(s32[16,8]{0,1:T(8,128)} %param.12) | copy-start | bytes 1540
  4.0 27.3 %copy-start.8 = (s32[16,32]{1,0:T(8,128)S(1)}, s32[16,32]{1,0:T(8,128)}, u32[]{:S(2)}) copy-start(s32[16,32]{1,0:T(8,128)} %param.18) | copy-start | bytes 6148
  4.0 27.3 %copy-start.10 = (s32[16,32]{1,0:T(8,128)S(1)}, s32[16,32]{1,0:T(8,128)}, u32[]{:S(2)}) copy-start(s32[16,32]{1,0:T(8,128)} %param.19) | copy-start | bytes 6148
  4.0 18.8 %collective-permute-start.1 = (bf16[64,4096]{1,0:T(8,128)(2,1)S(1)}, bf16[64,4096]{1,0:T(8,128)(2,1)S(1)}, u32[]{:S(2)}, u32[]{:S(2)}) collective-permute-start(bf16[64,4096]{1,0:T(8,128)(2,1)S(1)} %get-tuple-element.16.own), channel_id=1, source_target_pairs={{0,8},{8,16},{16,24},{1,9},{9,17},{17,25},{2,10},{10,18},{18,26},{... | collective-permute-start | bytes 1572872 | tf_op jit(solution)/shard_map/ppermute | solution.py:440
  6.5 16.2 %collective-permute-start.2 = (bf16[64,4096]{1,0:T(8,128)(2,1)S(1)}, bf16[64,4096]{1,0:T(8,128)(2,1)S(1)}, u32[]{:S(2)}, u32[]{:S(2)}) collective-permute-start(bf16[64,4096]{1,0:T(8,128)(2,1)S(1)} %get-tuple-element.16.own), channel_id=1, source_target_pairs={{8,0},{16,8},{24,16},{9,1},{17,9},{25,17},{10,2},{18,10},{26,18},{... | collective-permute-start | bytes 1572872 | tf_op jit(solution)/shard_map/ppermute | solution.py:441
  7.8 14.9 %collective-permute-start = (bf16[1040,128]{1,0:T(8,128)(2,1)S(1)}, bf16[1040,128]{1,0:T(8,128)(2,1)S(1)}, u32[]{:S(2)}, u32[]{:S(2)}) collective-permute-start(bf16[1040,128]{1,0:T(8,128)(2,1)S(1)} %get-tuple-element.15.own), channel_id=1, source_target_pairs={{0,4},{4,0},{1,5},{5,1},{2,6},{6,2},{3,7},{7,3},{8,12},{12,8},{9,1... | collective-permute-start | bytes 798728 | tf_op jit(solution)/shard_map/ppermute | solution.py:437
  22.7 2.3 %copy-start.1 = (bf16[64,4096]{1,0:T(8,128)(2,1)}, bf16[64,4096]{1,0:T(8,128)(2,1)S(1)}, u32[]{:S(2)}) copy-start(bf16[64,4096]{1,0:T(8,128)(2,1)S(1)} %collective-permute-done.1.before) | copy-start | bytes 1572868
  22.8 2.3 %copy-start.3 = (bf16[64,4096]{1,0:T(8,128)(2,1)}, bf16[64,4096]{1,0:T(8,128)(2,1)S(1)}, u32[]{:S(2)}) copy-start(bf16[64,4096]{1,0:T(8,128)(2,1)S(1)} %collective-permute-done.2.after) | copy-start | bytes 1572868
  22.8 9.0 %copy-start.7 = (s32[16]{0:T(128)S(1)}, s32[16]{0:T(128)}, u32[]{:S(2)}) copy-start(s32[16]{0:T(128)} %count_ref.1) | copy-start | bytes 196
  25.0 34.1 %all-to-all-start = ((bf16[16,16,4096]{2,1,0:T(8,128)(2,1)}), bf16[16,16,4096]{2,1,0:T(8,128)(2,1)S(1)}, u32[]{:S(2)}, u32[]{:S(2)}) async-start(bf16[16,16,4096]{2,1,0:T(8,128)(2,1)} %bitcast.3), calls=%async_computation | async-start | bytes 4194304 | tf_op jit(solution)/shard_map/all_to_all | solution.py:293
  31.8 1.0 copy-start.2
  32.9 1.0 copy-start.4
  91.4 4.7 %collective-permute-start.3 = (f32[32,128]{1,0:T(8,128)S(1)}, f32[32,128]{1,0:T(8,128)S(1)}, u32[]{:S(2)}, u32[]{:S(2)}) collective-permute-start(f32[32,128]{1,0:T(8,128)S(1)} %get-tuple-element.22), channel_id=1, source_target_pairs={{0,4},{4,0},{1,5},{5,1},{2,6},{6,2},{3,7},{7,3},{8,12},{12,8},{9,1... | collective-permute-start | bytes 49160 | tf_op jit(solution)/shard_map/ppermute | solution.py:465

commit v5 on v4

--- a/solution.py
+++ b/solution.py
@@ -58,35 +58,28 @@
     out[part * tall :, :] = lists[...].astype(BF16)
 
 
-def relay_kernel(halves, slots, leaves, near_devices, side, own, given, out):
+def choose_kernel(halves, slots, leaves, near_devices, side, given, out):
     tall, terms = leaves * halves, given.shape[1]
     rows, part = out.shape[0], out.shape[1] // terms
-    each = 2 * slots * halves
-    peers = 2 * rows // each
+    each = slots * halves
     receiver = lax.broadcasted_iota(jnp.int32, (rows, terms), 0) // each
     far_part, near_part = receiver // near_devices, receiver % near_devices
     device = far_part * (2 * near_devices) + side[0] * near_devices + near_part
     hot = (device == lax.broadcasted_iota(jnp.int32, (rows, terms), 1)).astype(F32).astype(BF16)
-    spread = [dot_nt(hot, ref[part * tall :, :]) for ref in (own, given)]
-    row = lax.broadcasted_iota(jnp.int32, spread[0].shape, 0)
-    lane = lax.broadcasted_iota(jnp.int32, spread[0].shape, 1)
-    spread = jnp.where(row // (slots * halves) % 2 == 0, spread[0], spread[1])
+    spread = dot_nt(hot, given[part * tall :, :])
+    row = lax.broadcasted_iota(jnp.int32, spread.shape, 0)
+    lane = lax.broadcasted_iota(jnp.int32, spread.shape, 1)
     slot = row // halves % slots
     leaf = jnp.sum(jnp.where(lane == slot, spread, 0.0), axis=1, keepdims=True)
     live = jnp.sum(jnp.where(lane == slots, spread, 0.0), axis=1, keepdims=True)
-    row = lax.broadcasted_iota(jnp.int32, (rows, 2 * tall), 0)
-    lane = lax.broadcasted_iota(jnp.int32, (rows, 2 * tall), 1).astype(F32)
-    offset = row // (slots * halves) % 2 * tall + row % halves
+    row = lax.broadcasted_iota(jnp.int32, (rows, tall), 0)
+    lane = lax.broadcasted_iota(jnp.int32, (rows, tall), 1).astype(F32)
     held = (row // halves % slots).astype(F32) < live
-    chosen = ((lane == leaf * halves + offset.astype(F32)) & held).astype(F32).astype(BF16)
+    wanted = leaf * halves + (row % halves).astype(F32)
+    chosen = ((lane == wanted) & held).astype(F32).astype(BF16)
     for j in range(part // 2):
-        pairs = [
-            jnp.concatenate(
-                [ref[i * tall : (i + 1) * tall, :] for i in (2 * j, 2 * j + 1)], axis=1
-            )
-            for ref in (own, given)
-        ]
-        got = dot(chosen, jnp.concatenate(pairs, axis=0))
+        pair = [given[i * tall : (i + 1) * tall, :] for i in (2 * j, 2 * j + 1)]
+        got = dot(chosen, jnp.concatenate(pair, axis=1))
         out[:, j * 2 * terms : (j + 1) * 2 * terms] = got.astype(BF16)
 
 
@@ -114,34 +107,37 @@
         ],
         compiler_params=params(16),
         name="send",
-    )(in_hbm(basis), in_hbm(p2m), listed, counts)
-
-
-def relayed_multipoles(side, own, given, leaves, slots, halves, rhs, receivers):
-    terms = own.shape[1]
-    shape = (receivers * 2 * slots * halves, rhs // halves * terms)
-    return pl.pallas_call(
-        functools.partial(relay_kernel, halves, slots, leaves, lax.axis_size("lo")),
+    )(in_hbm(basis), in_hbm(p2m), in_hbm(listed), in_hbm(counts))
+
+
+def chosen_multipoles(side, given, leaves, slots, halves, rhs, receivers):
+    terms = given.shape[1]
+    shape = (receivers * slots * halves, rhs // halves * terms)
+    return pl.pallas_call(
+        functools.partial(choose_kernel, halves, slots, leaves, lax.axis_size("lo")),
         grid=(1,),
         out_shape=jax.ShapeDtypeStruct(shape, BF16),
-        in_specs=[
-            pl.BlockSpec(memory_space=pltpu.SMEM),
-            whole(own.shape),
-            whole(given.shape),
-        ],
+        in_specs=[pl.BlockSpec(memory_space=pltpu.SMEM), whole(given.shape)],
         out_specs=whole(shape),
         compiler_params=params(16),
-        name="relay",
-    )(side, own, given)
-
-
-def near_kernel(src_ref, count_ref, before, own, after, blocks_ref, out_ref, wide):
+        name="choose",
+    )(side, given)
+
+
+def near_kernel(src_ref, count_ref, before, own, after, blocks_ref, *refs):
+    brought = len(refs) // 2 - 1
+    out_ref, wide, sems = refs[brought], refs[-2], refs[-1]
+    moves = [
+        pltpu.make_async_copy(refs[i], refs[brought + 1 + i], sems.at[i]) for i in range(brought)
+    ]
     columns = own.shape[1]
     slots, panels = blocks_ref.shape[1], blocks_ref.shape[2]
     g = pl.program_id(0)
 
     @pl.when(g == 0)
     def _():
+        for move in moves:
+            move.start()
         wide[:, :columns] = before[...]
         wide[:, columns : 2 * columns] = own[...]
         wide[:, 2 * columns :] = after[...]
@@ -157,10 +153,16 @@
             total[k % 2] += dot_nt(source, blocks_ref[i, k])
         out_ref[:, i * panels : (i + 1) * panels] = total[0] + total[1]
 
-
-def near_field(near_src, near_count, before, own, after, near_blocks):
+    @pl.when(g == pl.num_programs(0) - 1)
+    def _():
+        for move in moves:
+            move.wait()
+
+
+def near_field(near_src, near_count, before, own, after, near_blocks, bring):
     leaves, slots, panels, _ = near_blocks.shape
     rhs, columns = own.shape
+    anywhere = pl.BlockSpec(memory_space=pl.ANY)
     grid_spec = pltpu.PrefetchScalarGridSpec(
         num_scalar_prefetch=2,
         grid=(leaves // 2,),
@@ -169,14 +171,20 @@
             whole((rhs, columns)),
             whole((rhs, columns)),
             pl.BlockSpec((2, slots, panels, panels), lambda g, *_: (g, 0, 0, 0)),
+        ]
+        + [anywhere] * len(bring),
+        out_specs=[pl.BlockSpec((rhs, 2 * panels), lambda g, *_: (0, g))]
+        + [anywhere] * len(bring),
+        scratch_shapes=[
+            pltpu.VMEM((rhs, 3 * columns), BF16),
+            pltpu.SemaphoreType.DMA((len(bring),)),
         ],
-        out_specs=pl.BlockSpec((rhs, 2 * panels), lambda g, *_: (0, g)),
-        scratch_shapes=[pltpu.VMEM((rhs, 3 * columns), BF16)],
     )
     return pl.pallas_call(
         near_kernel,
         grid_spec=grid_spec,
-        out_shape=jax.ShapeDtypeStruct((rhs, columns), F32),
+        out_shape=[jax.ShapeDtypeStruct((rhs, columns), F32)]
+        + [pltpu.VMEM(a.shape, a.dtype) for a in bring],
         compiler_params=params(16),
         cost_estimate=pl.CostEstimate(
             flops=2 * rhs * near_blocks.size,
@@ -184,26 +192,27 @@
             transcendentals=0,
         ),
         name="near",
-    )(near_src, near_count, before, in_hbm(own), after, in_hbm(near_blocks))
+    )(
+        near_src,
+        near_count,
+        before,
+        in_hbm(own),
+        after,
+        in_hbm(near_blocks),
+        *[in_hbm(a) for a in bring],
+    )
 
 
 def far_kernel(
-    halves, recv, pick, near, m2l_hbm, p2m_hbm, basis_hbm, image_ref, sums_ref, *scratch
+    halves, ours, theirs, pick, near, m2l, p2m, basis, image_ref, sums_ref, recv, lhs, loc, both
 ):
-    lhs, loc, both, m2l, p2m, basis, sems = scratch
-    moves = [
-        pltpu.make_async_copy(source, target, sems.at[i])
-        for i, (source, target) in enumerate(
-            ((m2l_hbm, m2l), (p2m_hbm, p2m), (basis_hbm, basis))
-        )
-    ]
-    for move in moves:
-        move.start()
     leaves, panels, terms = p2m.shape
     classes = m2l.shape[0]
     blocks, rhs, columns = basis.shape
     part = rhs // halves
     group = 8
+    rows = ours.shape[0]
+    recv[:rows], recv[rows:] = ours[...], theirs[...]
     for h in range(halves):
         for j in range(0, part, group):
             got = dot(pick[h], recv[:, j * terms : (j + group) * terms]).astype(BF16)
@@ -213,7 +222,6 @@
                     lhs[base : base + leaves, c * terms : (c + 1) * terms] = got[
                         c * leaves : (c + 1) * leaves, t * terms : (t + 1) * terms
                     ]
-    moves[0].wait()
     weights = m2l[...].reshape(classes * terms, terms)
     tall = 256
     for i in range(rhs * leaves // tall):
@@ -221,13 +229,11 @@
         loc[i * tall // leaves : (i + 1) * tall // leaves] = got.reshape(
             tall // leaves, leaves, terms
         )
-    moves[1].wait()
     for g in range(leaves):
         cols = slice(g * panels, (g + 1) * panels)
         image = near[:, cols] + dot_nt(loc[:, g, :].astype(BF16), p2m[g])
         image_ref[:, cols] = image
         both[:rhs, cols], both[rhs:, cols] = split_parts(image)
-    moves[2].wait()
     inner = dot_nt(both[...], basis[...].reshape(blocks * rhs, columns))
     pack(inner[:rhs] + inner[rhs:], sums_ref)
 
@@ -259,13 +265,12 @@
     )
 
 
-def far_field(recv, pick, m2l, p2m, near, basis, halves, peers):
+def far_field(ours, theirs, pick, m2l, p2m, near, basis, halves, peers):
     leaves, panels, terms = p2m.shape
     classes = m2l.shape[0]
     blocks, rhs, columns = basis.shape
     _, piece = pack_sizes(rhs, blocks * rhs, peers)
-    args = (recv, pick, near)
-    anywhere = pl.BlockSpec(memory_space=pl.ANY)
+    args = (ours, theirs, pick, near, m2l, p2m, basis)
     return pl.pallas_call(
         functools.partial(far_kernel, halves),
         grid=(1,),
@@ -273,20 +278,17 @@
             jax.ShapeDtypeStruct((rhs, columns), F32),
             jax.ShapeDtypeStruct((peers, piece, 128), F32),
         ),
-        in_specs=[whole(a.shape) for a in args] + [anywhere] * 3,
+        in_specs=[whole(a.shape) for a in args],
         out_specs=(whole((rhs, columns)), whole((peers, piece, 128))),
         scratch_shapes=[
+            pltpu.VMEM((2 * ours.shape[0], ours.shape[1]), BF16),
             pltpu.VMEM((rhs * leaves, classes * terms), BF16),
             pltpu.VMEM((rhs, leaves, terms), F32),
             pltpu.VMEM((2 * rhs, columns), BF16),
-            pltpu.VMEM(m2l.shape, BF16),
-            pltpu.VMEM(p2m.shape, BF16),
-            pltpu.VMEM(basis.shape, BF16),
-            pltpu.SemaphoreType.DMA((3,)),
         ],
         compiler_params=params(32),
         name="far",
-    )(*args, in_hbm(m2l), in_hbm(p2m), in_hbm(basis))
+    )(*args)
 
 
 def exchange(pieces, axes=AXES):
@@ -311,22 +313,15 @@
     )(pieces)
 
 
-def resid_kernel(total_rows, sums, image, basis_hbm, resid_ref, gram_ref, proj_ref, basis, sems):
+def resid_kernel(total_rows, sums, image, basis, resid_ref, gram_ref, proj_ref):
     blocks, rhs, columns = basis.shape
     wide = blocks * rhs
-    steps = sems.shape[0]
-    step = columns // steps
-    moves = []
-    for i in range(steps):
-        part = (slice(None), slice(None), pl.ds(i * step, step))
-        moves.append(pltpu.make_async_copy(basis_hbm.at[part], basis.at[part], sems.at[i]))
-        moves[i].start()
     proj = unpack(sums, rhs, wide) * (1.0 / total_rows)
     proj_ref[...] = proj.T
     coef = jnp.concatenate(split_parts(proj), axis=0)
-    for i in range(steps):
+    step = 1024
+    for i in range(columns // step):
         cols = slice(i * step, (i + 1) * step)
-        moves[i].wait()
         by_basis = dot(coef, basis[:, :, cols].reshape(wide, step))
         resid = image[:, cols] - (by_basis[:rhs] + by_basis[rhs:])
         resid_ref[:rhs, cols], resid_ref[rhs:, cols] = split_parts(resid)
@@ -340,7 +335,7 @@
 
 def residual(sums, basis, image, total_rows):
     blocks, rhs, columns = basis.shape
-    args = (sums, image)
+    args = (sums, image, basis)
     shapes = (
         jax.ShapeDtypeStruct((2 * rhs, columns), BF16),
         jax.ShapeDtypeStruct((rhs // 2, 2 * rhs), F32),
@@ -350,12 +345,11 @@
         functools.partial(resid_kernel, total_rows),
         grid=(1,),
         out_shape=shapes,
-        in_specs=[whole(a.shape) for a in args] + [pl.BlockSpec(memory_space=pl.ANY)],
+        in_specs=[whole(a.shape) for a in args],
         out_specs=tuple(whole(s.shape) for s in shapes),
-        scratch_shapes=[pltpu.VMEM(basis.shape, BF16), pltpu.SemaphoreType.DMA((4,))],
         compiler_params=params(24),
         name="residual",
-    )(*args, in_hbm(basis))
+    )(*args)
 
 
 def factored(gram):
@@ -440,17 +434,19 @@
     before = lax.ppermute(own, "gx", up)
     after = lax.ppermute(own, "gx", down)
     given, before, after = lax.optimization_barrier((given, before, after))
-    relayed = relayed_multipoles(
-        side[None], payload, given, leaves, slots, halves, rhs, peers // 2
-    )
-    received = exchange(relayed.reshape(peers // 2, 2 * slots * halves, -1), same_side)
-    received = received.reshape(relayed.shape)
-
-    near = near_field(near_src, near_count, before, own, after, near_blocks)
+    received = []
+    for multipoles in (payload, given):
+        chosen = chosen_multipoles(side[None], multipoles, leaves, slots, halves, rhs, peers // 2)
+        got = exchange(chosen.reshape(peers // 2, slots * halves, -1), same_side)
+        received.append(got.reshape(chosen.shape))
+
+    near, basis_near, p2m_near, m2l_near = near_field(
+        near_src, near_count, before, own, after, near_blocks, (basis, p2m, m2l)
+    )
 
     sender = far_src // slots
     place = sender // (2 * near_devices) * near_devices + sender % near_devices
-    place = place * 2 + (sender // near_devices % 2 != side).astype(jnp.int32)
+    place = place + jnp.where(sender // near_devices % 2 == side, 0, peers // 2)
     place = place * slots + far_src % slots
     class_hot = (far_class[:, None, :] == jnp.arange(classes)[None, :, None]).astype(BF16)
     rows = jnp.arange(peers * slots * halves)[None, None, None, :]
@@ -459,9 +455,11 @@
     pick = jnp.einsum("gce,hgef->hcgf", class_hot, source_hot, preferred_element_type=F32)
     pick = pick.astype(BF16).reshape(halves, classes * leaves, -1)
 
-    image, sums = far_field(received, pick, m2l, p2m, near, basis, halves, peers)
+    image, sums = far_field(
+        *received, pick, m2l_near, p2m_near, near, basis_near, halves, peers
+    )
     sums = exchange(added(exchange(sums), peers))
-    resid, gram, projections = residual(sums, basis, image, total_rows)
+    resid, gram, projections = residual(sums, basis_near, image, total_rows)
     pair = jnp.stack([gram, lax.ppermute(gram, "hi", flip)])
     grams = exchange(added(pair, peers // 2), same_side)
     next_block, factor = tail(grams, resid)

time: 113 us -> 114 us (level)
  waiting for transfers between devices: 28.4 us -> 15.1 us
  local copies, waits for them, and re-layouts: 3.67 us -> 12.1 us
  starting transfers between devices: 14.8 us -> 21.9 us
    all_to_all x1 -> x2, waiting for transfers between devices: 13.7 us -> 0.01 us  [exchange(): return lax.all_to_all(pieces, axes, split_axis=0, concat_axis=0, tiled=True)]
    unnamed x23 -> x31, local copies, waits for them, and re-layouts: 3.52 us -> 11.9 us
    all_to_all x1 -> x2, starting transfers between devices: 6.1 us -> 14.2 us  [exchange(): return lax.all_to_all(pieces, axes, split_axis=0, concat_axis=0, tiled=True)]
    pallas_call x2 -> x3, Pallas kernels: 13.8 us -> 15.7 us  [the longest x1 12.4 us: near_field(): pl.pallas_call(near_kernel, grid_spec=grid_spec, out_shape=[jax.ShapeDtyp...]
    pallas_call x1, Pallas kernels: 5.62 us -> 4.21 us  [far_field(): pl.pallas_call(functools.partial(far_kernel, halves), grid=(1,), out_shap...]
    pallas_call x1, Pallas kernels: 3.42 us -> 2.09 us  [residual(): pl.pallas_call(functools.partial(resid_kernel, total_rows), grid=(1,), ou...]
  transfers between devices with their start and end apart: 5 -> 6, of which waited for: 3 -> 2; matrix products, arithmetic and copies ran while one was open for 1% -> 1% of each run, Pallas kernels for 10% -> 12%
where the time goes in v5:
time: 114 us; the launch traced here: 113 us
  blocking collectives  32 us (28%)
  Pallas kernels  30.8 us (27%)
  starting transfers between devices  21.9 us (19%)
  waiting for transfers between devices  15.1 us (13%)
  local copies, waits for them, and re-layouts  12.1 us (11%)
    all_to_all x3, blocking collectives, exchange(): return lax.all_to_all(pieces, axes, split_axis=0, concat_axis=0, tiled=True)  32 us
    all_to_all x2, starting transfers between devices, exchange(): return lax.all_to_all(pieces, axes, split_axis=0, concat_axis=0, tiled=True)  14.2 us
    pallas_call x1, Pallas kernels, near_field(): pl.pallas_call(near_kernel, grid_spec=grid_spec, out_shape=[jax.ShapeDtyp...  12.4 us
    unnamed x31, local copies, waits for them, and re-layouts  11.9 us
    ppermute x1, waiting for transfers between devices, shards(): given = lax.ppermute(payload, 'hi', flip)  11.9 us
    pallas_call x1, Pallas kernels, tail(): pl.pallas_call(tail_kernel, grid=(1,), out_shape=shapes, in_specs=[whole(...  6.85 us
    pallas_call x1, Pallas kernels, far_field(): pl.pallas_call(functools.partial(far_kernel, halves), grid=(1,), out_shap...  4.21 us
    ppermute x1, waiting for transfers between devices, shards(): pair = jnp.stack([gram, lax.ppermute(gram, 'hi', flip)])  3.28 us
  transfers between devices with their start and end apart: 6, of which 2 were waited for; matrix products, arithmetic and copies ran while one was open for 1% of the time, Pallas kernels for 12%

profile of v5, /device:TPU:0, one launch (start us, length us, event | category | flops | bytes accessed | tf_op | source)
XLA Modules:
  0.0 113.2 jit_solution(5573109604417411864)
XLA Ops:
  0.6 1.9 %send.1 = (bf16[1040,128]{1,0:T(8,128)(2,1)S(1)}, bf16[64,4096]{1,0:T(8,128)(2,1)S(1)}) custom-call(bf16[8,64,4096]{2,1,0:T(8,128)(2,1)} %refs_0_.1, bf16[16,256,128]{2,1,0:T(8,128)(2,1)} %refs_1_.1, s32[4,32]{1,0:T(4,128)} %bitcast.24, s32[1,32]{1,0:T(1,128)} %counts.1), custom_call_target="tpu_custom_call" | custom-call | tf_op jit(solution)/shard_map/send/pallas_call | solution.py:93
  2.6 1.6 %choose.2 = bf16[128,4096]{1,0:T(8,128)(2,1)} custom-call(s32[1]{0:T(128)} %bitcast.side, bf16[1040,128]{1,0:T(8,128)(2,1)S(1)} %get-tuple-element.19.given), custom_call_target="tpu_custom_call" | custom-call | tf_op jit(solution)/shard_map/choose/pallas_call | solution.py:116
  4.3 6.3 %all-to-all-start = ((bf16[16,8,4096]{2,1,0:T(8,128)(2,1)}), bf16[16,8,4096]{2,1,0:T(8,128)(2,1)S(1)}, u32[]{:S(2)}, u32[]{:S(2)}) async-start(bf16[16,8,4096]{2,1,0:T(8,128)(2,1)} %bitcast.3), calls=%async_computation | async-start | bytes 2097152 | tf_op jit(solution)/shard_map/all_to_all | solution.py:295
  10.6 2.3 %collective-permute-start.1 = (bf16[64,4096]{1,0:T(8,128)(2,1)S(1)}, bf16[64,4096]{1,0:T(8,128)(2,1)S(1)}, u32[]{:S(2)}, u32[]{:S(2)}) collective-permute-start(bf16[64,4096]{1,0:T(8,128)(2,1)S(1)} %get-tuple-element.20.own), channel_id=1, source_target_pairs={{0,8},{8,16},{16,24},{1,9},{9,17},{17,25},{2,10},{10,18},{18,26},{... | collective-permute-start | bytes 1572872 | tf_op jit(solution)/shard_map/ppermute | solution.py:434
  12.9 1.3 %collective-permute-start.2 = (bf16[64,4096]{1,0:T(8,128)(2,1)S(1)}, bf16[64,4096]{1,0:T(8,128)(2,1)S(1)}, u32[]{:S(2)}, u32[]{:S(2)}) collective-permute-start(bf16[64,4096]{1,0:T(8,128)(2,1)S(1)} %get-tuple-element.20.own), channel_id=1, source_target_pairs={{8,0},{16,8},{24,16},{9,1},{17,9},{25,17},{10,2},{18,10},{26,18},{... | collective-permute-start | bytes 1572872 | tf_op jit(solution)/shard_map/ppermute | solution.py:435
  14.2 2.7 %collective-permute-start = (bf16[1040,128]{1,0:T(8,128)(2,1)S(1)}, bf16[1040,128]{1,0:T(8,128)(2,1)S(1)}, u32[]{:S(2)}, u32[]{:S(2)}) collective-permute-start(bf16[1040,128]{1,0:T(8,128)(2,1)S(1)} %get-tuple-element.19.given), channel_id=1, source_target_pairs={{0,4},{4,0},{1,5},{5,1},{2,6},{6,2},{3,7},{7,3},{8,12},{12,8},{9,1... | collective-permute-start | bytes 798728 | tf_op jit(solution)/shard_map/ppermute | solution.py:431
  16.9 11.9 %collective-permute-done.given = bf16[1040,128]{1,0:T(8,128)(2,1)S(1)} collective-permute-done((bf16[1040,128]{1,0:T(8,128)(2,1)S(1)}, bf16[1040,128]{1,0:T(8,128)(2,1)S(1)}, u32[]{:S(2)}, u32[]{:S(2)}) %collective-permute-start) | collective-permute-done | bytes 266272 | tf_op jit(solution)/shard_map/ppermute | solution.py:431
  30.3 1.6 %choose.3 = bf16[128,4096]{1,0:T(8,128)(2,1)} custom-call(s32[1]{0:T(128)} %bitcast.side, bf16[1040,128]{1,0:T(8,128)(2,1)S(1)} %collective-permute-done.given), custom_call_target="tpu_custom_call" | custom-call | tf_op jit(solution)/shard_map/choose/pallas_call | solution.py:116
  31.9 7.9 %all-to-all-start.1 = ((bf16[16,8,4096]{2,1,0:T(8,128)(2,1)}), bf16[16,8,4096]{2,1,0:T(8,128)(2,1)S(1)}, u32[]{:S(2)}, u32[]{:S(2)}) async-start(bf16[16,8,4096]{2,1,0:T(8,128)(2,1)} %bitcast.5), calls=%async_computation.1 | async-start | bytes 2097152 | tf_op jit(solution)/shard_map/all_to_all | solution.py:295
  40.6 1.0 copy-done.6
  41.6 1.0 copy-done.8
  42.7 12.4 %near.1 = (f32[64,4096]{1,0:T(8,128)S(1)}, bf16[8,64,4096]{2,1,0:T(8,128)(2,1)S(1)}, bf16[16,256,128]{2,1,0:T(8,128)(2,1)S(1)}, bf16[16,128,128]{2,1,0:T(8,128)(2,1)S(1)}) custom-call(s32[16,8]{1,0:T(8,128)S(1)} %copy.14.src_ref, s32[16]{0:T(128)S(1)} %copy-done.11, bf16[64,4096]{1,0:T(8,128)(2,1)S(1)} %copy-done.6, bf16[64,4096]{1,0:T(8,128)(2,1)} %copy-done.4, ...), custom_call_target="tpu_custom_call" | custom-call | flops 1073741824 | bytes 20447232 | tf_op jit(solution)/shard_map/near/pallas_call | solution.py:183
  55.1 1.9 %copy-done = bf16[8,64,4096]{2,1,0:T(8,128)(2,1)} copy-done((bf16[8,64,4096]{2,1,0:T(8,128)(2,1)}, bf16[8,64,4096]{2,1,0:T(8,128)(2,1)S(1)}, u32[]{:S(2)}) %copy-start) | copy-done | bytes 4194328
  58.8 2.2 %copy-done.1 = bf16[8,64,4096]{2,1,0:T(8,128)(2,1)S(1)} copy-done((bf16[8,64,4096]{2,1,0:T(8,128)(2,1)S(1)}, bf16[8,64,4096]{2,1,0:T(8,128)(2,1)}, u32[]{:S(2)}) %copy-start.1) | copy-done | bytes 4194328
  61.0 1.2 %copy-done.3 = bf16[16,256,128]{2,1,0:T(8,128)(2,1)S(1)} copy-done((bf16[16,256,128]{2,1,0:T(8,128)(2,1)S(1)}, bf16[16,256,128]{2,1,0:T(8,128)(2,1)}, u32[]{:S(2)}) %copy-start.3) | copy-done | bytes 1048600
  62.2 1.0 copy-done.10
  63.3 4.2 %far.1 = (f32[64,4096]{1,0:T(8,128)S(1)}, f32[32,8,128]{2,1,0:T(8,128)S(1)}) custom-call(bf16[128,4096]{1,0:T(8,128)(2,1)S(1)} %bitcast.19, bf16[128,4096]{1,0:T(8,128)(2,1)S(1)} %bitcast.20, bf16[2,256,256]{2,1,0:T(8,128)(2,1)S(1)} %bitcast.21, f32[64,4096]{1,0:T(8,128)S(1)} %get-tuple-element.24.near, bf16[16,128,128]{2,1,0:T(8,128)(2,1)S(1)} %copy-done.10, ...), custom_call_target="tpu_custom_call" | custom-call | tf_op jit(solution)/shard_map/far/pallas_call | solution.py:274
  67.5 12.2 %all_to_all.25.in_ref = f32[32,8,128]{2,1,0:T(8,128)S(1)} all-to-all(f32[32,8,128]{2,1,0:T(8,128)S(1)} %get-tuple-element.28), channel_id=1, replica_groups=mesh['gx'=4,'hi'=2,'lo'=4] {'gx','hi','lo'}, dimensions={0} | all-to-all | bytes 262144 | tf_op jit(solution)/shard_map/all_to_all | solution.py:295
  79.8 10.0 %all_to_all.26.sums = f32[32,8,128]{2,1,0:T(8,128)S(1)} all-to-all(f32[32,8,128]{2,1,0:T(8,128)S(1)} %add.88), channel_id=1, replica_groups=mesh['gx'=4,'hi'=2,'lo'=4] {'gx','hi','lo'}, dimensions={0} | all-to-all | bytes 262144 | tf_op jit(solution)/shard_map/all_to_all | solution.py:295
  89.8 2.1 %residual.1 = (bf16[128,4096]{1,0:T(8,128)(2,1)S(1)}, f32[32,128]{1,0:T(8,128)S(1)}, f32[512,64]{1,0:T(8,128)}) custom-call(f32[32,8,128]{2,1,0:T(8,128)S(1)} %all_to_all.26.sums, f32[64,4096]{1,0:T(8,128)S(1)} %get-tuple-element.29.image, bf16[8,64,4096]{2,1,0:T(8,128)(2,1)S(1)} %copy-done.1), custom_call_target="tpu_custom_call" | custom-call | tf_op jit(solution)/shard_map/residual/pallas_call | solution.py:344
  91.8 1.4 %collective-permute-start.3 = (f32[32,128]{1,0:T(8,128)S(1)}, f32[32,128]{1,0:T(8,128)S(1)}, u32[]{:S(2)}, u32[]{:S(2)}) collective-permute-start(f32[32,128]{1,0:T(8,128)S(1)} %get-tuple-element.30), channel_id=1, source_target_pairs={{0,4},{4,0},{1,5},{5,1},{2,6},{6,2},{3,7},{7,3},{8,12},{12,8},{9,1... | collective-permute-start | bytes 49160 | tf_op jit(solution)/shard_map/ppermute | solution.py:463
  93.2 3.3 %collective-permute-done.3 = f32[32,128]{1,0:T(8,128)S(1)} collective-permute-done((f32[32,128]{1,0:T(8,128)S(1)}, f32[32,128]{1,0:T(8,128)S(1)}, u32[]{:S(2)}, u32[]{:S(2)}) %collective-permute-start.3) | collective-permute-done | bytes 16416 | tf_op jit(solution)/shard_map/ppermute | solution.py:463
  96.5 9.8 %all_to_all.27.grams = f32[16,32,128]{2,1,0:T(8,128)S(1)} all-to-all(f32[16,32,128]{2,1,0:T(8,128)S(1)} %add.89), channel_id=1, replica_groups=mesh['gx'=4,'hi'=2,'lo'=4] {'gx','lo'}, dimensions={0} | all-to-all | bytes 524288 | tf_op jit(solution)/shard_map/all_to_all | solution.py:295
  106.3 6.8 %tail.1 = (bf16[64,4096]{1,0:T(8,128)(2,1)}, f32[64,64]{1,0:T(8,128)}) custom-call(f32[16,32,128]{2,1,0:T(8,128)S(1)} %all_to_all.27.grams, bf16[128,4096]{1,0:T(8,128)(2,1)S(1)} %get-tuple-element.31.resid), custom_call_target="tpu_custom_call" | custom-call | tf_op jit(solution)/shard_map/tail/pallas_call | solution.py:404
  (36 shorter events, 4.1 us)
Async XLA Ops:
  2.6 29.4 %copy-start.4 = (bf16[64,4096]{1,0:T(8,128)(2,1)}, bf16[64,4096]{1,0:T(8,128)(2,1)S(1)}, u32[]{:S(2)}) copy-start(bf16[64,4096]{1,0:T(8,128)(2,1)S(1)} %get-tuple-element.20.own) | copy-start | bytes 1572868
  2.6 37.3 %copy-start.13 = (s32[16,8]{0,1:T(8,128)S(1)}, s32[16,8]{0,1:T(8,128)}, u32[]{:S(2)}) copy-start(s32[16,8]{0,1:T(8,128)} %param.12) | copy-start | bytes 1540
  2.6 37.4 %copy-start.12 = (s32[16,32]{1,0:T(8,128)S(1)}, s32[16,32]{1,0:T(8,128)}, u32[]{:S(2)}) copy-start(s32[16,32]{1,0:T(8,128)} %param.18) | copy-start | bytes 6148
  2.6 37.4 %copy-start.14 = (s32[16,32]{1,0:T(8,128)S(1)}, s32[16,32]{1,0:T(8,128)}, u32[]{:S(2)}) copy-start(s32[16,32]{1,0:T(8,128)} %param.19) | copy-start | bytes 6148
  2.6 37.9 %copy-start.11 = (s32[16]{0:T(128)S(1)}, s32[16]{0:T(128)}, u32[]{:S(2)}) copy-start(s32[16]{0:T(128)} %count_ref.1) | copy-start | bytes 196
  4.3 27.7 %all-to-all-start = ((bf16[16,8,4096]{2,1,0:T(8,128)(2,1)}), bf16[16,8,4096]{2,1,0:T(8,128)(2,1)S(1)}, u32[]{:S(2)}, u32[]{:S(2)}) async-start(bf16[16,8,4096]{2,1,0:T(8,128)(2,1)} %bitcast.3), calls=%async_computation | async-start | bytes 2097152 | tf_op jit(solution)/shard_map/all_to_all | solution.py:295
  10.6 18.2 %collective-permute-start.1 = (bf16[64,4096]{1,0:T(8,128)(2,1)S(1)}, bf16[64,4096]{1,0:T(8,128)(2,1)S(1)}, u32[]{:S(2)}, u32[]{:S(2)}) collective-permute-start(bf16[64,4096]{1,0:T(8,128)(2,1)S(1)} %get-tuple-element.20.own), channel_id=1, source_target_pairs={{0,8},{8,16},{16,24},{1,9},{9,17},{17,25},{2,10},{10,18},{18,26},{... | collective-permute-start | bytes 1572872 | tf_op jit(solution)/shard_map/ppermute | solution.py:434
  12.9 16.6 %collective-permute-start.2 = (bf16[64,4096]{1,0:T(8,128)(2,1)S(1)}, bf16[64,4096]{1,0:T(8,128)(2,1)S(1)}, u32[]{:S(2)}, u32[]{:S(2)}) collective-permute-start(bf16[64,4096]{1,0:T(8,128)(2,1)S(1)} %get-tuple-element.20.own), channel_id=1, source_target_pairs={{8,0},{16,8},{24,16},{9,1},{17,9},{25,17},{10,2},{18,10},{26,18},{... | collective-permute-start | bytes 1572872 | tf_op jit(solution)/shard_map/ppermute | solution.py:435
  14.2 14.5 %collective-permute-start = (bf16[1040,128]{1,0:T(8,128)(2,1)S(1)}, bf16[1040,128]{1,0:T(8,128)(2,1)S(1)}, u32[]{:S(2)}, u32[]{:S(2)}) collective-permute-start(bf16[1040,128]{1,0:T(8,128)(2,1)S(1)} %get-tuple-element.19.given), channel_id=1, source_target_pairs={{0,4},{4,0},{1,5},{5,1},{2,6},{6,2},{3,7},{7,3},{8,12},{12,8},{9,1... | collective-permute-start | bytes 798728 | tf_op jit(solution)/shard_map/ppermute | solution.py:431
  28.7 0.8 copy-start.5
  29.5 0.8 copy-start.7
  31.9 26.9 %all-to-all-start.1 = ((bf16[16,8,4096]{2,1,0:T(8,128)(2,1)}), bf16[16,8,4096]{2,1,0:T(8,128)(2,1)S(1)}, u32[]{:S(2)}, u32[]{:S(2)}) async-start(bf16[16,8,4096]{2,1,0:T(8,128)(2,1)} %bitcast.5), calls=%async_computation.1 | async-start | bytes 2097152 | tf_op jit(solution)/shard_map/all_to_all | solution.py:295
  40.6 1.0 copy-start.6
  41.6 1.0 copy-start.8
  55.1 2.0 %copy-start = (bf16[8,64,4096]{2,1,0:T(8,128)(2,1)}, bf16[8,64,4096]{2,1,0:T(8,128)(2,1)S(1)}, u32[]{:S(2)}) copy-start(bf16[8,64,4096]{2,1,0:T(8,128)(2,1)S(1)} %get-tuple-element.27.basis) | copy-start | bytes 12582916
  57.1 1.0 copy-start.2
  58.0 0.8 copy-start.9
  58.8 2.2 %copy-start.1 = (bf16[8,64,4096]{2,1,0:T(8,128)(2,1)S(1)}, bf16[8,64,4096]{2,1,0:T(8,128)(2,1)}, u32[]{:S(2)}) copy-start(bf16[8,64,4096]{2,1,0:T(8,128)(2,1)} %copy-done) | copy-start | bytes 12582916
  61.0 1.2 %copy-start.3 = (bf16[16,256,128]{2,1,0:T(8,128)(2,1)S(1)}, bf16[16,256,128]{2,1,0:T(8,128)(2,1)}, u32[]{:S(2)}) copy-start(bf16[16,256,128]{2,1,0:T(8,128)(2,1)} %copy-done.2) | copy-start | bytes 3145732
  62.2 1.0 copy-start.10
  91.8 4.6 %collective-permute-start.3 = (f32[32,128]{1,0:T(8,128)S(1)}, f32[32,128]{1,0:T(8,128)S(1)}, u32[]{:S(2)}, u32[]{:S(2)}) collective-permute-start(f32[32,128]{1,0:T(8,128)S(1)} %get-tuple-element.30), channel_id=1, source_target_pairs={{0,4},{4,0},{1,5},{5,1},{2,6},{6,2},{3,7},{7,3},{8,12},{12,8},{9,1... | collective-permute-start | bytes 49160 | tf_op jit(solution)/shard_map/ppermute | solution.py:463

commit v6 on v5

--- a/solution.py
+++ b/solution.py
@@ -105,7 +105,7 @@
             pltpu.VMEM((rhs // halves, leaves * halves, terms), F32),
             pltpu.VMEM((16, terms), F32),
         ],
-        compiler_params=params(16),
+        compiler_params=params(8),
         name="send",
     )(in_hbm(basis), in_hbm(p2m), in_hbm(listed), in_hbm(counts))
 
@@ -119,7 +119,7 @@
         out_shape=jax.ShapeDtypeStruct(shape, BF16),
         in_specs=[pl.BlockSpec(memory_space=pltpu.SMEM), whole(given.shape)],
         out_specs=whole(shape),
-        compiler_params=params(16),
+        compiler_params=params(8),
         name="choose",
     )(side, given)
 
@@ -185,7 +185,7 @@
         grid_spec=grid_spec,
         out_shape=[jax.ShapeDtypeStruct((rhs, columns), F32)]
         + [pltpu.VMEM(a.shape, a.dtype) for a in bring],
-        compiler_params=params(16),
+        compiler_params=params(12),
         cost_estimate=pl.CostEstimate(
             flops=2 * rhs * near_blocks.size,
             bytes_accessed=near_blocks.size * 2 + 7 * rhs * columns * 2,
@@ -286,7 +286,7 @@
             pltpu.VMEM((rhs, leaves, terms), F32),
             pltpu.VMEM((2 * rhs, columns), BF16),
         ],
-        compiler_params=params(32),
+        compiler_params=params(16),
         name="far",
     )(*args)
 
@@ -308,7 +308,7 @@
         out_shape=jax.ShapeDtypeStruct(shape, F32),
         in_specs=[whole(pieces.shape)],
         out_specs=whole(shape),
-        compiler_params=params(16),
+        compiler_params=params(4),
         name="add",
     )(pieces)
 
@@ -347,7 +347,7 @@
         out_shape=shapes,
         in_specs=[whole(a.shape) for a in args],
         out_specs=tuple(whole(s.shape) for s in shapes),
-        compiler_params=params(24),
+        compiler_params=params(10),
         name="residual",
     )(*args)
 
@@ -407,7 +407,7 @@
         out_shape=shapes,
         in_specs=[whole(a.shape) for a in args],
         out_specs=tuple(whole(s.shape) for s in shapes),
-        compiler_params=params(16),
+        compiler_params=params(6),
         name="tail",
     )(*args)
 
@@ -433,10 +433,10 @@
     down = [(j, i) for i, j in up]
     before = lax.ppermute(own, "gx", up)
     after = lax.ppermute(own, "gx", down)
-    given, before, after = lax.optimization_barrier((given, before, after))
     received = []
     for multipoles in (payload, given):
         chosen = chosen_multipoles(side[None], multipoles, leaves, slots, halves, rhs, peers // 2)
+        chosen, before, after = lax.optimization_barrier((chosen, before, after))
         got = exchange(chosen.reshape(peers // 2, slots * halves, -1), same_side)
         received.append(got.reshape(chosen.shape))
 

time: 114 us -> 124 us (1.088)
  blocking collectives: 32 us -> 56 us
  starting transfers between devices: 21.9 us -> 12.3 us
  waiting for transfers between devices: 15.1 us -> 13.1 us
    all_to_all x3 -> x4, blocking collectives: 32 us -> 56 us  [exchange(): return lax.all_to_all(pieces, axes, split_axis=0, concat_axis=0, tiled=True)]
    all_to_all x2 -> x1, starting transfers between devices: 14.2 us -> 3.65 us  [exchange(): return lax.all_to_all(pieces, axes, split_axis=0, concat_axis=0, tiled=True)]
    ppermute x1, waiting for transfers between devices: 11.9 us -> 9.82 us  [shards(): given = lax.ppermute(payload, 'hi', flip)]
  transfers between devices with their start and end apart: 6 -> 5, of which waited for: 2 -> 2; matrix products, arithmetic and copies ran while one was open for 1% -> 1% of each run, Pallas kernels for 12% -> 12%
where the time goes in v6:
time: 124 us
  blocking collectives  56 us (45%)
  Pallas kernels  29.8 us (24%)
  waiting for transfers between devices  13.1 us (11%)
  starting transfers between devices  12.3 us (10%)
  local copies, waits for them, and re-layouts  11.3 us (9%)
    all_to_all x4, blocking collectives, exchange(): return lax.all_to_all(pieces, axes, split_axis=0, concat_axis=0, tiled=True)  56 us
    pallas_call x1, Pallas kernels, near_field(): pl.pallas_call(near_kernel, grid_spec=grid_spec, out_shape=[jax.ShapeDtyp...  12.4 us
    unnamed x31, local copies, waits for them, and re-layouts  11.1 us
    ppermute x1, waiting for transfers between devices, shards(): given = lax.ppermute(payload, 'hi', flip)  9.82 us
    pallas_call x1, Pallas kernels, tail(): pl.pallas_call(tail_kernel, grid=(1,), out_shape=shapes, in_specs=[whole(...  6.85 us
    pallas_call x1, Pallas kernels, far_field(): pl.pallas_call(functools.partial(far_kernel, halves), grid=(1,), out_shap...  4.21 us
    all_to_all x1, starting transfers between devices, exchange(): return lax.all_to_all(pieces, axes, split_axis=0, concat_axis=0, tiled=True)  3.65 us
    ppermute x1, starting transfers between devices, shards(): given = lax.ppermute(payload, 'hi', flip)  3.48 us
  transfers between devices with their start and end apart: 5, of which 2 were waited for; matrix products, arithmetic and copies ran while one was open for 1% of the time, Pallas kernels for 12%

profile of v6, /device:TPU:0, one launch (start us, length us, event | category | flops | bytes accessed | tf_op | source)
XLA Modules:
  0.0 123.8 jit_solution(2408286473630975850)
XLA Ops:
  0.6 1.9 %send.1 = (bf16[1040,128]{1,0:T(8,128)(2,1)S(1)}, bf16[64,4096]{1,0:T(8,128)(2,1)S(1)}) custom-call(bf16[8,64,4096]{2,1,0:T(8,128)(2,1)} %refs_0_.1, bf16[16,256,128]{2,1,0:T(8,128)(2,1)} %refs_1_.1, s32[4,32]{1,0:T(4,128)} %bitcast.25, s32[1,32]{1,0:T(1,128)} %counts.1), custom_call_target="tpu_custom_call" | custom-call | tf_op jit(solution)/shard_map/send/pallas_call | solution.py:93
  2.6 2.5 %collective-permute-start = (bf16[64,4096]{1,0:T(8,128)(2,1)S(1)}, bf16[64,4096]{1,0:T(8,128)(2,1)S(1)}, u32[]{:S(2)}, u32[]{:S(2)}) collective-permute-start(bf16[64,4096]{1,0:T(8,128)(2,1)S(1)} %get-tuple-element.23.own), channel_id=1, source_target_pairs={{0,8},{8,16},{16,24},{1,9},{9,17},{17,25},{2,10},{10,18},{18,26},{... | collective-permute-start | bytes 1572872 | tf_op jit(solution)/shard_map/ppermute | solution.py:434
  5.2 1.3 %collective-permute-start.1 = (bf16[64,4096]{1,0:T(8,128)(2,1)S(1)}, bf16[64,4096]{1,0:T(8,128)(2,1)S(1)}, u32[]{:S(2)}, u32[]{:S(2)}) collective-permute-start(bf16[64,4096]{1,0:T(8,128)(2,1)S(1)} %get-tuple-element.23.own), channel_id=1, source_target_pairs={{8,0},{16,8},{24,16},{9,1},{17,9},{25,17},{10,2},{18,10},{26,18},{... | collective-permute-start | bytes 1572872 | tf_op jit(solution)/shard_map/ppermute | solution.py:435
  6.5 3.5 %collective-permute-start.2 = (bf16[1040,128]{1,0:T(8,128)(2,1)S(1)}, bf16[1040,128]{1,0:T(8,128)(2,1)S(1)}, u32[]{:S(2)}, u32[]{:S(2)}) collective-permute-start(bf16[1040,128]{1,0:T(8,128)(2,1)S(1)} %get-tuple-element.22.given), channel_id=1, source_target_pairs={{0,4},{4,0},{1,5},{5,1},{2,6},{6,2},{3,7},{7,3},{8,12},{12,8},{9,1... | collective-permute-start | bytes 798728 | tf_op jit(solution)/shard_map/ppermute | solution.py:431
  9.9 1.6 %choose.2 = bf16[128,4096]{1,0:T(8,128)(2,1)} custom-call(s32[1]{0:T(128)} %bitcast.side, bf16[1040,128]{1,0:T(8,128)(2,1)S(1)} %get-tuple-element.22.given), custom_call_target="tpu_custom_call" | custom-call | tf_op jit(solution)/shard_map/choose/pallas_call | solution.py:116
  11.6 9.8 %collective-permute-done.2.given = bf16[1040,128]{1,0:T(8,128)(2,1)S(1)} collective-permute-done((bf16[1040,128]{1,0:T(8,128)(2,1)S(1)}, bf16[1040,128]{1,0:T(8,128)(2,1)S(1)}, u32[]{:S(2)}, u32[]{:S(2)}) %collective-permute-start.2) | collective-permute-done | bytes 266272 | tf_op jit(solution)/shard_map/ppermute | solution.py:431
  22.8 21.8 %all_to_all.25 = bf16[16,8,4096]{2,1,0:T(8,128)(2,1)S(1)} all-to-all(bf16[16,8,4096]{2,1,0:T(8,128)(2,1)S(1)} %bitcast.21), channel_id=1, replica_groups=mesh['gx'=4,'hi'=2,'lo'=4] {'gx','lo'}, dimensions={0} | all-to-all | bytes 2097152 | tf_op jit(solution)/shard_map/all_to_all | solution.py:295
  44.6 3.7 %all-to-all-start = ((bf16[16,8,4096]{2,1,0:T(8,128)(2,1)}), bf16[16,8,4096]{2,1,0:T(8,128)(2,1)S(1)}, u32[]{:S(2)}, u32[]{:S(2)}) async-start(bf16[16,8,4096]{2,1,0:T(8,128)(2,1)} %bitcast.3), calls=%async_computation | async-start | bytes 2097152 | tf_op jit(solution)/shard_map/all_to_all | solution.py:295
  49.0 1.0 copy-done.6
  50.0 1.0 copy-done.8
  51.0 12.4 %near.1 = (f32[64,4096]{1,0:T(8,128)S(1)}, bf16[8,64,4096]{2,1,0:T(8,128)(2,1)S(1)}, bf16[16,256,128]{2,1,0:T(8,128)(2,1)S(1)}, bf16[16,128,128]{2,1,0:T(8,128)(2,1)S(1)}) custom-call(s32[16,8]{1,0:T(8,128)S(1)} %copy.14.src_ref, s32[16]{0:T(128)S(1)} %copy-done.11, bf16[64,4096]{1,0:T(8,128)(2,1)S(1)} %copy-done.6, bf16[64,4096]{1,0:T(8,128)(2,1)} %copy-done.4, ...), custom_call_target="tpu_custom_call" | custom-call | flops 1073741824 | bytes 20447232 | tf_op jit(solution)/shard_map/near/pallas_call | solution.py:183
  63.5 1.9 %copy-done = bf16[8,64,4096]{2,1,0:T(8,128)(2,1)} copy-done((bf16[8,64,4096]{2,1,0:T(8,128)(2,1)}, bf16[8,64,4096]{2,1,0:T(8,128)(2,1)S(1)}, u32[]{:S(2)}) %copy-start) | copy-done | bytes 4194328
  65.4 1.0 copy-done.2
  67.2 2.2 %copy-done.1 = bf16[8,64,4096]{2,1,0:T(8,128)(2,1)S(1)} copy-done((bf16[8,64,4096]{2,1,0:T(8,128)(2,1)S(1)}, bf16[8,64,4096]{2,1,0:T(8,128)(2,1)}, u32[]{:S(2)}) %copy-start.1) | copy-done | bytes 4194328
  69.4 1.2 copy-done.3
  70.6 1.0 copy-done.10
  71.7 4.2 %far.1 = (f32[64,4096]{1,0:T(8,128)S(1)}, f32[32,8,128]{2,1,0:T(8,128)S(1)}) custom-call(bf16[128,4096]{1,0:T(8,128)(2,1)S(1)} %bitcast.20, bf16[128,4096]{1,0:T(8,128)(2,1)S(1)} %bitcast.19, bf16[2,256,256]{2,1,0:T(8,128)(2,1)S(1)} %bitcast.22, f32[64,4096]{1,0:T(8,128)S(1)} %get-tuple-element.30.near, bf16[16,128,128]{2,1,0:T(8,128)(2,1)S(1)} %copy-done.10, ...), custom_call_target="tpu_custom_call" | custom-call | tf_op jit(solution)/shard_map/far/pallas_call | solution.py:274
  75.9 14.4 %all_to_all.26.in_ref = f32[32,8,128]{2,1,0:T(8,128)S(1)} all-to-all(f32[32,8,128]{2,1,0:T(8,128)S(1)} %get-tuple-element.34), channel_id=1, replica_groups=mesh['gx'=4,'hi'=2,'lo'=4] {'gx','hi','lo'}, dimensions={0} | all-to-all | bytes 262144 | tf_op jit(solution)/shard_map/all_to_all | solution.py:295
  90.3 10.0 %all_to_all.27.sums = f32[32,8,128]{2,1,0:T(8,128)S(1)} all-to-all(f32[32,8,128]{2,1,0:T(8,128)S(1)} %add.88), channel_id=1, replica_groups=mesh['gx'=4,'hi'=2,'lo'=4] {'gx','hi','lo'}, dimensions={0} | all-to-all | bytes 262144 | tf_op jit(solution)/shard_map/all_to_all | solution.py:295
  100.3 2.1 %residual.1 = (bf16[128,4096]{1,0:T(8,128)(2,1)S(1)}, f32[32,128]{1,0:T(8,128)S(1)}, f32[512,64]{1,0:T(8,128)}) custom-call(f32[32,8,128]{2,1,0:T(8,128)S(1)} %all_to_all.27.sums, f32[64,4096]{1,0:T(8,128)S(1)} %get-tuple-element.35.image, bf16[8,64,4096]{2,1,0:T(8,128)(2,1)S(1)} %copy-done.1), custom_call_target="tpu_custom_call" | custom-call | tf_op jit(solution)/shard_map/residual/pallas_call | solution.py:344
  102.4 1.4 %collective-permute-start.3 = (f32[32,128]{1,0:T(8,128)S(1)}, f32[32,128]{1,0:T(8,128)S(1)}, u32[]{:S(2)}, u32[]{:S(2)}) collective-permute-start(f32[32,128]{1,0:T(8,128)S(1)} %get-tuple-element.36), channel_id=1, source_target_pairs={{0,4},{4,0},{1,5},{5,1},{2,6},{6,2},{3,7},{7,3},{8,12},{12,8},{9,1... | collective-permute-start | bytes 49160 | tf_op jit(solution)/shard_map/ppermute | solution.py:463
  103.8 3.3 %collective-permute-done.3 = f32[32,128]{1,0:T(8,128)S(1)} collective-permute-done((f32[32,128]{1,0:T(8,128)S(1)}, f32[32,128]{1,0:T(8,128)S(1)}, u32[]{:S(2)}, u32[]{:S(2)}) %collective-permute-start.3) | collective-permute-done | bytes 16416 | tf_op jit(solution)/shard_map/ppermute | solution.py:463
  107.1 9.8 %all_to_all.28.grams = f32[16,32,128]{2,1,0:T(8,128)S(1)} all-to-all(f32[16,32,128]{2,1,0:T(8,128)S(1)} %add.89), channel_id=1, replica_groups=mesh['gx'=4,'hi'=2,'lo'=4] {'gx','lo'}, dimensions={0} | all-to-all | bytes 524288 | tf_op jit(solution)/shard_map/all_to_all | solution.py:295
  116.9 6.8 %tail.1 = (bf16[64,4096]{1,0:T(8,128)(2,1)}, f32[64,64]{1,0:T(8,128)}) custom-call(f32[16,32,128]{2,1,0:T(8,128)S(1)} %all_to_all.28.grams, bf16[128,4096]{1,0:T(8,128)(2,1)S(1)} %get-tuple-element.37.resid), custom_call_target="tpu_custom_call" | custom-call | tf_op jit(solution)/shard_map/tail/pallas_call | solution.py:404
  (35 shorter events, 2.9 us)
Async XLA Ops:
  2.6 20.2 %copy-start.4 = (bf16[64,4096]{1,0:T(8,128)(2,1)}, bf16[64,4096]{1,0:T(8,128)(2,1)S(1)}, u32[]{:S(2)}) copy-start(bf16[64,4096]{1,0:T(8,128)(2,1)S(1)} %get-tuple-element.23.own) | copy-start | bytes 1572868
  2.6 45.7 %copy-start.13 = (s32[16,8]{0,1:T(8,128)S(1)}, s32[16,8]{0,1:T(8,128)}, u32[]{:S(2)}) copy-start(s32[16,8]{0,1:T(8,128)} %param.12) | copy-start | bytes 1540
  2.6 45.8 %copy-start.12 = (s32[16,32]{1,0:T(8,128)S(1)}, s32[16,32]{1,0:T(8,128)}, u32[]{:S(2)}) copy-start(s32[16,32]{1,0:T(8,128)} %param.18) | copy-start | bytes 6148
  2.6 45.8 %copy-start.14 = (s32[16,32]{1,0:T(8,128)S(1)}, s32[16,32]{1,0:T(8,128)}, u32[]{:S(2)}) copy-start(s32[16,32]{1,0:T(8,128)} %param.19) | copy-start | bytes 6148
  2.6 19.4 %collective-permute-start = (bf16[64,4096]{1,0:T(8,128)(2,1)S(1)}, bf16[64,4096]{1,0:T(8,128)(2,1)S(1)}, u32[]{:S(2)}, u32[]{:S(2)}) collective-permute-start(bf16[64,4096]{1,0:T(8,128)(2,1)S(1)} %get-tuple-element.23.own), channel_id=1, source_target_pairs={{0,8},{8,16},{16,24},{1,9},{9,17},{17,25},{2,10},{10,18},{18,26},{... | collective-permute-start | bytes 1572872 | tf_op jit(solution)/shard_map/ppermute | solution.py:434
  5.2 17.7 %collective-permute-start.1 = (bf16[64,4096]{1,0:T(8,128)(2,1)S(1)}, bf16[64,4096]{1,0:T(8,128)(2,1)S(1)}, u32[]{:S(2)}, u32[]{:S(2)}) collective-permute-start(bf16[64,4096]{1,0:T(8,128)(2,1)S(1)} %get-tuple-element.23.own), channel_id=1, source_target_pairs={{8,0},{16,8},{24,16},{9,1},{17,9},{25,17},{10,2},{18,10},{26,18},{... | collective-permute-start | bytes 1572872 | tf_op jit(solution)/shard_map/ppermute | solution.py:435
  6.5 14.9 %collective-permute-start.2 = (bf16[1040,128]{1,0:T(8,128)(2,1)S(1)}, bf16[1040,128]{1,0:T(8,128)(2,1)S(1)}, u32[]{:S(2)}, u32[]{:S(2)}) collective-permute-start(bf16[1040,128]{1,0:T(8,128)(2,1)S(1)} %get-tuple-element.22.given), channel_id=1, source_target_pairs={{0,4},{4,0},{1,5},{5,1},{2,6},{6,2},{3,7},{7,3},{8,12},{12,8},{9,1... | collective-permute-start | bytes 798728 | tf_op jit(solution)/shard_map/ppermute | solution.py:431
  9.9 39.0 %copy-start.11 = (s32[16]{0:T(128)S(1)}, s32[16]{0:T(128)}, u32[]{:S(2)}) copy-start(s32[16]{0:T(128)} %count_ref.1) | copy-start | bytes 196
  22.0 0.8 copy-start.5
  22.8 21.8 %copy-start.7 = (bf16[64,4096]{1,0:T(8,128)(2,1)}, bf16[64,4096]{1,0:T(8,128)(2,1)S(1)}, u32[]{:S(2)}) copy-start(bf16[64,4096]{1,0:T(8,128)(2,1)S(1)} %collective-permute-done.1.after) | copy-start | bytes 1572868
  44.6 22.6 %all-to-all-start = ((bf16[16,8,4096]{2,1,0:T(8,128)(2,1)}), bf16[16,8,4096]{2,1,0:T(8,128)(2,1)S(1)}, u32[]{:S(2)}, u32[]{:S(2)}) async-start(bf16[16,8,4096]{2,1,0:T(8,128)(2,1)} %bitcast.3), calls=%async_computation | async-start | bytes 2097152 | tf_op jit(solution)/shard_map/all_to_all | solution.py:295
  48.9 1.0 copy-start.6
  50.0 1.0 copy-start.8
  63.5 1.9 %copy-start = (bf16[8,64,4096]{2,1,0:T(8,128)(2,1)}, bf16[8,64,4096]{2,1,0:T(8,128)(2,1)S(1)}, u32[]{:S(2)}) copy-start(bf16[8,64,4096]{2,1,0:T(8,128)(2,1)S(1)} %get-tuple-element.33.basis) | copy-start | bytes 12582916
  65.4 1.0 copy-start.2
  66.4 0.8 copy-start.9
  67.2 2.2 %copy-start.1 = (bf16[8,64,4096]{2,1,0:T(8,128)(2,1)S(1)}, bf16[8,64,4096]{2,1,0:T(8,128)(2,1)}, u32[]{:S(2)}) copy-start(bf16[8,64,4096]{2,1,0:T(8,128)(2,1)} %copy-done) | copy-start | bytes 12582916
  69.4 1.2 copy-start.3
  70.6 1.0 copy-start.10
  102.4 4.6 %collective-permute-start.3 = (f32[32,128]{1,0:T(8,128)S(1)}, f32[32,128]{1,0:T(8,128)S(1)}, u32[]{:S(2)}, u32[]{:S(2)}) collective-permute-start(f32[32,128]{1,0:T(8,128)S(1)} %get-tuple-element.36), channel_id=1, source_target_pairs={{0,4},{4,0},{1,5},{5,1},{2,6},{6,2},{3,7},{7,3},{8,12},{12,8},{9,1... | collective-permute-start | bytes 49160 | tf_op jit(solution)/shard_map/ppermute | solution.py:463

commit v7 on v4

--- a/solution.py
+++ b/solution.py
@@ -58,35 +58,28 @@
     out[part * tall :, :] = lists[...].astype(BF16)
 
 
-def relay_kernel(halves, slots, leaves, near_devices, side, own, given, out):
+def choose_kernel(halves, slots, leaves, near_devices, side, given, out):
     tall, terms = leaves * halves, given.shape[1]
     rows, part = out.shape[0], out.shape[1] // terms
-    each = 2 * slots * halves
-    peers = 2 * rows // each
+    each = slots * halves
     receiver = lax.broadcasted_iota(jnp.int32, (rows, terms), 0) // each
     far_part, near_part = receiver // near_devices, receiver % near_devices
     device = far_part * (2 * near_devices) + side[0] * near_devices + near_part
     hot = (device == lax.broadcasted_iota(jnp.int32, (rows, terms), 1)).astype(F32).astype(BF16)
-    spread = [dot_nt(hot, ref[part * tall :, :]) for ref in (own, given)]
-    row = lax.broadcasted_iota(jnp.int32, spread[0].shape, 0)
-    lane = lax.broadcasted_iota(jnp.int32, spread[0].shape, 1)
-    spread = jnp.where(row // (slots * halves) % 2 == 0, spread[0], spread[1])
+    spread = dot_nt(hot, given[part * tall :, :])
+    row = lax.broadcasted_iota(jnp.int32, spread.shape, 0)
+    lane = lax.broadcasted_iota(jnp.int32, spread.shape, 1)
     slot = row // halves % slots
     leaf = jnp.sum(jnp.where(lane == slot, spread, 0.0), axis=1, keepdims=True)
     live = jnp.sum(jnp.where(lane == slots, spread, 0.0), axis=1, keepdims=True)
-    row = lax.broadcasted_iota(jnp.int32, (rows, 2 * tall), 0)
-    lane = lax.broadcasted_iota(jnp.int32, (rows, 2 * tall), 1).astype(F32)
-    offset = row // (slots * halves) % 2 * tall + row % halves
+    row = lax.broadcasted_iota(jnp.int32, (rows, tall), 0)
+    lane = lax.broadcasted_iota(jnp.int32, (rows, tall), 1).astype(F32)
     held = (row // halves % slots).astype(F32) < live
-    chosen = ((lane == leaf * halves + offset.astype(F32)) & held).astype(F32).astype(BF16)
+    wanted = leaf * halves + (row % halves).astype(F32)
+    chosen = ((lane == wanted) & held).astype(F32).astype(BF16)
     for j in range(part // 2):
-        pairs = [
-            jnp.concatenate(
-                [ref[i * tall : (i + 1) * tall, :] for i in (2 * j, 2 * j + 1)], axis=1
-            )
-            for ref in (own, given)
-        ]
-        got = dot(chosen, jnp.concatenate(pairs, axis=0))
+        pair = [given[i * tall : (i + 1) * tall, :] for i in (2 * j, 2 * j + 1)]
+        got = dot(chosen, jnp.concatenate(pair, axis=1))
         out[:, j * 2 * terms : (j + 1) * 2 * terms] = got.astype(BF16)
 
 
@@ -112,27 +105,23 @@
             pltpu.VMEM((rhs // halves, leaves * halves, terms), F32),
             pltpu.VMEM((16, terms), F32),
         ],
-        compiler_params=params(16),
+        compiler_params=params(8),
         name="send",
-    )(in_hbm(basis), in_hbm(p2m), listed, counts)
-
-
-def relayed_multipoles(side, own, given, leaves, slots, halves, rhs, receivers):
-    terms = own.shape[1]
-    shape = (receivers * 2 * slots * halves, rhs // halves * terms)
-    return pl.pallas_call(
-        functools.partial(relay_kernel, halves, slots, leaves, lax.axis_size("lo")),
+    )(in_hbm(basis), in_hbm(p2m), in_hbm(listed), in_hbm(counts))
+
+
+def chosen_multipoles(side, given, leaves, slots, halves, rhs, receivers):
+    terms = given.shape[1]
+    shape = (receivers * slots * halves, rhs // halves * terms)
+    return pl.pallas_call(
+        functools.partial(choose_kernel, halves, slots, leaves, lax.axis_size("lo")),
         grid=(1,),
         out_shape=jax.ShapeDtypeStruct(shape, BF16),
-        in_specs=[
-            pl.BlockSpec(memory_space=pltpu.SMEM),
-            whole(own.shape),
-            whole(given.shape),
-        ],
+        in_specs=[pl.BlockSpec(memory_space=pltpu.SMEM), whole(given.shape)],
         out_specs=whole(shape),
-        compiler_params=params(16),
-        name="relay",
-    )(side, own, given)
+        compiler_params=params(8),
+        name="choose",
+    )(side, given)
 
 
 def near_kernel(src_ref, count_ref, before, own, after, blocks_ref, out_ref, wide):
@@ -177,20 +166,20 @@
         near_kernel,
         grid_spec=grid_spec,
         out_shape=jax.ShapeDtypeStruct((rhs, columns), F32),
-        compiler_params=params(16),
+        compiler_params=params(12),
         cost_estimate=pl.CostEstimate(
             flops=2 * rhs * near_blocks.size,
             bytes_accessed=near_blocks.size * 2 + 7 * rhs * columns * 2,
             transcendentals=0,
         ),
         name="near",
-    )(near_src, near_count, before, in_hbm(own), after, in_hbm(near_blocks))
+    )(near_src, near_count, in_hbm(before), in_hbm(own), in_hbm(after), in_hbm(near_blocks))
 
 
 def far_kernel(
-    halves, recv, pick, near, m2l_hbm, p2m_hbm, basis_hbm, image_ref, sums_ref, *scratch
+    halves, ours, theirs, pick, near, m2l_hbm, p2m_hbm, basis_hbm, image_ref, sums_ref, *scratch
 ):
-    lhs, loc, both, m2l, p2m, basis, sems = scratch
+    recv, lhs, loc, both, m2l, p2m, basis, sems = scratch
     moves = [
         pltpu.make_async_copy(source, target, sems.at[i])
         for i, (source, target) in enumerate(
@@ -204,6 +193,8 @@
     blocks, rhs, columns = basis.shape
     part = rhs // halves
     group = 8
+    rows = ours.shape[0]
+    recv[:rows], recv[rows:] = ours[...], theirs[...]
     for h in range(halves):
         for j in range(0, part, group):
             got = dot(pick[h], recv[:, j * terms : (j + group) * terms]).astype(BF16)
@@ -259,12 +250,12 @@
     )
 
 
-def far_field(recv, pick, m2l, p2m, near, basis, halves, peers):
+def far_field(ours, theirs, pick, m2l, p2m, near, basis, halves, peers):
     leaves, panels, terms = p2m.shape
     classes = m2l.shape[0]
     blocks, rhs, columns = basis.shape
     _, piece = pack_sizes(rhs, blocks * rhs, peers)
-    args = (recv, pick, near)
+    args = (ours, theirs, pick, near)
     anywhere = pl.BlockSpec(memory_space=pl.ANY)
     return pl.pallas_call(
         functools.partial(far_kernel, halves),
@@ -276,6 +267,7 @@
         in_specs=[whole(a.shape) for a in args] + [anywhere] * 3,
         out_specs=(whole((rhs, columns)), whole((peers, piece, 128))),
         scratch_shapes=[
+            pltpu.VMEM((2 * ours.shape[0], ours.shape[1]), BF16),
             pltpu.VMEM((rhs * leaves, classes * terms), BF16),
             pltpu.VMEM((rhs, leaves, terms), F32),
             pltpu.VMEM((2 * rhs, columns), BF16),
@@ -284,7 +276,7 @@
             pltpu.VMEM(basis.shape, BF16),
             pltpu.SemaphoreType.DMA((3,)),
         ],
-        compiler_params=params(32),
+        compiler_params=params(24),
         name="far",
     )(*args, in_hbm(m2l), in_hbm(p2m), in_hbm(basis))
 
@@ -306,7 +298,7 @@
         out_shape=jax.ShapeDtypeStruct(shape, F32),
         in_specs=[whole(pieces.shape)],
         out_specs=whole(shape),
-        compiler_params=params(16),
+        compiler_params=params(4),
         name="add",
     )(pieces)
 
@@ -353,43 +345,40 @@
         in_specs=[whole(a.shape) for a in args] + [pl.BlockSpec(memory_space=pl.ANY)],
         out_specs=tuple(whole(s.shape) for s in shapes),
         scratch_shapes=[pltpu.VMEM(basis.shape, BF16), pltpu.SemaphoreType.DMA((4,))],
-        compiler_params=params(24),
+        compiler_params=params(16),
         name="residual",
     )(*args, in_hbm(basis))
 
 
-def factored(gram):
+def factored(gram, done):
     size = gram.shape[0]
     rows = lax.broadcasted_iota(jnp.int32, (size, size), 0)
     cols = lax.broadcasted_iota(jnp.int32, (size, size), 1)
-    eye = (rows == cols).astype(F32)
-    both = jnp.concatenate([gram, eye], axis=1)
+    both = jnp.concatenate([gram, (rows == cols).astype(F32)], axis=1)
     tiles = [both[8 * i : 8 * i + 8] for i in range(size // 8)]
-    sub = lax.broadcasted_iota(jnp.int32, (8, 2 * size), 0)
-    for j in range(size):
+    for j in range(0, size, 2):
         t, o = divmod(j, 8)
-        row = tiles[t][o : o + 1]
-        pivot = 1.0 / row[:, j : j + 1]
-        scaled = row * pivot
+        first, second = tiles[t][o : o + 1], tiles[t][o + 1 : o + 2]
+        a, b, c = first[:, j : j + 1], first[:, j + 1 : j + 2], second[:, j + 1 : j + 2]
+        scale = 1.0 / (a * c - b * b)
+        upper = (c * first - b * second) * scale
+        lower = (a * second - b * first) * scale
         for i in range(t, size // 8):
-            column = tiles[i][:, j : j + 1]
-            change = column * scaled
-            if i == t:
-                change = jnp.where(sub > o, change, 0.0)
+            change = tiles[i][:, j : j + 1] * upper + tiles[i][:, j + 1 : j + 2] * lower
             tiles[i] = tiles[i] - change
-    both = jnp.concatenate(tiles, axis=0)
-    pivots = jnp.sum(both[:, :size] * eye, axis=1, keepdims=True)
-    both = both * (1.0 / jnp.sqrt(pivots))
-    upper = jnp.where(cols >= rows, both[:, :size], 0.0)
-    return upper.T, both[:, size:]
-
-
-def tail_kernel(grams, resid, next_ref, factor_ref):
+        ratio = b / a
+        done[j : j + 1, :] = first / jnp.sqrt(a)
+        done[j + 1 : j + 2, :] = (second - ratio * first) / jnp.sqrt(c - ratio * b)
+    both = done[...]
+    return jnp.where(cols >= rows, both[:, :size], 0.0).T, both[:, size:]
+
+
+def tail_kernel(grams, resid, next_ref, factor_ref, done):
     rhs = factor_ref.shape[0]
     columns = resid.shape[1]
     folded = jnp.sum(grams[...], axis=0)
     gram = jnp.concatenate([folded[:, :rhs], folded[:, rhs:]], axis=0)
-    lower, inverse = factored(gram)
+    lower, inverse = factored(gram, done)
     factor_ref[...] = lower
     coef = jnp.concatenate(split_parts(inverse), axis=0)
     step = 1024
@@ -413,7 +402,8 @@
         out_shape=shapes,
         in_specs=[whole(a.shape) for a in args],
         out_specs=tuple(whole(s.shape) for s in shapes),
-        compiler_params=params(16),
+        scratch_shapes=[pltpu.VMEM((rhs, 2 * rhs), F32)],
+        compiler_params=params(6),
         name="tail",
     )(*args)
 
@@ -440,17 +430,17 @@
     before = lax.ppermute(own, "gx", up)
     after = lax.ppermute(own, "gx", down)
     given, before, after = lax.optimization_barrier((given, before, after))
-    relayed = relayed_multipoles(
-        side[None], payload, given, leaves, slots, halves, rhs, peers // 2
-    )
-    received = exchange(relayed.reshape(peers // 2, 2 * slots * halves, -1), same_side)
-    received = received.reshape(relayed.shape)
+    received = []
+    for multipoles in (payload, given):
+        chosen = chosen_multipoles(side[None], multipoles, leaves, slots, halves, rhs, peers // 2)
+        got = exchange(chosen.reshape(peers // 2, slots * halves, -1), same_side)
+        received.append(got.reshape(chosen.shape))
 
     near = near_field(near_src, near_count, before, own, after, near_blocks)
 
     sender = far_src // slots
     place = sender // (2 * near_devices) * near_devices + sender % near_devices
-    place = place * 2 + (sender // near_devices % 2 != side).astype(jnp.int32)
+    place = place + jnp.where(sender // near_devices % 2 == side, 0, peers // 2)
     place = place * slots + far_src % slots
     class_hot = (far_class[:, None, :] == jnp.arange(classes)[None, :, None]).astype(BF16)
     rows = jnp.arange(peers * slots * halves)[None, None, None, :]
@@ -459,7 +449,7 @@
     pick = jnp.einsum("gce,hgef->hcgf", class_hot, source_hot, preferred_element_type=F32)
     pick = pick.astype(BF16).reshape(halves, classes * leaves, -1)
 
-    image, sums = far_field(received, pick, m2l, p2m, near, basis, halves, peers)
+    image, sums = far_field(*received, pick, m2l, p2m, near, basis, halves, peers)
     sums = exchange(added(exchange(sums), peers))
     resid, gram, projections = residual(sums, basis, image, total_rows)
     pair = jnp.stack([gram, lax.ppermute(gram, "hi", flip)])

time: 113 us -> 108 us (0.956)
  waiting for transfers between devices: 28.4 us -> 14.5 us
  starting transfers between devices: 14.8 us -> 23.4 us
  blocking collectives: 33 us -> 31.5 us
  local copies, waits for them, and re-layouts: 3.67 us -> 2.37 us
    all_to_all x1 -> x2, waiting for transfers between devices: 13.7 us -> 0.82 us  [exchange(): return lax.all_to_all(pieces, axes, split_axis=0, concat_axis=0, tiled=True)]
    all_to_all x1 -> x2, starting transfers between devices: 6.1 us -> 14.2 us  [exchange(): return lax.all_to_all(pieces, axes, split_axis=0, concat_axis=0, tiled=True)]
    all_to_all x3, blocking collectives: 33 us -> 31.5 us  [exchange(): return lax.all_to_all(pieces, axes, split_axis=0, concat_axis=0, tiled=True)]
    ppermute x1, starting transfers between devices: 2.52 us -> 3.84 us  [shards(): before = lax.ppermute(own, 'gx', up)]
    unnamed x23 -> x7, local copies, waits for them, and re-layouts: 3.52 us -> 2.22 us
    pallas_call x1 -> x2, Pallas kernels: 2.24 us -> 3.22 us  [chosen_multipoles(): pl.pallas_call(functools.partial(choose_kernel, halves, slots, leaves, la...]
  transfers between devices with their start and end apart: 5 -> 6, of which waited for: 3 -> 3; matrix products, arithmetic and copies ran while one was open for 1% -> 3% of each run, Pallas kernels for 10% -> 13%
where the time goes in v7:
time: 108 us; the launch traced here: 107 us
  Pallas kernels  32.6 us (30%)
  blocking collectives  31.5 us (29%)
  starting transfers between devices  23.4 us (22%)
  waiting for transfers between devices  14.5 us (13%)
  local copies, waits for them, and re-layouts  2.37 us (2%)
    all_to_all x3, blocking collectives, exchange(): return lax.all_to_all(pieces, axes, split_axis=0, concat_axis=0, tiled=True)  31.5 us
    all_to_all x2, starting transfers between devices, exchange(): return lax.all_to_all(pieces, axes, split_axis=0, concat_axis=0, tiled=True)  14.2 us
    pallas_call x1, Pallas kernels, near_field(): pl.pallas_call(near_kernel, grid_spec=grid_spec, out_shape=jax.ShapeDtype...  11.9 us
    ppermute x1, waiting for transfers between devices, shards(): given = lax.ppermute(payload, 'hi', flip)  10.4 us
    pallas_call x1, Pallas kernels, tail(): pl.pallas_call(tail_kernel, grid=(1,), out_shape=shapes, in_specs=[whole(...  6.49 us
    pallas_call x1, Pallas kernels, far_field(): pl.pallas_call(functools.partial(far_kernel, halves), grid=(1,), out_shap...  5.62 us
    ppermute x1, starting transfers between devices, shards(): before = lax.ppermute(own, 'gx', up)  3.84 us
    pallas_call x1, Pallas kernels, residual(): pl.pallas_call(functools.partial(resid_kernel, total_rows), grid=(1,), ou...  3.42 us
  transfers between devices with their start and end apart: 6, of which 3 were waited for; matrix products, arithmetic and copies ran while one was open for 3% of the time, Pallas kernels for 13%

profile of v7, /device:TPU:0, one launch (start us, length us, event | category | flops | bytes accessed | tf_op | source)
XLA Modules:
  0.0 107.0 jit_solution(11214197743212483396)
XLA Ops:
  0.6 1.9 %send.1 = (bf16[1040,128]{1,0:T(8,128)(2,1)S(1)}, bf16[64,4096]{1,0:T(8,128)(2,1)S(1)}) custom-call(bf16[8,64,4096]{2,1,0:T(8,128)(2,1)} %basis_hbm.3, bf16[16,256,128]{2,1,0:T(8,128)(2,1)} %p2m_hbm.1, s32[4,32]{1,0:T(4,128)} %bitcast.24, s32[1,32]{1,0:T(1,128)} %counts.1), custom_call_target="tpu_custom_call" | custom-call | tf_op jit(solution)/shard_map/send/pallas_call | solution.py:93
  2.6 1.6 %choose.2 = bf16[128,4096]{1,0:T(8,128)(2,1)} custom-call(s32[1]{0:T(128)} %bitcast.side, bf16[1040,128]{1,0:T(8,128)(2,1)S(1)} %get-tuple-element.15.given), custom_call_target="tpu_custom_call" | custom-call | tf_op jit(solution)/shard_map/choose/pallas_call | solution.py:116
  4.2 6.3 %all-to-all-start = ((bf16[16,8,4096]{2,1,0:T(8,128)(2,1)}), bf16[16,8,4096]{2,1,0:T(8,128)(2,1)S(1)}, u32[]{:S(2)}, u32[]{:S(2)}) async-start(bf16[16,8,4096]{2,1,0:T(8,128)(2,1)} %bitcast.3), calls=%async_computation | async-start | bytes 2097152 | tf_op jit(solution)/shard_map/all_to_all | solution.py:285
  10.5 1.3 %collective-permute-start.2 = (bf16[64,4096]{1,0:T(8,128)(2,1)S(1)}, bf16[64,4096]{1,0:T(8,128)(2,1)S(1)}, u32[]{:S(2)}, u32[]{:S(2)}) collective-permute-start(bf16[64,4096]{1,0:T(8,128)(2,1)S(1)} %get-tuple-element.16.own), channel_id=1, source_target_pairs={{8,0},{16,8},{24,16},{9,1},{17,9},{25,17},{10,2},{18,10},{26,18},{... | collective-permute-start | bytes 1572872 | tf_op jit(solution)/shard_map/ppermute | solution.py:431
  11.8 3.8 %collective-permute-start.1 = (bf16[64,4096]{1,0:T(8,128)(2,1)S(1)}, bf16[64,4096]{1,0:T(8,128)(2,1)}, u32[]{:S(2)}, u32[]{:S(2)}) collective-permute-start(bf16[64,4096]{1,0:T(8,128)(2,1)S(1)} %get-tuple-element.16.own), channel_id=1, source_target_pairs={{0,8},{8,16},{16,24},{1,9},{9,17},{17,25},{2,10},{10,18},{18,26},{... | collective-permute-start | bytes 1572872 | tf_op jit(solution)/shard_map/ppermute | solution.py:430
  15.6 2.6 %collective-permute-start = (bf16[1040,128]{1,0:T(8,128)(2,1)S(1)}, bf16[1040,128]{1,0:T(8,128)(2,1)S(1)}, u32[]{:S(2)}, u32[]{:S(2)}) collective-permute-start(bf16[1040,128]{1,0:T(8,128)(2,1)S(1)} %get-tuple-element.15.given), channel_id=1, source_target_pairs={{0,4},{4,0},{1,5},{5,1},{2,6},{6,2},{3,7},{7,3},{8,12},{12,8},{9,1... | collective-permute-start | bytes 798728 | tf_op jit(solution)/shard_map/ppermute | solution.py:427
  18.2 10.4 %collective-permute-done.given = bf16[1040,128]{1,0:T(8,128)(2,1)S(1)} collective-permute-done((bf16[1040,128]{1,0:T(8,128)(2,1)S(1)}, bf16[1040,128]{1,0:T(8,128)(2,1)S(1)}, u32[]{:S(2)}, u32[]{:S(2)}) %collective-permute-start) | collective-permute-done | bytes 266272 | tf_op jit(solution)/shard_map/ppermute | solution.py:427
  28.6 0.8 copy-done.2
  29.5 1.6 %choose.3 = bf16[128,4096]{1,0:T(8,128)(2,1)} custom-call(s32[1]{0:T(128)} %bitcast.side, bf16[1040,128]{1,0:T(8,128)(2,1)S(1)} %collective-permute-done.given), custom_call_target="tpu_custom_call" | custom-call | tf_op jit(solution)/shard_map/choose/pallas_call | solution.py:116
  31.1 7.9 %all-to-all-start.1 = ((bf16[16,8,4096]{2,1,0:T(8,128)(2,1)}), bf16[16,8,4096]{2,1,0:T(8,128)(2,1)S(1)}, u32[]{:S(2)}, u32[]{:S(2)}) async-start(bf16[16,8,4096]{2,1,0:T(8,128)(2,1)} %bitcast.5), calls=%async_computation.1 | async-start | bytes 2097152 | tf_op jit(solution)/shard_map/all_to_all | solution.py:285
  39.0 0.8 copy.14.src_ref
  39.8 0.7 fusion.11
  40.5 1.1 fusion
  41.8 0.6 copy-done.1
  42.4 11.9 %near.1 = f32[64,4096]{1,0:T(8,128)S(1)} custom-call(s32[16,8]{1,0:T(8,128)S(1)} %copy.14.src_ref, s32[16]{0:T(128)S(1)} %copy-done.1, bf16[64,4096]{1,0:T(8,128)(2,1)} %collective-permute-done.1.before, bf16[64,4096]{1,0:T(8,128)(2,1)} %copy-done, bf16[64,4096]{1,0:T(8,128)(2,1)} %copy-done.2, bf16[16,8,256,256]{3,2,1,0:T(8,128)(2,1)} %blocks_ref.1), custom_call_target="tpu_custom_call" | custom-call | flops 1073741824 | bytes 20447232 | tf_op jit(solution)/shard_map/near/pallas_call | solution.py:165
  54.3 0.8 all-to-all-done.1
  55.1 5.6 %far.1 = (f32[64,4096]{1,0:T(8,128)S(1)}, f32[32,8,128]{2,1,0:T(8,128)S(1)}) custom-call(bf16[128,4096]{1,0:T(8,128)(2,1)S(1)} %bitcast.19, bf16[128,4096]{1,0:T(8,128)(2,1)S(1)} %bitcast.20, bf16[2,256,256]{2,1,0:T(8,128)(2,1)S(1)} %bitcast.21, f32[64,4096]{1,0:T(8,128)S(1)} %near.1, bf16[16,128,128]{2,1,0:T(8,128)(2,1)} %m2l_hbm.1, ...), custom_call_target="tpu_custom_call" | custom-call | tf_op jit(solution)/shard_map/far/pallas_call | solution.py:260
  60.7 11.7 %all_to_all.25.in_ref = f32[32,8,128]{2,1,0:T(8,128)S(1)} all-to-all(f32[32,8,128]{2,1,0:T(8,128)S(1)} %get-tuple-element.20), channel_id=1, replica_groups=mesh['gx'=4,'hi'=2,'lo'=4] {'gx','hi','lo'}, dimensions={0} | all-to-all | bytes 262144 | tf_op jit(solution)/shard_map/all_to_all | solution.py:285
  72.5 10.0 %all_to_all.26.sums = f32[32,8,128]{2,1,0:T(8,128)S(1)} all-to-all(f32[32,8,128]{2,1,0:T(8,128)S(1)} %add.88), channel_id=1, replica_groups=mesh['gx'=4,'hi'=2,'lo'=4] {'gx','hi','lo'}, dimensions={0} | all-to-all | bytes 262144 | tf_op jit(solution)/shard_map/all_to_all | solution.py:285
  82.5 3.4 %residual.1 = (bf16[128,4096]{1,0:T(8,128)(2,1)S(1)}, f32[32,128]{1,0:T(8,128)S(1)}, f32[512,64]{1,0:T(8,128)}) custom-call(f32[32,8,128]{2,1,0:T(8,128)S(1)} %all_to_all.26.sums, f32[64,4096]{1,0:T(8,128)S(1)} %get-tuple-element.21.image, bf16[8,64,4096]{2,1,0:T(8,128)(2,1)} %basis_hbm.3), custom_call_target="tpu_custom_call" | custom-call | tf_op jit(solution)/shard_map/residual/pallas_call | solution.py:341
  85.9 1.4 %collective-permute-start.3 = (f32[32,128]{1,0:T(8,128)S(1)}, f32[32,128]{1,0:T(8,128)S(1)}, u32[]{:S(2)}, u32[]{:S(2)}) collective-permute-start(f32[32,128]{1,0:T(8,128)S(1)} %get-tuple-element.22), channel_id=1, source_target_pairs={{0,4},{4,0},{1,5},{5,1},{2,6},{6,2},{3,7},{7,3},{8,12},{12,8},{9,1... | collective-permute-start | bytes 49160 | tf_op jit(solution)/shard_map/ppermute | solution.py:455
  87.3 3.3 %collective-permute-done.3 = f32[32,128]{1,0:T(8,128)S(1)} collective-permute-done((f32[32,128]{1,0:T(8,128)S(1)}, f32[32,128]{1,0:T(8,128)S(1)}, u32[]{:S(2)}, u32[]{:S(2)}) %collective-permute-start.3) | collective-permute-done | bytes 16416 | tf_op jit(solution)/shard_map/ppermute | solution.py:455
  90.6 9.8 %all_to_all.27.grams = f32[16,32,128]{2,1,0:T(8,128)S(1)} all-to-all(f32[16,32,128]{2,1,0:T(8,128)S(1)} %add.89), channel_id=1, replica_groups=mesh['gx'=4,'hi'=2,'lo'=4] {'gx','lo'}, dimensions={0} | all-to-all | bytes 524288 | tf_op jit(solution)/shard_map/all_to_all | solution.py:285
  100.5 6.5 %tail.1 = (bf16[64,4096]{1,0:T(8,128)(2,1)}, f32[64,64]{1,0:T(8,128)}) custom-call(f32[16,32,128]{2,1,0:T(8,128)S(1)} %all_to_all.27.grams, bf16[128,4096]{1,0:T(8,128)(2,1)S(1)} %get-tuple-element.23.resid), custom_call_target="tpu_custom_call" | custom-call | tf_op jit(solution)/shard_map/tail/pallas_call | solution.py:399
  (12 shorter events, 0.2 us)
Async XLA Ops:
  2.6 28.5 %copy-start = (bf16[64,4096]{1,0:T(8,128)(2,1)}, bf16[64,4096]{1,0:T(8,128)(2,1)S(1)}, u32[]{:S(2)}) copy-start(bf16[64,4096]{1,0:T(8,128)(2,1)S(1)} %get-tuple-element.16.own) | copy-start | bytes 1572868
  4.2 26.9 %all-to-all-start = ((bf16[16,8,4096]{2,1,0:T(8,128)(2,1)}), bf16[16,8,4096]{2,1,0:T(8,128)(2,1)S(1)}, u32[]{:S(2)}, u32[]{:S(2)}) async-start(bf16[16,8,4096]{2,1,0:T(8,128)(2,1)} %bitcast.3), calls=%async_computation | async-start | bytes 2097152 | tf_op jit(solution)/shard_map/all_to_all | solution.py:285
  10.5 18.2 %collective-permute-start.2 = (bf16[64,4096]{1,0:T(8,128)(2,1)S(1)}, bf16[64,4096]{1,0:T(8,128)(2,1)S(1)}, u32[]{:S(2)}, u32[]{:S(2)}) collective-permute-start(bf16[64,4096]{1,0:T(8,128)(2,1)S(1)} %get-tuple-element.16.own), channel_id=1, source_target_pairs={{8,0},{16,8},{24,16},{9,1},{17,9},{25,17},{10,2},{18,10},{26,18},{... | collective-permute-start | bytes 1572872 | tf_op jit(solution)/shard_map/ppermute | solution.py:431
  11.8 17.7 %collective-permute-start.1 = (bf16[64,4096]{1,0:T(8,128)(2,1)S(1)}, bf16[64,4096]{1,0:T(8,128)(2,1)}, u32[]{:S(2)}, u32[]{:S(2)}) collective-permute-start(bf16[64,4096]{1,0:T(8,128)(2,1)S(1)} %get-tuple-element.16.own), channel_id=1, source_target_pairs={{0,8},{8,16},{16,24},{1,9},{9,17},{17,25},{2,10},{10,18},{18,26},{... | collective-permute-start | bytes 1572872 | tf_op jit(solution)/shard_map/ppermute | solution.py:430
  15.6 13.0 %collective-permute-start = (bf16[1040,128]{1,0:T(8,128)(2,1)S(1)}, bf16[1040,128]{1,0:T(8,128)(2,1)S(1)}, u32[]{:S(2)}, u32[]{:S(2)}) collective-permute-start(bf16[1040,128]{1,0:T(8,128)(2,1)S(1)} %get-tuple-element.15.given), channel_id=1, source_target_pairs={{0,4},{4,0},{1,5},{5,1},{2,6},{6,2},{3,7},{7,3},{8,12},{12,8},{9,1... | collective-permute-start | bytes 798728 | tf_op jit(solution)/shard_map/ppermute | solution.py:427
  28.6 0.8 copy-start.2
  31.1 24.0 %all-to-all-start.1 = ((bf16[16,8,4096]{2,1,0:T(8,128)(2,1)}), bf16[16,8,4096]{2,1,0:T(8,128)(2,1)S(1)}, u32[]{:S(2)}, u32[]{:S(2)}) async-start(bf16[16,8,4096]{2,1,0:T(8,128)(2,1)} %bitcast.5), calls=%async_computation.1 | async-start | bytes 2097152 | tf_op jit(solution)/shard_map/all_to_all | solution.py:285
  41.8 0.7 copy-start.1
  85.9 4.7 %collective-permute-start.3 = (f32[32,128]{1,0:T(8,128)S(1)}, f32[32,128]{1,0:T(8,128)S(1)}, u32[]{:S(2)}, u32[]{:S(2)}) collective-permute-start(f32[32,128]{1,0:T(8,128)S(1)} %get-tuple-element.22), channel_id=1, source_target_pairs={{0,4},{4,0},{1,5},{5,1},{2,6},{6,2},{3,7},{7,3},{8,12},{12,8},{9,1... | collective-permute-start | bytes 49160 | tf_op jit(solution)/shard_map/ppermute | solution.py:455

commit v8 on v7

--- a/solution.py
+++ b/solution.py
@@ -39,12 +39,12 @@
     return pl.BlockSpec(shape, lambda *_: (0,) * len(shape))
 
 
-def send_kernel(halves, x, p2m, listed, counts, out, own, scratch, lists):
+def send_kernel(halves, x, p2m, listed, counts, out, own_top, own_low, scratch, lists):
     leaves, panels, terms = p2m.shape
     rhs = x.shape[1]
     part = rhs // halves
     slots, peers = listed.shape
-    own[...] = x[0]
+    own_top[...], own_low[...] = x[0, : rhs // 2], x[0, rhs // 2 :]
     for g in range(leaves):
         mult = dot(x[0, :, g * panels : (g + 1) * panels], p2m[g])
         for h in range(halves):
@@ -88,7 +88,8 @@
     leaves, panels, terms = p2m.shape
     shapes = (
         jax.ShapeDtypeStruct((rhs * leaves + 16, terms), BF16),
-        jax.ShapeDtypeStruct((rhs, columns), BF16),
+        jax.ShapeDtypeStruct((rhs // 2, columns), BF16),
+        jax.ShapeDtypeStruct((rhs // 2, columns), BF16),
     )
     return pl.pallas_call(
         functools.partial(send_kernel, halves),
@@ -124,39 +125,39 @@
     )(side, given)
 
 
-def near_kernel(src_ref, count_ref, before, own, after, blocks_ref, out_ref, wide):
-    columns = own.shape[1]
+def near_kernel(src_ref, count_ref, *refs):
+    pieces, (blocks_ref, out_ref, wide) = refs[:6], refs[6:]
+    half, columns = pieces[0].shape
     slots, panels = blocks_ref.shape[1], blocks_ref.shape[2]
     g = pl.program_id(0)
 
     @pl.when(g == 0)
     def _():
-        wide[:, :columns] = before[...]
-        wide[:, columns : 2 * columns] = own[...]
-        wide[:, 2 * columns :] = after[...]
+        for i, piece in enumerate(pieces):
+            rows, place = slice(i % 2 * half, (i % 2 + 1) * half), i // 2 * columns
+            wide[rows, place : place + columns] = piece[...]
 
     for i in range(blocks_ref.shape[0]):
         leaf = g * blocks_ref.shape[0] + i
         here = pl.ds(pl.multiple_of(columns + leaf * panels, panels), panels)
         total = [wide[:, here].astype(F32), 0.0]
         for k in range(slots):
-            place = pl.multiple_of(src_ref[leaf, k] * panels, panels)
+            place = pl.multiple_of(src_ref[k, leaf] * panels, panels)
             source = wide[:, pl.ds(place, panels)]
             source = jnp.where(k < count_ref[leaf], source, jnp.zeros_like(source))
             total[k % 2] += dot_nt(source, blocks_ref[i, k])
         out_ref[:, i * panels : (i + 1) * panels] = total[0] + total[1]
 
 
-def near_field(near_src, near_count, before, own, after, near_blocks):
+def near_field(near_src, near_count, pieces, near_blocks):
     leaves, slots, panels, _ = near_blocks.shape
-    rhs, columns = own.shape
+    half, columns = pieces[0].shape
+    rhs = 2 * half
     grid_spec = pltpu.PrefetchScalarGridSpec(
         num_scalar_prefetch=2,
         grid=(leaves // 2,),
         in_specs=[
-            whole((rhs, columns)),
-            whole((rhs, columns)),
-            whole((rhs, columns)),
+            *[whole((half, columns))] * 6,
             pl.BlockSpec((2, slots, panels, panels), lambda g, *_: (g, 0, 0, 0)),
         ],
         out_specs=pl.BlockSpec((rhs, 2 * panels), lambda g, *_: (0, g)),
@@ -173,13 +174,13 @@
             transcendentals=0,
         ),
         name="near",
-    )(near_src, near_count, in_hbm(before), in_hbm(own), in_hbm(after), in_hbm(near_blocks))
+    )(near_src.T, near_count, *[in_hbm(p) for p in pieces], in_hbm(near_blocks))
 
 
 def far_kernel(
-    halves, ours, theirs, pick, near, m2l_hbm, p2m_hbm, basis_hbm, image_ref, sums_ref, *scratch
+    halves, ours, theirs, pick, near, m2l_hbm, p2m_hbm, basis_hbm, image_ref, sums_ref, basis, *scratch
 ):
-    recv, lhs, loc, both, m2l, p2m, basis, sems = scratch
+    recv, lhs, loc, both, m2l, p2m, sems = scratch
     moves = [
         pltpu.make_async_copy(source, target, sems.at[i])
         for i, (source, target) in enumerate(
@@ -263,9 +264,14 @@
         out_shape=(
             jax.ShapeDtypeStruct((rhs, columns), F32),
             jax.ShapeDtypeStruct((peers, piece, 128), F32),
+            pltpu.VMEM(basis.shape, BF16),
         ),
         in_specs=[whole(a.shape) for a in args] + [anywhere] * 3,
-        out_specs=(whole((rhs, columns)), whole((peers, piece, 128))),
+        out_specs=(
+            whole((rhs, columns)),
+            whole((peers, piece, 128)),
+            pl.BlockSpec(memory_space=pltpu.VMEM),
+        ),
         scratch_shapes=[
             pltpu.VMEM((2 * ours.shape[0], ours.shape[1]), BF16),
             pltpu.VMEM((rhs * leaves, classes * terms), BF16),
@@ -273,7 +279,6 @@
             pltpu.VMEM((2 * rhs, columns), BF16),
             pltpu.VMEM(m2l.shape, BF16),
             pltpu.VMEM(p2m.shape, BF16),
-            pltpu.VMEM(basis.shape, BF16),
             pltpu.SemaphoreType.DMA((3,)),
         ],
         compiler_params=params(24),
@@ -303,22 +308,15 @@
     )(pieces)
 
 
-def resid_kernel(total_rows, sums, image, basis_hbm, resid_ref, gram_ref, proj_ref, basis, sems):
+def resid_kernel(total_rows, sums, image, basis, resid_ref, gram_ref, proj_ref):
     blocks, rhs, columns = basis.shape
     wide = blocks * rhs
-    steps = sems.shape[0]
-    step = columns // steps
-    moves = []
-    for i in range(steps):
-        part = (slice(None), slice(None), pl.ds(i * step, step))
-        moves.append(pltpu.make_async_copy(basis_hbm.at[part], basis.at[part], sems.at[i]))
-        moves[i].start()
     proj = unpack(sums, rhs, wide) * (1.0 / total_rows)
     proj_ref[...] = proj.T
     coef = jnp.concatenate(split_parts(proj), axis=0)
-    for i in range(steps):
+    step = 1024
+    for i in range(columns // step):
         cols = slice(i * step, (i + 1) * step)
-        moves[i].wait()
         by_basis = dot(coef, basis[:, :, cols].reshape(wide, step))
         resid = image[:, cols] - (by_basis[:rhs] + by_basis[rhs:])
         resid_ref[:rhs, cols], resid_ref[rhs:, cols] = split_parts(resid)
@@ -332,7 +330,7 @@
 
 def residual(sums, basis, image, total_rows):
     blocks, rhs, columns = basis.shape
-    args = (sums, image)
+    args = (sums, image, basis)
     shapes = (
         jax.ShapeDtypeStruct((2 * rhs, columns), BF16),
         jax.ShapeDtypeStruct((rhs // 2, 2 * rhs), F32),
@@ -342,12 +340,11 @@
         functools.partial(resid_kernel, total_rows),
         grid=(1,),
         out_shape=shapes,
-        in_specs=[whole(a.shape) for a in args] + [pl.BlockSpec(memory_space=pl.ANY)],
+        in_specs=[whole(a.shape) for a in args],
         out_specs=tuple(whole(s.shape) for s in shapes),
-        scratch_shapes=[pltpu.VMEM(basis.shape, BF16), pltpu.SemaphoreType.DMA((4,))],
-        compiler_params=params(16),
+        compiler_params=params(24),
         name="residual",
-    )(*args, in_hbm(basis))
+    )(*args)
 
 
 def factored(gram, done):
@@ -422,21 +419,12 @@
     side = lax.axis_index("hi")
     same_side = ("gx", "lo")
 
-    payload, own = all_multipoles(basis, p2m, send_list[0].T, send_count, halves)
+    payload, *own = all_multipoles(basis, p2m, send_list[0].T, send_count, halves)
     flip = [(0, 1), (1, 0)]
     given = lax.ppermute(payload, "hi", flip)
     up = [(i, i + 1) for i in range(devices - 1)]
     down = [(j, i) for i, j in up]
-    before = lax.ppermute(own, "gx", up)
-    after = lax.ppermute(own, "gx", down)
-    given, before, after = lax.optimization_barrier((given, before, after))
-    received = []
-    for multipoles in (payload, given):
-        chosen = chosen_multipoles(side[None], multipoles, leaves, slots, halves, rhs, peers // 2)
-        got = exchange(chosen.reshape(peers // 2, slots * halves, -1), same_side)
-        received.append(got.reshape(chosen.shape))
-
-    near = near_field(near_src, near_count, before, own, after, near_blocks)
+    pieces = [lax.ppermute(half, "gx", way) for way in (up, down) for half in own]
 
     sender = far_src // slots
     place = sender // (2 * near_devices) * near_devices + sender % near_devices
@@ -449,9 +437,20 @@
     pick = jnp.einsum("gce,hgef->hcgf", class_hot, source_hot, preferred_element_type=F32)
     pick = pick.astype(BF16).reshape(halves, classes * leaves, -1)
 
-    image, sums = far_field(*received, pick, m2l, p2m, near, basis, halves, peers)
+    given, pick = lax.optimization_barrier((given, pick))
+    received = []
+    for multipoles in (payload, given):
+        chosen = chosen_multipoles(side[None], multipoles, leaves, slots, halves, rhs, peers // 2)
+        if multipoles is given:
+            chosen, *pieces = lax.optimization_barrier((chosen, *pieces))
+        got = exchange(chosen.reshape(peers // 2, slots * halves, -1), same_side)
+        received.append(got.reshape(chosen.shape))
+
+    pieces = [*pieces[:2], *own, *pieces[2:]]
+    near = near_field(near_src, near_count, pieces, near_blocks)
+    image, sums, basis_near = far_field(*received, pick, m2l, p2m, near, basis, halves, peers)
     sums = exchange(added(exchange(sums), peers))
-    resid, gram, projections = residual(sums, basis, image, total_rows)
+    resid, gram, projections = residual(sums, basis_near, image, total_rows)
     pair = jnp.stack([gram, lax.ppermute(gram, "hi", flip)])
     grams = exchange(added(pair, peers // 2), same_side)
     next_block, factor = tail(grams, resid)

time: 108 us -> 110 us (1.019)
  waiting for transfers between devices: 14.5 us -> 20 us
  Pallas kernels: 32.6 us -> 31.2 us
  local copies, waits for them, and re-layouts: 2.37 us -> 0.99 us
    ppermute x2 -> x4, starting transfers between devices: 5.13 us -> 10.5 us  [shards(): lax.ppermute(half, 'gx', way)]
    all_to_all x2, starting transfers between devices: 14.2 us -> 9.94 us  [exchange(): return lax.all_to_all(pieces, axes, split_axis=0, concat_axis=0, tiled=True)]
    all_to_all x2, waiting for transfers between devices: 0.82 us -> 4.16 us  [exchange(): return lax.all_to_all(pieces, axes, split_axis=0, concat_axis=0, tiled=True)]
    ppermute x1, waiting for transfers between devices: 10.4 us -> 12.6 us  [shards(): given = lax.ppermute(payload, 'hi', flip)]
    unnamed x7 -> x18, local copies, waits for them, and re-layouts: 2.22 us -> 0.84 us
    pallas_call x1, Pallas kernels: 3.42 us -> 2.09 us  [residual(): pl.pallas_call(functools.partial(resid_kernel, total_rows), grid=(1,), ou...]
  transfers between devices with their start and end apart: 6 -> 8, of which waited for: 3 -> 3; matrix products, arithmetic and copies ran while one was open for 3% -> 1% of each run, Pallas kernels for 13% -> 12%
where the time goes in v8:
time: 110 us
  blocking collectives  31.7 us (29%)
  Pallas kernels  31.2 us (28%)
  starting transfers between devices  24.4 us (22%)
  waiting for transfers between devices  20 us (18%)
    all_to_all x3, blocking collectives, exchange(): return lax.all_to_all(pieces, axes, split_axis=0, concat_axis=0, tiled=True)  31.7 us
    ppermute x1, waiting for transfers between devices, shards(): given = lax.ppermute(payload, 'hi', flip)  12.6 us
    pallas_call x1, Pallas kernels, near_field(): pl.pallas_call(near_kernel, grid_spec=grid_spec, out_shape=jax.ShapeDtype...  11.8 us
    ppermute x4, starting transfers between devices, shards(): lax.ppermute(half, 'gx', way)  10.5 us
    all_to_all x2, starting transfers between devices, exchange(): return lax.all_to_all(pieces, axes, split_axis=0, concat_axis=0, tiled=True)  9.94 us
    pallas_call x1, Pallas kernels, tail(): pl.pallas_call(tail_kernel, grid=(1,), out_shape=shapes, in_specs=[whole(...  6.5 us
    pallas_call x1, Pallas kernels, far_field(): pl.pallas_call(functools.partial(far_kernel, halves), grid=(1,), out_shap...  5.61 us
    all_to_all x2, waiting for transfers between devices, exchange(): return lax.all_to_all(pieces, axes, split_axis=0, concat_axis=0, tiled=True)  4.16 us
  transfers between devices with their start and end apart: 8, of which 3 were waited for; matrix products, arithmetic and copies ran while one was open for 1% of the time, Pallas kernels for 12%

profile of v8, /device:TPU:0, one launch (start us, length us, event | category | flops | bytes accessed | tf_op | source)
XLA Modules:
  0.0 109.6 jit_solution(10610736474788574325)
XLA Ops:
  0.7 1.9 %send.1 = (bf16[1040,128]{1,0:T(8,128)(2,1)S(1)}, bf16[32,4096]{1,0:T(8,128)(2,1)S(1)}, bf16[32,4096]{1,0:T(8,128)(2,1)S(1)}) custom-call(bf16[8,64,4096]{2,1,0:T(8,128)(2,1)} %basis_hbm.1, bf16[16,256,128]{2,1,0:T(8,128)(2,1)} %p2m_hbm.1, s32[4,32]{1,0:T(4,128)} %bitcast.26, s32[1,32]{1,0:T(1,128)} %counts.1), custom_call_target="tpu_custom_call" | custom-call | tf_op jit(solution)/shard_map/send/pallas_call | solution.py:94
  2.7 1.6 %choose.2 = bf16[128,4096]{1,0:T(8,128)(2,1)} custom-call(s32[1]{0:T(128)} %bitcast.side, bf16[1040,128]{1,0:T(8,128)(2,1)S(1)} %get-tuple-element.21.given), custom_call_target="tpu_custom_call" | custom-call | tf_op jit(solution)/shard_map/choose/pallas_call | solution.py:117
  4.2 6.3 %all-to-all-start = ((bf16[16,8,4096]{2,1,0:T(8,128)(2,1)}), bf16[16,8,4096]{2,1,0:T(8,128)(2,1)S(1)}, u32[]{:S(2)}, u32[]{:S(2)}) async-start(bf16[16,8,4096]{2,1,0:T(8,128)(2,1)} %bitcast.3), calls=%async_computation | async-start | bytes 2097152 | tf_op jit(solution)/shard_map/all_to_all | solution.py:290
  10.5 1.3 %collective-permute-start.3 = (bf16[32,4096]{1,0:T(8,128)(2,1)S(1)}, bf16[32,4096]{1,0:T(8,128)(2,1)S(1)}, u32[]{:S(2)}, u32[]{:S(2)}) collective-permute-start(bf16[32,4096]{1,0:T(8,128)(2,1)S(1)} %get-tuple-element.23.refs_2_), channel_id=1, source_target_pairs={{8,0},{16,8},{24,16},{9,1},{17,9},{25,17},{10,2},{18,10},{26,18},{... | collective-permute-start | bytes 786440 | tf_op jit(solution)/shard_map/ppermute | solution.py:427
  11.8 3.0 %collective-permute-start.1 = (bf16[32,4096]{1,0:T(8,128)(2,1)S(1)}, bf16[32,4096]{1,0:T(8,128)(2,1)S(1)}, u32[]{:S(2)}, u32[]{:S(2)}) collective-permute-start(bf16[32,4096]{1,0:T(8,128)(2,1)S(1)} %get-tuple-element.23.refs_2_), channel_id=1, source_target_pairs={{0,8},{8,16},{16,24},{1,9},{9,17},{17,25},{2,10},{10,18},{18,26},{... | collective-permute-start | bytes 786440 | tf_op jit(solution)/shard_map/ppermute | solution.py:427
  14.9 1.3 %collective-permute-start.4 = (bf16[32,4096]{1,0:T(8,128)(2,1)S(1)}, bf16[32,4096]{1,0:T(8,128)(2,1)S(1)}, u32[]{:S(2)}, u32[]{:S(2)}) collective-permute-start(bf16[32,4096]{1,0:T(8,128)(2,1)S(1)} %get-tuple-element.24.refs_3_), channel_id=1, source_target_pairs={{8,0},{16,8},{24,16},{9,1},{17,9},{25,17},{10,2},{18,10},{26,18},{... | collective-permute-start | bytes 786440 | tf_op jit(solution)/shard_map/ppermute | solution.py:427
  16.2 4.9 %collective-permute-start.2 = (bf16[32,4096]{1,0:T(8,128)(2,1)S(1)}, bf16[32,4096]{1,0:T(8,128)(2,1)}, u32[]{:S(2)}, u32[]{:S(2)}) collective-permute-start(bf16[32,4096]{1,0:T(8,128)(2,1)S(1)} %get-tuple-element.24.refs_3_), channel_id=1, source_target_pairs={{0,8},{8,16},{16,24},{1,9},{9,17},{17,25},{2,10},{10,18},{18,26},{... | collective-permute-start | bytes 786440 | tf_op jit(solution)/shard_map/ppermute | solution.py:427
  21.1 2.6 %collective-permute-start = (bf16[1040,128]{1,0:T(8,128)(2,1)S(1)}, bf16[1040,128]{1,0:T(8,128)(2,1)S(1)}, u32[]{:S(2)}, u32[]{:S(2)}) collective-permute-start(bf16[1040,128]{1,0:T(8,128)(2,1)S(1)} %get-tuple-element.21.given), channel_id=1, source_target_pairs={{0,4},{4,0},{1,5},{5,1},{2,6},{6,2},{3,7},{7,3},{8,12},{12,8},{9,1... | collective-permute-start | bytes 798728 | tf_op jit(solution)/shard_map/ppermute | solution.py:424
  23.7 0.4 fusion
  24.1 0.2 copy.13
  24.2 12.6 %collective-permute-done.given = bf16[1040,128]{1,0:T(8,128)(2,1)S(1)} collective-permute-done((bf16[1040,128]{1,0:T(8,128)(2,1)S(1)}, bf16[1040,128]{1,0:T(8,128)(2,1)S(1)}, u32[]{:S(2)}, u32[]{:S(2)}) %collective-permute-start) | collective-permute-done | bytes 266272 | tf_op jit(solution)/shard_map/ppermute | solution.py:424
  36.8 1.6 %choose.3 = bf16[128,4096]{1,0:T(8,128)(2,1)} custom-call(s32[1]{0:T(128)} %bitcast.side, bf16[1040,128]{1,0:T(8,128)(2,1)S(1)} %collective-permute-done.given), custom_call_target="tpu_custom_call" | custom-call | tf_op jit(solution)/shard_map/choose/pallas_call | solution.py:117
  38.5 0.7 copy-done.4
  39.3 3.7 %all-to-all-start.1 = ((bf16[16,8,4096]{2,1,0:T(8,128)(2,1)}), bf16[16,8,4096]{2,1,0:T(8,128)(2,1)S(1)}, u32[]{:S(2)}, u32[]{:S(2)}) async-start(bf16[16,8,4096]{2,1,0:T(8,128)(2,1)} %bitcast.9), calls=%async_computation.1 | async-start | bytes 2097152 | tf_op jit(solution)/shard_map/all_to_all | solution.py:290
  43.0 11.8 %near.1 = f32[64,4096]{1,0:T(8,128)S(1)} custom-call(s32[8,16]{1,0:T(8,128)S(1)} %bitcast.24, s32[16]{0:T(128)S(1)} %copy-done.3, bf16[32,4096]{1,0:T(8,128)(2,1)} %copy-done.5, bf16[32,4096]{1,0:T(8,128)(2,1)} %collective-permute-done.2.refs_1_, bf16[32,4096]{1,0:T(8,128)(2,1)} %copy-done, bf16[32,4096]{1,0:T(8,128)(2,1)} %copy-done.1, ...), custom_call_target="tpu_custom_call" | custom-call | flops 1073741824 | bytes 20447232 | tf_op jit(solution)/shard_map/near/pallas_call | solution.py:166
  54.8 4.2 %all-to-all-done.1 = bf16[16,8,4096]{2,1,0:T(8,128)(2,1)S(1)} async-done(((bf16[16,8,4096]{2,1,0:T(8,128)(2,1)}), bf16[16,8,4096]{2,1,0:T(8,128)(2,1)S(1)}, u32[]{:S(2)}, u32[]{:S(2)}) %all-to-all-start.1) | async-done | bytes 1048608 | tf_op jit(solution)/shard_map/all_to_all | solution.py:290
  59.0 5.6 %far.1 = (f32[64,4096]{1,0:T(8,128)S(1)}, f32[32,8,128]{2,1,0:T(8,128)S(1)}, bf16[8,64,4096]{2,1,0:T(8,128)(2,1)S(1)}) custom-call(bf16[128,4096]{1,0:T(8,128)(2,1)S(1)} %bitcast.20, bf16[128,4096]{1,0:T(8,128)(2,1)S(1)} %bitcast.21, bf16[2,256,256]{2,1,0:T(8,128)(2,1)S(1)} %bitcast.22, f32[64,4096]{1,0:T(8,128)S(1)} %near.1, bf16[16,128,128]{2,1,0:T(8,128)(2,1)} %m2l_hbm.1, ...), custom_call_target="tpu_custom_call" | custom-call | tf_op jit(solution)/shard_map/far/pallas_call | solution.py:261
  64.6 11.9 %all_to_all.25.in_ref = f32[32,8,128]{2,1,0:T(8,128)S(1)} all-to-all(f32[32,8,128]{2,1,0:T(8,128)S(1)} %get-tuple-element.31), channel_id=1, replica_groups=mesh['gx'=4,'hi'=2,'lo'=4] {'gx','hi','lo'}, dimensions={0} | all-to-all | bytes 262144 | tf_op jit(solution)/shard_map/all_to_all | solution.py:290
  76.5 10.0 %all_to_all.26.sums = f32[32,8,128]{2,1,0:T(8,128)S(1)} all-to-all(f32[32,8,128]{2,1,0:T(8,128)S(1)} %add.88), channel_id=1, replica_groups=mesh['gx'=4,'hi'=2,'lo'=4] {'gx','hi','lo'}, dimensions={0} | all-to-all | bytes 262144 | tf_op jit(solution)/shard_map/all_to_all | solution.py:290
  86.5 2.1 %residual.1 = (bf16[128,4096]{1,0:T(8,128)(2,1)S(1)}, f32[32,128]{1,0:T(8,128)S(1)}, f32[512,64]{1,0:T(8,128)}) custom-call(f32[32,8,128]{2,1,0:T(8,128)S(1)} %all_to_all.26.sums, f32[64,4096]{1,0:T(8,128)S(1)} %get-tuple-element.32.image, bf16[8,64,4096]{2,1,0:T(8,128)(2,1)S(1)} %get-tuple-element.33.basis), custom_call_target="tpu_custom_call" | custom-call | tf_op jit(solution)/shard_map/residual/pallas_call | solution.py:339
  88.6 1.4 %collective-permute-start.5 = (f32[32,128]{1,0:T(8,128)S(1)}, f32[32,128]{1,0:T(8,128)S(1)}, u32[]{:S(2)}, u32[]{:S(2)}) collective-permute-start(f32[32,128]{1,0:T(8,128)S(1)} %get-tuple-element.34), channel_id=1, source_target_pairs={{0,4},{4,0},{1,5},{5,1},{2,6},{6,2},{3,7},{7,3},{8,12},{12,8},{9,1... | collective-permute-start | bytes 49160 | tf_op jit(solution)/shard_map/ppermute | solution.py:454
  90.0 3.3 %collective-permute-done.5 = f32[32,128]{1,0:T(8,128)S(1)} collective-permute-done((f32[32,128]{1,0:T(8,128)S(1)}, f32[32,128]{1,0:T(8,128)S(1)}, u32[]{:S(2)}, u32[]{:S(2)}) %collective-permute-start.5) | collective-permute-done | bytes 16416 | tf_op jit(solution)/shard_map/ppermute | solution.py:454
  93.3 9.8 %all_to_all.27.grams = f32[16,32,128]{2,1,0:T(8,128)S(1)} all-to-all(f32[16,32,128]{2,1,0:T(8,128)S(1)} %add.89), channel_id=1, replica_groups=mesh['gx'=4,'hi'=2,'lo'=4] {'gx','lo'}, dimensions={0} | all-to-all | bytes 524288 | tf_op jit(solution)/shard_map/all_to_all | solution.py:290
  103.1 6.5 %tail.1 = (bf16[64,4096]{1,0:T(8,128)(2,1)}, f32[64,64]{1,0:T(8,128)}) custom-call(f32[16,32,128]{2,1,0:T(8,128)S(1)} %all_to_all.27.grams, bf16[128,4096]{1,0:T(8,128)(2,1)S(1)} %get-tuple-element.35.resid), custom_call_target="tpu_custom_call" | custom-call | tf_op jit(solution)/shard_map/tail/pallas_call | solution.py:396
  (27 shorter events, 0.3 us)
Async XLA Ops:
  0.6 23.0 %copy-start.7 = (s32[16,32]{1,0:T(8,128)S(1)}, s32[16,32]{1,0:T(8,128)}, u32[]{:S(2)}) copy-start(s32[16,32]{1,0:T(8,128)} %param.18) | copy-start | bytes 6148
  0.6 23.1 %copy-start.8 = (s32[16,32]{1,0:T(8,128)S(1)}, s32[16,32]{1,0:T(8,128)}, u32[]{:S(2)}) copy-start(s32[16,32]{1,0:T(8,128)} %param.19) | copy-start | bytes 6148
  2.6 35.9 %copy-start.1 = (bf16[32,4096]{1,0:T(8,128)(2,1)}, bf16[32,4096]{1,0:T(8,128)(2,1)S(1)}, u32[]{:S(2)}) copy-start(bf16[32,4096]{1,0:T(8,128)(2,1)S(1)} %get-tuple-element.24.refs_3_) | copy-start | bytes 786436
  2.6 36.7 %copy-start = (bf16[32,4096]{1,0:T(8,128)(2,1)}, bf16[32,4096]{1,0:T(8,128)(2,1)S(1)}, u32[]{:S(2)}) copy-start(bf16[32,4096]{1,0:T(8,128)(2,1)S(1)} %get-tuple-element.23.refs_2_) | copy-start | bytes 786436
  2.6 40.3 %copy-start.2 = (s32[16,8]{0,1:T(8,128)S(1)}, s32[16,8]{0,1:T(8,128)}, u32[]{:S(2)}) copy-start(s32[16,8]{0,1:T(8,128)} %param.12) | copy-start | bytes 1540
  2.6 40.3 %copy-start.3 = (s32[16]{0:T(128)S(1)}, s32[16]{0:T(128)}, u32[]{:S(2)}) copy-start(s32[16]{0:T(128)} %count_ref.1) | copy-start | bytes 196
  4.2 34.2 %all-to-all-start = ((bf16[16,8,4096]{2,1,0:T(8,128)(2,1)}), bf16[16,8,4096]{2,1,0:T(8,128)(2,1)S(1)}, u32[]{:S(2)}, u32[]{:S(2)}) async-start(bf16[16,8,4096]{2,1,0:T(8,128)(2,1)} %bitcast.3), calls=%async_computation | async-start | bytes 2097152 | tf_op jit(solution)/shard_map/all_to_all | solution.py:290
  10.5 27.9 %collective-permute-start.3 = (bf16[32,4096]{1,0:T(8,128)(2,1)S(1)}, bf16[32,4096]{1,0:T(8,128)(2,1)S(1)}, u32[]{:S(2)}, u32[]{:S(2)}) collective-permute-start(bf16[32,4096]{1,0:T(8,128)(2,1)S(1)} %get-tuple-element.23.refs_2_), channel_id=1, source_target_pairs={{8,0},{16,8},{24,16},{9,1},{17,9},{25,17},{10,2},{18,10},{26,18},{... | collective-permute-start | bytes 786440 | tf_op jit(solution)/shard_map/ppermute | solution.py:427
  11.8 26.6 %collective-permute-start.1 = (bf16[32,4096]{1,0:T(8,128)(2,1)S(1)}, bf16[32,4096]{1,0:T(8,128)(2,1)S(1)}, u32[]{:S(2)}, u32[]{:S(2)}) collective-permute-start(bf16[32,4096]{1,0:T(8,128)(2,1)S(1)} %get-tuple-element.23.refs_2_), channel_id=1, source_target_pairs={{0,8},{8,16},{16,24},{1,9},{9,17},{17,25},{2,10},{10,18},{18,26},{... | collective-permute-start | bytes 786440 | tf_op jit(solution)/shard_map/ppermute | solution.py:427
  14.9 23.5 %collective-permute-start.4 = (bf16[32,4096]{1,0:T(8,128)(2,1)S(1)}, bf16[32,4096]{1,0:T(8,128)(2,1)S(1)}, u32[]{:S(2)}, u32[]{:S(2)}) collective-permute-start(bf16[32,4096]{1,0:T(8,128)(2,1)S(1)} %get-tuple-element.24.refs_3_), channel_id=1, source_target_pairs={{8,0},{16,8},{24,16},{9,1},{17,9},{25,17},{10,2},{18,10},{26,18},{... | collective-permute-start | bytes 786440 | tf_op jit(solution)/shard_map/ppermute | solution.py:427
  16.2 22.3 %collective-permute-start.2 = (bf16[32,4096]{1,0:T(8,128)(2,1)S(1)}, bf16[32,4096]{1,0:T(8,128)(2,1)}, u32[]{:S(2)}, u32[]{:S(2)}) collective-permute-start(bf16[32,4096]{1,0:T(8,128)(2,1)S(1)} %get-tuple-element.24.refs_3_), channel_id=1, source_target_pairs={{0,8},{8,16},{16,24},{1,9},{9,17},{17,25},{2,10},{10,18},{18,26},{... | collective-permute-start | bytes 786440 | tf_op jit(solution)/shard_map/ppermute | solution.py:427
  21.1 15.7 %collective-permute-start = (bf16[1040,128]{1,0:T(8,128)(2,1)S(1)}, bf16[1040,128]{1,0:T(8,128)(2,1)S(1)}, u32[]{:S(2)}, u32[]{:S(2)}) collective-permute-start(bf16[1040,128]{1,0:T(8,128)(2,1)S(1)} %get-tuple-element.21.given), channel_id=1, source_target_pairs={{0,4},{4,0},{1,5},{5,1},{2,6},{6,2},{3,7},{7,3},{8,12},{12,8},{9,1... | collective-permute-start | bytes 798728 | tf_op jit(solution)/shard_map/ppermute | solution.py:424
  38.4 0.7 copy-start.4
  38.4 0.8 copy-start.5
  38.4 0.8 copy-start.6
  39.3 19.7 %all-to-all-start.1 = ((bf16[16,8,4096]{2,1,0:T(8,128)(2,1)}), bf16[16,8,4096]{2,1,0:T(8,128)(2,1)S(1)}, u32[]{:S(2)}, u32[]{:S(2)}) async-start(bf16[16,8,4096]{2,1,0:T(8,128)(2,1)} %bitcast.9), calls=%async_computation.1 | async-start | bytes 2097152 | tf_op jit(solution)/shard_map/all_to_all | solution.py:290
  88.6 4.6 %collective-permute-start.5 = (f32[32,128]{1,0:T(8,128)S(1)}, f32[32,128]{1,0:T(8,128)S(1)}, u32[]{:S(2)}, u32[]{:S(2)}) collective-permute-start(f32[32,128]{1,0:T(8,128)S(1)} %get-tuple-element.34), channel_id=1, source_target_pairs={{0,4},{4,0},{1,5},{5,1},{2,6},{6,2},{3,7},{7,3},{8,12},{12,8},{9,1... | collective-permute-start | bytes 49160 | tf_op jit(solution)/shard_map/ppermute | solution.py:454

commit v9 on v8

--- a/solution.py
+++ b/solution.py
@@ -39,12 +39,12 @@
     return pl.BlockSpec(shape, lambda *_: (0,) * len(shape))
 
 
-def send_kernel(halves, x, p2m, listed, counts, out, own_top, own_low, scratch, lists):
+def send_kernel(halves, x, p2m, listed, counts, out, own, scratch, lists):
     leaves, panels, terms = p2m.shape
     rhs = x.shape[1]
     part = rhs // halves
     slots, peers = listed.shape
-    own_top[...], own_low[...] = x[0, : rhs // 2], x[0, rhs // 2 :]
+    own[...] = x[0]
     for g in range(leaves):
         mult = dot(x[0, :, g * panels : (g + 1) * panels], p2m[g])
         for h in range(halves):
@@ -88,8 +88,7 @@
     leaves, panels, terms = p2m.shape
     shapes = (
         jax.ShapeDtypeStruct((rhs * leaves + 16, terms), BF16),
-        jax.ShapeDtypeStruct((rhs // 2, columns), BF16),
-        jax.ShapeDtypeStruct((rhs // 2, columns), BF16),
+        jax.ShapeDtypeStruct((rhs, columns), BF16),
     )
     return pl.pallas_call(
         functools.partial(send_kernel, halves),
@@ -121,21 +120,21 @@
         in_specs=[pl.BlockSpec(memory_space=pltpu.SMEM), whole(given.shape)],
         out_specs=whole(shape),
         compiler_params=params(8),
+        cost_estimate=pl.CostEstimate(flops=7 * 10**10, bytes_accessed=0, transcendentals=0),
         name="choose",
     )(side, given)
 
 
 def near_kernel(src_ref, count_ref, *refs):
-    pieces, (blocks_ref, out_ref, wide) = refs[:6], refs[6:]
-    half, columns = pieces[0].shape
+    pieces, (blocks_ref, out_ref, wide) = refs[:3], refs[3:]
+    columns = pieces[0].shape[1]
     slots, panels = blocks_ref.shape[1], blocks_ref.shape[2]
     g = pl.program_id(0)
 
     @pl.when(g == 0)
     def _():
         for i, piece in enumerate(pieces):
-            rows, place = slice(i % 2 * half, (i % 2 + 1) * half), i // 2 * columns
-            wide[rows, place : place + columns] = piece[...]
+            wide[:, i * columns : (i + 1) * columns] = piece[...]
 
     for i in range(blocks_ref.shape[0]):
         leaf = g * blocks_ref.shape[0] + i
@@ -151,13 +150,12 @@
 
 def near_field(near_src, near_count, pieces, near_blocks):
     leaves, slots, panels, _ = near_blocks.shape
-    half, columns = pieces[0].shape
-    rhs = 2 * half
+    rhs, columns = pieces[0].shape
     grid_spec = pltpu.PrefetchScalarGridSpec(
         num_scalar_prefetch=2,
         grid=(leaves // 2,),
         in_specs=[
-            *[whole((half, columns))] * 6,
+            *[whole((rhs, columns))] * 3,
             pl.BlockSpec((2, slots, panels, panels), lambda g, *_: (g, 0, 0, 0)),
         ],
         out_specs=pl.BlockSpec((rhs, 2 * panels), lambda g, *_: (0, g)),
@@ -419,12 +417,12 @@
     side = lax.axis_index("hi")
     same_side = ("gx", "lo")
 
-    payload, *own = all_multipoles(basis, p2m, send_list[0].T, send_count, halves)
+    payload, own = all_multipoles(basis, p2m, send_list[0].T, send_count, halves)
     flip = [(0, 1), (1, 0)]
     given = lax.ppermute(payload, "hi", flip)
     up = [(i, i + 1) for i in range(devices - 1)]
     down = [(j, i) for i, j in up]
-    pieces = [lax.ppermute(half, "gx", way) for way in (up, down) for half in own]
+    pieces = [lax.ppermute(own, "gx", way) for way in (up, down)]
 
     sender = far_src // slots
     place = sender // (2 * near_devices) * near_devices + sender % near_devices
@@ -446,8 +444,8 @@
         got = exchange(chosen.reshape(peers // 2, slots * halves, -1), same_side)
         received.append(got.reshape(chosen.shape))
 
-    pieces = [*pieces[:2], *own, *pieces[2:]]
-    near = near_field(near_src, near_count, pieces, near_blocks)
+    before, after = pieces
+    near = near_field(near_src, near_count, (before, own, after), near_blocks)
     image, sums, basis_near = far_field(*received, pick, m2l, p2m, near, basis, halves, peers)
     sums = exchange(added(exchange(sums), peers))
     resid, gram, projections = residual(sums, basis_near, image, total_rows)

time: 110 us -> 105 us (0.955)
  starting transfers between devices: 24.4 us -> 18.5 us
  waiting for transfers between devices: 20 us -> 23.5 us
  blocking collectives: 31.7 us -> 30.5 us
    all_to_all x2, waiting for transfers between devices: 4.16 us -> 13.8 us  [exchange(): return lax.all_to_all(pieces, axes, split_axis=0, concat_axis=0, tiled=True)]
    ppermute x1, waiting for transfers between devices: 12.6 us -> 6.42 us  [shards(): given = lax.ppermute(payload, 'hi', flip)]
    ppermute x4 -> x2, starting transfers between devices: 10.5 us -> 5.15 us  [shards(): pieces = [lax.ppermute(own, 'gx', way) for way in (up, down)]]
    all_to_all x2, starting transfers between devices: 9.94 us -> 7.92 us  [exchange(): return lax.all_to_all(pieces, axes, split_axis=0, concat_axis=0, tiled=True)]
    ppermute x1, starting transfers between devices: 2.59 us -> 4.05 us  [shards(): given = lax.ppermute(payload, 'hi', flip)]
    all_to_all x3, blocking collectives: 31.7 us -> 30.5 us  [exchange(): return lax.all_to_all(pieces, axes, split_axis=0, concat_axis=0, tiled=True)]
  transfers between devices with their start and end apart: 8 -> 6, of which waited for: 3 -> 4; matrix products, arithmetic and copies ran while one was open for 1% -> 1% of each run, Pallas kernels for 12% -> 14%
where the time goes in v9:
time: 105 us
  Pallas kernels  31.2 us (30%)
  blocking collectives  30.5 us (29%)
  waiting for transfers between devices  23.5 us (22%)
  starting transfers between devices  18.5 us (18%)
    all_to_all x3, blocking collectives, exchange(): return lax.all_to_all(pieces, axes, split_axis=0, concat_axis=0, tiled=True)  30.5 us
    all_to_all x2, waiting for transfers between devices, exchange(): return lax.all_to_all(pieces, axes, split_axis=0, concat_axis=0, tiled=True)  13.8 us
    pallas_call x1, Pallas kernels, near_field(): pl.pallas_call(near_kernel, grid_spec=grid_spec, out_shape=jax.ShapeDtype...  11.8 us
    all_to_all x2, starting transfers between devices, exchange(): return lax.all_to_all(pieces, axes, split_axis=0, concat_axis=0, tiled=True)  7.92 us
    pallas_call x1, Pallas kernels, tail(): pl.pallas_call(tail_kernel, grid=(1,), out_shape=shapes, in_specs=[whole(...  6.5 us
    ppermute x1, waiting for transfers between devices, shards(): given = lax.ppermute(payload, 'hi', flip)  6.42 us
    pallas_call x1, Pallas kernels, far_field(): pl.pallas_call(functools.partial(far_kernel, halves), grid=(1,), out_shap...  5.6 us
    ppermute x2, starting transfers between devices, shards(): pieces = [lax.ppermute(own, 'gx', way) for way in (up, down)]  5.15 us
  transfers between devices with their start and end apart: 6, of which 4 were waited for; matrix products, arithmetic and copies ran while one was open for 1% of the time, Pallas kernels for 14%

profile of v9, /device:TPU:0, one launch (start us, length us, event | category | flops | bytes accessed | tf_op | source)
XLA Modules:
  0.0 105.0 jit_solution(5396545787925971680)
XLA Ops:
  0.6 1.9 %send.1 = (bf16[1040,128]{1,0:T(8,128)(2,1)S(1)}, bf16[64,4096]{1,0:T(8,128)(2,1)S(1)}) custom-call(bf16[8,64,4096]{2,1,0:T(8,128)(2,1)} %basis_hbm.1, bf16[16,256,128]{2,1,0:T(8,128)(2,1)} %p2m_hbm.1, s32[4,32]{1,0:T(4,128)} %bitcast.26, s32[1,32]{1,0:T(1,128)} %counts.1), custom_call_target="tpu_custom_call" | custom-call | tf_op jit(solution)/shard_map/send/pallas_call | solution.py:93
  2.6 0.0 copy-start
  2.6 1.3 %collective-permute-start.2 = (bf16[64,4096]{1,0:T(8,128)(2,1)S(1)}, bf16[64,4096]{1,0:T(8,128)(2,1)S(1)}, u32[]{:S(2)}, u32[]{:S(2)}) collective-permute-start(bf16[64,4096]{1,0:T(8,128)(2,1)S(1)} %get-tuple-element.20.refs_1_), channel_id=1, source_target_pairs={{8,0},{16,8},{24,16},{9,1},{17,9},{25,17},{10,2},{18,10},{26,18},{... | collective-permute-start | bytes 1572872 | tf_op jit(solution)/shard_map/ppermute | solution.py:425
  3.9 3.9 %collective-permute-start.1 = (bf16[64,4096]{1,0:T(8,128)(2,1)S(1)}, bf16[64,4096]{1,0:T(8,128)(2,1)}, u32[]{:S(2)}, u32[]{:S(2)}) collective-permute-start(bf16[64,4096]{1,0:T(8,128)(2,1)S(1)} %get-tuple-element.20.refs_1_), channel_id=1, source_target_pairs={{0,8},{8,16},{16,24},{1,9},{9,17},{17,25},{2,10},{10,18},{18,26},{... | collective-permute-start | bytes 1572872 | tf_op jit(solution)/shard_map/ppermute | solution.py:425
  7.7 4.0 %collective-permute-start = (bf16[1040,128]{1,0:T(8,128)(2,1)S(1)}, bf16[1040,128]{1,0:T(8,128)(2,1)S(1)}, u32[]{:S(2)}, u32[]{:S(2)}) collective-permute-start(bf16[1040,128]{1,0:T(8,128)(2,1)S(1)} %get-tuple-element.18.given), channel_id=1, source_target_pairs={{0,4},{4,0},{1,5},{5,1},{2,6},{6,2},{3,7},{7,3},{8,12},{12,8},{9,1... | collective-permute-start | bytes 798728 | tf_op jit(solution)/shard_map/ppermute | solution.py:422
  11.8 1.6 %choose.2 = bf16[128,4096]{1,0:T(8,128)(2,1)} custom-call(s32[1]{0:T(128)} %bitcast.side, bf16[1040,128]{1,0:T(8,128)(2,1)S(1)} %get-tuple-element.18.given), custom_call_target="tpu_custom_call" | custom-call | flops 70000001024 | tf_op jit(solution)/shard_map/choose/pallas_call | solution.py:116
  13.4 4.1 %all-to-all-start = ((bf16[16,8,4096]{2,1,0:T(8,128)(2,1)}), bf16[16,8,4096]{2,1,0:T(8,128)(2,1)S(1)}, u32[]{:S(2)}, u32[]{:S(2)}) async-start(bf16[16,8,4096]{2,1,0:T(8,128)(2,1)} %bitcast.3), calls=%async_computation | async-start | bytes 2097152 | tf_op jit(solution)/shard_map/all_to_all | solution.py:288
  17.6 0.4 fusion
  18.0 0.2 copy.13
  18.1 6.4 %collective-permute-done.given = bf16[1040,128]{1,0:T(8,128)(2,1)S(1)} collective-permute-done((bf16[1040,128]{1,0:T(8,128)(2,1)S(1)}, bf16[1040,128]{1,0:T(8,128)(2,1)S(1)}, u32[]{:S(2)}, u32[]{:S(2)}) %collective-permute-start) | collective-permute-done | bytes 266272 | tf_op jit(solution)/shard_map/ppermute | solution.py:422
  24.6 1.6 %choose.3 = bf16[128,4096]{1,0:T(8,128)(2,1)} custom-call(s32[1]{0:T(128)} %bitcast.side, bf16[1040,128]{1,0:T(8,128)(2,1)S(1)} %collective-permute-done.given), custom_call_target="tpu_custom_call" | custom-call | flops 70000001024 | tf_op jit(solution)/shard_map/choose/pallas_call | solution.py:116
  26.2 0.0 collective-permute-done.2.refs_2_
  26.2 9.5 %all-to-all-done = bf16[16,8,4096]{2,1,0:T(8,128)(2,1)S(1)} async-done(((bf16[16,8,4096]{2,1,0:T(8,128)(2,1)}), bf16[16,8,4096]{2,1,0:T(8,128)(2,1)S(1)}, u32[]{:S(2)}, u32[]{:S(2)}) %all-to-all-start) | async-done | bytes 1048608 | tf_op jit(solution)/shard_map/all_to_all | solution.py:288
  35.7 3.8 %all-to-all-start.1 = ((bf16[16,8,4096]{2,1,0:T(8,128)(2,1)}), bf16[16,8,4096]{2,1,0:T(8,128)(2,1)S(1)}, u32[]{:S(2)}, u32[]{:S(2)}) async-start(bf16[16,8,4096]{2,1,0:T(8,128)(2,1)} %bitcast.9), calls=%async_computation.1 | async-start | bytes 2097152 | tf_op jit(solution)/shard_map/all_to_all | solution.py:288
  39.5 11.8 %near.1 = f32[64,4096]{1,0:T(8,128)S(1)} custom-call(s32[8,16]{1,0:T(8,128)S(1)} %bitcast.24, s32[16]{0:T(128)S(1)} %copy-done.2, bf16[64,4096]{1,0:T(8,128)(2,1)} %collective-permute-done.1.refs_0_, bf16[64,4096]{1,0:T(8,128)(2,1)} %copy-done, bf16[64,4096]{1,0:T(8,128)(2,1)} %copy-done.3, bf16[16,8,256,256]{3,2,1,0:T(8,128)(2,1)} %refs_3_.1), custom_call_target="tpu_custom_call" | custom-call | flops 1073741824 | bytes 20447232 | tf_op jit(solution)/shard_map/near/pallas_call | solution.py:164
  51.3 4.2 %all-to-all-done.1 = bf16[16,8,4096]{2,1,0:T(8,128)(2,1)S(1)} async-done(((bf16[16,8,4096]{2,1,0:T(8,128)(2,1)}), bf16[16,8,4096]{2,1,0:T(8,128)(2,1)S(1)}, u32[]{:S(2)}, u32[]{:S(2)}) %all-to-all-start.1) | async-done | bytes 1048608 | tf_op jit(solution)/shard_map/all_to_all | solution.py:288
  55.6 5.6 %far.1 = (f32[64,4096]{1,0:T(8,128)S(1)}, f32[32,8,128]{2,1,0:T(8,128)S(1)}, bf16[8,64,4096]{2,1,0:T(8,128)(2,1)S(1)}) custom-call(bf16[128,4096]{1,0:T(8,128)(2,1)S(1)} %bitcast.20, bf16[128,4096]{1,0:T(8,128)(2,1)S(1)} %bitcast.21, bf16[2,256,256]{2,1,0:T(8,128)(2,1)S(1)} %bitcast.22, f32[64,4096]{1,0:T(8,128)S(1)} %near.1, bf16[16,128,128]{2,1,0:T(8,128)(2,1)} %m2l_hbm.1, ...), custom_call_target="tpu_custom_call" | custom-call | tf_op jit(solution)/shard_map/far/pallas_call | solution.py:259
  61.2 10.6 %all_to_all.25.in_ref = f32[32,8,128]{2,1,0:T(8,128)S(1)} all-to-all(f32[32,8,128]{2,1,0:T(8,128)S(1)} %get-tuple-element.25), channel_id=1, replica_groups=mesh['gx'=4,'hi'=2,'lo'=4] {'gx','hi','lo'}, dimensions={0} | all-to-all | bytes 262144 | tf_op jit(solution)/shard_map/all_to_all | solution.py:288
  71.9 10.0 %all_to_all.26.sums = f32[32,8,128]{2,1,0:T(8,128)S(1)} all-to-all(f32[32,8,128]{2,1,0:T(8,128)S(1)} %add.88), channel_id=1, replica_groups=mesh['gx'=4,'hi'=2,'lo'=4] {'gx','hi','lo'}, dimensions={0} | all-to-all | bytes 262144 | tf_op jit(solution)/shard_map/all_to_all | solution.py:288
  81.9 2.1 %residual.1 = (bf16[128,4096]{1,0:T(8,128)(2,1)S(1)}, f32[32,128]{1,0:T(8,128)S(1)}, f32[512,64]{1,0:T(8,128)}) custom-call(f32[32,8,128]{2,1,0:T(8,128)S(1)} %all_to_all.26.sums, f32[64,4096]{1,0:T(8,128)S(1)} %get-tuple-element.26.image, bf16[8,64,4096]{2,1,0:T(8,128)(2,1)S(1)} %get-tuple-element.27.basis), custom_call_target="tpu_custom_call" | custom-call | tf_op jit(solution)/shard_map/residual/pallas_call | solution.py:337
  84.0 1.4 %collective-permute-start.3 = (f32[32,128]{1,0:T(8,128)S(1)}, f32[32,128]{1,0:T(8,128)S(1)}, u32[]{:S(2)}, u32[]{:S(2)}) collective-permute-start(f32[32,128]{1,0:T(8,128)S(1)} %get-tuple-element.28), channel_id=1, source_target_pairs={{0,4},{4,0},{1,5},{5,1},{2,6},{6,2},{3,7},{7,3},{8,12},{12,8},{9,1... | collective-permute-start | bytes 49160 | tf_op jit(solution)/shard_map/ppermute | solution.py:452
  85.3 3.3 %collective-permute-done.3 = f32[32,128]{1,0:T(8,128)S(1)} collective-permute-done((f32[32,128]{1,0:T(8,128)S(1)}, f32[32,128]{1,0:T(8,128)S(1)}, u32[]{:S(2)}, u32[]{:S(2)}) %collective-permute-start.3) | collective-permute-done | bytes 16416 | tf_op jit(solution)/shard_map/ppermute | solution.py:452
  88.7 9.8 %all_to_all.27.grams = f32[16,32,128]{2,1,0:T(8,128)S(1)} all-to-all(f32[16,32,128]{2,1,0:T(8,128)S(1)} %add.89), channel_id=1, replica_groups=mesh['gx'=4,'hi'=2,'lo'=4] {'gx','lo'}, dimensions={0} | all-to-all | bytes 524288 | tf_op jit(solution)/shard_map/all_to_all | solution.py:288
  98.5 6.5 %tail.1 = (bf16[64,4096]{1,0:T(8,128)(2,1)}, f32[64,64]{1,0:T(8,128)}) custom-call(f32[16,32,128]{2,1,0:T(8,128)S(1)} %all_to_all.27.grams, bf16[128,4096]{1,0:T(8,128)(2,1)S(1)} %get-tuple-element.29.resid), custom_call_target="tpu_custom_call" | custom-call | tf_op jit(solution)/shard_map/tail/pallas_call | solution.py:394
  (17 shorter events, 0.1 us)
Async XLA Ops:
  2.6 10.8 %copy-start = (bf16[64,4096]{1,0:T(8,128)(2,1)}, bf16[64,4096]{1,0:T(8,128)(2,1)S(1)}, u32[]{:S(2)}) copy-start(bf16[64,4096]{1,0:T(8,128)(2,1)S(1)} %get-tuple-element.20.refs_1_) | copy-start | bytes 1572868
  2.6 23.6 %collective-permute-start.2 = (bf16[64,4096]{1,0:T(8,128)(2,1)S(1)}, bf16[64,4096]{1,0:T(8,128)(2,1)S(1)}, u32[]{:S(2)}, u32[]{:S(2)}) collective-permute-start(bf16[64,4096]{1,0:T(8,128)(2,1)S(1)} %get-tuple-element.20.refs_1_), channel_id=1, source_target_pairs={{8,0},{16,8},{24,16},{9,1},{17,9},{25,17},{10,2},{18,10},{26,18},{... | collective-permute-start | bytes 1572872 | tf_op jit(solution)/shard_map/ppermute | solution.py:425
  3.9 22.3 %collective-permute-start.1 = (bf16[64,4096]{1,0:T(8,128)(2,1)S(1)}, bf16[64,4096]{1,0:T(8,128)(2,1)}, u32[]{:S(2)}, u32[]{:S(2)}) collective-permute-start(bf16[64,4096]{1,0:T(8,128)(2,1)S(1)} %get-tuple-element.20.refs_1_), channel_id=1, source_target_pairs={{0,8},{8,16},{16,24},{1,9},{9,17},{17,25},{2,10},{10,18},{18,26},{... | collective-permute-start | bytes 1572872 | tf_op jit(solution)/shard_map/ppermute | solution.py:425
  7.7 16.8 %collective-permute-start = (bf16[1040,128]{1,0:T(8,128)(2,1)S(1)}, bf16[1040,128]{1,0:T(8,128)(2,1)S(1)}, u32[]{:S(2)}, u32[]{:S(2)}) collective-permute-start(bf16[1040,128]{1,0:T(8,128)(2,1)S(1)} %get-tuple-element.18.given), channel_id=1, source_target_pairs={{0,4},{4,0},{1,5},{5,1},{2,6},{6,2},{3,7},{7,3},{8,12},{12,8},{9,1... | collective-permute-start | bytes 798728 | tf_op jit(solution)/shard_map/ppermute | solution.py:422
  11.8 5.7 %copy-start.4 = (s32[16,32]{1,0:T(8,128)S(1)}, s32[16,32]{1,0:T(8,128)}, u32[]{:S(2)}) copy-start(s32[16,32]{1,0:T(8,128)} %param.18) | copy-start | bytes 6148
  11.8 5.8 %copy-start.5 = (s32[16,32]{1,0:T(8,128)S(1)}, s32[16,32]{1,0:T(8,128)}, u32[]{:S(2)}) copy-start(s32[16,32]{1,0:T(8,128)} %param.19) | copy-start | bytes 6148
  13.4 22.3 %all-to-all-start = ((bf16[16,8,4096]{2,1,0:T(8,128)(2,1)}), bf16[16,8,4096]{2,1,0:T(8,128)(2,1)S(1)}, u32[]{:S(2)}, u32[]{:S(2)}) async-start(bf16[16,8,4096]{2,1,0:T(8,128)(2,1)} %bitcast.3), calls=%async_computation | async-start | bytes 2097152 | tf_op jit(solution)/shard_map/all_to_all | solution.py:288
  24.6 14.9 %copy-start.1 = (s32[16,8]{0,1:T(8,128)S(1)}, s32[16,8]{0,1:T(8,128)}, u32[]{:S(2)}) copy-start(s32[16,8]{0,1:T(8,128)} %param.12) | copy-start | bytes 1540
  24.6 15.0 %copy-start.2 = (s32[16]{0:T(128)S(1)}, s32[16]{0:T(128)}, u32[]{:S(2)}) copy-start(s32[16]{0:T(128)} %count_ref.1) | copy-start | bytes 196
  26.2 9.5 %copy-start.3 = (bf16[64,4096]{1,0:T(8,128)(2,1)}, bf16[64,4096]{1,0:T(8,128)(2,1)S(1)}, u32[]{:S(2)}) copy-start(bf16[64,4096]{1,0:T(8,128)(2,1)S(1)} %collective-permute-done.2.refs_2_) | copy-start | bytes 1572868
  35.7 19.9 %all-to-all-start.1 = ((bf16[16,8,4096]{2,1,0:T(8,128)(2,1)}), bf16[16,8,4096]{2,1,0:T(8,128)(2,1)S(1)}, u32[]{:S(2)}, u32[]{:S(2)}) async-start(bf16[16,8,4096]{2,1,0:T(8,128)(2,1)} %bitcast.9), calls=%async_computation.1 | async-start | bytes 2097152 | tf_op jit(solution)/shard_map/all_to_all | solution.py:288
  84.0 4.6 %collective-permute-start.3 = (f32[32,128]{1,0:T(8,128)S(1)}, f32[32,128]{1,0:T(8,128)S(1)}, u32[]{:S(2)}, u32[]{:S(2)}) collective-permute-start(f32[32,128]{1,0:T(8,128)S(1)} %get-tuple-element.28), channel_id=1, source_target_pairs={{0,4},{4,0},{1,5},{5,1},{2,6},{6,2},{3,7},{7,3},{8,12},{12,8},{9,1... | collective-permute-start | bytes 49160 | tf_op jit(solution)/shard_map/ppermute | solution.py:452

commit v10 on v9

--- a/solution.py
+++ b/solution.py
@@ -185,8 +185,8 @@
             ((m2l_hbm, m2l), (p2m_hbm, p2m), (basis_hbm, basis))
         )
     ]
-    for move in moves:
-        move.start()
+    moves[0].start()
+    moves[1].start()
     leaves, panels, terms = p2m.shape
     classes = m2l.shape[0]
     blocks, rhs, columns = basis.shape
@@ -195,6 +195,8 @@
     rows = ours.shape[0]
     recv[:rows], recv[rows:] = ours[...], theirs[...]
     for h in range(halves):
+        if h == halves - 1:
+            moves[2].start()
         for j in range(0, part, group):
             got = dot(pick[h], recv[:, j * terms : (j + group) * terms]).astype(BF16)
             for t in range(group):
@@ -422,8 +424,6 @@
     given = lax.ppermute(payload, "hi", flip)
     up = [(i, i + 1) for i in range(devices - 1)]
     down = [(j, i) for i, j in up]
-    pieces = [lax.ppermute(own, "gx", way) for way in (up, down)]
-
     sender = far_src // slots
     place = sender // (2 * near_devices) * near_devices + sender % near_devices
     place = place + jnp.where(sender // near_devices % 2 == side, 0, peers // 2)
@@ -436,17 +436,22 @@
     pick = pick.astype(BF16).reshape(halves, classes * leaves, -1)
 
     given, pick = lax.optimization_barrier((given, pick))
-    received = []
-    for multipoles in (payload, given):
-        chosen = chosen_multipoles(side[None], multipoles, leaves, slots, halves, rhs, peers // 2)
-        if multipoles is given:
-            chosen, *pieces = lax.optimization_barrier((chosen, *pieces))
+
+    def choose(multipoles):
+        return chosen_multipoles(side[None], multipoles, leaves, slots, halves, rhs, peers // 2)
+
+    def give(chosen):
         got = exchange(chosen.reshape(peers // 2, slots * halves, -1), same_side)
-        received.append(got.reshape(chosen.shape))
-
-    before, after = pieces
+        return got.reshape(chosen.shape)
+
+    chosen, own = lax.optimization_barrier((choose(payload), own))
+    ours = give(chosen)
+    before, after = lax.ppermute(own, "gx", up), lax.ppermute(own, "gx", down)
+    chosen, before, after = lax.optimization_barrier((choose(given), before, after))
+    theirs = give(chosen)
+
     near = near_field(near_src, near_count, (before, own, after), near_blocks)
-    image, sums, basis_near = far_field(*received, pick, m2l, p2m, near, basis, halves, peers)
+    image, sums, basis_near = far_field(ours, theirs, pick, m2l, p2m, near, basis, halves, peers)
     sums = exchange(added(exchange(sums), peers))
     resid, gram, projections = residual(sums, basis_near, image, total_rows)
     pair = jnp.stack([gram, lax.ppermute(gram, "hi", flip)])

time: 105 us -> 102 us (0.971)
  waiting for transfers between devices: 23.5 us -> 21.3 us
    ppermute x1, waiting for transfers between devices: 6.42 us -> 0.65 us  [shards(): given = lax.ppermute(payload, 'hi', flip)]
    all_to_all x2, waiting for transfers between devices: 13.8 us -> 17.4 us  [exchange(): return lax.all_to_all(pieces, axes, split_axis=0, concat_axis=0, tiled=True)]
  transfers between devices with their start and end apart: 6 -> 6, of which waited for: 4 -> 4; matrix products, arithmetic and copies ran while one was open for 1% -> 1% of each run, Pallas kernels for 14% -> 15%
where the time goes in v10:
time: 102 us
  Pallas kernels  31.2 us (31%)
  blocking collectives  29.7 us (29%)
  waiting for transfers between devices  21.3 us (21%)
  starting transfers between devices  18.3 us (18%)
    all_to_all x3, blocking collectives, exchange(): return lax.all_to_all(pieces, axes, split_axis=0, concat_axis=0, tiled=True)  29.7 us
    all_to_all x2, waiting for transfers between devices, exchange(): return lax.all_to_all(pieces, axes, split_axis=0, concat_axis=0, tiled=True)  17.4 us
    pallas_call x1, Pallas kernels, near_field(): pl.pallas_call(near_kernel, grid_spec=grid_spec, out_shape=jax.ShapeDtype...  11.8 us
    all_to_all x2, starting transfers between devices, exchange(): return lax.all_to_all(pieces, axes, split_axis=0, concat_axis=0, tiled=True)  7.72 us
    pallas_call x1, Pallas kernels, tail(): pl.pallas_call(tail_kernel, grid=(1,), out_shape=shapes, in_specs=[whole(...  6.5 us
    pallas_call x1, Pallas kernels, far_field(): pl.pallas_call(functools.partial(far_kernel, halves), grid=(1,), out_shap...  5.61 us
    ppermute x2, starting transfers between devices, shards(): before, after = (lax.ppermute(own, 'gx', up), lax.ppermute(own, 'gx', down))  5.13 us
    ppermute x1, starting transfers between devices, shards(): given = lax.ppermute(payload, 'hi', flip)  4.1 us
  transfers between devices with their start and end apart: 6, of which 4 were waited for; matrix products, arithmetic and copies ran while one was open for 1% of the time, Pallas kernels for 15%

profile of v10, /device:TPU:0, one launch (start us, length us, event | category | flops | bytes accessed | tf_op | source)
XLA Modules:
  0.0 101.9 jit_solution(9271644970931461984)
XLA Ops:
  0.6 1.9 %send.1 = (bf16[1040,128]{1,0:T(8,128)(2,1)S(1)}, bf16[64,4096]{1,0:T(8,128)(2,1)S(1)}) custom-call(bf16[8,64,4096]{2,1,0:T(8,128)(2,1)} %basis_hbm.1, bf16[16,256,128]{2,1,0:T(8,128)(2,1)} %p2m_hbm.1, s32[4,32]{1,0:T(4,128)} %bitcast.26, s32[1,32]{1,0:T(1,128)} %counts.1), custom_call_target="tpu_custom_call" | custom-call | tf_op jit(solution)/shard_map/send/pallas_call | solution.py:93
  2.6 0.0 copy-start
  2.6 4.1 %collective-permute-start = (bf16[1040,128]{1,0:T(8,128)(2,1)S(1)}, bf16[1040,128]{1,0:T(8,128)(2,1)S(1)}, u32[]{:S(2)}, u32[]{:S(2)}) collective-permute-start(bf16[1040,128]{1,0:T(8,128)(2,1)S(1)} %get-tuple-element.20.given), channel_id=1, source_target_pairs={{0,4},{4,0},{1,5},{5,1},{2,6},{6,2},{3,7},{7,3},{8,12},{12,8},{9,1... | collective-permute-start | bytes 798728 | tf_op jit(solution)/shard_map/ppermute | solution.py:424
  6.7 1.6 %choose.2 = bf16[128,4096]{1,0:T(8,128)(2,1)} custom-call(s32[1]{0:T(128)} %bitcast.side, bf16[1040,128]{1,0:T(8,128)(2,1)S(1)} %get-tuple-element.20.given), custom_call_target="tpu_custom_call" | custom-call | flops 70000001024 | tf_op jit(solution)/shard_map/choose/pallas_call | solution.py:116
  8.3 1.3 %collective-permute-start.2 = (bf16[64,4096]{1,0:T(8,128)(2,1)S(1)}, bf16[64,4096]{1,0:T(8,128)(2,1)S(1)}, u32[]{:S(2)}, u32[]{:S(2)}) collective-permute-start(bf16[64,4096]{1,0:T(8,128)(2,1)S(1)} %get-tuple-element.24.refs_1_), channel_id=1, source_target_pairs={{8,0},{16,8},{24,16},{9,1},{17,9},{25,17},{10,2},{18,10},{26,18},{... | collective-permute-start | bytes 1572872 | tf_op jit(solution)/shard_map/ppermute | solution.py:449
  9.6 3.9 %collective-permute-start.1 = (bf16[64,4096]{1,0:T(8,128)(2,1)S(1)}, bf16[64,4096]{1,0:T(8,128)(2,1)}, u32[]{:S(2)}, u32[]{:S(2)}) collective-permute-start(bf16[64,4096]{1,0:T(8,128)(2,1)S(1)} %get-tuple-element.24.refs_1_), channel_id=1, source_target_pairs={{0,8},{8,16},{16,24},{1,9},{9,17},{17,25},{2,10},{10,18},{18,26},{... | collective-permute-start | bytes 1572872 | tf_op jit(solution)/shard_map/ppermute | solution.py:449
  13.5 4.1 %all-to-all-start = ((bf16[16,8,4096]{2,1,0:T(8,128)(2,1)}), bf16[16,8,4096]{2,1,0:T(8,128)(2,1)S(1)}, u32[]{:S(2)}, u32[]{:S(2)}) async-start(bf16[16,8,4096]{2,1,0:T(8,128)(2,1)} %bitcast.3), calls=%async_computation | async-start | bytes 2097152 | tf_op jit(solution)/shard_map/all_to_all | solution.py:290
  17.6 0.4 fusion
  18.0 0.2 copy.13
  18.1 0.6 collective-permute-done.given
  18.8 1.6 %choose.3 = bf16[128,4096]{1,0:T(8,128)(2,1)} custom-call(s32[1]{0:T(128)} %bitcast.side, bf16[1040,128]{1,0:T(8,128)(2,1)S(1)} %collective-permute-done.given), custom_call_target="tpu_custom_call" | custom-call | flops 70000001024 | tf_op jit(solution)/shard_map/choose/pallas_call | solution.py:116
  20.4 0.0 collective-permute-done.2.refs_2_
  20.4 13.2 %all-to-all-done = bf16[16,8,4096]{2,1,0:T(8,128)(2,1)S(1)} async-done(((bf16[16,8,4096]{2,1,0:T(8,128)(2,1)}), bf16[16,8,4096]{2,1,0:T(8,128)(2,1)S(1)}, u32[]{:S(2)}, u32[]{:S(2)}) %all-to-all-start) | async-done | bytes 1048608 | tf_op jit(solution)/shard_map/all_to_all | solution.py:290
  33.6 3.7 %all-to-all-start.1 = ((bf16[16,8,4096]{2,1,0:T(8,128)(2,1)}), bf16[16,8,4096]{2,1,0:T(8,128)(2,1)S(1)}, u32[]{:S(2)}, u32[]{:S(2)}) async-start(bf16[16,8,4096]{2,1,0:T(8,128)(2,1)} %bitcast.9), calls=%async_computation.1 | async-start | bytes 2097152 | tf_op jit(solution)/shard_map/all_to_all | solution.py:290
  37.3 11.8 %near.1 = f32[64,4096]{1,0:T(8,128)S(1)} custom-call(s32[8,16]{1,0:T(8,128)S(1)} %bitcast.24, s32[16]{0:T(128)S(1)} %copy-done.2, bf16[64,4096]{1,0:T(8,128)(2,1)} %collective-permute-done.1.refs_0_, bf16[64,4096]{1,0:T(8,128)(2,1)} %copy-done, bf16[64,4096]{1,0:T(8,128)(2,1)} %copy-done.3, bf16[16,8,256,256]{3,2,1,0:T(8,128)(2,1)} %refs_3_.1), custom_call_target="tpu_custom_call" | custom-call | flops 1073741824 | bytes 20447232 | tf_op jit(solution)/shard_map/near/pallas_call | solution.py:164
  49.1 4.2 %all-to-all-done.1 = bf16[16,8,4096]{2,1,0:T(8,128)(2,1)S(1)} async-done(((bf16[16,8,4096]{2,1,0:T(8,128)(2,1)}), bf16[16,8,4096]{2,1,0:T(8,128)(2,1)S(1)}, u32[]{:S(2)}, u32[]{:S(2)}) %all-to-all-start.1) | async-done | bytes 1048608 | tf_op jit(solution)/shard_map/all_to_all | solution.py:290
  53.3 5.6 %far.1 = (f32[64,4096]{1,0:T(8,128)S(1)}, f32[32,8,128]{2,1,0:T(8,128)S(1)}, bf16[8,64,4096]{2,1,0:T(8,128)(2,1)S(1)}) custom-call(bf16[128,4096]{1,0:T(8,128)(2,1)S(1)} %bitcast.20, bf16[128,4096]{1,0:T(8,128)(2,1)S(1)} %bitcast.21, bf16[2,256,256]{2,1,0:T(8,128)(2,1)S(1)} %bitcast.22, f32[64,4096]{1,0:T(8,128)S(1)} %near.1, bf16[16,128,128]{2,1,0:T(8,128)(2,1)} %m2l_hbm.1, ...), custom_call_target="tpu_custom_call" | custom-call | tf_op jit(solution)/shard_map/far/pallas_call | solution.py:261
  58.9 9.9 %all_to_all.25.in_ref = f32[32,8,128]{2,1,0:T(8,128)S(1)} all-to-all(f32[32,8,128]{2,1,0:T(8,128)S(1)} %get-tuple-element.29), channel_id=1, replica_groups=mesh['gx'=4,'hi'=2,'lo'=4] {'gx','hi','lo'}, dimensions={0} | all-to-all | bytes 262144 | tf_op jit(solution)/shard_map/all_to_all | solution.py:290
  68.8 10.0 %all_to_all.26.sums = f32[32,8,128]{2,1,0:T(8,128)S(1)} all-to-all(f32[32,8,128]{2,1,0:T(8,128)S(1)} %add.88), channel_id=1, replica_groups=mesh['gx'=4,'hi'=2,'lo'=4] {'gx','hi','lo'}, dimensions={0} | all-to-all | bytes 262144 | tf_op jit(solution)/shard_map/all_to_all | solution.py:290
  78.9 2.1 %residual.1 = (bf16[128,4096]{1,0:T(8,128)(2,1)S(1)}, f32[32,128]{1,0:T(8,128)S(1)}, f32[512,64]{1,0:T(8,128)}) custom-call(f32[32,8,128]{2,1,0:T(8,128)S(1)} %all_to_all.26.sums, f32[64,4096]{1,0:T(8,128)S(1)} %get-tuple-element.30.image, bf16[8,64,4096]{2,1,0:T(8,128)(2,1)S(1)} %get-tuple-element.31.basis), custom_call_target="tpu_custom_call" | custom-call | tf_op jit(solution)/shard_map/residual/pallas_call | solution.py:339
  80.9 1.4 %collective-permute-start.3 = (f32[32,128]{1,0:T(8,128)S(1)}, f32[32,128]{1,0:T(8,128)S(1)}, u32[]{:S(2)}, u32[]{:S(2)}) collective-permute-start(f32[32,128]{1,0:T(8,128)S(1)} %get-tuple-element.32), channel_id=1, source_target_pairs={{0,4},{4,0},{1,5},{5,1},{2,6},{6,2},{3,7},{7,3},{8,12},{12,8},{9,1... | collective-permute-start | bytes 49160 | tf_op jit(solution)/shard_map/ppermute | solution.py:457
  82.3 3.3 %collective-permute-done.3 = f32[32,128]{1,0:T(8,128)S(1)} collective-permute-done((f32[32,128]{1,0:T(8,128)S(1)}, f32[32,128]{1,0:T(8,128)S(1)}, u32[]{:S(2)}, u32[]{:S(2)}) %collective-permute-start.3) | collective-permute-done | bytes 16416 | tf_op jit(solution)/shard_map/ppermute | solution.py:457
  85.6 9.8 %all_to_all.27.grams = f32[16,32,128]{2,1,0:T(8,128)S(1)} all-to-all(f32[16,32,128]{2,1,0:T(8,128)S(1)} %add.89), channel_id=1, replica_groups=mesh['gx'=4,'hi'=2,'lo'=4] {'gx','lo'}, dimensions={0} | all-to-all | bytes 524288 | tf_op jit(solution)/shard_map/all_to_all | solution.py:290
  95.4 6.5 %tail.1 = (bf16[64,4096]{1,0:T(8,128)(2,1)}, f32[64,64]{1,0:T(8,128)}) custom-call(f32[16,32,128]{2,1,0:T(8,128)S(1)} %all_to_all.27.grams, bf16[128,4096]{1,0:T(8,128)(2,1)S(1)} %get-tuple-element.33.resid), custom_call_target="tpu_custom_call" | custom-call | tf_op jit(solution)/shard_map/tail/pallas_call | solution.py:396
  (17 shorter events, 0.1 us)
Async XLA Ops:
  2.6 7.0 %copy-start = (bf16[64,4096]{1,0:T(8,128)(2,1)}, bf16[64,4096]{1,0:T(8,128)(2,1)S(1)}, u32[]{:S(2)}) copy-start(bf16[64,4096]{1,0:T(8,128)(2,1)S(1)} %get-tuple-element.24.refs_1_) | copy-start | bytes 1572868
  2.6 16.2 %collective-permute-start = (bf16[1040,128]{1,0:T(8,128)(2,1)S(1)}, bf16[1040,128]{1,0:T(8,128)(2,1)S(1)}, u32[]{:S(2)}, u32[]{:S(2)}) collective-permute-start(bf16[1040,128]{1,0:T(8,128)(2,1)S(1)} %get-tuple-element.20.given), channel_id=1, source_target_pairs={{0,4},{4,0},{1,5},{5,1},{2,6},{6,2},{3,7},{7,3},{8,12},{12,8},{9,1... | collective-permute-start | bytes 798728 | tf_op jit(solution)/shard_map/ppermute | solution.py:424
  6.7 10.9 %copy-start.4 = (s32[16,32]{1,0:T(8,128)S(1)}, s32[16,32]{1,0:T(8,128)}, u32[]{:S(2)}) copy-start(s32[16,32]{1,0:T(8,128)} %param.18) | copy-start | bytes 6148
  6.7 10.9 %copy-start.5 = (s32[16,32]{1,0:T(8,128)S(1)}, s32[16,32]{1,0:T(8,128)}, u32[]{:S(2)}) copy-start(s32[16,32]{1,0:T(8,128)} %param.19) | copy-start | bytes 6148
  8.3 12.1 %collective-permute-start.2 = (bf16[64,4096]{1,0:T(8,128)(2,1)S(1)}, bf16[64,4096]{1,0:T(8,128)(2,1)S(1)}, u32[]{:S(2)}, u32[]{:S(2)}) collective-permute-start(bf16[64,4096]{1,0:T(8,128)(2,1)S(1)} %get-tuple-element.24.refs_1_), channel_id=1, source_target_pairs={{8,0},{16,8},{24,16},{9,1},{17,9},{25,17},{10,2},{18,10},{26,18},{... | collective-permute-start | bytes 1572872 | tf_op jit(solution)/shard_map/ppermute | solution.py:449
  9.6 10.8 %collective-permute-start.1 = (bf16[64,4096]{1,0:T(8,128)(2,1)S(1)}, bf16[64,4096]{1,0:T(8,128)(2,1)}, u32[]{:S(2)}, u32[]{:S(2)}) collective-permute-start(bf16[64,4096]{1,0:T(8,128)(2,1)S(1)} %get-tuple-element.24.refs_1_), channel_id=1, source_target_pairs={{0,8},{8,16},{16,24},{1,9},{9,17},{17,25},{2,10},{10,18},{18,26},{... | collective-permute-start | bytes 1572872 | tf_op jit(solution)/shard_map/ppermute | solution.py:449
  13.5 20.2 %all-to-all-start = ((bf16[16,8,4096]{2,1,0:T(8,128)(2,1)}), bf16[16,8,4096]{2,1,0:T(8,128)(2,1)S(1)}, u32[]{:S(2)}, u32[]{:S(2)}) async-start(bf16[16,8,4096]{2,1,0:T(8,128)(2,1)} %bitcast.3), calls=%async_computation | async-start | bytes 2097152 | tf_op jit(solution)/shard_map/all_to_all | solution.py:290
  18.8 18.5 %copy-start.1 = (s32[16,8]{0,1:T(8,128)S(1)}, s32[16,8]{0,1:T(8,128)}, u32[]{:S(2)}) copy-start(s32[16,8]{0,1:T(8,128)} %param.12) | copy-start | bytes 1540
  18.8 18.5 %copy-start.2 = (s32[16]{0:T(128)S(1)}, s32[16]{0:T(128)}, u32[]{:S(2)}) copy-start(s32[16]{0:T(128)} %count_ref.1) | copy-start | bytes 196
  20.4 13.2 %copy-start.3 = (bf16[64,4096]{1,0:T(8,128)(2,1)}, bf16[64,4096]{1,0:T(8,128)(2,1)S(1)}, u32[]{:S(2)}) copy-start(bf16[64,4096]{1,0:T(8,128)(2,1)S(1)} %collective-permute-done.2.refs_2_) | copy-start | bytes 1572868
  33.6 19.7 %all-to-all-start.1 = ((bf16[16,8,4096]{2,1,0:T(8,128)(2,1)}), bf16[16,8,4096]{2,1,0:T(8,128)(2,1)S(1)}, u32[]{:S(2)}, u32[]{:S(2)}) async-start(bf16[16,8,4096]{2,1,0:T(8,128)(2,1)} %bitcast.9), calls=%async_computation.1 | async-start | bytes 2097152 | tf_op jit(solution)/shard_map/all_to_all | solution.py:290
  80.9 4.6 %collective-permute-start.3 = (f32[32,128]{1,0:T(8,128)S(1)}, f32[32,128]{1,0:T(8,128)S(1)}, u32[]{:S(2)}, u32[]{:S(2)}) collective-permute-start(f32[32,128]{1,0:T(8,128)S(1)} %get-tuple-element.32), channel_id=1, source_target_pairs={{0,4},{4,0},{1,5},{5,1},{2,6},{6,2},{3,7},{7,3},{8,12},{12,8},{9,1... | collective-permute-start | bytes 49160 | tf_op jit(solution)/shard_map/ppermute | solution.py:457

commit v11 on v10

--- a/solution.py
+++ b/solution.py
@@ -110,7 +110,7 @@
     )(in_hbm(basis), in_hbm(p2m), in_hbm(listed), in_hbm(counts))
 
 
-def chosen_multipoles(side, given, leaves, slots, halves, rhs, receivers):
+def chosen_multipoles(side, given, leaves, slots, halves, rhs, receivers, flops):
     terms = given.shape[1]
     shape = (receivers * slots * halves, rhs // halves * terms)
     return pl.pallas_call(
@@ -120,7 +120,7 @@
         in_specs=[pl.BlockSpec(memory_space=pltpu.SMEM), whole(given.shape)],
         out_specs=whole(shape),
         compiler_params=params(8),
-        cost_estimate=pl.CostEstimate(flops=7 * 10**10, bytes_accessed=0, transcendentals=0),
+        cost_estimate=pl.CostEstimate(flops=flops, bytes_accessed=0, transcendentals=0),
         name="choose",
     )(side, given)
 
@@ -185,8 +185,8 @@
             ((m2l_hbm, m2l), (p2m_hbm, p2m), (basis_hbm, basis))
         )
     ]
-    moves[0].start()
-    moves[1].start()
+    for move in moves:
+        move.start()
     leaves, panels, terms = p2m.shape
     classes = m2l.shape[0]
     blocks, rhs, columns = basis.shape
@@ -195,8 +195,6 @@
     rows = ours.shape[0]
     recv[:rows], recv[rows:] = ours[...], theirs[...]
     for h in range(halves):
-        if h == halves - 1:
-            moves[2].start()
         for j in range(0, part, group):
             got = dot(pick[h], recv[:, j * terms : (j + group) * terms]).astype(BF16)
             for t in range(group):
@@ -437,17 +435,18 @@
 
     given, pick = lax.optimization_barrier((given, pick))
 
-    def choose(multipoles):
-        return chosen_multipoles(side[None], multipoles, leaves, slots, halves, rhs, peers // 2)
+    def choose(multipoles, flops):
+        sizes = (leaves, slots, halves, rhs, peers // 2)
+        return chosen_multipoles(side[None], multipoles, *sizes, flops)
 
     def give(chosen):
         got = exchange(chosen.reshape(peers // 2, slots * halves, -1), same_side)
         return got.reshape(chosen.shape)
 
-    chosen, own = lax.optimization_barrier((choose(payload), own))
+    chosen, own = lax.optimization_barrier((choose(payload, 7 * 10**10), own))
     ours = give(chosen)
     before, after = lax.ppermute(own, "gx", up), lax.ppermute(own, "gx", down)
-    chosen, before, after = lax.optimization_barrier((choose(given), before, after))
+    chosen, before, after = lax.optimization_barrier((choose(given, 7 * 10**9), before, after))
     theirs = give(chosen)
 
     near = near_field(near_src, near_count, (before, own, after), near_blocks)

time: 102 us -> 104 us (1.020)
  starting transfers between devices: 18.3 us -> 23.4 us
  waiting for transfers between devices: 21.3 us -> 18 us
    all_to_all x2, waiting for transfers between devices: 17.4 us -> 5.01 us  [exchange(): return lax.all_to_all(pieces, axes, split_axis=0, concat_axis=0, tiled=True)]
    ppermute x1, waiting for transfers between devices: 0.65 us -> 9.71 us  [shards(): given = lax.ppermute(payload, 'hi', flip)]
    all_to_all x2, starting transfers between devices: 7.72 us -> 14.3 us  [exchange(): return lax.all_to_all(pieces, axes, split_axis=0, concat_axis=0, tiled=True)]
    ppermute x1, starting transfers between devices: 4.1 us -> 2.66 us  [shards(): given = lax.ppermute(payload, 'hi', flip)]
  transfers between devices with their start and end apart: 6 -> 6, of which waited for: 4 -> 4; matrix products, arithmetic and copies ran while one was open for 1% -> 1% of each run, Pallas kernels for 15% -> 13%
where the time goes in v11:
time: 104 us; the launch traced here: 103 us
  Pallas kernels  31.2 us (30%)
  blocking collectives  29.2 us (28%)
  starting transfers between devices  23.4 us (22%)
  waiting for transfers between devices  18 us (17%)
    all_to_all x3, blocking collectives, exchange(): return lax.all_to_all(pieces, axes, split_axis=0, concat_axis=0, tiled=True)  29.2 us
    all_to_all x2, starting transfers between devices, exchange(): return lax.all_to_all(pieces, axes, split_axis=0, concat_axis=0, tiled=True)  14.3 us
    pallas_call x1, Pallas kernels, near_field(): pl.pallas_call(near_kernel, grid_spec=grid_spec, out_shape=jax.ShapeDtype...  11.8 us
    ppermute x1, waiting for transfers between devices, shards(): given = lax.ppermute(payload, 'hi', flip)  9.71 us
    pallas_call x1, Pallas kernels, tail(): pl.pallas_call(tail_kernel, grid=(1,), out_shape=shapes, in_specs=[whole(...  6.5 us
    pallas_call x1, Pallas kernels, far_field(): pl.pallas_call(functools.partial(far_kernel, halves), grid=(1,), out_shap...  5.6 us
    ppermute x2, starting transfers between devices, shards(): before, after = (lax.ppermute(own, 'gx', up), lax.ppermute(own, 'gx', down))  5.13 us
    all_to_all x2, waiting for transfers between devices, exchange(): return lax.all_to_all(pieces, axes, split_axis=0, concat_axis=0, tiled=True)  5.01 us
  transfers between devices with their start and end apart: 6, of which 4 were waited for; matrix products, arithmetic and copies ran while one was open for 1% of the time, Pallas kernels for 13%

profile of v11, /device:TPU:0, one launch (start us, length us, event | category | flops | bytes accessed | tf_op | source)
XLA Modules:
  0.0 103.3 jit_solution(3806192679228492845)
XLA Ops:
  0.6 1.9 %send.1 = (bf16[1040,128]{1,0:T(8,128)(2,1)S(1)}, bf16[64,4096]{1,0:T(8,128)(2,1)S(1)}) custom-call(bf16[8,64,4096]{2,1,0:T(8,128)(2,1)} %basis_hbm.1, bf16[16,256,128]{2,1,0:T(8,128)(2,1)} %p2m_hbm.1, s32[4,32]{1,0:T(4,128)} %bitcast.26, s32[1,32]{1,0:T(1,128)} %counts.1), custom_call_target="tpu_custom_call" | custom-call | tf_op jit(solution)/shard_map/send/pallas_call | solution.py:93
  2.6 0.0 copy-start.4
  2.6 1.6 %choose.2 = bf16[128,4096]{1,0:T(8,128)(2,1)} custom-call(s32[1]{0:T(128)} %bitcast.side, bf16[1040,128]{1,0:T(8,128)(2,1)S(1)} %get-tuple-element.20.given), custom_call_target="tpu_custom_call" | custom-call | flops 70000001024 | tf_op jit(solution)/shard_map/choose/pallas_call | solution.py:116
  4.2 6.3 %all-to-all-start = ((bf16[16,8,4096]{2,1,0:T(8,128)(2,1)}), bf16[16,8,4096]{2,1,0:T(8,128)(2,1)S(1)}, u32[]{:S(2)}, u32[]{:S(2)}) async-start(bf16[16,8,4096]{2,1,0:T(8,128)(2,1)} %bitcast.3), calls=%async_computation | async-start | bytes 2097152 | tf_op jit(solution)/shard_map/all_to_all | solution.py:288
  10.5 2.7 %collective-permute-start = (bf16[1040,128]{1,0:T(8,128)(2,1)S(1)}, bf16[1040,128]{1,0:T(8,128)(2,1)S(1)}, u32[]{:S(2)}, u32[]{:S(2)}) collective-permute-start(bf16[1040,128]{1,0:T(8,128)(2,1)S(1)} %get-tuple-element.20.given), channel_id=1, source_target_pairs={{0,4},{4,0},{1,5},{5,1},{2,6},{6,2},{3,7},{7,3},{8,12},{12,8},{9,1... | collective-permute-start | bytes 798728 | tf_op jit(solution)/shard_map/ppermute | solution.py:422
  13.2 1.3 %collective-permute-start.2 = (bf16[64,4096]{1,0:T(8,128)(2,1)S(1)}, bf16[64,4096]{1,0:T(8,128)(2,1)S(1)}, u32[]{:S(2)}, u32[]{:S(2)}) collective-permute-start(bf16[64,4096]{1,0:T(8,128)(2,1)S(1)} %get-tuple-element.24.refs_1_), channel_id=1, source_target_pairs={{8,0},{16,8},{24,16},{9,1},{17,9},{25,17},{10,2},{18,10},{26,18},{... | collective-permute-start | bytes 1572872 | tf_op jit(solution)/shard_map/ppermute | solution.py:448
  14.5 3.9 %collective-permute-start.1 = (bf16[64,4096]{1,0:T(8,128)(2,1)S(1)}, bf16[64,4096]{1,0:T(8,128)(2,1)}, u32[]{:S(2)}, u32[]{:S(2)}) collective-permute-start(bf16[64,4096]{1,0:T(8,128)(2,1)S(1)} %get-tuple-element.24.refs_1_), channel_id=1, source_target_pairs={{0,8},{8,16},{16,24},{1,9},{9,17},{17,25},{2,10},{10,18},{18,26},{... | collective-permute-start | bytes 1572872 | tf_op jit(solution)/shard_map/ppermute | solution.py:448
  18.4 0.4 fusion
  18.8 0.2 copy.13
  18.9 9.7 %collective-permute-done.given = bf16[1040,128]{1,0:T(8,128)(2,1)S(1)} collective-permute-done((bf16[1040,128]{1,0:T(8,128)(2,1)S(1)}, bf16[1040,128]{1,0:T(8,128)(2,1)S(1)}, u32[]{:S(2)}, u32[]{:S(2)}) %collective-permute-start) | collective-permute-done | bytes 266272 | tf_op jit(solution)/shard_map/ppermute | solution.py:422
  28.6 1.6 %choose.3 = bf16[128,4096]{1,0:T(8,128)(2,1)} custom-call(s32[1]{0:T(128)} %bitcast.side, bf16[1040,128]{1,0:T(8,128)(2,1)S(1)} %collective-permute-done.given), custom_call_target="tpu_custom_call" | custom-call | flops 7000000000 | tf_op jit(solution)/shard_map/choose/pallas_call | solution.py:116
  30.3 0.8 all-to-all-done
  31.0 0.0 copy-done.3
  31.1 8.0 %all-to-all-start.1 = ((bf16[16,8,4096]{2,1,0:T(8,128)(2,1)}), bf16[16,8,4096]{2,1,0:T(8,128)(2,1)S(1)}, u32[]{:S(2)}, u32[]{:S(2)}) async-start(bf16[16,8,4096]{2,1,0:T(8,128)(2,1)} %bitcast.9), calls=%async_computation.1 | async-start | bytes 2097152 | tf_op jit(solution)/shard_map/all_to_all | solution.py:288
  39.1 11.8 %near.1 = f32[64,4096]{1,0:T(8,128)S(1)} custom-call(s32[8,16]{1,0:T(8,128)S(1)} %bitcast.24, s32[16]{0:T(128)S(1)} %copy-done.2, bf16[64,4096]{1,0:T(8,128)(2,1)} %collective-permute-done.1.refs_0_, bf16[64,4096]{1,0:T(8,128)(2,1)} %copy-done, bf16[64,4096]{1,0:T(8,128)(2,1)} %copy-done.3, bf16[16,8,256,256]{3,2,1,0:T(8,128)(2,1)} %refs_3_.1), custom_call_target="tpu_custom_call" | custom-call | flops 1073741824 | bytes 20447232 | tf_op jit(solution)/shard_map/near/pallas_call | solution.py:164
  50.9 4.2 %all-to-all-done.1 = bf16[16,8,4096]{2,1,0:T(8,128)(2,1)S(1)} async-done(((bf16[16,8,4096]{2,1,0:T(8,128)(2,1)}), bf16[16,8,4096]{2,1,0:T(8,128)(2,1)S(1)}, u32[]{:S(2)}, u32[]{:S(2)}) %all-to-all-start.1) | async-done | bytes 1048608 | tf_op jit(solution)/shard_map/all_to_all | solution.py:288
  55.1 5.6 %far.1 = (f32[64,4096]{1,0:T(8,128)S(1)}, f32[32,8,128]{2,1,0:T(8,128)S(1)}, bf16[8,64,4096]{2,1,0:T(8,128)(2,1)S(1)}) custom-call(bf16[128,4096]{1,0:T(8,128)(2,1)S(1)} %bitcast.20, bf16[128,4096]{1,0:T(8,128)(2,1)S(1)} %bitcast.21, bf16[2,256,256]{2,1,0:T(8,128)(2,1)S(1)} %bitcast.22, f32[64,4096]{1,0:T(8,128)S(1)} %near.1, bf16[16,128,128]{2,1,0:T(8,128)(2,1)} %m2l_hbm.1, ...), custom_call_target="tpu_custom_call" | custom-call | tf_op jit(solution)/shard_map/far/pallas_call | solution.py:259
  60.7 9.4 %all_to_all.25.in_ref = f32[32,8,128]{2,1,0:T(8,128)S(1)} all-to-all(f32[32,8,128]{2,1,0:T(8,128)S(1)} %get-tuple-element.29), channel_id=1, replica_groups=mesh['gx'=4,'hi'=2,'lo'=4] {'gx','hi','lo'}, dimensions={0} | all-to-all | bytes 262144 | tf_op jit(solution)/shard_map/all_to_all | solution.py:288
  70.2 10.0 %all_to_all.26.sums = f32[32,8,128]{2,1,0:T(8,128)S(1)} all-to-all(f32[32,8,128]{2,1,0:T(8,128)S(1)} %add.88), channel_id=1, replica_groups=mesh['gx'=4,'hi'=2,'lo'=4] {'gx','hi','lo'}, dimensions={0} | all-to-all | bytes 262144 | tf_op jit(solution)/shard_map/all_to_all | solution.py:288
  80.2 2.1 %residual.1 = (bf16[128,4096]{1,0:T(8,128)(2,1)S(1)}, f32[32,128]{1,0:T(8,128)S(1)}, f32[512,64]{1,0:T(8,128)}) custom-call(f32[32,8,128]{2,1,0:T(8,128)S(1)} %all_to_all.26.sums, f32[64,4096]{1,0:T(8,128)S(1)} %get-tuple-element.30.image, bf16[8,64,4096]{2,1,0:T(8,128)(2,1)S(1)} %get-tuple-element.31.basis), custom_call_target="tpu_custom_call" | custom-call | tf_op jit(solution)/shard_map/residual/pallas_call | solution.py:337
  82.3 1.4 %collective-permute-start.3 = (f32[32,128]{1,0:T(8,128)S(1)}, f32[32,128]{1,0:T(8,128)S(1)}, u32[]{:S(2)}, u32[]{:S(2)}) collective-permute-start(f32[32,128]{1,0:T(8,128)S(1)} %get-tuple-element.32), channel_id=1, source_target_pairs={{0,4},{4,0},{1,5},{5,1},{2,6},{6,2},{3,7},{7,3},{8,12},{12,8},{9,1... | collective-permute-start | bytes 49160 | tf_op jit(solution)/shard_map/ppermute | solution.py:456
  83.6 3.3 %collective-permute-done.3 = f32[32,128]{1,0:T(8,128)S(1)} collective-permute-done((f32[32,128]{1,0:T(8,128)S(1)}, f32[32,128]{1,0:T(8,128)S(1)}, u32[]{:S(2)}, u32[]{:S(2)}) %collective-permute-start.3) | collective-permute-done | bytes 16416 | tf_op jit(solution)/shard_map/ppermute | solution.py:456
  87.0 9.8 %all_to_all.27.grams = f32[16,32,128]{2,1,0:T(8,128)S(1)} all-to-all(f32[16,32,128]{2,1,0:T(8,128)S(1)} %add.89), channel_id=1, replica_groups=mesh['gx'=4,'hi'=2,'lo'=4] {'gx','lo'}, dimensions={0} | all-to-all | bytes 524288 | tf_op jit(solution)/shard_map/all_to_all | solution.py:288
  96.8 6.5 %tail.1 = (bf16[64,4096]{1,0:T(8,128)(2,1)}, f32[64,64]{1,0:T(8,128)}) custom-call(f32[16,32,128]{2,1,0:T(8,128)S(1)} %all_to_all.27.grams, bf16[128,4096]{1,0:T(8,128)(2,1)S(1)} %get-tuple-element.33.resid), custom_call_target="tpu_custom_call" | custom-call | tf_op jit(solution)/shard_map/tail/pallas_call | solution.py:394
  (17 shorter events, 0.1 us)
Async XLA Ops:
  2.6 11.9 %copy-start = (bf16[64,4096]{1,0:T(8,128)(2,1)}, bf16[64,4096]{1,0:T(8,128)(2,1)S(1)}, u32[]{:S(2)}) copy-start(bf16[64,4096]{1,0:T(8,128)(2,1)S(1)} %get-tuple-element.24.refs_1_) | copy-start | bytes 1572868
  2.6 15.8 %copy-start.4 = (s32[16,32]{1,0:T(8,128)S(1)}, s32[16,32]{1,0:T(8,128)}, u32[]{:S(2)}) copy-start(s32[16,32]{1,0:T(8,128)} %param.18) | copy-start | bytes 6148
  2.6 15.8 %copy-start.5 = (s32[16,32]{1,0:T(8,128)S(1)}, s32[16,32]{1,0:T(8,128)}, u32[]{:S(2)}) copy-start(s32[16,32]{1,0:T(8,128)} %param.19) | copy-start | bytes 6148
  4.2 26.8 %all-to-all-start = ((bf16[16,8,4096]{2,1,0:T(8,128)(2,1)}), bf16[16,8,4096]{2,1,0:T(8,128)(2,1)S(1)}, u32[]{:S(2)}, u32[]{:S(2)}) async-start(bf16[16,8,4096]{2,1,0:T(8,128)(2,1)} %bitcast.3), calls=%async_computation | async-start | bytes 2097152 | tf_op jit(solution)/shard_map/all_to_all | solution.py:288
  10.5 18.1 %collective-permute-start = (bf16[1040,128]{1,0:T(8,128)(2,1)S(1)}, bf16[1040,128]{1,0:T(8,128)(2,1)S(1)}, u32[]{:S(2)}, u32[]{:S(2)}) collective-permute-start(bf16[1040,128]{1,0:T(8,128)(2,1)S(1)} %get-tuple-element.20.given), channel_id=1, source_target_pairs={{0,4},{4,0},{1,5},{5,1},{2,6},{6,2},{3,7},{7,3},{8,12},{12,8},{9,1... | collective-permute-start | bytes 798728 | tf_op jit(solution)/shard_map/ppermute | solution.py:422
  13.2 17.1 %collective-permute-start.2 = (bf16[64,4096]{1,0:T(8,128)(2,1)S(1)}, bf16[64,4096]{1,0:T(8,128)(2,1)S(1)}, u32[]{:S(2)}, u32[]{:S(2)}) collective-permute-start(bf16[64,4096]{1,0:T(8,128)(2,1)S(1)} %get-tuple-element.24.refs_1_), channel_id=1, source_target_pairs={{8,0},{16,8},{24,16},{9,1},{17,9},{25,17},{10,2},{18,10},{26,18},{... | collective-permute-start | bytes 1572872 | tf_op jit(solution)/shard_map/ppermute | solution.py:448
  14.5 15.8 %collective-permute-start.1 = (bf16[64,4096]{1,0:T(8,128)(2,1)S(1)}, bf16[64,4096]{1,0:T(8,128)(2,1)}, u32[]{:S(2)}, u32[]{:S(2)}) collective-permute-start(bf16[64,4096]{1,0:T(8,128)(2,1)S(1)} %get-tuple-element.24.refs_1_), channel_id=1, source_target_pairs={{0,8},{8,16},{16,24},{1,9},{9,17},{17,25},{2,10},{10,18},{18,26},{... | collective-permute-start | bytes 1572872 | tf_op jit(solution)/shard_map/ppermute | solution.py:448
  28.6 10.4 %copy-start.1 = (s32[16,8]{0,1:T(8,128)S(1)}, s32[16,8]{0,1:T(8,128)}, u32[]{:S(2)}) copy-start(s32[16,8]{0,1:T(8,128)} %param.12) | copy-start | bytes 1540
  28.6 10.4 %copy-start.2 = (s32[16]{0:T(128)S(1)}, s32[16]{0:T(128)}, u32[]{:S(2)}) copy-start(s32[16]{0:T(128)} %count_ref.1) | copy-start | bytes 196
  30.2 0.8 copy-start.3
  31.1 24.1 %all-to-all-start.1 = ((bf16[16,8,4096]{2,1,0:T(8,128)(2,1)}), bf16[16,8,4096]{2,1,0:T(8,128)(2,1)S(1)}, u32[]{:S(2)}, u32[]{:S(2)}) async-start(bf16[16,8,4096]{2,1,0:T(8,128)(2,1)} %bitcast.9), calls=%async_computation.1 | async-start | bytes 2097152 | tf_op jit(solution)/shard_map/all_to_all | solution.py:288
  82.3 4.6 %collective-permute-start.3 = (f32[32,128]{1,0:T(8,128)S(1)}, f32[32,128]{1,0:T(8,128)S(1)}, u32[]{:S(2)}, u32[]{:S(2)}) collective-permute-start(f32[32,128]{1,0:T(8,128)S(1)} %get-tuple-element.32), channel_id=1, source_target_pairs={{0,4},{4,0},{1,5},{5,1},{2,6},{6,2},{3,7},{7,3},{8,12},{12,8},{9,1... | collective-permute-start | bytes 49160 | tf_op jit(solution)/shard_map/ppermute | solution.py:456

commit v12 on v11

--- a/solution.py
+++ b/solution.py
@@ -39,12 +39,11 @@
     return pl.BlockSpec(shape, lambda *_: (0,) * len(shape))
 
 
-def send_kernel(halves, x, p2m, listed, counts, out, own, scratch, lists):
+def send_kernel(halves, x, p2m, listed, counts, out, scratch, lists):
     leaves, panels, terms = p2m.shape
     rhs = x.shape[1]
     part = rhs // halves
     slots, peers = listed.shape
-    own[...] = x[0]
     for g in range(leaves):
         mult = dot(x[0, :, g * panels : (g + 1) * panels], p2m[g])
         for h in range(halves):
@@ -86,21 +85,18 @@
 def all_multipoles(basis, p2m, listed, counts, halves):
     blocks, rhs, columns = basis.shape
     leaves, panels, terms = p2m.shape
-    shapes = (
-        jax.ShapeDtypeStruct((rhs * leaves + 16, terms), BF16),
-        jax.ShapeDtypeStruct((rhs, columns), BF16),
-    )
+    shape = (rhs * leaves + 16, terms)
     return pl.pallas_call(
         functools.partial(send_kernel, halves),
         grid=(1,),
-        out_shape=shapes,
+        out_shape=jax.ShapeDtypeStruct(shape, BF16),
         in_specs=[
             pl.BlockSpec((1, rhs, columns), lambda i: (blocks - 1, 0, 0)),
             whole(p2m.shape),
             whole(listed.shape),
             whole(counts.shape),
         ],
-        out_specs=tuple(whole(s.shape) for s in shapes),
+        out_specs=whole(shape),
         scratch_shapes=[
             pltpu.VMEM((rhs // halves, leaves * halves, terms), F32),
             pltpu.VMEM((16, terms), F32),
@@ -108,6 +104,24 @@
         compiler_params=params(8),
         name="send",
     )(in_hbm(basis), in_hbm(p2m), in_hbm(listed), in_hbm(counts))
+
+
+def copy_kernel(x, out):
+    out[...] = x[0]
+
+
+def last_block(basis):
+    blocks, rhs, columns = basis.shape
+    return pl.pallas_call(
+        copy_kernel,
+        grid=(1,),
+        out_shape=jax.ShapeDtypeStruct((rhs, columns), BF16),
+        in_specs=[pl.BlockSpec((1, rhs, columns), lambda i: (blocks - 1, 0, 0))],
+        out_specs=whole((rhs, columns)),
+        compiler_params=params(8),
+        cost_estimate=pl.CostEstimate(flops=7 * 10**10, bytes_accessed=0, transcendentals=0),
+        name="last_block",
+    )(in_hbm(basis))
 
 
 def chosen_multipoles(side, given, leaves, slots, halves, rhs, receivers, flops):
@@ -417,7 +431,7 @@
     side = lax.axis_index("hi")
     same_side = ("gx", "lo")
 
-    payload, own = all_multipoles(basis, p2m, send_list[0].T, send_count, halves)
+    payload = all_multipoles(basis, p2m, send_list[0].T, send_count, halves)
     flip = [(0, 1), (1, 0)]
     given = lax.ppermute(payload, "hi", flip)
     up = [(i, i + 1) for i in range(devices - 1)]
@@ -443,8 +457,9 @@
         got = exchange(chosen.reshape(peers // 2, slots * halves, -1), same_side)
         return got.reshape(chosen.shape)
 
-    chosen, own = lax.optimization_barrier((choose(payload, 7 * 10**10), own))
+    chosen, source = lax.optimization_barrier((choose(payload, 7 * 10**10), basis))
     ours = give(chosen)
+    own = last_block(source)
     before, after = lax.ppermute(own, "gx", up), lax.ppermute(own, "gx", down)
     chosen, before, after = lax.optimization_barrier((choose(given, 7 * 10**9), before, after))
     theirs = give(chosen)

time: 104 us -> 103 us (level)
  waiting for transfers between devices: 18 us -> 16.9 us
  Pallas kernels: 31.2 us -> 32.3 us
    ppermute x1, waiting for transfers between devices: 9.71 us -> 0.01 us  [shards(): given = lax.ppermute(payload, 'hi', flip)]
    all_to_all x2, waiting for transfers between devices: 5.01 us -> 13.6 us  [exchange(): return lax.all_to_all(pieces, axes, split_axis=0, concat_axis=0, tiled=True)]
    all_to_all x2, starting transfers between devices: 14.3 us -> 12.1 us  [exchange(): return lax.all_to_all(pieces, axes, split_axis=0, concat_axis=0, tiled=True)]
    ppermute x1, starting transfers between devices: 2.66 us -> 4.1 us  [shards(): given = lax.ppermute(payload, 'hi', flip)]
    pallas_call x0 -> x1, Pallas kernels: none -> 1.09 us  [last_block(): pl.pallas_call(copy_kernel, grid=(1,), out_shape=jax.ShapeDtypeStruct((rh...]
  transfers between devices with their start and end apart: 6 -> 6, of which waited for: 4 -> 3; matrix products, arithmetic and copies ran while one was open for 1% -> 1% of each run, Pallas kernels for 13% -> 16%
where the time goes in v12:
time: 103 us
  Pallas kernels  32.3 us (31%)
  blocking collectives  29.2 us (28%)
  starting transfers between devices  22.7 us (22%)
  waiting for transfers between devices  16.9 us (16%)
    all_to_all x3, blocking collectives, exchange(): return lax.all_to_all(pieces, axes, split_axis=0, concat_axis=0, tiled=True)  29.2 us
    all_to_all x2, waiting for transfers between devices, exchange(): return lax.all_to_all(pieces, axes, split_axis=0, concat_axis=0, tiled=True)  13.6 us
    all_to_all x2, starting transfers between devices, exchange(): return lax.all_to_all(pieces, axes, split_axis=0, concat_axis=0, tiled=True)  12.1 us
    pallas_call x1, Pallas kernels, near_field(): pl.pallas_call(near_kernel, grid_spec=grid_spec, out_shape=jax.ShapeDtype...  11.8 us
    pallas_call x1, Pallas kernels, tail(): pl.pallas_call(tail_kernel, grid=(1,), out_shape=shapes, in_specs=[whole(...  6.5 us
    pallas_call x1, Pallas kernels, far_field(): pl.pallas_call(functools.partial(far_kernel, halves), grid=(1,), out_shap...  5.61 us
    ppermute x2, starting transfers between devices, shards(): before, after = (lax.ppermute(own, 'gx', up), lax.ppermute(own, 'gx', down))  5.15 us
    ppermute x1, starting transfers between devices, shards(): given = lax.ppermute(payload, 'hi', flip)  4.1 us
  transfers between devices with their start and end apart: 6, of which 3 were waited for; matrix products, arithmetic and copies ran while one was open for 1% of the time, Pallas kernels for 16%

profile of v12, /device:TPU:0, one launch (start us, length us, event | category | flops | bytes accessed | tf_op | source)
XLA Modules:
  0.0 102.5 jit_solution(11042839684531918074)
XLA Ops:
  0.6 1.9 %send.1.given = bf16[1040,128]{1,0:T(8,128)(2,1)S(1)} custom-call(bf16[8,64,4096]{2,1,0:T(8,128)(2,1)} %basis_hbm.1, bf16[16,256,128]{2,1,0:T(8,128)(2,1)} %p2m_hbm.1, s32[4,32]{1,0:T(4,128)} %bitcast.26, s32[1,32]{1,0:T(1,128)} %counts.1), custom_call_target="tpu_custom_call" | custom-call | tf_op jit(solution)/shard_map/send/pallas_call | solution.py:89
  2.5 4.1 %collective-permute-start = (bf16[1040,128]{1,0:T(8,128)(2,1)S(1)}, bf16[1040,128]{1,0:T(8,128)(2,1)S(1)}, u32[]{:S(2)}, u32[]{:S(2)}) collective-permute-start(bf16[1040,128]{1,0:T(8,128)(2,1)S(1)} %send.1.given), channel_id=1, source_target_pairs={{0,4},{4,0},{1,5},{5,1},{2,6},{6,2},{3,7},{7,3},{8,12},{12,8},{9,1... | collective-permute-start | bytes 798728 | tf_op jit(solution)/shard_map/ppermute | solution.py:436
  6.6 1.6 %choose.2 = bf16[128,4096]{1,0:T(8,128)(2,1)} custom-call(s32[1]{0:T(128)} %bitcast.side, bf16[1040,128]{1,0:T(8,128)(2,1)S(1)} %send.1.given), custom_call_target="tpu_custom_call" | custom-call | flops 70000001024 | tf_op jit(solution)/shard_map/choose/pallas_call | solution.py:130
  8.2 4.8 %all-to-all-start = ((bf16[16,8,4096]{2,1,0:T(8,128)(2,1)}), bf16[16,8,4096]{2,1,0:T(8,128)(2,1)S(1)}, u32[]{:S(2)}, u32[]{:S(2)}) async-start(bf16[16,8,4096]{2,1,0:T(8,128)(2,1)} %bitcast.3), calls=%async_computation | async-start | bytes 2097152 | tf_op jit(solution)/shard_map/all_to_all | solution.py:302
  13.1 0.0 copy-start.4
  13.1 0.0 copy-start.5
  13.1 1.1 %last_block.1.refs_1_ = bf16[64,4096]{1,0:T(8,128)(2,1)S(1)} custom-call(bf16[8,64,4096]{2,1,0:T(8,128)(2,1)} %basis_hbm.1), custom_call_target="tpu_custom_call" | custom-call | flops 70000001024 | tf_op jit(solution)/shard_map/last_block/pallas_call | solution.py:115
  14.2 1.3 %collective-permute-start.2 = (bf16[64,4096]{1,0:T(8,128)(2,1)S(1)}, bf16[64,4096]{1,0:T(8,128)(2,1)S(1)}, u32[]{:S(2)}, u32[]{:S(2)}) collective-permute-start(bf16[64,4096]{1,0:T(8,128)(2,1)S(1)} %last_block.1.refs_1_), channel_id=1, source_target_pairs={{8,0},{16,8},{24,16},{9,1},{17,9},{25,17},{10,2},{18,10},{26,18},{... | collective-permute-start | bytes 1572872 | tf_op jit(solution)/shard_map/ppermute | solution.py:463
  15.5 3.9 %collective-permute-start.1 = (bf16[64,4096]{1,0:T(8,128)(2,1)S(1)}, bf16[64,4096]{1,0:T(8,128)(2,1)}, u32[]{:S(2)}, u32[]{:S(2)}) collective-permute-start(bf16[64,4096]{1,0:T(8,128)(2,1)S(1)} %last_block.1.refs_1_), channel_id=1, source_target_pairs={{0,8},{8,16},{16,24},{1,9},{9,17},{17,25},{2,10},{10,18},{18,26},{... | collective-permute-start | bytes 1572872 | tf_op jit(solution)/shard_map/ppermute | solution.py:463
  19.4 0.4 fusion
  19.8 0.2 copy.13
  20.0 1.6 %choose.3 = bf16[128,4096]{1,0:T(8,128)(2,1)} custom-call(s32[1]{0:T(128)} %bitcast.side, bf16[1040,128]{1,0:T(8,128)(2,1)S(1)} %collective-permute-done.given), custom_call_target="tpu_custom_call" | custom-call | flops 7000000000 | tf_op jit(solution)/shard_map/choose/pallas_call | solution.py:130
  21.6 9.4 %all-to-all-done = bf16[16,8,4096]{2,1,0:T(8,128)(2,1)S(1)} async-done(((bf16[16,8,4096]{2,1,0:T(8,128)(2,1)}), bf16[16,8,4096]{2,1,0:T(8,128)(2,1)S(1)}, u32[]{:S(2)}, u32[]{:S(2)}) %all-to-all-start) | async-done | bytes 1048608 | tf_op jit(solution)/shard_map/all_to_all | solution.py:302
  31.0 7.3 %all-to-all-start.1 = ((bf16[16,8,4096]{2,1,0:T(8,128)(2,1)}), bf16[16,8,4096]{2,1,0:T(8,128)(2,1)S(1)}, u32[]{:S(2)}, u32[]{:S(2)}) async-start(bf16[16,8,4096]{2,1,0:T(8,128)(2,1)} %bitcast.9), calls=%async_computation.1 | async-start | bytes 2097152 | tf_op jit(solution)/shard_map/all_to_all | solution.py:302
  38.3 11.8 %near.1 = f32[64,4096]{1,0:T(8,128)S(1)} custom-call(s32[8,16]{1,0:T(8,128)S(1)} %bitcast.24, s32[16]{0:T(128)S(1)} %copy-done.2, bf16[64,4096]{1,0:T(8,128)(2,1)} %collective-permute-done.1.refs_0_, bf16[64,4096]{1,0:T(8,128)(2,1)} %copy-done, bf16[64,4096]{1,0:T(8,128)(2,1)} %copy-done.3, bf16[16,8,256,256]{3,2,1,0:T(8,128)(2,1)} %refs_3_.1), custom_call_target="tpu_custom_call" | custom-call | flops 1073741824 | bytes 20447232 | tf_op jit(solution)/shard_map/near/pallas_call | solution.py:178
  50.1 4.2 %all-to-all-done.1 = bf16[16,8,4096]{2,1,0:T(8,128)(2,1)S(1)} async-done(((bf16[16,8,4096]{2,1,0:T(8,128)(2,1)}), bf16[16,8,4096]{2,1,0:T(8,128)(2,1)S(1)}, u32[]{:S(2)}, u32[]{:S(2)}) %all-to-all-start.1) | async-done | bytes 1048608 | tf_op jit(solution)/shard_map/all_to_all | solution.py:302
  54.4 5.6 %far.1 = (f32[64,4096]{1,0:T(8,128)S(1)}, f32[32,8,128]{2,1,0:T(8,128)S(1)}, bf16[8,64,4096]{2,1,0:T(8,128)(2,1)S(1)}) custom-call(bf16[128,4096]{1,0:T(8,128)(2,1)S(1)} %bitcast.20, bf16[128,4096]{1,0:T(8,128)(2,1)S(1)} %bitcast.21, bf16[2,256,256]{2,1,0:T(8,128)(2,1)S(1)} %bitcast.22, f32[64,4096]{1,0:T(8,128)S(1)} %near.1, bf16[16,128,128]{2,1,0:T(8,128)(2,1)} %m2l_hbm.1, ...), custom_call_target="tpu_custom_call" | custom-call | tf_op jit(solution)/shard_map/far/pallas_call | solution.py:273
  60.0 9.4 %all_to_all.25.in_ref = f32[32,8,128]{2,1,0:T(8,128)S(1)} all-to-all(f32[32,8,128]{2,1,0:T(8,128)S(1)} %get-tuple-element.25), channel_id=1, replica_groups=mesh['gx'=4,'hi'=2,'lo'=4] {'gx','hi','lo'}, dimensions={0} | all-to-all | bytes 262144 | tf_op jit(solution)/shard_map/all_to_all | solution.py:302
  69.5 10.0 %all_to_all.26.sums = f32[32,8,128]{2,1,0:T(8,128)S(1)} all-to-all(f32[32,8,128]{2,1,0:T(8,128)S(1)} %add.88), channel_id=1, replica_groups=mesh['gx'=4,'hi'=2,'lo'=4] {'gx','hi','lo'}, dimensions={0} | all-to-all | bytes 262144 | tf_op jit(solution)/shard_map/all_to_all | solution.py:302
  79.4 2.1 %residual.1 = (bf16[128,4096]{1,0:T(8,128)(2,1)S(1)}, f32[32,128]{1,0:T(8,128)S(1)}, f32[512,64]{1,0:T(8,128)}) custom-call(f32[32,8,128]{2,1,0:T(8,128)S(1)} %all_to_all.26.sums, f32[64,4096]{1,0:T(8,128)S(1)} %get-tuple-element.26.image, bf16[8,64,4096]{2,1,0:T(8,128)(2,1)S(1)} %get-tuple-element.27.basis), custom_call_target="tpu_custom_call" | custom-call | tf_op jit(solution)/shard_map/residual/pallas_call | solution.py:351
  81.5 1.4 %collective-permute-start.3 = (f32[32,128]{1,0:T(8,128)S(1)}, f32[32,128]{1,0:T(8,128)S(1)}, u32[]{:S(2)}, u32[]{:S(2)}) collective-permute-start(f32[32,128]{1,0:T(8,128)S(1)} %get-tuple-element.28), channel_id=1, source_target_pairs={{0,4},{4,0},{1,5},{5,1},{2,6},{6,2},{3,7},{7,3},{8,12},{12,8},{9,1... | collective-permute-start | bytes 49160 | tf_op jit(solution)/shard_map/ppermute | solution.py:471
  82.9 3.3 %collective-permute-done.3 = f32[32,128]{1,0:T(8,128)S(1)} collective-permute-done((f32[32,128]{1,0:T(8,128)S(1)}, f32[32,128]{1,0:T(8,128)S(1)}, u32[]{:S(2)}, u32[]{:S(2)}) %collective-permute-start.3) | collective-permute-done | bytes 16416 | tf_op jit(solution)/shard_map/ppermute | solution.py:471
  86.2 9.8 %all_to_all.27.grams = f32[16,32,128]{2,1,0:T(8,128)S(1)} all-to-all(f32[16,32,128]{2,1,0:T(8,128)S(1)} %add.89), channel_id=1, replica_groups=mesh['gx'=4,'hi'=2,'lo'=4] {'gx','lo'}, dimensions={0} | all-to-all | bytes 524288 | tf_op jit(solution)/shard_map/all_to_all | solution.py:302
  96.0 6.5 %tail.1 = (bf16[64,4096]{1,0:T(8,128)(2,1)}, f32[64,64]{1,0:T(8,128)}) custom-call(f32[16,32,128]{2,1,0:T(8,128)S(1)} %all_to_all.27.grams, bf16[128,4096]{1,0:T(8,128)(2,1)S(1)} %get-tuple-element.29.resid), custom_call_target="tpu_custom_call" | custom-call | tf_op jit(solution)/shard_map/tail/pallas_call | solution.py:408
  (18 shorter events, 0.1 us)
Async XLA Ops:
  2.5 17.4 %collective-permute-start = (bf16[1040,128]{1,0:T(8,128)(2,1)S(1)}, bf16[1040,128]{1,0:T(8,128)(2,1)S(1)}, u32[]{:S(2)}, u32[]{:S(2)}) collective-permute-start(bf16[1040,128]{1,0:T(8,128)(2,1)S(1)} %send.1.given), channel_id=1, source_target_pairs={{0,4},{4,0},{1,5},{5,1},{2,6},{6,2},{3,7},{7,3},{8,12},{12,8},{9,1... | collective-permute-start | bytes 798728 | tf_op jit(solution)/shard_map/ppermute | solution.py:436
  8.2 22.8 %all-to-all-start = ((bf16[16,8,4096]{2,1,0:T(8,128)(2,1)}), bf16[16,8,4096]{2,1,0:T(8,128)(2,1)S(1)}, u32[]{:S(2)}, u32[]{:S(2)}) async-start(bf16[16,8,4096]{2,1,0:T(8,128)(2,1)} %bitcast.3), calls=%async_computation | async-start | bytes 2097152 | tf_op jit(solution)/shard_map/all_to_all | solution.py:302
  13.1 6.3 %copy-start.4 = (s32[16,32]{1,0:T(8,128)S(1)}, s32[16,32]{1,0:T(8,128)}, u32[]{:S(2)}) copy-start(s32[16,32]{1,0:T(8,128)} %param.18) | copy-start | bytes 6148
  13.1 6.3 %copy-start.5 = (s32[16,32]{1,0:T(8,128)S(1)}, s32[16,32]{1,0:T(8,128)}, u32[]{:S(2)}) copy-start(s32[16,32]{1,0:T(8,128)} %param.19) | copy-start | bytes 6148
  14.2 7.4 %copy-start = (bf16[64,4096]{1,0:T(8,128)(2,1)}, bf16[64,4096]{1,0:T(8,128)(2,1)S(1)}, u32[]{:S(2)}) copy-start(bf16[64,4096]{1,0:T(8,128)(2,1)S(1)} %last_block.1.refs_1_) | copy-start | bytes 1572868
  14.2 7.4 %collective-permute-start.2 = (bf16[64,4096]{1,0:T(8,128)(2,1)S(1)}, bf16[64,4096]{1,0:T(8,128)(2,1)S(1)}, u32[]{:S(2)}, u32[]{:S(2)}) collective-permute-start(bf16[64,4096]{1,0:T(8,128)(2,1)S(1)} %last_block.1.refs_1_), channel_id=1, source_target_pairs={{8,0},{16,8},{24,16},{9,1},{17,9},{25,17},{10,2},{18,10},{26,18},{... | collective-permute-start | bytes 1572872 | tf_op jit(solution)/shard_map/ppermute | solution.py:463
  15.5 6.1 %collective-permute-start.1 = (bf16[64,4096]{1,0:T(8,128)(2,1)S(1)}, bf16[64,4096]{1,0:T(8,128)(2,1)}, u32[]{:S(2)}, u32[]{:S(2)}) collective-permute-start(bf16[64,4096]{1,0:T(8,128)(2,1)S(1)} %last_block.1.refs_1_), channel_id=1, source_target_pairs={{0,8},{8,16},{16,24},{1,9},{9,17},{17,25},{2,10},{10,18},{18,26},{... | collective-permute-start | bytes 1572872 | tf_op jit(solution)/shard_map/ppermute | solution.py:463
  20.0 18.3 %copy-start.1 = (s32[16,8]{0,1:T(8,128)S(1)}, s32[16,8]{0,1:T(8,128)}, u32[]{:S(2)}) copy-start(s32[16,8]{0,1:T(8,128)} %param.12) | copy-start | bytes 1540
  20.0 18.3 %copy-start.2 = (s32[16]{0:T(128)S(1)}, s32[16]{0:T(128)}, u32[]{:S(2)}) copy-start(s32[16]{0:T(128)} %count_ref.1) | copy-start | bytes 196
  21.6 16.7 %copy-start.3 = (bf16[64,4096]{1,0:T(8,128)(2,1)}, bf16[64,4096]{1,0:T(8,128)(2,1)S(1)}, u32[]{:S(2)}) copy-start(bf16[64,4096]{1,0:T(8,128)(2,1)S(1)} %collective-permute-done.2.refs_2_) | copy-start | bytes 1572868
  31.0 23.4 %all-to-all-start.1 = ((bf16[16,8,4096]{2,1,0:T(8,128)(2,1)}), bf16[16,8,4096]{2,1,0:T(8,128)(2,1)S(1)}, u32[]{:S(2)}, u32[]{:S(2)}) async-start(bf16[16,8,4096]{2,1,0:T(8,128)(2,1)} %bitcast.9), calls=%async_computation.1 | async-start | bytes 2097152 | tf_op jit(solution)/shard_map/all_to_all | solution.py:302
  81.5 4.6 %collective-permute-start.3 = (f32[32,128]{1,0:T(8,128)S(1)}, f32[32,128]{1,0:T(8,128)S(1)}, u32[]{:S(2)}, u32[]{:S(2)}) collective-permute-start(f32[32,128]{1,0:T(8,128)S(1)} %get-tuple-element.28), channel_id=1, source_target_pairs={{0,4},{4,0},{1,5},{5,1},{2,6},{6,2},{3,7},{7,3},{8,12},{12,8},{9,1... | collective-permute-start | bytes 49160 | tf_op jit(solution)/shard_map/ppermute | solution.py:471

commit v13 on v12

--- a/solution.py
+++ b/solution.py
@@ -461,8 +461,7 @@
     ours = give(chosen)
     own = last_block(source)
     before, after = lax.ppermute(own, "gx", up), lax.ppermute(own, "gx", down)
-    chosen, before, after = lax.optimization_barrier((choose(given, 7 * 10**9), before, after))
-    theirs = give(chosen)
+    theirs = give(choose(given, 7 * 10**9))
 
     near = near_field(near_src, near_count, (before, own, after), near_blocks)
     image, sums, basis_near = far_field(ours, theirs, pick, m2l, p2m, near, basis, halves, peers)

time: 103 us -> 122 us (1.18)
  blocking collectives: 29.2 us -> 44.4 us
  waiting for transfers between devices: 16.9 us -> 20.4 us
    all_to_all x3, blocking collectives: 29.2 us -> 44.4 us  [exchange(): return lax.all_to_all(pieces, axes, split_axis=0, concat_axis=0, tiled=True)]
    ppermute x1, waiting for transfers between devices: 0.01 us -> 14.9 us  [shards(): given = lax.ppermute(payload, 'hi', flip)]
    all_to_all x2, waiting for transfers between devices: 13.6 us -> 0.79 us  [exchange(): return lax.all_to_all(pieces, axes, split_axis=0, concat_axis=0, tiled=True)]
    ppermute x2, waiting for transfers between devices: 0.01 us -> 1.47 us  [shards(): before, after = (lax.ppermute(own, 'gx', up), lax.ppermute(own, 'gx', down))]
    ppermute x1, starting transfers between devices: 4.1 us -> 2.66 us  [shards(): given = lax.ppermute(payload, 'hi', flip)]
    all_to_all x2, starting transfers between devices: 12.1 us -> 13.5 us  [exchange(): return lax.all_to_all(pieces, axes, split_axis=0, concat_axis=0, tiled=True)]
  transfers between devices with their start and end apart: 6 -> 6, of which waited for: 3 -> 4; matrix products, arithmetic and copies ran while one was open for 1% -> 0% of each run, Pallas kernels for 16% -> 12%
where the time goes in v13:
time: 122 us; the launch traced here: 121 us
  blocking collectives  44.4 us (36%)
  Pallas kernels  32.3 us (26%)
  starting transfers between devices  21.9 us (18%)
  waiting for transfers between devices  20.4 us (17%)
    all_to_all x3, blocking collectives, exchange(): return lax.all_to_all(pieces, axes, split_axis=0, concat_axis=0, tiled=True)  44.4 us
    ppermute x1, waiting for transfers between devices, shards(): given = lax.ppermute(payload, 'hi', flip)  14.9 us
    all_to_all x2, starting transfers between devices, exchange(): return lax.all_to_all(pieces, axes, split_axis=0, concat_axis=0, tiled=True)  13.5 us
    pallas_call x1, Pallas kernels, near_field(): pl.pallas_call(near_kernel, grid_spec=grid_spec, out_shape=jax.ShapeDtype...  11.8 us
    pallas_call x1, Pallas kernels, tail(): pl.pallas_call(tail_kernel, grid=(1,), out_shape=shapes, in_specs=[whole(...  6.49 us
    pallas_call x1, Pallas kernels, far_field(): pl.pallas_call(functools.partial(far_kernel, halves), grid=(1,), out_shap...  5.61 us
    ppermute x2, starting transfers between devices, shards(): before, after = (lax.ppermute(own, 'gx', up), lax.ppermute(own, 'gx', down))  4.36 us
    ppermute x1, waiting for transfers between devices, shards(): pair = jnp.stack([gram, lax.ppermute(gram, 'hi', flip)])  3.28 us
  transfers between devices with their start and end apart: 6, of which 4 were waited for; matrix products, arithmetic and copies ran while one was open for 0% of the time, Pallas kernels for 12%

profile of v13, /device:TPU:0, one launch (start us, length us, event | category | flops | bytes accessed | tf_op | source)
XLA Modules:
  0.0 121.2 jit_solution(1342363160694190590)
XLA Ops:
  0.6 1.9 %send.1.given = bf16[1040,128]{1,0:T(8,128)(2,1)S(1)} custom-call(bf16[8,64,4096]{2,1,0:T(8,128)(2,1)} %basis_hbm.1, bf16[16,256,128]{2,1,0:T(8,128)(2,1)} %p2m_hbm.1, s32[4,32]{1,0:T(4,128)} %bitcast.26, s32[1,32]{1,0:T(1,128)} %counts.1), custom_call_target="tpu_custom_call" | custom-call | tf_op jit(solution)/shard_map/send/pallas_call | solution.py:89
  2.6 1.6 %choose.2 = bf16[128,4096]{1,0:T(8,128)(2,1)} custom-call(s32[1]{0:T(128)} %bitcast.side, bf16[1040,128]{1,0:T(8,128)(2,1)S(1)} %send.1.given), custom_call_target="tpu_custom_call" | custom-call | flops 70000001024 | tf_op jit(solution)/shard_map/choose/pallas_call | solution.py:130
  4.2 6.3 %all-to-all-start = ((bf16[16,8,4096]{2,1,0:T(8,128)(2,1)}), bf16[16,8,4096]{2,1,0:T(8,128)(2,1)S(1)}, u32[]{:S(2)}, u32[]{:S(2)}) async-start(bf16[16,8,4096]{2,1,0:T(8,128)(2,1)} %bitcast.3), calls=%async_computation | async-start | bytes 2097152 | tf_op jit(solution)/shard_map/all_to_all | solution.py:302
  10.5 2.7 %collective-permute-start = (bf16[1040,128]{1,0:T(8,128)(2,1)S(1)}, bf16[1040,128]{1,0:T(8,128)(2,1)S(1)}, u32[]{:S(2)}, u32[]{:S(2)}) collective-permute-start(bf16[1040,128]{1,0:T(8,128)(2,1)S(1)} %send.1.given), channel_id=1, source_target_pairs={{0,4},{4,0},{1,5},{5,1},{2,6},{6,2},{3,7},{7,3},{8,12},{12,8},{9,1... | collective-permute-start | bytes 798728 | tf_op jit(solution)/shard_map/ppermute | solution.py:436
  13.2 0.4 fusion
  13.6 0.2 copy.13
  13.7 14.9 %collective-permute-done.given = bf16[1040,128]{1,0:T(8,128)(2,1)S(1)} collective-permute-done((bf16[1040,128]{1,0:T(8,128)(2,1)S(1)}, bf16[1040,128]{1,0:T(8,128)(2,1)S(1)}, u32[]{:S(2)}, u32[]{:S(2)}) %collective-permute-start) | collective-permute-done | bytes 266272 | tf_op jit(solution)/shard_map/ppermute | solution.py:436
  28.6 1.6 %choose.3 = bf16[128,4096]{1,0:T(8,128)(2,1)} custom-call(s32[1]{0:T(128)} %bitcast.side, bf16[1040,128]{1,0:T(8,128)(2,1)S(1)} %collective-permute-done.given), custom_call_target="tpu_custom_call" | custom-call | flops 7000000000 | tf_op jit(solution)/shard_map/choose/pallas_call | solution.py:130
  30.2 0.8 all-to-all-done
  31.0 7.2 %all-to-all-start.1 = ((bf16[16,8,4096]{2,1,0:T(8,128)(2,1)}), bf16[16,8,4096]{2,1,0:T(8,128)(2,1)S(1)}, u32[]{:S(2)}, u32[]{:S(2)}) async-start(bf16[16,8,4096]{2,1,0:T(8,128)(2,1)} %bitcast.9), calls=%async_computation.1 | async-start | bytes 2097152 | tf_op jit(solution)/shard_map/all_to_all | solution.py:302
  38.2 1.1 last_block.1.refs_1_
  39.3 1.3 %collective-permute-start.2 = (bf16[64,4096]{1,0:T(8,128)(2,1)S(1)}, bf16[64,4096]{1,0:T(8,128)(2,1)S(1)}, u32[]{:S(2)}, u32[]{:S(2)}) collective-permute-start(bf16[64,4096]{1,0:T(8,128)(2,1)S(1)} %last_block.1.refs_1_), channel_id=1, source_target_pairs={{8,0},{16,8},{24,16},{9,1},{17,9},{25,17},{10,2},{18,10},{26,18},{... | collective-permute-start | bytes 1572872 | tf_op jit(solution)/shard_map/ppermute | solution.py:463
  40.6 3.1 %collective-permute-start.1 = (bf16[64,4096]{1,0:T(8,128)(2,1)S(1)}, bf16[64,4096]{1,0:T(8,128)(2,1)S(1)}, u32[]{:S(2)}, u32[]{:S(2)}) collective-permute-start(bf16[64,4096]{1,0:T(8,128)(2,1)S(1)} %last_block.1.refs_1_), channel_id=1, source_target_pairs={{0,8},{8,16},{16,24},{1,9},{9,17},{17,25},{2,10},{10,18},{18,26},{... | collective-permute-start | bytes 1572872 | tf_op jit(solution)/shard_map/ppermute | solution.py:463
  43.7 1.5 %collective-permute-done.1.refs_0_ = bf16[64,4096]{1,0:T(8,128)(2,1)S(1)} collective-permute-done((bf16[64,4096]{1,0:T(8,128)(2,1)S(1)}, bf16[64,4096]{1,0:T(8,128)(2,1)S(1)}, u32[]{:S(2)}, u32[]{:S(2)}) %collective-permute-start.1) | collective-permute-done | bytes 524320 | tf_op jit(solution)/shard_map/ppermute | solution.py:463
  45.2 0.8 copy-done.4
  46.0 11.8 %near.1 = f32[64,4096]{1,0:T(8,128)S(1)} custom-call(s32[8,16]{1,0:T(8,128)S(1)} %bitcast.24, s32[16]{0:T(128)S(1)} %copy-done.2, bf16[64,4096]{1,0:T(8,128)(2,1)} %copy-done.4, bf16[64,4096]{1,0:T(8,128)(2,1)} %copy-done, bf16[64,4096]{1,0:T(8,128)(2,1)} %copy-done.3, bf16[16,8,256,256]{3,2,1,0:T(8,128)(2,1)} %refs_3_.1), custom_call_target="tpu_custom_call" | custom-call | flops 1073741824 | bytes 20447232 | tf_op jit(solution)/shard_map/near/pallas_call | solution.py:178
  57.8 5.6 %far.1 = (f32[64,4096]{1,0:T(8,128)S(1)}, f32[32,8,128]{2,1,0:T(8,128)S(1)}, bf16[8,64,4096]{2,1,0:T(8,128)(2,1)S(1)}) custom-call(bf16[128,4096]{1,0:T(8,128)(2,1)S(1)} %bitcast.20, bf16[128,4096]{1,0:T(8,128)(2,1)S(1)} %bitcast.21, bf16[2,256,256]{2,1,0:T(8,128)(2,1)S(1)} %bitcast.22, f32[64,4096]{1,0:T(8,128)S(1)} %near.1, bf16[16,128,128]{2,1,0:T(8,128)(2,1)} %m2l_hbm.1, ...), custom_call_target="tpu_custom_call" | custom-call | tf_op jit(solution)/shard_map/far/pallas_call | solution.py:273
  63.4 24.6 %all_to_all.25.in_ref = f32[32,8,128]{2,1,0:T(8,128)S(1)} all-to-all(f32[32,8,128]{2,1,0:T(8,128)S(1)} %get-tuple-element.19), channel_id=1, replica_groups=mesh['gx'=4,'hi'=2,'lo'=4] {'gx','hi','lo'}, dimensions={0} | all-to-all | bytes 262144 | tf_op jit(solution)/shard_map/all_to_all | solution.py:302
  88.1 10.0 %all_to_all.26.sums = f32[32,8,128]{2,1,0:T(8,128)S(1)} all-to-all(f32[32,8,128]{2,1,0:T(8,128)S(1)} %add.88), channel_id=1, replica_groups=mesh['gx'=4,'hi'=2,'lo'=4] {'gx','hi','lo'}, dimensions={0} | all-to-all | bytes 262144 | tf_op jit(solution)/shard_map/all_to_all | solution.py:302
  98.1 2.1 %residual.1 = (bf16[128,4096]{1,0:T(8,128)(2,1)S(1)}, f32[32,128]{1,0:T(8,128)S(1)}, f32[512,64]{1,0:T(8,128)}) custom-call(f32[32,8,128]{2,1,0:T(8,128)S(1)} %all_to_all.26.sums, f32[64,4096]{1,0:T(8,128)S(1)} %get-tuple-element.20.image, bf16[8,64,4096]{2,1,0:T(8,128)(2,1)S(1)} %get-tuple-element.21.basis), custom_call_target="tpu_custom_call" | custom-call | tf_op jit(solution)/shard_map/residual/pallas_call | solution.py:351
  100.2 1.4 %collective-permute-start.3 = (f32[32,128]{1,0:T(8,128)S(1)}, f32[32,128]{1,0:T(8,128)S(1)}, u32[]{:S(2)}, u32[]{:S(2)}) collective-permute-start(f32[32,128]{1,0:T(8,128)S(1)} %get-tuple-element.22), channel_id=1, source_target_pairs={{0,4},{4,0},{1,5},{5,1},{2,6},{6,2},{3,7},{7,3},{8,12},{12,8},{9,1... | collective-permute-start | bytes 49160 | tf_op jit(solution)/shard_map/ppermute | solution.py:470
  101.5 3.3 %collective-permute-done.3 = f32[32,128]{1,0:T(8,128)S(1)} collective-permute-done((f32[32,128]{1,0:T(8,128)S(1)}, f32[32,128]{1,0:T(8,128)S(1)}, u32[]{:S(2)}, u32[]{:S(2)}) %collective-permute-start.3) | collective-permute-done | bytes 16416 | tf_op jit(solution)/shard_map/ppermute | solution.py:470
  104.9 9.8 %all_to_all.27.grams = f32[16,32,128]{2,1,0:T(8,128)S(1)} all-to-all(f32[16,32,128]{2,1,0:T(8,128)S(1)} %add.89), channel_id=1, replica_groups=mesh['gx'=4,'hi'=2,'lo'=4] {'gx','lo'}, dimensions={0} | all-to-all | bytes 524288 | tf_op jit(solution)/shard_map/all_to_all | solution.py:302
  114.7 6.5 %tail.1 = (bf16[64,4096]{1,0:T(8,128)(2,1)}, f32[64,64]{1,0:T(8,128)}) custom-call(f32[16,32,128]{2,1,0:T(8,128)S(1)} %all_to_all.27.grams, bf16[128,4096]{1,0:T(8,128)(2,1)S(1)} %get-tuple-element.23.resid), custom_call_target="tpu_custom_call" | custom-call | tf_op jit(solution)/shard_map/tail/pallas_call | solution.py:408
  (20 shorter events, 0.1 us)
Async XLA Ops:
  2.5 10.6 %copy-start.5 = (s32[16,32]{1,0:T(8,128)S(1)}, s32[16,32]{1,0:T(8,128)}, u32[]{:S(2)}) copy-start(s32[16,32]{1,0:T(8,128)} %param.18) | copy-start | bytes 6148
  2.6 10.6 %copy-start.6 = (s32[16,32]{1,0:T(8,128)S(1)}, s32[16,32]{1,0:T(8,128)}, u32[]{:S(2)}) copy-start(s32[16,32]{1,0:T(8,128)} %param.19) | copy-start | bytes 6148
  4.2 26.8 %all-to-all-start = ((bf16[16,8,4096]{2,1,0:T(8,128)(2,1)}), bf16[16,8,4096]{2,1,0:T(8,128)(2,1)S(1)}, u32[]{:S(2)}, u32[]{:S(2)}) async-start(bf16[16,8,4096]{2,1,0:T(8,128)(2,1)} %bitcast.3), calls=%async_computation | async-start | bytes 2097152 | tf_op jit(solution)/shard_map/all_to_all | solution.py:302
  10.5 18.1 %collective-permute-start = (bf16[1040,128]{1,0:T(8,128)(2,1)S(1)}, bf16[1040,128]{1,0:T(8,128)(2,1)S(1)}, u32[]{:S(2)}, u32[]{:S(2)}) collective-permute-start(bf16[1040,128]{1,0:T(8,128)(2,1)S(1)} %send.1.given), channel_id=1, source_target_pairs={{0,4},{4,0},{1,5},{5,1},{2,6},{6,2},{3,7},{7,3},{8,12},{12,8},{9,1... | collective-permute-start | bytes 798728 | tf_op jit(solution)/shard_map/ppermute | solution.py:436
  31.0 26.8 %all-to-all-start.1 = ((bf16[16,8,4096]{2,1,0:T(8,128)(2,1)}), bf16[16,8,4096]{2,1,0:T(8,128)(2,1)S(1)}, u32[]{:S(2)}, u32[]{:S(2)}) async-start(bf16[16,8,4096]{2,1,0:T(8,128)(2,1)} %bitcast.9), calls=%async_computation.1 | async-start | bytes 2097152 | tf_op jit(solution)/shard_map/all_to_all | solution.py:302
  38.2 7.8 %copy-start.1 = (s32[16,8]{0,1:T(8,128)S(1)}, s32[16,8]{0,1:T(8,128)}, u32[]{:S(2)}) copy-start(s32[16,8]{0,1:T(8,128)} %param.12) | copy-start | bytes 1540
  38.2 7.8 %copy-start.2 = (s32[16]{0:T(128)S(1)}, s32[16]{0:T(128)}, u32[]{:S(2)}) copy-start(s32[16]{0:T(128)} %count_ref.1) | copy-start | bytes 196
  39.3 5.9 %copy-start = (bf16[64,4096]{1,0:T(8,128)(2,1)}, bf16[64,4096]{1,0:T(8,128)(2,1)S(1)}, u32[]{:S(2)}) copy-start(bf16[64,4096]{1,0:T(8,128)(2,1)S(1)} %last_block.1.refs_1_) | copy-start | bytes 1572868
  39.3 4.4 %collective-permute-start.2 = (bf16[64,4096]{1,0:T(8,128)(2,1)S(1)}, bf16[64,4096]{1,0:T(8,128)(2,1)S(1)}, u32[]{:S(2)}, u32[]{:S(2)}) collective-permute-start(bf16[64,4096]{1,0:T(8,128)(2,1)S(1)} %last_block.1.refs_1_), channel_id=1, source_target_pairs={{8,0},{16,8},{24,16},{9,1},{17,9},{25,17},{10,2},{18,10},{26,18},{... | collective-permute-start | bytes 1572872 | tf_op jit(solution)/shard_map/ppermute | solution.py:463
  40.6 4.6 %collective-permute-start.1 = (bf16[64,4096]{1,0:T(8,128)(2,1)S(1)}, bf16[64,4096]{1,0:T(8,128)(2,1)S(1)}, u32[]{:S(2)}, u32[]{:S(2)}) collective-permute-start(bf16[64,4096]{1,0:T(8,128)(2,1)S(1)} %last_block.1.refs_1_), channel_id=1, source_target_pairs={{0,8},{8,16},{16,24},{1,9},{9,17},{17,25},{2,10},{10,18},{18,26},{... | collective-permute-start | bytes 1572872 | tf_op jit(solution)/shard_map/ppermute | solution.py:463
  43.7 1.5 %copy-start.3 = (bf16[64,4096]{1,0:T(8,128)(2,1)}, bf16[64,4096]{1,0:T(8,128)(2,1)S(1)}, u32[]{:S(2)}) copy-start(bf16[64,4096]{1,0:T(8,128)(2,1)S(1)} %collective-permute-done.2.refs_2_) | copy-start | bytes 1572868
  45.2 0.8 copy-start.4
  100.2 4.6 %collective-permute-start.3 = (f32[32,128]{1,0:T(8,128)S(1)}, f32[32,128]{1,0:T(8,128)S(1)}, u32[]{:S(2)}, u32[]{:S(2)}) collective-permute-start(f32[32,128]{1,0:T(8,128)S(1)} %get-tuple-element.22), channel_id=1, source_target_pairs={{0,4},{4,0},{1,5},{5,1},{2,6},{6,2},{3,7},{7,3},{8,12},{12,8},{9,1... | collective-permute-start | bytes 49160 | tf_op jit(solution)/shard_map/ppermute | solution.py:470

commit v14 on v10

--- a/solution.py
+++ b/solution.py
@@ -185,8 +185,8 @@
             ((m2l_hbm, m2l), (p2m_hbm, p2m), (basis_hbm, basis))
         )
     ]
-    moves[0].start()
-    moves[1].start()
+    for move in moves:
+        move.start()
     leaves, panels, terms = p2m.shape
     classes = m2l.shape[0]
     blocks, rhs, columns = basis.shape
@@ -195,8 +195,6 @@
     rows = ours.shape[0]
     recv[:rows], recv[rows:] = ours[...], theirs[...]
     for h in range(halves):
-        if h == halves - 1:
-            moves[2].start()
         for j in range(0, part, group):
             got = dot(pick[h], recv[:, j * terms : (j + group) * terms]).astype(BF16)
             for t in range(group):
@@ -377,13 +375,15 @@
     gram = jnp.concatenate([folded[:, :rhs], folded[:, rhs:]], axis=0)
     lower, inverse = factored(gram, done)
     factor_ref[...] = lower
-    coef = jnp.concatenate(split_parts(inverse), axis=0)
+    upper, lower = split_parts(inverse)
+    left = jnp.concatenate([upper, lower], axis=0)
+    right = jnp.concatenate([upper, jnp.zeros_like(upper)], axis=0)
+    coef = jnp.concatenate([left, right], axis=1)
     step = 1024
     for i in range(columns // step):
         cols = slice(i * step, (i + 1) * step)
-        first = dot(coef, resid[:rhs, cols])
-        second = dot(coef[:rhs], resid[rhs:, cols])
-        next_ref[:, cols] = (first[:rhs] + first[rhs:] + second).astype(BF16)
+        both = dot(coef, resid[:, cols])
+        next_ref[:, cols] = (both[:rhs] + both[rhs:]).astype(BF16)
 
 
 def tail(grams, resid):

time: 102 us -> 102 us (level)
  no operation moved by 1% of the time
where the time goes in v14:
time: 102 us
  Pallas kernels  31.1 us (30%)
  blocking collectives  29.7 us (29%)
  waiting for transfers between devices  21.3 us (21%)
  starting transfers between devices  18.3 us (18%)
    all_to_all x3, blocking collectives, exchange(): return lax.all_to_all(pieces, axes, split_axis=0, concat_axis=0, tiled=True)  29.7 us
    all_to_all x2, waiting for transfers between devices, exchange(): return lax.all_to_all(pieces, axes, split_axis=0, concat_axis=0, tiled=True)  17.4 us
    pallas_call x1, Pallas kernels, near_field(): pl.pallas_call(near_kernel, grid_spec=grid_spec, out_shape=jax.ShapeDtype...  11.8 us
    all_to_all x2, starting transfers between devices, exchange(): return lax.all_to_all(pieces, axes, split_axis=0, concat_axis=0, tiled=True)  7.72 us
    pallas_call x1, Pallas kernels, tail(): pl.pallas_call(tail_kernel, grid=(1,), out_shape=shapes, in_specs=[whole(...  6.36 us
    pallas_call x1, Pallas kernels, far_field(): pl.pallas_call(functools.partial(far_kernel, halves), grid=(1,), out_shap...  5.61 us
    ppermute x2, starting transfers between devices, shards(): before, after = (lax.ppermute(own, 'gx', up), lax.ppermute(own, 'gx', down))  5.13 us
    ppermute x1, starting transfers between devices, shards(): given = lax.ppermute(payload, 'hi', flip)  4.1 us
  transfers between devices with their start and end apart: 6, of which 4 were waited for; matrix products, arithmetic and copies ran while one was open for 1% of the time, Pallas kernels for 15%

profile of v14, /device:TPU:0, one launch (start us, length us, event | category | flops | bytes accessed | tf_op | source)
XLA Modules:
  0.0 101.8 jit_solution(6675460345403483048)
XLA Ops:
  0.6 1.9 %send.1 = (bf16[1040,128]{1,0:T(8,128)(2,1)S(1)}, bf16[64,4096]{1,0:T(8,128)(2,1)S(1)}) custom-call(bf16[8,64,4096]{2,1,0:T(8,128)(2,1)} %basis_hbm.1, bf16[16,256,128]{2,1,0:T(8,128)(2,1)} %p2m_hbm.1, s32[4,32]{1,0:T(4,128)} %bitcast.26, s32[1,32]{1,0:T(1,128)} %counts.1), custom_call_target="tpu_custom_call" | custom-call | tf_op jit(solution)/shard_map/send/pallas_call | solution.py:93
  2.6 0.0 copy-start
  2.6 4.1 %collective-permute-start = (bf16[1040,128]{1,0:T(8,128)(2,1)S(1)}, bf16[1040,128]{1,0:T(8,128)(2,1)S(1)}, u32[]{:S(2)}, u32[]{:S(2)}) collective-permute-start(bf16[1040,128]{1,0:T(8,128)(2,1)S(1)} %get-tuple-element.20.given), channel_id=1, source_target_pairs={{0,4},{4,0},{1,5},{5,1},{2,6},{6,2},{3,7},{7,3},{8,12},{12,8},{9,1... | collective-permute-start | bytes 798728 | tf_op jit(solution)/shard_map/ppermute | solution.py:424
  6.7 1.6 %choose.2 = bf16[128,4096]{1,0:T(8,128)(2,1)} custom-call(s32[1]{0:T(128)} %bitcast.side, bf16[1040,128]{1,0:T(8,128)(2,1)S(1)} %get-tuple-element.20.given), custom_call_target="tpu_custom_call" | custom-call | flops 70000001024 | tf_op jit(solution)/shard_map/choose/pallas_call | solution.py:116
  8.3 1.3 %collective-permute-start.2 = (bf16[64,4096]{1,0:T(8,128)(2,1)S(1)}, bf16[64,4096]{1,0:T(8,128)(2,1)S(1)}, u32[]{:S(2)}, u32[]{:S(2)}) collective-permute-start(bf16[64,4096]{1,0:T(8,128)(2,1)S(1)} %get-tuple-element.24.refs_1_), channel_id=1, source_target_pairs={{8,0},{16,8},{24,16},{9,1},{17,9},{25,17},{10,2},{18,10},{26,18},{... | collective-permute-start | bytes 1572872 | tf_op jit(solution)/shard_map/ppermute | solution.py:449
  9.6 3.9 %collective-permute-start.1 = (bf16[64,4096]{1,0:T(8,128)(2,1)S(1)}, bf16[64,4096]{1,0:T(8,128)(2,1)}, u32[]{:S(2)}, u32[]{:S(2)}) collective-permute-start(bf16[64,4096]{1,0:T(8,128)(2,1)S(1)} %get-tuple-element.24.refs_1_), channel_id=1, source_target_pairs={{0,8},{8,16},{16,24},{1,9},{9,17},{17,25},{2,10},{10,18},{18,26},{... | collective-permute-start | bytes 1572872 | tf_op jit(solution)/shard_map/ppermute | solution.py:449
  13.5 4.1 %all-to-all-start = ((bf16[16,8,4096]{2,1,0:T(8,128)(2,1)}), bf16[16,8,4096]{2,1,0:T(8,128)(2,1)S(1)}, u32[]{:S(2)}, u32[]{:S(2)}) async-start(bf16[16,8,4096]{2,1,0:T(8,128)(2,1)} %bitcast.3), calls=%async_computation | async-start | bytes 2097152 | tf_op jit(solution)/shard_map/all_to_all | solution.py:288
  17.6 0.4 fusion
  18.0 0.2 copy.13
  18.1 0.6 collective-permute-done.given
  18.8 1.6 %choose.3 = bf16[128,4096]{1,0:T(8,128)(2,1)} custom-call(s32[1]{0:T(128)} %bitcast.side, bf16[1040,128]{1,0:T(8,128)(2,1)S(1)} %collective-permute-done.given), custom_call_target="tpu_custom_call" | custom-call | flops 70000001024 | tf_op jit(solution)/shard_map/choose/pallas_call | solution.py:116
  20.4 0.0 collective-permute-done.2.refs_2_
  20.4 13.2 %all-to-all-done = bf16[16,8,4096]{2,1,0:T(8,128)(2,1)S(1)} async-done(((bf16[16,8,4096]{2,1,0:T(8,128)(2,1)}), bf16[16,8,4096]{2,1,0:T(8,128)(2,1)S(1)}, u32[]{:S(2)}, u32[]{:S(2)}) %all-to-all-start) | async-done | bytes 1048608 | tf_op jit(solution)/shard_map/all_to_all | solution.py:288
  33.6 3.7 %all-to-all-start.1 = ((bf16[16,8,4096]{2,1,0:T(8,128)(2,1)}), bf16[16,8,4096]{2,1,0:T(8,128)(2,1)S(1)}, u32[]{:S(2)}, u32[]{:S(2)}) async-start(bf16[16,8,4096]{2,1,0:T(8,128)(2,1)} %bitcast.9), calls=%async_computation.1 | async-start | bytes 2097152 | tf_op jit(solution)/shard_map/all_to_all | solution.py:288
  37.3 11.8 %near.1 = f32[64,4096]{1,0:T(8,128)S(1)} custom-call(s32[8,16]{1,0:T(8,128)S(1)} %bitcast.24, s32[16]{0:T(128)S(1)} %copy-done.2, bf16[64,4096]{1,0:T(8,128)(2,1)} %collective-permute-done.1.refs_0_, bf16[64,4096]{1,0:T(8,128)(2,1)} %copy-done, bf16[64,4096]{1,0:T(8,128)(2,1)} %copy-done.3, bf16[16,8,256,256]{3,2,1,0:T(8,128)(2,1)} %refs_3_.1), custom_call_target="tpu_custom_call" | custom-call | flops 1073741824 | bytes 20447232 | tf_op jit(solution)/shard_map/near/pallas_call | solution.py:164
  49.1 4.2 %all-to-all-done.1 = bf16[16,8,4096]{2,1,0:T(8,128)(2,1)S(1)} async-done(((bf16[16,8,4096]{2,1,0:T(8,128)(2,1)}), bf16[16,8,4096]{2,1,0:T(8,128)(2,1)S(1)}, u32[]{:S(2)}, u32[]{:S(2)}) %all-to-all-start.1) | async-done | bytes 1048608 | tf_op jit(solution)/shard_map/all_to_all | solution.py:288
  53.3 5.6 %far.1 = (f32[64,4096]{1,0:T(8,128)S(1)}, f32[32,8,128]{2,1,0:T(8,128)S(1)}, bf16[8,64,4096]{2,1,0:T(8,128)(2,1)S(1)}) custom-call(bf16[128,4096]{1,0:T(8,128)(2,1)S(1)} %bitcast.20, bf16[128,4096]{1,0:T(8,128)(2,1)S(1)} %bitcast.21, bf16[2,256,256]{2,1,0:T(8,128)(2,1)S(1)} %bitcast.22, f32[64,4096]{1,0:T(8,128)S(1)} %near.1, bf16[16,128,128]{2,1,0:T(8,128)(2,1)} %m2l_hbm.1, ...), custom_call_target="tpu_custom_call" | custom-call | tf_op jit(solution)/shard_map/far/pallas_call | solution.py:259
  58.9 9.9 %all_to_all.25.in_ref = f32[32,8,128]{2,1,0:T(8,128)S(1)} all-to-all(f32[32,8,128]{2,1,0:T(8,128)S(1)} %get-tuple-element.29), channel_id=1, replica_groups=mesh['gx'=4,'hi'=2,'lo'=4] {'gx','hi','lo'}, dimensions={0} | all-to-all | bytes 262144 | tf_op jit(solution)/shard_map/all_to_all | solution.py:288
  68.8 10.0 %all_to_all.26.sums = f32[32,8,128]{2,1,0:T(8,128)S(1)} all-to-all(f32[32,8,128]{2,1,0:T(8,128)S(1)} %add.88), channel_id=1, replica_groups=mesh['gx'=4,'hi'=2,'lo'=4] {'gx','hi','lo'}, dimensions={0} | all-to-all | bytes 262144 | tf_op jit(solution)/shard_map/all_to_all | solution.py:288
  78.9 2.1 %residual.1 = (bf16[128,4096]{1,0:T(8,128)(2,1)S(1)}, f32[32,128]{1,0:T(8,128)S(1)}, f32[512,64]{1,0:T(8,128)}) custom-call(f32[32,8,128]{2,1,0:T(8,128)S(1)} %all_to_all.26.sums, f32[64,4096]{1,0:T(8,128)S(1)} %get-tuple-element.30.image, bf16[8,64,4096]{2,1,0:T(8,128)(2,1)S(1)} %get-tuple-element.31.basis), custom_call_target="tpu_custom_call" | custom-call | tf_op jit(solution)/shard_map/residual/pallas_call | solution.py:337
  80.9 1.4 %collective-permute-start.3 = (f32[32,128]{1,0:T(8,128)S(1)}, f32[32,128]{1,0:T(8,128)S(1)}, u32[]{:S(2)}, u32[]{:S(2)}) collective-permute-start(f32[32,128]{1,0:T(8,128)S(1)} %get-tuple-element.32), channel_id=1, source_target_pairs={{0,4},{4,0},{1,5},{5,1},{2,6},{6,2},{3,7},{7,3},{8,12},{12,8},{9,1... | collective-permute-start | bytes 49160 | tf_op jit(solution)/shard_map/ppermute | solution.py:457
  82.3 3.3 %collective-permute-done.3 = f32[32,128]{1,0:T(8,128)S(1)} collective-permute-done((f32[32,128]{1,0:T(8,128)S(1)}, f32[32,128]{1,0:T(8,128)S(1)}, u32[]{:S(2)}, u32[]{:S(2)}) %collective-permute-start.3) | collective-permute-done | bytes 16416 | tf_op jit(solution)/shard_map/ppermute | solution.py:457
  85.6 9.8 %all_to_all.27.grams = f32[16,32,128]{2,1,0:T(8,128)S(1)} all-to-all(f32[16,32,128]{2,1,0:T(8,128)S(1)} %add.89), channel_id=1, replica_groups=mesh['gx'=4,'hi'=2,'lo'=4] {'gx','lo'}, dimensions={0} | all-to-all | bytes 524288 | tf_op jit(solution)/shard_map/all_to_all | solution.py:288
  95.4 6.4 %tail.1 = (bf16[64,4096]{1,0:T(8,128)(2,1)}, f32[64,64]{1,0:T(8,128)}) custom-call(f32[16,32,128]{2,1,0:T(8,128)S(1)} %all_to_all.27.grams, bf16[128,4096]{1,0:T(8,128)(2,1)S(1)} %get-tuple-element.33.resid), custom_call_target="tpu_custom_call" | custom-call | tf_op jit(solution)/shard_map/tail/pallas_call | solution.py:396
  (17 shorter events, 0.1 us)
Async XLA Ops:
  2.6 7.0 %copy-start = (bf16[64,4096]{1,0:T(8,128)(2,1)}, bf16[64,4096]{1,0:T(8,128)(2,1)S(1)}, u32[]{:S(2)}) copy-start(bf16[64,4096]{1,0:T(8,128)(2,1)S(1)} %get-tuple-element.24.refs_1_) | copy-start | bytes 1572868
  2.6 16.2 %collective-permute-start = (bf16[1040,128]{1,0:T(8,128)(2,1)S(1)}, bf16[1040,128]{1,0:T(8,128)(2,1)S(1)}, u32[]{:S(2)}, u32[]{:S(2)}) collective-permute-start(bf16[1040,128]{1,0:T(8,128)(2,1)S(1)} %get-tuple-element.20.given), channel_id=1, source_target_pairs={{0,4},{4,0},{1,5},{5,1},{2,6},{6,2},{3,7},{7,3},{8,12},{12,8},{9,1... | collective-permute-start | bytes 798728 | tf_op jit(solution)/shard_map/ppermute | solution.py:424
  6.7 10.9 %copy-start.4 = (s32[16,32]{1,0:T(8,128)S(1)}, s32[16,32]{1,0:T(8,128)}, u32[]{:S(2)}) copy-start(s32[16,32]{1,0:T(8,128)} %param.18) | copy-start | bytes 6148
  6.7 10.9 %copy-start.5 = (s32[16,32]{1,0:T(8,128)S(1)}, s32[16,32]{1,0:T(8,128)}, u32[]{:S(2)}) copy-start(s32[16,32]{1,0:T(8,128)} %param.19) | copy-start | bytes 6148
  8.3 12.1 %collective-permute-start.2 = (bf16[64,4096]{1,0:T(8,128)(2,1)S(1)}, bf16[64,4096]{1,0:T(8,128)(2,1)S(1)}, u32[]{:S(2)}, u32[]{:S(2)}) collective-permute-start(bf16[64,4096]{1,0:T(8,128)(2,1)S(1)} %get-tuple-element.24.refs_1_), channel_id=1, source_target_pairs={{8,0},{16,8},{24,16},{9,1},{17,9},{25,17},{10,2},{18,10},{26,18},{... | collective-permute-start | bytes 1572872 | tf_op jit(solution)/shard_map/ppermute | solution.py:449
  9.6 10.8 %collective-permute-start.1 = (bf16[64,4096]{1,0:T(8,128)(2,1)S(1)}, bf16[64,4096]{1,0:T(8,128)(2,1)}, u32[]{:S(2)}, u32[]{:S(2)}) collective-permute-start(bf16[64,4096]{1,0:T(8,128)(2,1)S(1)} %get-tuple-element.24.refs_1_), channel_id=1, source_target_pairs={{0,8},{8,16},{16,24},{1,9},{9,17},{17,25},{2,10},{10,18},{18,26},{... | collective-permute-start | bytes 1572872 | tf_op jit(solution)/shard_map/ppermute | solution.py:449
  13.5 20.2 %all-to-all-start = ((bf16[16,8,4096]{2,1,0:T(8,128)(2,1)}), bf16[16,8,4096]{2,1,0:T(8,128)(2,1)S(1)}, u32[]{:S(2)}, u32[]{:S(2)}) async-start(bf16[16,8,4096]{2,1,0:T(8,128)(2,1)} %bitcast.3), calls=%async_computation | async-start | bytes 2097152 | tf_op jit(solution)/shard_map/all_to_all | solution.py:288
  18.8 18.5 %copy-start.1 = (s32[16,8]{0,1:T(8,128)S(1)}, s32[16,8]{0,1:T(8,128)}, u32[]{:S(2)}) copy-start(s32[16,8]{0,1:T(8,128)} %param.12) | copy-start | bytes 1540
  18.8 18.5 %copy-start.2 = (s32[16]{0:T(128)S(1)}, s32[16]{0:T(128)}, u32[]{:S(2)}) copy-start(s32[16]{0:T(128)} %count_ref.1) | copy-start | bytes 196
  20.4 13.2 %copy-start.3 = (bf16[64,4096]{1,0:T(8,128)(2,1)}, bf16[64,4096]{1,0:T(8,128)(2,1)S(1)}, u32[]{:S(2)}) copy-start(bf16[64,4096]{1,0:T(8,128)(2,1)S(1)} %collective-permute-done.2.refs_2_) | copy-start | bytes 1572868
  33.6 19.7 %all-to-all-start.1 = ((bf16[16,8,4096]{2,1,0:T(8,128)(2,1)}), bf16[16,8,4096]{2,1,0:T(8,128)(2,1)S(1)}, u32[]{:S(2)}, u32[]{:S(2)}) async-start(bf16[16,8,4096]{2,1,0:T(8,128)(2,1)} %bitcast.9), calls=%async_computation.1 | async-start | bytes 2097152 | tf_op jit(solution)/shard_map/all_to_all | solution.py:288
  80.9 4.6 %collective-permute-start.3 = (f32[32,128]{1,0:T(8,128)S(1)}, f32[32,128]{1,0:T(8,128)S(1)}, u32[]{:S(2)}, u32[]{:S(2)}) collective-permute-start(f32[32,128]{1,0:T(8,128)S(1)} %get-tuple-element.32), channel_id=1, source_target_pairs={{0,4},{4,0},{1,5},{5,1},{2,6},{6,2},{3,7},{7,3},{8,12},{12,8},{9,1... | collective-permute-start | bytes 49160 | tf_op jit(solution)/shard_map/ppermute | solution.py:457
